TPU v7x, 32 devices: a whole 2x2x4 slice. The times are simulated.
32 devices in a mesh: dp: 8 (over z, x), mp: 4 (over y, core).
Axes of the slice: x: 2, y: 2, z: 4, core: 2. Of those that a mesh axis runs over, the one named last changes fastest.
Arguments:
- history: bfloat16 [13, 16384, 2048], P(None, 'dp', 'mp'), may hold values from -6 to 6
- depth_weights: float32 [13], replicated, may hold values from -1.5 to 1.5
- segment_ids: int32 [16, 1024], P('dp'), may hold values from 0 to 3, never falling along the last dimension, each value on 1 to 512 neighbouring positions
- first_gain: float32 [2048], P('mp'), may hold values from 0.5 to 1.5
- first_bias: float32 [2048], P('mp'), may hold values from -1.5 to 1.5
- qkv_weight: bfloat16 [2048, 6144], P(None, 'mp'), may hold values from -0.125 to 0.125
- out_weight: bfloat16 [2048, 2048], P('mp'), may hold values from -0.5 to 0.5
- second_gain: float32 [2048], P('mp'), may hold values from 0.5 to 1.5
- second_bias: float32 [2048], P('mp'), may hold values from -1.5 to 1.5
- up_weight: bfloat16 [2048, 8192], P(None, 'mp'), may hold values from -0.125 to 0.125
- up_bias: float32 [8192], P('mp'), may hold values from -1.5 to 1.5
- down_weight: bfloat16 [8192, 2048], P('mp'), may hold values from -0.0625 to 0.0625
- down_bias: float32 [2048], P('mp'), may hold values from -1.5 to 1.5
- cotangent: bfloat16 [16384, 2048], P('dp', 'mp'), may hold values from -7.2 to 7.2
Outputs:
- block_out: bfloat16 [16384, 2048], P('dp', 'mp')
- history_grad: bfloat16 [13, 16384, 2048], P(None, 'dp', 'mp')
- depth_grad: float32 [13], replicated
- first_gain_grad: float32 [2048], P('mp')
- first_bias_grad: float32 [2048], P('mp')
- qkv_weight_grad: float32 [2048, 6144], P('dp', 'mp')
- out_weight_grad: float32 [2048, 2048], P('mp', 'dp')
- second_gain_grad: float32 [2048], P('mp')
- second_bias_grad: float32 [2048], P('mp')
- up_weight_grad: float32 [2048, 8192], P('dp', 'mp')
- up_bias_grad: float32 [8192], P('mp')
- down_weight_grad: float32 [8192, 2048], P('mp', 'dp')
- down_bias_grad: float32 [2048], P('mp')
Inputs may be any that keep to these rules, and one draw needn't show every extreme that they name: `segment_ids`: segment numbers never fall along a packed row; in each row every document holds at most 512 tokens and one holds exactly that many.
All inputs are finite; a program needn't handle non-finite values.
Results may differ from a plain program's by a relative error of at most 0.015.
Values may be sent and summed in bfloat16 or wider, within the bound.
A program may use at most 384 MiB of HBM per device.

v0:
```python
import math

import jax
import jax.numpy as jnp
from jax import lax
from jax.sharding import PartitionSpec as P

HEAD = 128


EPSILON = 1e-05
EXACT = lax.Precision.HIGHEST
SQRT_HALF = 0.7071067811865476
INV_ROOT_TWO_PI = 0.3989422804014327


def gelu_value(up_proj):
    return 0.5 * up_proj * (1.0 + lax.erf(up_proj * SQRT_HALF))


def gelu_slope(up_proj):
    return 0.5 * (1.0 + lax.erf(up_proj * SQRT_HALF)) + up_proj * INV_ROOT_TWO_PI * jnp.exp(
        -0.5 * up_proj * up_proj
    )


def rope_tables(length, half_size):
    position = jnp.arange(length, dtype=jnp.float32)[:, None]
    rate = jnp.exp(jnp.arange(half_size, dtype=jnp.float32) * (-math.log(10000.0) / half_size))
    angle = position * rate[None, :]
    return (jnp.cos(angle)[:, None, :], jnp.sin(angle)[:, None, :])


def rotate(vector, cosine, sine):
    half_size = vector.shape[-1] // 2
    front_half = vector[..., :half_size]
    back_half = vector[..., half_size:]
    return jnp.concatenate(
        [front_half * cosine - back_half * sine, back_half * cosine + front_half * sine], -1
    )


def rotate_back(gradient, cosine, sine):
    half_size = gradient.shape[-1] // 2
    front_half = gradient[..., :half_size]
    back_half = gradient[..., half_size:]
    return jnp.concatenate(
        [front_half * cosine + back_half * sine, back_half * cosine - front_half * sine], -1
    )


def normalize(residual, gain_row, bias_row):
    local_width = residual.shape[1]
    full_width = local_width * lax.axis_size("mp")
    totals = lax.psum((jnp.sum(residual, 1), jnp.sum(residual * residual, 1)), "mp")
    row_mean = totals[0] / full_width
    inv_std = lax.rsqrt(totals[1] / full_width - row_mean * row_mean + EPSILON)
    scaled = (residual - row_mean[:, None]) * inv_std[:, None]
    normed = lax.all_gather(
        (scaled * gain_row + bias_row).astype(jnp.bfloat16), "mp", axis=1, tiled=True
    )
    return (normed, scaled, inv_std)


def normalize_back(gradient, scaled, inv_std, gain_row):
    full_width = gradient.shape[1] * lax.axis_size("mp")
    weighted = gradient * gain_row
    totals = lax.psum((jnp.sum(weighted, 1), jnp.sum(weighted * scaled, 1)), "mp")
    return inv_std[:, None] * (
        weighted - totals[0][:, None] / full_width - scaled * (totals[1][:, None] / full_width)
    )


def branch_partials(local_input, local_rows):
    return lax.psum_scatter(
        jnp.dot(local_input, local_rows, preferred_element_type=jnp.float32),
        "mp",
        scatter_dimension=1,
        tiled=True,
    )


def gather_grad(grad_low):
    return lax.all_gather(grad_low, "mp", axis=1, tiled=True)


def input_sum(partial_grad):
    return lax.psum_scatter(partial_grad, "mp", scatter_dimension=1, tiled=True)


def attend(query_vecs, key_vecs, value_vecs, seg_row, score_scale):
    length, heads, size = query_vecs.shape
    block_rows = min(512, length)
    block_count = length // block_rows
    positions = jnp.arange(length, dtype=jnp.int32)

    def score_block(pieces):
        q_block, seg_block, row_ids = pieces
        scores = (
            jnp.einsum("qhe,khe->hqk", q_block, key_vecs, preferred_element_type=jnp.float32)
            * score_scale
        )
        allowed = (seg_block[:, None] == seg_row[None, :]) & (
            positions[None, :] <= row_ids[:, None]
        )
        scores = jnp.where(allowed[None], scores, -1e30)
        row_max = jnp.max(scores, -1, keepdims=True)
        exp_scores = jnp.exp(scores - row_max)
        row_total = jnp.sum(exp_scores, -1, keepdims=True)
        probabilities = (exp_scores / row_total).astype(jnp.bfloat16)
        block_out = jnp.einsum(
            "hqk,khe->qhe", probabilities, value_vecs, preferred_element_type=jnp.float32
        )
        return (block_out, (row_max + jnp.log(row_total))[..., 0])

    block_outputs, log_totals = lax.map(
        score_block,
        (
            query_vecs.reshape(block_count, block_rows, heads, size),
            seg_row.reshape(block_count, block_rows),
            positions.reshape(block_count, block_rows),
        ),
    )
    return (block_outputs.reshape(length, heads, size), log_totals)


def attend_back(query_vecs, key_vecs, value_vecs, seg_row, log_totals, grad_att, score_scale):
    length, heads, size = query_vecs.shape
    block_rows = min(512, length)
    block_count = length // block_rows
    positions = jnp.arange(length, dtype=jnp.int32)

    def block_back(carry, pieces):
        key_grad, value_grad = carry
        q_block, seg_block, row_ids, total_block, g_block = pieces
        scores = (
            jnp.einsum("qhe,khe->hqk", q_block, key_vecs, preferred_element_type=jnp.float32)
            * score_scale
        )
        allowed = (seg_block[:, None] == seg_row[None, :]) & (
            positions[None, :] <= row_ids[:, None]
        )
        probabilities = jnp.where(allowed[None], jnp.exp(scores - total_block[:, :, None]), 0.0)
        value_grad = value_grad + jnp.einsum(
            "hqk,qhe->khe",
            probabilities.astype(jnp.bfloat16),
            g_block,
            preferred_element_type=jnp.float32,
        )
        prob_grad = jnp.einsum(
            "qhe,khe->hqk", g_block, value_vecs, preferred_element_type=jnp.float32
        )
        score_grad = (
            probabilities * (prob_grad - jnp.sum(prob_grad * probabilities, -1, keepdims=True))
        ).astype(jnp.bfloat16)
        query_grad = (
            jnp.einsum("hqk,khe->qhe", score_grad, key_vecs, preferred_element_type=jnp.float32)
            * score_scale
        )
        key_grad = (
            key_grad
            + jnp.einsum("hqk,qhe->khe", score_grad, q_block, preferred_element_type=jnp.float32)
            * score_scale
        )
        return ((key_grad, value_grad), query_grad)

    zero_grad = jnp.zeros((length, heads, size), jnp.float32)
    (key_grad, value_grad), query_grad = lax.scan(
        block_back,
        (zero_grad, zero_grad),
        (
            query_vecs.reshape(block_count, block_rows, heads, size),
            seg_row.reshape(block_count, block_rows),
            positions.reshape(block_count, block_rows),
            log_totals,
            grad_att.reshape(block_count, block_rows, heads, size),
        ),
    )
    return (query_grad.reshape(length, heads, size), key_grad, value_grad)


def local(
    history,
    depth_weights,
    segment_ids,
    first_gain,
    first_bias,
    qkv_weight,
    out_weight,
    second_gain,
    second_bias,
    up_weight,
    up_bias,
    down_weight,
    down_bias,
    cotangent,
):
    hist_count, tok_rows, local_width = history.shape
    row_count, length = segment_ids.shape
    heads_here = qkv_weight.shape[1] // (3 * HEAD)
    score_scale = HEAD ** (-0.5)
    cosine, sine = rope_tables(length, HEAD // 2)

    def row_step(carry, row_index):
        weight_sums, vector_parts, grad_hist = carry
        row_start = row_index * length
        hist_here = lax.dynamic_slice_in_dim(history, row_start, length, 1).astype(jnp.float32)
        seg_row = lax.dynamic_index_in_dim(segment_ids, row_index, 0, keepdims=False)
        residual = jnp.einsum("j,jtd->td", depth_weights, hist_here, precision=EXACT)
        normed1, scaled1, inv_std1 = normalize(residual, first_gain, first_bias)
        projected = jnp.dot(normed1, qkv_weight, preferred_element_type=jnp.float32).reshape(
            length, heads_here, 3, HEAD
        )
        query_vecs = rotate(projected[:, :, 0], cosine, sine).astype(jnp.bfloat16)
        key_vecs = rotate(projected[:, :, 1], cosine, sine).astype(jnp.bfloat16)
        value_vecs = projected[:, :, 2].astype(jnp.bfloat16)
        attended, log_totals = attend(query_vecs, key_vecs, value_vecs, seg_row, score_scale)
        attended = attended.reshape(length, heads_here * HEAD).astype(jnp.bfloat16)
        attn_branch = branch_partials(attended, out_weight)
        hidden = residual + attn_branch
        normed2, scaled2, inv_std2 = normalize(hidden, second_gain, second_bias)
        up_proj = jnp.dot(normed2, up_weight, preferred_element_type=jnp.float32) + up_bias
        activated = gelu_value(up_proj).astype(jnp.bfloat16)
        mlp_branch = branch_partials(activated, down_weight)
        output = hidden + (mlp_branch + down_bias)
        grad_out = lax.dynamic_slice_in_dim(cotangent, row_start, length, 0).astype(jnp.float32)
        mlp_low = grad_out.astype(jnp.bfloat16)
        down_bias_part = jnp.sum(mlp_low.astype(jnp.float32), 0)
        mlp_full = gather_grad(mlp_low)
        down_weight_part = jnp.einsum(
            "tf,td->fd", activated, mlp_full, preferred_element_type=jnp.float32
        )
        up_grad = (
            jnp.einsum("td,fd->tf", mlp_full, down_weight, preferred_element_type=jnp.float32)
            * gelu_slope(up_proj)
        ).astype(jnp.bfloat16)
        up_bias_part = jnp.sum(up_grad.astype(jnp.float32), 0)
        up_weight_part = jnp.einsum(
            "td,tf->df", normed2, up_grad, preferred_element_type=jnp.float32
        )
        normed2_grad = input_sum(
            jnp.einsum("tf,df->td", up_grad, up_weight, preferred_element_type=jnp.float32)
        )
        second_gain_part = jnp.sum(normed2_grad * scaled2, 0)
        second_bias_part = jnp.sum(normed2_grad, 0)
        hidden_grad = grad_out + normalize_back(normed2_grad, scaled2, inv_std2, second_gain)
        branch_low = hidden_grad.astype(jnp.bfloat16)
        branch_full = gather_grad(branch_low)
        out_weight_part = jnp.einsum(
            "tc,td->cd", attended, branch_full, preferred_element_type=jnp.float32
        )
        attended_grad = (
            jnp.einsum("td,cd->tc", branch_full, out_weight, preferred_element_type=jnp.float32)
            .astype(jnp.bfloat16)
            .reshape(length, heads_here, HEAD)
        )
        query_grad, key_grad, value_grad = attend_back(
            query_vecs, key_vecs, value_vecs, seg_row, log_totals, attended_grad, score_scale
        )
        qkv_grad = (
            jnp.stack(
                [
                    rotate_back(query_grad, cosine, sine),
                    rotate_back(key_grad, cosine, sine),
                    value_grad,
                ],
                2,
            )
            .reshape(length, 3 * heads_here * HEAD)
            .astype(jnp.bfloat16)
        )
        qkv_weight_part = jnp.einsum(
            "td,tc->dc", normed1, qkv_grad, preferred_element_type=jnp.float32
        )
        normed1_grad = input_sum(
            jnp.einsum("tc,dc->td", qkv_grad, qkv_weight, preferred_element_type=jnp.float32)
        )
        first_gain_part = jnp.sum(normed1_grad * scaled1, 0)
        first_bias_part = jnp.sum(normed1_grad, 0)
        residual_grad = hidden_grad + normalize_back(normed1_grad, scaled1, inv_std1, first_gain)
        depth_part = jnp.einsum("td,jtd->j", residual_grad, hist_here, precision=EXACT)
        history_rows_grad = (depth_weights[:, None, None] * residual_grad[None]).astype(
            jnp.bfloat16
        )
        grad_hist = lax.dynamic_update_slice_in_dim(grad_hist, history_rows_grad, row_start, 1)
        weight_terms = (qkv_weight_part, out_weight_part, up_weight_part, down_weight_part)
        vector_terms = (
            up_bias_part,
            down_bias_part,
            first_gain_part,
            first_bias_part,
            second_gain_part,
            second_bias_part,
            depth_part,
        )
        weight_sums = jax.tree.map(jnp.add, weight_sums, weight_terms)
        vector_parts = jax.tree.map(jnp.add, vector_parts, vector_terms)
        return ((weight_sums, vector_parts, grad_hist), output.astype(jnp.bfloat16))

    weight_init = tuple(
        (
            jnp.zeros(matrix.shape, jnp.float32)
            for matrix in (qkv_weight, out_weight, up_weight, down_weight)
        )
    )
    vector_init = (
        jnp.zeros(up_bias.shape, jnp.float32),
        jnp.zeros(down_bias.shape, jnp.float32),
        jnp.zeros(first_gain.shape, jnp.float32),
        jnp.zeros(first_bias.shape, jnp.float32),
        jnp.zeros(second_gain.shape, jnp.float32),
        jnp.zeros(second_bias.shape, jnp.float32),
        jnp.zeros(depth_weights.shape, jnp.float32),
    )
    initial = (weight_init, vector_init, jnp.zeros(history.shape, jnp.bfloat16))
    (weight_sums, vector_parts, grad_hist), row_outputs = lax.scan(
        row_step, initial, jnp.arange(row_count, dtype=jnp.int32)
    )
    weight_sums = (
        lax.psum_scatter(
            weight_sums[0].astype(jnp.bfloat16), "dp", scatter_dimension=0, tiled=True
        ).astype(jnp.float32),
        lax.psum_scatter(
            weight_sums[1].astype(jnp.bfloat16), "dp", scatter_dimension=1, tiled=True
        ).astype(jnp.float32),
        lax.psum_scatter(
            weight_sums[2].astype(jnp.bfloat16), "dp", scatter_dimension=0, tiled=True
        ).astype(jnp.float32),
        lax.psum_scatter(
            weight_sums[3].astype(jnp.bfloat16), "dp", scatter_dimension=1, tiled=True
        ).astype(jnp.float32),
    )
    vector_totals = lax.psum(
        (
            vector_parts[0],
            vector_parts[1],
            vector_parts[2],
            vector_parts[3],
            vector_parts[4],
            vector_parts[5],
            vector_parts[6],
        ),
        "dp",
    )
    depth_grad = lax.psum(vector_totals[6], "mp")
    qkv_total, out_total, up_total, down_total = weight_sums
    return (
        row_outputs.reshape(tok_rows, local_width),
        grad_hist,
        depth_grad,
        vector_totals[2],
        vector_totals[3],
        qkv_total,
        out_total,
        vector_totals[4],
        vector_totals[5],
        up_total,
        vector_totals[0],
        down_total,
        vector_totals[1],
    )


def solution(mesh):
    placed = (
        P(None, "dp", "mp"),
        P(),
        P("dp", None),
        P("mp"),
        P("mp"),
        P(None, "mp"),
        P("mp", None),
        P("mp"),
        P("mp"),
        P(None, "mp"),
        P("mp"),
        P("mp", None),
        P("mp"),
        P("dp", "mp"),
    )
    return jax.shard_map(
        local,
        mesh=mesh,
        in_specs=placed,
        out_specs=(
            P("dp", "mp"),
            P(None, "dp", "mp"),
            P(),
            P("mp"),
            P("mp"),
            P("dp", "mp"),
            P("mp", "dp"),
            P("mp"),
            P("mp"),
            P("dp", "mp"),
            P("mp"),
            P("mp", "dp"),
            P("mp"),
        ),
        check_vma=False,
    )
```

profile of v0, /device:TPU:0, one launch (start us, length us, event | category | flops | bytes accessed | tf_op | source)
XLA Modules:
  0.0 1808.2 jit_solution(10778167412355204521)
XLA Ops:
  8.8 9.2 broadcast_in_dim.52
  17.9 1285.5 %while.77 = (s32[]{:T(128)}, f32[2048,1536]{1,0:T(8,128)}, f32[512,2048]{1,0:T(8,128)}, f32[2048,2048]{1,0:T(8,128)}, f32[2048,2048]{1,0:T(8,128)}, /*index=5*/f...) while((s32[]{:T(128)}, f32[2048,1536]{1,0:T(8,128)}, ...), condition=%wide.region_34.35_spmd.clone.clone.clone.clone, body=%wide.region_0.34_spmd.clone.clone.clone.clone.sunk | while | flops 81362501632 | bytes 1012743296 | solution.py:316
  26.9 45.4 %fusion.180 = f32[1,1024,512]{2,0,1:T(1,128)S(1)} fusion(bf16[13,1024,512]{2,1,0:T(8,128)(2,1)S(1)} %constant_dynamic-slice_fusion.14, f32[13]{0:T(128)} %get-tuple-element.1679), kind=kOutput, calls=%fused_computation.56.clone.1 | convolution fusion | flops 81788928 | bytes 15728692 | tf_op jit(solution)/shard_map/while/body/eval_jaxpr/j,jtd->td/dot_general | solution.py:209
  89.0 29.2 %all-gather.5.cloned.1.call-done = bf16[1024,2048]{1,0:T(8,128)(2,1)} async-done(((bf16[1024,512]{1,0:T(8,128)(2,1)}), bf16[1024,2048]{1,0:T(8,128)(2,1)}) %all-gather.5.cloned.1.call-update) | async-done | bytes 4194320 | tf_op jit(solution)/shard_map/while/body/eval_jaxpr/all_gather | solution.py:59
  118.2 10.1 fusion.181
  141.6 18.3 %while.78 = (s32[]{:T(128)}, bf16[2,512,4,128]{3,1,2,0:T(8,128)(2,1)}, f32[2,4,512]{2,1,0:T(4,128)S(1)}, s32[2,512]{1,0:T(2,128)S(1)}, s32[1024]{0:T(1024)S(1)},...) while((s32[]{:T(128)}, ...), condition=%wide.region_8.8_spmd.clone, body=%wide.region_5.7_spmd.clone.sunk | while | flops 1100478464 | bytes 39403700 | solution.py:116
  171.0 71.8 %reduce-scatter.17.cloned.1.call-done = f32[1024,512]{1,0:T(8,128)} async-done(((f32[1024,2048]{1,0:T(8,128)}), f32[1024,512]{1,0:T(8,128)}) %reduce-scatter.17.cloned.1.call-update) | async-done | bytes 2097168 | tf_op jit(solution)/shard_map/while/body/eval_jaxpr/reduce_scatter | solution.py:75
  256.9 33.8 %all-gather.7.cloned.1.call-done = bf16[1024,2048]{1,0:T(8,128)(2,1)} async-done(((bf16[1024,512]{1,0:T(8,128)(2,1)}), bf16[1024,2048]{1,0:T(8,128)(2,1)}) %all-gather.7.cloned.1.call-update) | async-done | bytes 4194320 | tf_op jit(solution)/shard_map/while/body/eval_jaxpr/all_gather | solution.py:59
  290.7 15.8 multiply_convert_fusion.5
  306.5 20.8 %all-gather.9.cloned.1.call-done = bf16[1024,2048]{1,0:T(8,128)(2,1)} async-done(((bf16[1024,512]{1,0:T(8,128)(2,1)}), bf16[1024,2048]{1,0:T(8,128)(2,1)}) %all-gather.9.cloned.1.call-update) | async-done | bytes 4194320 | tf_op jit(solution)/shard_map/while/body/eval_jaxpr/all_gather | solution.py:84
  327.3 16.9 convert_reduce_fusion.5
  346.2 13.7 fusion.185
  360.0 71.9 %reduce-scatter.19.cloned.1.call-done = f32[1024,512]{1,0:T(8,128)} async-done(((f32[1024,2048]{1,0:T(8,128)}), f32[1024,512]{1,0:T(8,128)}) %reduce-scatter.19.cloned.1.call-update) | async-done | bytes 2097168 | tf_op jit(solution)/shard_map/while/body/eval_jaxpr/reduce_scatter | solution.py:88
  444.5 14.5 fusion.191
  459.2 21.1 %all-gather.11.cloned.1.call-done = bf16[1024,2048]{1,0:T(8,128)(2,1)} async-done(((bf16[1024,512]{1,0:T(8,128)(2,1)}), bf16[1024,2048]{1,0:T(8,128)(2,1)}) %all-gather.11.cloned.1.call-update) | async-done | bytes 4194320 | tf_op jit(solution)/shard_map/while/body/eval_jaxpr/all_gather | solution.py:84
  489.0 38.0 %while.79 = (s32[]{:T(128)}, f32[1024,4,128]{0,2,1:T(8,128)S(1)}, f32[1024,4,128]{0,2,1:T(8,128)}, f32[2,512,4,128]{3,1,0,2:T(8,128)}, bf16[2,512,4,128]{3,1,2,0...) while((s32[]{:T(128)}, f32[1024,4,128]{0,2,1:T(8,128)S(1)}, ...), condition=%wide.region_21.21_spmd.clone.clone, body=%wide.region_19.20_spmd.clone.sunk.clone.sunk | while | flops 2720266240 | bytes 105980192 | solution.py:168
  543.7 9.1 fusion.188
  553.6 17.2 select_add_fusion.20
  571.0 13.1 select_add_fusion.21
  592.0 10.6 select_add_fusion.18
  602.6 26.4 %reduce-scatter.21.cloned.1.call-done = f32[1024,512]{1,0:T(8,128)} async-done(((f32[1024,2048]{1,0:T(8,128)}), f32[1024,512]{1,0:T(8,128)}) %reduce-scatter.21.cloned.1.call-update) | async-done | bytes 2097168 | tf_op jit(solution)/shard_map/while/body/eval_jaxpr/reduce_scatter | solution.py:88
  650.1 9.5 fusion.190
  669.2 45.2 %fusion.180 = f32[1,1024,512]{2,0,1:T(1,128)S(1)} fusion(bf16[13,1024,512]{2,1,0:T(8,128)(2,1)S(1)} %constant_dynamic-slice_fusion.14, f32[13]{0:T(128)} %get-tuple-element.1679), kind=kOutput, calls=%fused_computation.56.clone.1 | convolution fusion | flops 81788928 | bytes 15728692 | tf_op jit(solution)/shard_map/while/body/eval_jaxpr/j,jtd->td/dot_general | solution.py:209
  728.3 30.4 %all-gather.5.cloned.1.call-done = bf16[1024,2048]{1,0:T(8,128)(2,1)} async-done(((bf16[1024,512]{1,0:T(8,128)(2,1)}), bf16[1024,2048]{1,0:T(8,128)(2,1)}) %all-gather.5.cloned.1.call-update) | async-done | bytes 4194320 | tf_op jit(solution)/shard_map/while/body/eval_jaxpr/all_gather | solution.py:59
  758.7 10.1 fusion.181
  782.1 18.3 %while.78 = (s32[]{:T(128)}, bf16[2,512,4,128]{3,1,2,0:T(8,128)(2,1)}, f32[2,4,512]{2,1,0:T(4,128)S(1)}, s32[2,512]{1,0:T(2,128)S(1)}, s32[1024]{0:T(1024)S(1)},...) while((s32[]{:T(128)}, ...), condition=%wide.region_8.8_spmd.clone, body=%wide.region_5.7_spmd.clone.sunk | while | flops 1100478464 | bytes 39403700 | solution.py:116
  811.5 71.8 %reduce-scatter.17.cloned.1.call-done = f32[1024,512]{1,0:T(8,128)} async-done(((f32[1024,2048]{1,0:T(8,128)}), f32[1024,512]{1,0:T(8,128)}) %reduce-scatter.17.cloned.1.call-update) | async-done | bytes 2097168 | tf_op jit(solution)/shard_map/while/body/eval_jaxpr/reduce_scatter | solution.py:75
  897.4 33.9 %all-gather.7.cloned.1.call-done = bf16[1024,2048]{1,0:T(8,128)(2,1)} async-done(((bf16[1024,512]{1,0:T(8,128)(2,1)}), bf16[1024,2048]{1,0:T(8,128)(2,1)}) %all-gather.7.cloned.1.call-update) | async-done | bytes 4194320 | tf_op jit(solution)/shard_map/while/body/eval_jaxpr/all_gather | solution.py:59
  931.3 15.8 multiply_convert_fusion.5
  947.1 20.8 %all-gather.9.cloned.1.call-done = bf16[1024,2048]{1,0:T(8,128)(2,1)} async-done(((bf16[1024,512]{1,0:T(8,128)(2,1)}), bf16[1024,2048]{1,0:T(8,128)(2,1)}) %all-gather.9.cloned.1.call-update) | async-done | bytes 4194320 | tf_op jit(solution)/shard_map/while/body/eval_jaxpr/all_gather | solution.py:84
  967.8 16.9 convert_reduce_fusion.5
  986.8 13.7 fusion.185
  1000.6 71.8 %reduce-scatter.19.cloned.1.call-done = f32[1024,512]{1,0:T(8,128)} async-done(((f32[1024,2048]{1,0:T(8,128)}), f32[1024,512]{1,0:T(8,128)}) %reduce-scatter.19.cloned.1.call-update) | async-done | bytes 2097168 | tf_op jit(solution)/shard_map/while/body/eval_jaxpr/reduce_scatter | solution.py:88
  1085.0 14.5 fusion.191
  1099.7 21.1 %all-gather.11.cloned.1.call-done = bf16[1024,2048]{1,0:T(8,128)(2,1)} async-done(((bf16[1024,512]{1,0:T(8,128)(2,1)}), bf16[1024,2048]{1,0:T(8,128)(2,1)}) %all-gather.11.cloned.1.call-update) | async-done | bytes 4194320 | tf_op jit(solution)/shard_map/while/body/eval_jaxpr/all_gather | solution.py:84
  1129.5 38.1 %while.79 = (s32[]{:T(128)}, f32[1024,4,128]{0,2,1:T(8,128)S(1)}, f32[1024,4,128]{0,2,1:T(8,128)}, f32[2,512,4,128]{3,1,0,2:T(8,128)}, bf16[2,512,4,128]{3,1,2,0...) while((s32[]{:T(128)}, f32[1024,4,128]{0,2,1:T(8,128)S(1)}, ...), condition=%wide.region_21.21_spmd.clone.clone, body=%wide.region_19.20_spmd.clone.sunk.clone.sunk | while | flops 2720266240 | bytes 105980192 | solution.py:168
  1184.3 9.1 fusion.188
  1194.2 19.1 %select_add_fusion.20 = f32[2048,2048]{1,0:T(8,128)} fusion(f32[2048,2048]{1,0:T(8,128)} %get-tuple-element.1628, pred[]{:T(512)S(6)} %compare.10, bf16[1024,2048]{1,0:T(8,128)(2,1)} %all-gather.7.cloned.1.call-done, bf16[1024,2048]{1,0:T(8,128)(2,1)} %copy-done.70), kind=kOutput, calls=%fused_computation.59.clone.1 | convolution fusion | flops 8598323200 | bytes 41943040 | tf_op jit(solution)/shard_map/while/body/eval_jaxpr/td,tf->df/dot_general | solution.py:238
  1213.4 16.6 select_add_fusion.21
  1240.4 13.8 select_add_fusion.18
  1254.1 15.1 reduce-scatter.21.cloned.1.call-done
  1290.3 9.5 fusion.190
  1315.4 9.3 convert_element_type.87
  1324.8 9.3 convert_element_type.89
  1334.9 38.0 %all-reduce.4 = (f32[13]{0:T(128)S(1)}, f32[512]{0:T(512)}, f32[512]{0:T(512)}, f32[512]{0:T(512)}, f32[512]{0:T(512)}, /*index=5*/f32[2048]{0:T(1024)}, f32[512]{0:T(512)}) all-reduce(f32[13]{0:T(128)S(1)} %copy-done.62, f32[512]{0:T(512)S(1)} %copy-done.51, f32[512]{0:T(512)S(1)} %copy-done.48, ...), channel_id=1, replica_groups=mesh['dp'=8,'mp'=4] {'dp'}, use_global_device_ids=true, to_apply=%region_35.36 | all-reduce | flops 4621 | bytes 36968 | tf_op jit(solution)/shard_map/psum | solution.py:333
  1381.2 116.3 %reduce-scatter.9.cloned.1.call-done = bf16[256,1536]{1,0:T(8,128)(2,1)} async-done(((bf16[2048,1536]{1,0:T(8,128)(2,1)}), bf16[256,1536]{1,0:T(8,128)(2,1)}) %reduce-scatter.9.cloned.1.call-update) | async-done | bytes 786448 | tf_op jit(solution)/shard_map/reduce_scatter | solution.py:320
  1500.0 147.3 %reduce-scatter.13.cloned.1.call-done = bf16[256,2048]{1,0:T(8,128)(2,1)} async-done(((bf16[2048,2048]{1,0:T(8,128)(2,1)}), bf16[256,2048]{1,0:T(8,128)(2,1)}) %reduce-scatter.13.cloned.1.call-update) | async-done | bytes 1048592 | tf_op jit(solution)/shard_map/reduce_scatter | solution.py:326
  1650.0 147.8 %reduce-scatter.15.cloned.1.call-done = bf16[2048,256]{1,0:T(8,128)(2,1)} async-done(((bf16[2048,2048]{1,0:T(8,128)(2,1)}), bf16[2048,256]{1,0:T(8,128)(2,1)}) %reduce-scatter.15.cloned.1.call-update) | async-done | bytes 1048592 | tf_op jit(solution)/shard_map/reduce_scatter | solution.py:329
  (546 shorter events, 403.6 us)
Async XLA Ops:
  18.2 69.0 %copy-start.63 = (f32[64]{0:T(128)}, f32[64]{0:T(128)S(1)}, u32[]{:S(2)}) copy-start(f32[64]{0:T(128)S(1)} %get-tuple-element.1692) | copy-start | bytes 772 | tf_op jit(solution)/shard_map/while
  18.2 100.0 %all-gather.5.cloned.1.call-start = ((), (), s32[]{:S(2)}) async-start(), calls=%async_computation.12 | async-start | bytes 5242880 | tf_op jit(solution)/shard_map/while/body/eval_jaxpr/all_gather | solution.py:59
  72.3 56.0 %copy-start = (f32[1,1024,512]{2,0,1:T(1,128)}, f32[1,1024,512]{2,0,1:T(1,128)S(1)}, u32[]{:S(2)}) copy-start(f32[1,1024,512]{2,0,1:T(1,128)S(1)} %fusion.180) | copy-start | bytes 6291460 | tf_op jit(solution)/shard_map/while
  83.3 159.6 %reduce-scatter.17.cloned.1.call-start = ((), (), s32[]{:S(2)}) async-start(), calls=%async_computation.13 | async-start | bytes 10485760 | tf_op jit(solution)/shard_map/while/body/eval_jaxpr/reduce_scatter | solution.py:75
  88.9 42.5 %copy-start.17 = (f32[1024,64]{0,1:T(8,128)}, f32[1024,64]{0,1:T(8,128)S(1)}, u32[]{:S(2)}) copy-start(f32[1024,64]{0,1:T(8,128)S(1)} %get-tuple-element.1433) | copy-start | bytes 786436 | tf_op jit(solution)/shard_map/while
  171.0 71.9 %copy-start.1 = (f32[1,1024,512]{2,0,1:T(1,128)S(1)}, f32[1,1024,512]{2,0,1:T(1,128)}, u32[]{:S(2)}) copy-start(f32[1,1024,512]{2,0,1:T(1,128)} %copy-done) | copy-start | bytes 6291460 | tf_op jit(solution)/shard_map/while
  171.0 119.7 %all-gather.7.cloned.1.call-start = ((), (), s32[]{:S(2)}) async-start(), calls=%async_computation.14 | async-start | bytes 5242880 | tf_op jit(solution)/shard_map/while/body/eval_jaxpr/all_gather | solution.py:59
  255.0 72.3 %all-gather.9.cloned.1.call-start = ((), (), s32[]{:S(2)}) async-start(), calls=%async_computation.15 | async-start | bytes 5242880 | tf_op jit(solution)/shard_map/while/body/eval_jaxpr/all_gather | solution.py:84
  256.8 175.0 %reduce-scatter.19.cloned.1.call-start = ((), (), s32[]{:S(2)}) async-start(), calls=%async_computation.16 | async-start | bytes 10485760 | tf_op jit(solution)/shard_map/while/body/eval_jaxpr/reduce_scatter | solution.py:88
  359.9 71.9 %copy-start.5 = (f32[1024,512]{1,0:T(8,128)S(1)}, f32[1024,512]{1,0:T(8,128)}, u32[]{:S(2)}) copy-start(f32[1024,512]{1,0:T(8,128)} %get-tuple-element.1443) | copy-start | bytes 6291460 | tf_op jit(solution)/shard_map/while
  359.9 120.3 %all-gather.11.cloned.1.call-start = ((), (), s32[]{:S(2)}) async-start(), calls=%async_computation.17 | async-start | bytes 5242880 | tf_op jit(solution)/shard_map/while/body/eval_jaxpr/all_gather | solution.py:84
  444.5 139.7 %reduce-scatter.23.cloned.1.call-start = ((), (), s32[]{:S(2)}) async-start(), calls=%async_computation.19 | async-start | bytes 10485760 | tf_op jit(solution)/shard_map/while/body/eval_jaxpr/reduce_scatter | solution.py:75
  459.1 170.0 %reduce-scatter.21.cloned.1.call-start = ((), (), s32[]{:S(2)}) async-start(), calls=%async_computation.18 | async-start | bytes 10485760 | tf_op jit(solution)/shard_map/while/body/eval_jaxpr/reduce_scatter | solution.py:88
  553.6 17.3 copy-start.53
  553.6 17.3 copy-start.34
  553.6 17.3 copy-start.66
  553.6 17.3 copy-start.69
  592.0 37.1 %copy-start.2 = (f32[1,1024,512]{2,0,1:T(1,128)S(1)}, f32[1,1024,512]{2,0,1:T(1,128)}, u32[]{:S(2)}) copy-start(f32[1,1024,512]{2,0,1:T(1,128)} %copy-done) | copy-start | bytes 6291460 | tf_op jit(solution)/shard_map/while
  592.0 37.1 %copy-start.26 = (f32[1024]{0:T(1024)S(1)}, f32[1024]{0:T(1024)}, u32[]{:S(2)}) copy-start(f32[1024]{0:T(1024)} %copy-done.25) | copy-start | bytes 12292 | tf_op jit(solution)/shard_map/while
  592.0 37.1 %copy-start.28 = (f32[1024]{0:T(1024)S(1)}, f32[1024]{0:T(1024)}, u32[]{:S(2)}) copy-start(f32[1024]{0:T(1024)} %copy-done.27) | copy-start | bytes 12292 | tf_op jit(solution)/shard_map/while
  592.0 37.1 %copy-start.30 = (f32[512]{0:T(512)S(1)}, f32[512]{0:T(512)}, u32[]{:S(2)}) copy-start(f32[512]{0:T(512)} %get-tuple-element.1789) | copy-start | bytes 6148 | tf_op jit(solution)/shard_map/while
  660.5 66.0 %copy-start.63 = (f32[64]{0:T(128)}, f32[64]{0:T(128)S(1)}, u32[]{:S(2)}) copy-start(f32[64]{0:T(128)S(1)} %get-tuple-element.1692) | copy-start | bytes 772 | tf_op jit(solution)/shard_map/while
  660.5 98.2 %all-gather.5.cloned.1.call-start = ((), (), s32[]{:S(2)}) async-start(), calls=%async_computation.12 | async-start | bytes 5242880 | tf_op jit(solution)/shard_map/while/body/eval_jaxpr/all_gather | solution.py:59
  714.4 54.4 %copy-start = (f32[1,1024,512]{2,0,1:T(1,128)}, f32[1,1024,512]{2,0,1:T(1,128)S(1)}, u32[]{:S(2)}) copy-start(f32[1,1024,512]{2,0,1:T(1,128)S(1)} %fusion.180) | copy-start | bytes 6291460 | tf_op jit(solution)/shard_map/while
  722.6 160.8 %reduce-scatter.17.cloned.1.call-start = ((), (), s32[]{:S(2)}) async-start(), calls=%async_computation.13 | async-start | bytes 10485760 | tf_op jit(solution)/shard_map/while/body/eval_jaxpr/reduce_scatter | solution.py:75
  728.3 43.7 %copy-start.17 = (f32[1024,64]{0,1:T(8,128)}, f32[1024,64]{0,1:T(8,128)S(1)}, u32[]{:S(2)}) copy-start(f32[1024,64]{0,1:T(8,128)S(1)} %get-tuple-element.1433) | copy-start | bytes 786436 | tf_op jit(solution)/shard_map/while
  811.4 71.9 %copy-start.1 = (f32[1,1024,512]{2,0,1:T(1,128)S(1)}, f32[1,1024,512]{2,0,1:T(1,128)}, u32[]{:S(2)}) copy-start(f32[1,1024,512]{2,0,1:T(1,128)} %copy-done) | copy-start | bytes 6291460 | tf_op jit(solution)/shard_map/while
  811.5 119.8 %all-gather.7.cloned.1.call-start = ((), (), s32[]{:S(2)}) async-start(), calls=%async_computation.14 | async-start | bytes 5242880 | tf_op jit(solution)/shard_map/while/body/eval_jaxpr/all_gather | solution.py:59
  895.5 72.4 %all-gather.9.cloned.1.call-start = ((), (), s32[]{:S(2)}) async-start(), calls=%async_computation.15 | async-start | bytes 5242880 | tf_op jit(solution)/shard_map/while/body/eval_jaxpr/all_gather | solution.py:84
  897.3 175.0 %reduce-scatter.19.cloned.1.call-start = ((), (), s32[]{:S(2)}) async-start(), calls=%async_computation.16 | async-start | bytes 10485760 | tf_op jit(solution)/shard_map/while/body/eval_jaxpr/reduce_scatter | solution.py:88
  1000.5 71.9 %copy-start.5 = (f32[1024,512]{1,0:T(8,128)S(1)}, f32[1024,512]{1,0:T(8,128)}, u32[]{:S(2)}) copy-start(f32[1024,512]{1,0:T(8,128)} %get-tuple-element.1443) | copy-start | bytes 6291460 | tf_op jit(solution)/shard_map/while
  1000.5 120.2 %all-gather.11.cloned.1.call-start = ((), (), s32[]{:S(2)}) async-start(), calls=%async_computation.17 | async-start | bytes 5242880 | tf_op jit(solution)/shard_map/while/body/eval_jaxpr/all_gather | solution.py:84
  1085.0 145.1 %reduce-scatter.23.cloned.1.call-start = ((), (), s32[]{:S(2)}) async-start(), calls=%async_computation.19 | async-start | bytes 10485760 | tf_op jit(solution)/shard_map/while/body/eval_jaxpr/reduce_scatter | solution.py:75
  1099.6 169.7 %reduce-scatter.21.cloned.1.call-start = ((), (), s32[]{:S(2)}) async-start(), calls=%async_computation.18 | async-start | bytes 10485760 | tf_op jit(solution)/shard_map/while/body/eval_jaxpr/reduce_scatter | solution.py:88
  1194.2 19.1 %copy-start.53 = (f32[512]{0:T(512)}, f32[512]{0:T(512)S(1)}, u32[]{:S(2)}) copy-start(f32[512]{0:T(512)S(1)} %select_add_fusion.23) | copy-start | bytes 6148 | tf_op jit(solution)/shard_map/while
  1194.2 19.1 %copy-start.34 = (f32[2048]{0:T(1024)}, f32[2048]{0:T(1024)S(1)}, u32[]{:S(2)}) copy-start(f32[2048]{0:T(1024)S(1)} %select_add_fusion.22) | copy-start | bytes 24580 | tf_op jit(solution)/shard_map/while
  1194.2 19.1 %copy-start.66 = (bf16[1024,2048]{1,0:T(8,128)(2,1)S(1)}, bf16[1024,2048]{1,0:T(8,128)(2,1)}, u32[]{:S(2)}) copy-start(bf16[1024,2048]{1,0:T(8,128)(2,1)} %all-gather.9.cloned.1.call-done) | copy-start | bytes 12582916 | tf_op jit(solution)/shard_map/while
  1194.2 19.1 %copy-start.69 = (bf16[1024,2048]{1,0:T(8,128)(2,1)S(1)}, bf16[1024,2048]{1,0:T(8,128)(2,1)}, u32[]{:S(2)}) copy-start(bf16[1024,2048]{1,0:T(8,128)(2,1)} %get-tuple-element.1467) | copy-start | bytes 12582916 | tf_op jit(solution)/shard_map/while
  1213.4 16.7 copy-start.6
  1213.4 16.7 copy-start.55
  1240.3 29.0 %copy-start.2 = (f32[1,1024,512]{2,0,1:T(1,128)S(1)}, f32[1,1024,512]{2,0,1:T(1,128)}, u32[]{:S(2)}) copy-start(f32[1,1024,512]{2,0,1:T(1,128)} %copy-done) | copy-start | bytes 6291460 | tf_op jit(solution)/shard_map/while
  1240.3 29.0 %copy-start.26 = (f32[1024]{0:T(1024)S(1)}, f32[1024]{0:T(1024)}, u32[]{:S(2)}) copy-start(f32[1024]{0:T(1024)} %copy-done.25) | copy-start | bytes 12292 | tf_op jit(solution)/shard_map/while
  1240.3 28.9 %copy-start.28 = (f32[1024]{0:T(1024)S(1)}, f32[1024]{0:T(1024)}, u32[]{:S(2)}) copy-start(f32[1024]{0:T(1024)} %copy-done.27) | copy-start | bytes 12292 | tf_op jit(solution)/shard_map/while
  1240.3 28.9 %copy-start.30 = (f32[512]{0:T(512)S(1)}, f32[512]{0:T(512)}, u32[]{:S(2)}) copy-start(f32[512]{0:T(512)} %get-tuple-element.1789) | copy-start | bytes 6148 | tf_op jit(solution)/shard_map/while
  1303.4 76.0 %reduce-scatter.11.cloned.1.call-start = ((), (), s32[]{:S(2)}) async-start(), calls=%async_computation.9 | async-start | bytes 2359296 | tf_op jit(solution)/shard_map/reduce_scatter | solution.py:323
  1307.3 190.2 %reduce-scatter.9.cloned.1.call-start = ((), (), s32[]{:S(2)}) async-start(), calls=%async_computation.8 | async-start | bytes 7077888 | tf_op jit(solution)/shard_map/reduce_scatter | solution.py:320
  1315.3 331.9 %reduce-scatter.13.cloned.1.call-start = ((), (), s32[]{:S(2)}) async-start(), calls=%async_computation.10 | async-start | bytes 9437184 | tf_op jit(solution)/shard_map/reduce_scatter | solution.py:326
  1324.7 473.2 %reduce-scatter.15.cloned.1.call-start = ((), (), s32[]{:S(2)}) async-start(), calls=%async_computation.11 | async-start | bytes 9437184 | tf_op jit(solution)/shard_map/reduce_scatter | solution.py:329
  (118 other events, 624.6 us)
Sparse Core Ops, SparseCore 0:
  83.4 34.7 all-gather.4
  171.1 71.6 reduce-scatter.16
  255.1 35.5 all-gather.6
  292.8 34.4 all-gather.8
  360.1 71.7 reduce-scatter.18
  444.6 35.6 all-gather.10
  482.8 71.7 reduce-scatter.22
  557.3 71.6 reduce-scatter.20
  722.7 35.9 all-gather.4
  811.6 71.7 reduce-scatter.16
  895.6 35.6 all-gather.6
  933.3 34.4 all-gather.8
  1000.6 71.6 reduce-scatter.18
  1085.1 35.5 all-gather.10
  1123.2 71.7 reduce-scatter.22
  1197.5 71.6 reduce-scatter.20
Sparse Core Ops, SparseCore 1:
  1308.0 69.4 reduce-scatter.10
  1380.9 116.5 reduce-scatter.8
  1501.0 146.2 reduce-scatter.12
  1651.3 146.5 reduce-scatter.14
where the time goes:
time: 1810 us
  waiting for transfers between devices  952 us (53%)
  matrix products  452 us (25%)
  other arithmetic  177 us (10%)
  local copies, waits for them, and re-layouts  105 us (6%)
  blocking collectives  94.1 us (5%)
    reduce_scatter x4, waiting for transfers between devices, input_sum(): return lax.psum_scatter(partial_grad, 'mp', scatter_dimension=1, tiled=True)  185 us
    reduce_scatter x1, waiting for transfers between devices, local(): lax.psum_scatter(weight_sums[3].astype(jnp.bfloat16), 'dp', scatter_dimen...  148 us
    reduce_scatter x1, waiting for transfers between devices, local(): lax.psum_scatter(weight_sums[2].astype(jnp.bfloat16), 'dp', scatter_dimen...  147 us
    reduce_scatter x4, waiting for transfers between devices, branch_partials(): lax.psum_scatter(jnp.dot(local_input, local_rows, preferred_element_type=...  144 us
    all_gather x4, waiting for transfers between devices, normalize(): lax.all_gather((scaled * gain_row + bias_row).astype(jnp.bfloat16), 'mp',...  127 us
    reduce_scatter x1, waiting for transfers between devices, local(): lax.psum_scatter(weight_sums[0].astype(jnp.bfloat16), 'dp', scatter_dimen...  116 us
    dot_general x2, matrix products, row_step(): jnp.einsum('j,jtd->td', depth_weights, hist_here, precision=EXACT)  90.6 us
    all_gather x4, waiting for transfers between devices, gather_grad(): return lax.all_gather(grad_low, 'mp', axis=1, tiled=True)  83.7 us
  transfers between devices with their start and end apart: 20, of which 17 were waited for; matrix products, arithmetic and copies ran while one was open for 19% of the time, Pallas kernels for 0%

commit v1 on v0

v1 whole, which is shorter than its diff:
```python
import math

import jax
import jax.numpy as jnp
import numpy as np
from jax import lax
from jax.experimental import pallas as pl
from jax.experimental.pallas import tpu as pltpu
from jax.sharding import PartitionSpec as P

HEAD = 128
MAX_DOC = 512
EPSILON = 1e-05
SQRT_HALF = 0.7071067811865476
INV_ROOT_TWO_PI = 0.3989422804014327
LOG2E = 1.4426950408889634
SCALE = HEAD ** (-0.5)
MIB = 2**20
BF16 = jnp.bfloat16
F32 = jnp.float32


def dot_nn(a, b):
    return jnp.dot(a, b, preferred_element_type=F32)


def dot_nt(a, b):
    return lax.dot_general(a, b, (((1,), (1,)), ((), ())), preferred_element_type=F32)


def dot_tn(a, b):
    return lax.dot_general(a, b, (((0,), (0,)), ((), ())), preferred_element_type=F32)


def call(name, body, grid, args, in_specs, outs, out_specs, scratch=(), flops=0, trans=0, **kw):
    moved = sum(a.size * a.dtype.itemsize for a in args)
    moved += sum(math.prod(o.shape) * o.dtype.itemsize for o in outs)
    return pl.pallas_call(
        body,
        grid=grid,
        in_specs=in_specs,
        out_specs=out_specs,
        out_shape=outs,
        scratch_shapes=list(scratch),
        compiler_params=pltpu.CompilerParams(vmem_limit_bytes=60 * MIB),
        cost_estimate=pl.CostEstimate(flops=flops, bytes_accessed=moved, transcendentals=trans),
        name=name,
        **kw,
    )(*args)


def shape(dims, dtype):
    return jax.ShapeDtypeStruct(dims, dtype)


SMEM = pl.BlockSpec(memory_space=pltpu.SMEM)
ANY = pl.BlockSpec(memory_space=pl.ANY)


def rows_of(block):
    return pl.BlockSpec(block, lambda i: (i, 0))


def cols_of(block):
    return pl.BlockSpec(block, lambda i: (0, i))


def fixed(block):
    return pl.BlockSpec(block, lambda i: (0,) * len(block))


def start_all(copies):
    @pl.when(pl.program_id(0) == 0)
    def _():
        for one in copies:
            one.start()


def wait_all(copies):
    @pl.when(pl.program_id(0) == 0)
    def _():
        for one in copies:
            one.wait()


def row_blocks(me, n, width, source, target, sems, base):
    return [
        pltpu.make_async_copy(
            source.at[pl.ds(pl.multiple_of((me ^ j) * width, width), width), :],
            target.at[pl.ds(j * width, width), :],
            sems.at[base + j],
        )
        for j in range(n)
    ]


def col_blocks(me, n, width, source, target, sems, base):
    return [
        pltpu.make_async_copy(
            source.at[:, pl.ds(pl.multiple_of((me ^ j) * width, width), width)],
            target.at[:, pl.ds(j * width, width)],
            sems.at[base + j],
        )
        for j in range(n)
    ]


def stat_columns(first, second):
    lane = lax.broadcasted_iota(jnp.int32, (first.shape[0], 128), 1)
    return jnp.where(lane == 0, first, jnp.where(lane == 1, second, 0.0))


def fold_rows(values):
    return jnp.sum(values.reshape(values.shape[0] // 8, 8, values.shape[1]), 0)


def accumulate(ref, value):
    @pl.when(pl.program_id(0) == 0)
    def _():
        ref[...] = value

    @pl.when(pl.program_id(0) != 0)
    def _():
        ref[...] += value


def average_body(weights, history, wide, low):
    total = weights[0] * history[0].astype(F32)
    for j in range(1, history.shape[0]):
        total += weights[j] * history[j].astype(F32)
    wide[...] = total
    low[...] = total.astype(BF16)


def average(weights, history, row, length):
    count, _, width = history.shape
    tile = min(256, length)
    steps = length // tile
    return call(
        "average",
        average_body,
        (steps,),
        (weights, history),
        [SMEM, pl.BlockSpec((count, tile, width), lambda i: (0, row * steps + i, 0))],
        [shape((length, width), F32), shape((length, width), BF16)],
        [rows_of((tile, width))] * 2,
        flops=2 * count * length * width,
    )


def project_body(n, me, *refs):
    xs = refs[:n]
    gain, bias, cosine, sine, weight, qkv, normed, stat, held, sems = refs[n:]
    width = xs[0].shape[1]
    full = n * width
    copies = row_blocks(me[0], n, width, weight, held, sems, 0)
    start_all(copies)
    total = square = 0.0
    for x in xs:
        value = x[...].astype(F32)
        total += jnp.sum(value, 1, keepdims=True)
        square += jnp.sum(value * value, 1, keepdims=True)
    mean = total / full
    inv = lax.rsqrt(square / full - mean * mean + EPSILON)
    stat[...] = stat_columns(mean, inv)
    for j, x in enumerate(xs):
        part = slice(j * width, (j + 1) * width)
        normed[:, part] = (
            (x[...].astype(F32) - mean) * inv * gain[0:1, part] + bias[0:1, part]
        ).astype(BF16)
    wait_all(copies)
    for h in range(held.shape[1] // (3 * HEAD)):
        base = 3 * h * HEAD
        out = dot_nn(normed[...], held[:, base : base + 3 * HEAD])
        for s in range(2):
            v = out[:, s * HEAD : (s + 1) * HEAD]
            turned = v * cosine[...] + pltpu.roll(v, HEAD // 2, 1) * sine[...]
            qkv[:, base + s * HEAD : base + (s + 1) * HEAD] = turned.astype(BF16)
        qkv[:, base + 2 * HEAD : base + 3 * HEAD] = out[:, 2 * HEAD :].astype(BF16)


def project(me, xs, gain, bias, tables, weight):
    n, (length, width) = len(xs), xs[0].shape
    full, out = weight.shape
    tile = min(256, length)
    return call(
        "project",
        lambda *refs: project_body(n, *refs),
        (length // tile,),
        (me, *xs, gain, bias, *tables, weight),
        [SMEM]
        + [rows_of((tile, width))] * n
        + [fixed((8, full))] * 2
        + [rows_of((tile, HEAD))] * 2
        + [ANY],
        [shape((length, out), BF16), shape((length, full), BF16), shape((length, 128), F32)],
        [rows_of((tile, out)), rows_of((tile, full)), rows_of((tile, 128))],
        scratch=[pltpu.VMEM((full, out), BF16), pltpu.SemaphoreType.DMA((n,))],
        flops=2 * length * full * out,
    )


def windows(length):
    block = min(256, length)
    for i in range(length // block):
        low = max(0, i * block - (MAX_DOC - 1)) // block * block
        yield slice(i * block, (i + 1) * block), slice(low, (i + 1) * block)


def score_mask(start, q_part, k_part):
    dims = (k_part.stop - k_part.start, q_part.stop - q_part.start)
    k_pos = lax.broadcasted_iota(jnp.int32, dims, 0) + k_part.start
    q_pos = lax.broadcasted_iota(jnp.int32, dims, 1) + q_part.start
    return (k_pos >= start[0:1, q_part]) & (k_pos <= q_pos)


def attend_body(start, qkv, out, logs):
    length = qkv.shape[0]
    value_t = qkv[:, 2 * HEAD :].T
    for q_part, k_part in windows(length):
        query, key = qkv[q_part, :HEAD], qkv[k_part, HEAD : 2 * HEAD]
        scores = dot_nt(key, query) * (SCALE * LOG2E)
        scores = jnp.where(score_mask(start, q_part, k_part), scores, -1e30)
        top = jnp.max(scores, 0, keepdims=True)
        probs = jnp.exp2(scores - top)
        total = jnp.sum(probs, 0, keepdims=True)
        logs[0, :, q_part] = jnp.broadcast_to(top + jnp.log2(total), (8, q_part.stop - q_part.start))
        got = dot_nn(value_t[:, k_part], probs.astype(BF16)) / total
        out[q_part, :] = got.T.astype(BF16)


def attend(start, qkv):
    length, width = qkv.shape
    heads = width // (3 * HEAD)
    return call(
        "attend",
        attend_body,
        (heads,),
        (start, qkv),
        [fixed((8, length)), cols_of((length, 3 * HEAD))],
        [shape((length, heads * HEAD), BF16), shape((heads, 8, length), F32)],
        [cols_of((length, HEAD)), pl.BlockSpec((1, 8, length), lambda i: (i, 0, 0))],
        flops=4 * length * 768 * HEAD * heads,
    )


def attend_back_body(start, cosine, sine, qkv, grad, logs, out, key_sum, value_sum):
    length = qkv.shape[0]
    key_t = qkv[:, HEAD : 2 * HEAD].T
    key_sum[...] = jnp.zeros_like(key_sum)
    value_sum[...] = jnp.zeros_like(value_sum)

    def turn_back(v, part):
        return (
            v * cosine[part, :] - pltpu.roll(v, HEAD // 2, 1) * sine[part, :]
        ).astype(BF16)

    for q_part, k_part in windows(length):
        query, key = qkv[q_part, :HEAD], qkv[k_part, HEAD : 2 * HEAD]
        value, g = qkv[k_part, 2 * HEAD :], grad[q_part, :]
        scores = dot_nt(key, query) * (SCALE * LOG2E) - logs[0, 0:1, q_part]
        probs = jnp.exp2(jnp.where(score_mask(start, q_part, k_part), scores, -1e30))
        prob_grad = dot_nt(value, g)
        mean = jnp.sum(prob_grad * probs, 0, keepdims=True)
        score_grad = (probs * (prob_grad - mean)).astype(BF16)
        value_sum[k_part, :] += dot_nn(probs.astype(BF16), g)
        key_sum[k_part, :] += dot_nn(score_grad, query)
        query_grad = dot_nn(key_t[:, k_part], score_grad) * SCALE
        out[q_part, :HEAD] = turn_back(query_grad.T, q_part)
    for q_part, _ in windows(length):
        out[q_part, HEAD : 2 * HEAD] = turn_back(key_sum[q_part, :] * SCALE, q_part)
        out[q_part, 2 * HEAD :] = value_sum[q_part, :].astype(BF16)


def attend_back(start, tables, qkv, grad, logs):
    length, width = qkv.shape
    heads = width // (3 * HEAD)
    return call(
        "attend_back",
        attend_back_body,
        (heads,),
        (start, *tables, qkv, grad, logs),
        [fixed((8, length))]
        + [fixed((length, HEAD))] * 2
        + [
            cols_of((length, 3 * HEAD)),
            cols_of((length, HEAD)),
            pl.BlockSpec((1, 8, length), lambda i: (i, 0, 0)),
        ],
        [shape((length, width), BF16)],
        [cols_of((length, 3 * HEAD))],
        scratch=[pltpu.VMEM((length, HEAD), F32)] * 2,
        flops=10 * length * 768 * HEAD * heads,
    )[0]


def feed_body(n, me, *refs):
    attended, xs, outs_w = refs[:n], refs[n : 2 * n], refs[2 * n : 3 * n]
    own, gain, bias, up_bias, up_weight, down_weight = refs[3 * n : 3 * n + 6]
    hidden, normed, stat, activated, slope = refs[3 * n + 6 : 3 * n + 11]
    parts = refs[3 * n + 11 : 4 * n + 11]
    out_held, up_held, down_held, joined, whole, sems = refs[4 * n + 11 :]
    width = xs[0].shape[1]
    full = n * width
    inner = up_held.shape[1]
    out_copies = []
    for k in range(n):
        for j in range(n):
            out_copies.append(
                pltpu.make_async_copy(
                    outs_w[k].at[:, pl.ds(pl.multiple_of((me[0] ^ j) * width, width), width)],
                    out_held.at[pl.ds(k * width, width), pl.ds(j * width, width)],
                    sems.at[k * n + j],
                )
            )
    up_copies = row_blocks(me[0], n, width, up_weight, up_held, sems, n * n)
    down_copies = col_blocks(me[0], n, width, down_weight, down_held, sems, n * n + n)
    start_all(out_copies + up_copies + down_copies)
    for j in range(n):
        joined[:, j * width : (j + 1) * width] = attended[j][...]
    wait_all(out_copies)
    total = square = 0.0
    for j in range(n):
        part = slice(j * width, (j + 1) * width)
        base = own[...] if j == 0 else xs[j][...].astype(F32)
        value = base + dot_nn(joined[...], out_held[:, part])
        whole[:, part] = value
        if j == 0:
            hidden[...] = value
        total += jnp.sum(value, 1, keepdims=True)
        square += jnp.sum(value * value, 1, keepdims=True)
    mean = total / full
    inv = lax.rsqrt(square / full - mean * mean + EPSILON)
    stat[...] = stat_columns(mean, inv)
    for j in range(n):
        part = slice(j * width, (j + 1) * width)
        normed[:, part] = (
            (whole[:, part] - mean) * inv * gain[0:1, part] + bias[0:1, part]
        ).astype(BF16)
    wait_all(up_copies)
    step = min(512, inner)
    for c in range(inner // step):
        part = slice(c * step, (c + 1) * step)
        up = dot_nn(normed[...], up_held[:, part]) + up_bias[0:1, part]
        half = 0.5 * (1.0 + lax.erf(up * SQRT_HALF))
        activated[:, part] = (up * half).astype(BF16)
        slope[:, part] = (half + up * INV_ROOT_TWO_PI * jnp.exp(-0.5 * up * up)).astype(BF16)
    wait_all(down_copies)
    for j in range(n):
        parts[j][...] = dot_nn(
            activated[...], down_held[:, j * width : (j + 1) * width]
        ).astype(BF16)


def feed(me, attended, xs, outs_w, own, gain, bias, up_bias, up_weight, down_weight):
    n, (length, width) = len(xs), own.shape
    full, inner = up_weight.shape
    tile = min(256, length)
    got = call(
        "feed",
        lambda *refs: feed_body(n, *refs),
        (length // tile,),
        (me, *attended, *xs, *outs_w, own, gain, bias, up_bias, up_weight, down_weight),
        [SMEM]
        + [rows_of((tile, width))] * (2 * n)
        + [ANY] * n
        + [rows_of((tile, width))]
        + [fixed((8, full))] * 2
        + [fixed((8, inner))]
        + [ANY] * 2,
        [
            shape((length, width), F32),
            shape((length, full), BF16),
            shape((length, 128), F32),
            shape((length, inner), BF16),
            shape((length, inner), BF16),
        ]
        + [shape((length, width), BF16)] * n,
        [
            rows_of((tile, width)),
            rows_of((tile, full)),
            rows_of((tile, 128)),
            rows_of((tile, inner)),
            rows_of((tile, inner)),
        ]
        + [rows_of((tile, width))] * n,
        scratch=[
            pltpu.VMEM((full, full), BF16),
            pltpu.VMEM((full, inner), BF16),
            pltpu.VMEM((inner, full), BF16),
            pltpu.VMEM((tile, full), BF16),
            pltpu.VMEM((tile, full), F32),
            pltpu.SemaphoreType.DMA((n * n + 2 * n,)),
        ],
        flops=2 * length * full * (full + 2 * inner),
    )
    return (*got[:5], got[5:])


def row_stats(total, weighted):
    return stat_columns(total, weighted).T[0:8, :]


def feed_back_body(n, me, *refs):
    cots = refs[:n]
    slope, normed, gain, bias, up_weight, down_weight = refs[n : n + 6]
    cot_full, up_grad, sums, up_bias_sum, down_bias_sum = refs[n + 6 : n + 11]
    parts = refs[n + 11 : 2 * n + 11]
    up_held, down_held, sems = refs[2 * n + 11 :]
    width = cots[0].shape[1]
    inner = up_held.shape[1]
    down_copies = col_blocks(me[0], n, width, down_weight, down_held, sems, 0)
    up_copies = row_blocks(me[0], n, width, up_weight, up_held, sems, n)
    start_all(down_copies + up_copies)
    for j in range(n):
        cot_full[:, j * width : (j + 1) * width] = cots[j][...]
    accumulate(down_bias_sum, fold_rows(cots[0][...].astype(F32)))
    wait_all(down_copies)
    step = min(512, inner)
    for c in range(inner // step):
        part = slice(c * step, (c + 1) * step)
        value = dot_nt(cot_full[...], down_held[part, :]) * slope[:, part].astype(F32)
        up_grad[:, part] = value.astype(BF16)
    accumulate(up_bias_sum, fold_rows(up_grad[...].astype(F32)))
    wait_all(up_copies)
    total = weighted = 0.0
    for j in range(n):
        part = slice(j * width, (j + 1) * width)
        value = dot_nt(up_grad[...], up_held[part, :])
        parts[j][...] = value.astype(BF16)
        total += jnp.sum(value * gain[0:1, part], 1, keepdims=True)
        weighted += jnp.sum(
            value * (normed[:, part].astype(F32) - bias[0:1, part]), 1, keepdims=True
        )
    sums[...] = row_stats(total, weighted)


def feed_back(me, cots, slope, normed, gain, bias, up_weight, down_weight):
    n, (length, width) = len(cots), cots[0].shape
    full, inner = up_weight.shape
    tile = min(256, length)
    got = call(
        "feed_back",
        lambda *refs: feed_back_body(n, *refs),
        (length // tile,),
        (me, *cots, slope, normed, gain, bias, up_weight, down_weight),
        [SMEM]
        + [rows_of((tile, width))] * n
        + [rows_of((tile, inner)), rows_of((tile, full))]
        + [fixed((8, full))] * 2
        + [ANY] * 2,
        [
            shape((length, full), BF16),
            shape((length, inner), BF16),
            shape((8, length), F32),
            shape((8, inner), F32),
            shape((8, width), F32),
        ]
        + [shape((length, width), BF16)] * n,
        [
            rows_of((tile, full)),
            rows_of((tile, inner)),
            cols_of((8, tile)),
            fixed((8, inner)),
            fixed((8, width)),
        ]
        + [rows_of((tile, width))] * n,
        scratch=[
            pltpu.VMEM((full, inner), BF16),
            pltpu.VMEM((inner, full), BF16),
            pltpu.SemaphoreType.DMA((2 * n,)),
        ],
        flops=4 * length * full * inner,
    )
    return (*got[:5], got[5:])


def norm_back(refs, n_parts, source, stat, sums, gain, full):
    grad = refs[0][...].astype(F32)
    for ref in refs[1:n_parts]:
        grad += ref[...].astype(F32)
    columns = sums[...].T
    mean, inv = stat[:, 0:1], stat[:, 1:2]
    scaled = (source[...] - mean) * inv
    back = inv * (
        grad * gain[0:1, :] - columns[:, 0:1] * (1.0 / full) - scaled * (columns[:, 1:2] * (1.0 / full))
    )
    return back, fold_rows(grad * scaled), fold_rows(grad)


def hidden_back_body(k, full, *refs):
    parts = refs[:k]
    cot, hidden, stat, sums, gain, wide, low, gain_sum, bias_sum = refs[k:]
    back, gain_part, bias_part = norm_back(parts, k, hidden, stat, sums, gain, full)
    value = cot[...].astype(F32) + back
    wide[...] = value
    low[...] = value.astype(BF16)
    accumulate(gain_sum, gain_part)
    accumulate(bias_sum, bias_part)


def hidden_back(parts, cotangent, row, hidden, stat, sums, gain, full):
    k, (length, width) = len(parts), hidden.shape
    tile = min(256, length)
    steps = length // tile
    return call(
        "hidden_back",
        lambda *refs: hidden_back_body(k, full, *refs),
        (steps,),
        (*parts, cotangent, hidden, stat, sums, gain),
        [rows_of((tile, width))] * k
        + [
            pl.BlockSpec((tile, width), lambda i: (row * steps + i, 0)),
            rows_of((tile, width)),
            rows_of((tile, 128)),
            cols_of((8, tile)),
            fixed((8, width)),
        ],
        [shape((length, width), F32), shape((length, width), BF16)] + [shape((8, width), F32)] * 2,
        [rows_of((tile, width))] * 2 + [fixed((8, width))] * 2,
        flops=20 * length * width,
    )


def attended_back_body(n, me, *refs):
    grads = refs[:n]
    weight, joined, out, held, sems = refs[n:]
    width = grads[0].shape[1]
    copies = col_blocks(me[0], n, width, weight, held, sems, 0)
    start_all(copies)
    for j in range(n):
        joined[:, j * width : (j + 1) * width] = grads[j][...]
    wait_all(copies)
    out[...] = dot_nt(joined[...], held[...]).astype(BF16)


def attended_back(me, grads, weight):
    n, (length, width) = len(grads), grads[0].shape
    rows, full = weight.shape
    tile = min(256, length)
    return call(
        "attended_back",
        lambda *refs: attended_back_body(n, *refs),
        (length // tile,),
        (me, *grads, weight),
        [SMEM] + [rows_of((tile, width))] * n + [ANY],
        [shape((length, full), BF16), shape((length, rows), BF16)],
        [rows_of((tile, full)), rows_of((tile, rows))],
        scratch=[pltpu.VMEM((rows, full), BF16), pltpu.SemaphoreType.DMA((n,))],
        flops=2 * length * full * rows,
    )


def project_back_body(n, me, grad, normed, gain, bias, weight, sums, *refs):
    parts = refs[:n]
    held, sems = refs[n:]
    width = parts[0].shape[1]
    copies = row_blocks(me[0], n, width, weight, held, sems, 0)
    start_all(copies)
    wait_all(copies)
    total = weighted = 0.0
    for j in range(n):
        part = slice(j * width, (j + 1) * width)
        value = dot_nt(grad[...], held[part, :])
        parts[j][...] = value.astype(BF16)
        total += jnp.sum(value * gain[0:1, part], 1, keepdims=True)
        weighted += jnp.sum(
            value * (normed[:, part].astype(F32) - bias[0:1, part]), 1, keepdims=True
        )
    sums[...] = row_stats(total, weighted)


def project_back(me, n, grad, normed, gain, bias, weight):
    length, out = grad.shape
    full = weight.shape[0]
    width = full // n
    tile = min(256, length)
    got = call(
        "project_back",
        lambda *refs: project_back_body(n, *refs),
        (length // tile,),
        (me, grad, normed, gain, bias, weight),
        [SMEM, rows_of((tile, out)), rows_of((tile, full))] + [fixed((8, full))] * 2 + [ANY],
        [shape((8, length), F32)] + [shape((length, width), BF16)] * n,
        [cols_of((8, tile))] + [rows_of((tile, width))] * n,
        scratch=[pltpu.VMEM((full, out), BF16), pltpu.SemaphoreType.DMA((n,))],
        flops=2 * length * full * out,
    )
    return got[0], got[1:]


def average_back_body(k, full, count, *refs):
    weights, parts = refs[0], refs[1 : k + 1]
    source, stat, sums, gain, hidden_grad, history = refs[k + 1 : k + 7]
    grad_history, depth_sum, gain_sum, bias_sum = refs[-4:]
    back, gain_part, bias_part = norm_back(parts, k, source, stat, sums, gain, full)
    value = hidden_grad[...] + back
    accumulate(gain_sum, gain_part)
    accumulate(bias_sum, bias_part)
    lanes = value.shape[1] // 128
    for j in range(count):
        grad_history[j] = (weights[j] * value).astype(BF16)
        product = fold_rows(value * history[j].astype(F32))
        folded = product[:, 0:128]
        for c in range(1, lanes):
            folded += product[:, c * 128 : (c + 1) * 128]
        accumulate(depth_sum.at[j], folded)


def average_back(weights, parts, source, stat, sums, gain, hidden_grad, history, row, made):
    k, (length, width) = len(parts), source.shape
    count = history.shape[0]
    tile = min(256, length)
    steps = length // tile
    full = gain[1]
    block = pl.BlockSpec((count, tile, width), lambda i: (0, row * steps + i, 0))
    args = (weights, *parts, source, stat, sums, gain[0], hidden_grad, history)
    specs = (
        [SMEM]
        + [rows_of((tile, width))] * (k + 1)
        + [rows_of((tile, 128)), cols_of((8, tile)), fixed((8, width)), rows_of((tile, width)), block]
    )
    more = {}
    if made is not None:
        more = {"input_output_aliases": {len(args): 0}}
        args, specs = (*args, made), specs + [ANY]
    return call(
        "average_back",
        lambda *refs: average_back_body(k, full, count, *refs),
        (steps,),
        args,
        specs,
        [shape(history.shape, BF16), shape((count, 8, 128), F32)] + [shape((8, width), F32)] * 2,
        [block, fixed((count, 8, 128))] + [fixed((8, width))] * 2,
        flops=6 * count * length * width,
        **more,
    )


def weight_body(rows, me, *refs):
    out = refs[-1]
    total = dot_tn(refs[0][...], refs[rows][...])
    for r in range(1, rows):
        total += dot_tn(refs[r][...], refs[rows + r][...])
    out[...] = total.astype(BF16)


def divisor(size, most):
    return max(d for d in range(128, most + 1, 128) if size % d == 0)


def weight_grad(me, lefts, rights, width, turned):
    rows, (length, high), wide = len(lefts), lefts[0].shape, rights[0].shape[1]
    tall, across = divisor(high, 512), divisor(wide, 1024)
    if turned == 0:
        tall = min(tall, width)
    if turned == 1:
        across = min(across, width)
    per = width // (tall if turned == 0 else across)

    def place(i, j, me):
        if turned == 0:
            i = (me[0] ^ (i // per)) * per + i % per
        if turned == 1:
            j = (me[0] ^ (j // per)) * per + j % per
        return i, j

    return pl.pallas_call(
        lambda *refs: weight_body(rows, *refs),
        grid_spec=pltpu.PrefetchScalarGridSpec(
            num_scalar_prefetch=1,
            grid=(high // tall, wide // across),
            in_specs=[pl.BlockSpec((length, tall), lambda i, j, me: (0, i))] * rows
            + [pl.BlockSpec((length, across), lambda i, j, me: (0, j))] * rows,
            out_specs=pl.BlockSpec((tall, across), place),
        ),
        out_shape=shape((high, wide), BF16),
        compiler_params=pltpu.CompilerParams(vmem_limit_bytes=60 * MIB),
        cost_estimate=pl.CostEstimate(
            flops=2 * rows * length * high * wide,
            bytes_accessed=2 * (rows * length * (high + wide) + high * wide),
            transcendentals=0,
        ),
        name="weight_grad",
    )(me, *lefts, *rights)


class Ring:
    def __init__(self):
        self.n = lax.axis_size("mp")
        self.me = lax.axis_index("mp").astype(jnp.int32)
        self.pairs = self.n == 4
        self.core = [(i, i ^ 1) for i in range(self.n)]
        self.chip = [(i, i ^ 2) for i in range(self.n)]

    def over_core(self, value):
        return lax.ppermute(value, "mp", self.core)

    def over_chip(self, value):
        return lax.ppermute(value, "mp", self.chip)

    def gather(self, block):
        if self.pairs:
            sibling = self.over_core(block)
            across = self.over_chip(block)
            return [block, sibling, across, self.over_core(across)]
        every = lax.all_gather(block, "mp")
        return [
            lax.dynamic_index_in_dim(every, self.me ^ j, 0, keepdims=False) for j in range(self.n)
        ]

    def scatter(self, parts):
        if self.pairs:
            mine, other = self.over_core(parts[1]), self.over_core(parts[3])
            chip_sum = (parts[2].astype(F32) + other.astype(F32)).astype(BF16)
            return [parts[0], mine, self.over_chip(chip_sum)]
        stacked = jnp.stack([part.astype(F32) for part in parts])
        ordered = jnp.take(stacked, self.me ^ jnp.arange(self.n), axis=0)
        return [lax.psum_scatter(ordered, "mp", scatter_dimension=0, tiled=False)]

    def total(self, value):
        if self.pairs:
            value = value + self.over_core(value)
            return value + self.over_chip(value)
        return lax.psum(value, "mp")

    def out_blocks(self, weight):
        rows = weight.shape[0]
        groups = lax.axis_size("dp")
        if self.pairs and rows % (16 * groups) == 0:
            size = rows // groups
            piece = lax.dynamic_slice_in_dim(weight, lax.axis_index("dp") * size, size, 0)
            across = lax.all_gather(self.over_chip(piece), "dp", axis=0, tiled=True)
            return [weight, self.over_core(weight), across, self.over_core(across)]
        return self.gather(weight)


def tables_of(length):
    half = HEAD // 2
    rate = np.exp(np.arange(half, dtype=np.float64) * (-math.log(10000.0) / half))
    angle = np.arange(length, dtype=np.float64)[:, None] * rate[None, :]
    cosine, sine = np.cos(angle), np.sin(angle)
    return (
        jnp.asarray(np.concatenate([cosine, cosine], 1), F32),
        jnp.asarray(np.concatenate([-sine, sine], 1), F32),
    )


def local(
    history,
    depth_weights,
    segment_ids,
    first_gain,
    first_bias,
    qkv_weight,
    out_weight,
    second_gain,
    second_bias,
    up_weight,
    up_bias,
    down_weight,
    down_bias,
    cotangent,
):
    ring = Ring()
    n = ring.n
    me = ring.me[None]
    width = history.shape[2]
    full = n * width
    row_count, length = segment_ids.shape
    rows = range(row_count)
    tables = tables_of(length)
    earlier = (segment_ids[:, None, :] < segment_ids[:, :, None]).astype(jnp.int32)
    starts = jnp.broadcast_to(jnp.sum(earlier, -1)[:, None, :], (row_count, 8, length))

    vectors = jnp.stack([first_gain, first_bias, second_gain, second_bias])
    vectors = jnp.concatenate(ring.gather(jnp.repeat(vectors, 8, 0)), 1)
    gain1, bias1, gain2, bias2 = (vectors[8 * i : 8 * i + 8] for i in range(4))
    own1, own2 = gain1[:, :width], gain2[:, :width]
    up_bias8 = jnp.broadcast_to(up_bias[None], (8, up_bias.shape[0]))

    wide, low = zip(*[average(depth_weights, history, r, length) for r in rows])
    xs = [ring.gather(low[r]) for r in rows]
    cots = [
        ring.gather(lax.slice_in_dim(cotangent, r * length, (r + 1) * length)) for r in rows
    ]
    out_w = ring.out_blocks(out_weight)

    qkv, normed1, stat1, attended, logs = [], [], [], [], []
    for r in rows:
        got = project(me, xs[r], gain1, bias1, tables, qkv_weight)
        qkv.append(got[0])
        normed1.append(got[1])
        stat1.append(got[2])
        got = attend(starts[r], qkv[r])
        attended.append(got[0])
        logs.append(got[1])
    heads = [ring.gather(attended[r]) for r in rows]

    hidden, normed2, stat2, activated, slope, outputs = [], [], [], [], [], []
    for r in rows:
        got = feed(
            me, heads[r], xs[r], out_w, wide[r], gain2, bias2, up_bias8, up_weight, down_weight
        )
        hidden.append(got[0])
        normed2.append(got[1])
        stat2.append(got[2])
        activated.append(got[3])
        slope.append(got[4])
        branch = ring.scatter(got[5])
        mlp = sum(part.astype(F32) for part in branch)
        outputs.append((got[0] + (mlp + down_bias)).astype(BF16))

    cot_full, up_grad, parts2, sums2, up_bias_sum, down_bias_sum = [], [], [], [], 0.0, 0.0
    for r in rows:
        got = feed_back(
            me, cots[r], slope[r], normed2[r], gain2, bias2, up_weight, down_weight
        )
        cot_full.append(got[0])
        up_grad.append(got[1])
        sums2.append(ring.total(got[2]))
        up_bias_sum += got[3]
        down_bias_sum += got[4]
        parts2.append(ring.scatter(got[5]))

    down_part = weight_grad(me, activated, cot_full, width, 1)
    up_part = weight_grad(me, normed2, up_grad, width, 0)

    hidden_grad, gain2_sum, bias2_sum, grads = [], 0.0, 0.0, []
    for r in rows:
        got = hidden_back(parts2[r], cotangent, r, hidden[r], stat2[r], sums2[r], own2, full)
        hidden_grad.append(got[0])
        gain2_sum += got[2]
        bias2_sum += got[3]
        grads.append(ring.gather(got[1]))

    grad_full, qkv_grad, parts1, sums1 = [], [], [], []
    for r in rows:
        got = attended_back(me, grads[r], out_weight)
        grad_full.append(got[0])
        qkv_grad.append(attend_back(starts[r], tables, qkv[r], got[1], logs[r]))
        sums, parts = project_back(me, n, qkv_grad[r], normed1[r], gain1, bias1, qkv_weight)
        sums1.append(ring.total(sums))
        parts1.append(ring.scatter(parts))

    out_part = weight_grad(me, attended, grad_full, width, 1)
    qkv_part = weight_grad(me, normed1, qkv_grad, width, 0)

    grad_history, depth_sum, gain1_sum, bias1_sum = None, 0.0, 0.0, 0.0
    for r in rows:
        got = average_back(
            depth_weights,
            parts1[r],
            wide[r],
            stat1[r],
            sums1[r],
            (own1, full),
            hidden_grad[r],
            history,
            r,
            grad_history,
        )
        grad_history = got[0]
        depth_sum += got[1]
        gain1_sum += got[2]
        bias1_sum += got[3]

    down_total = lax.psum_scatter(down_part, "dp", scatter_dimension=1, tiled=True).astype(F32)
    up_total = lax.psum_scatter(up_part, "dp", scatter_dimension=0, tiled=True).astype(F32)
    out_total = lax.psum_scatter(out_part, "dp", scatter_dimension=1, tiled=True).astype(F32)
    qkv_total = lax.psum_scatter(qkv_part, "dp", scatter_dimension=0, tiled=True).astype(F32)

    early = lax.psum(
        tuple(jnp.sum(v, 0) for v in (up_bias_sum, down_bias_sum, gain2_sum, bias2_sum)), "dp"
    )
    late = lax.psum(
        (jnp.sum(gain1_sum, 0), jnp.sum(bias1_sum, 0), jnp.sum(depth_sum, (1, 2))), "dp"
    )
    depth_grad = lax.psum(late[2], "mp")
    return (
        jnp.concatenate(outputs),
        grad_history,
        depth_grad,
        late[0],
        late[1],
        qkv_total,
        out_total,
        early[2],
        early[3],
        up_total,
        early[0],
        down_total,
        early[1],
    )


def solution(mesh):
    placed = (
        P(None, "dp", "mp"),
        P(),
        P("dp", None),
        P("mp"),
        P("mp"),
        P(None, "mp"),
        P("mp", None),
        P("mp"),
        P("mp"),
        P(None, "mp"),
        P("mp"),
        P("mp", None),
        P("mp"),
        P("dp", "mp"),
    )
    return jax.shard_map(
        local,
        mesh=mesh,
        in_specs=placed,
        out_specs=(
            P("dp", "mp"),
            P(None, "dp", "mp"),
            P(),
            P("mp"),
            P("mp"),
            P("dp", "mp"),
            P("mp", "dp"),
            P("mp"),
            P("mp"),
            P("dp", "mp"),
            P("mp"),
            P("mp", "dp"),
            P("mp"),
        ),
        check_vma=False,
    )
```

time: 1810 us -> 953 us (0.53)
  waiting for transfers between devices: 952 us -> 418 us
  matrix products: 452 us -> 0 us
  Pallas kernels: 0 us -> 402 us
  other arithmetic: 177 us -> 22.7 us
  local copies, waits for them, and re-layouts: 105 us -> 12.7 us
  blocking collectives: 94.1 us -> 44.5 us
  starting transfers between devices: 0.88 us -> 28.9 us
    reduce_scatter x12 -> x4, waiting for transfers between devices: 740 us -> 176 us  [the longest x1 149 us: local(): lax.psum_scatter(up_part, 'dp', scatter_dimension=0, tiled=True).astype(F32)]
    dot_general x54 -> x0, matrix products: 452 us -> none  [the longest x2 90.6 us: row_step(): jnp.einsum('j,jtd->td', depth_weights, hist_here, precision=EXACT)]
    pallas_call x0 -> x24, Pallas kernels: none -> 402 us  [the longest x20 315 us: call(): pl.pallas_call(body, grid=grid, in_specs=in_specs, out_specs=out_specs, o...]
    ppermute x0 -> x56, waiting for transfers between devices: none -> 241 us  [the longest x20 236 us: over_chip(): return lax.ppermute(value, 'mp', self.chip)]
    all_gather x8 -> x1, waiting for transfers between devices: 211 us -> 0.01 us  [out_blocks(): across = lax.all_gather(self.over_chip(piece), 'dp', axis=0, tiled=True)]
    convert_element_type x18 -> x11, other arithmetic: 65.6 us -> 15.8 us  [the longest x6 3.15 us: scatter(): chip_sum = (parts[2].astype(F32) + other.astype(F32)).astype(BF16)]
    psum x10 -> x2, blocking collectives: 94.1 us -> 44.5 us  [the longest x1 38 us: local(): lax.psum((jnp.sum(gain1_sum, 0), jnp.sum(bias1_sum, 0), jnp.sum(depth_sum...]
    while x276 -> x0, local copies, waits for them, and re-layouts: 36.8 us -> none
  transfers between devices with their start and end apart: 20 -> 61, of which waited for: 17 -> 18; matrix products, arithmetic and copies ran while one was open for 19% -> 3% of each run, Pallas kernels for 0% -> 41%
where the time goes in v1:
time: 953 us; the launch traced here: 943 us
  waiting for transfers between devices  418 us (44%)
  Pallas kernels  402 us (42%)
  blocking collectives  44.5 us (5%)
  starting transfers between devices  28.9 us (3%)
  other arithmetic  22.7 us (2%)
  between operations  15.1 us (2%)
  local copies, waits for them, and re-layouts  12.7 us (1%)
    pallas_call x20, Pallas kernels, call(): pl.pallas_call(body, grid=grid, in_specs=in_specs, out_specs=out_specs, o...  315 us
    ppermute x20, waiting for transfers between devices, over_chip(): return lax.ppermute(value, 'mp', self.chip)  236 us
    reduce_scatter x1, waiting for transfers between devices, local(): lax.psum_scatter(up_part, 'dp', scatter_dimension=0, tiled=True).astype(F32)  149 us
    pallas_call x4, Pallas kernels, weight_grad(): pl.pallas_call(lambda *refs: weight_body(rows, *refs), grid_spec=pltpu.Pr...  86.5 us
    psum x1, blocking collectives, local(): lax.psum((jnp.sum(gain1_sum, 0), jnp.sum(bias1_sum, 0), jnp.sum(depth_sum...  38 us
    reduce_scatter x1, waiting for transfers between devices, local(): lax.psum_scatter(down_part, 'dp', scatter_dimension=1, tiled=True)  26.7 us
    ppermute x20, starting transfers between devices, over_chip(): return lax.ppermute(value, 'mp', self.chip)  21.1 us
  transfers between devices with their start and end apart: 61, of which 18 were waited for; matrix products, arithmetic and copies ran while one was open for 3% of the time, Pallas kernels for 41%

profile of v1, /device:TPU:0, one launch (start us, length us, event | category | flops | bytes accessed | tf_op | source)
XLA Modules:
  0.0 943.0 jit_solution(15953986852282855343)
XLA Ops:
  8.2 3.0 collective-permute-start.10
  11.2 6.3 collective-permute-done.10
  18.4 7.8 average.3
  28.9 7.8 average.2
  39.6 13.0 %collective-permute-done.16.refs_3_.refs_7_ = bf16[1024,512]{1,0:T(8,128)(2,1)} collective-permute-done((bf16[1024,512]{1,0:T(8,128)(2,1)}, bf16[1024,512]{1,0:T(8,128)(2,1)}, u32[]{:S(2)}, u32[]{:S(2)}) %collective-permute-start.16) | collective-permute-done | bytes 1048608 | tf_op jit(solution)/shard_map/ppermute | solution.py:700
  57.9 18.6 %collective-permute-done.1.refs_3_.refs_7_ = bf16[1024,512]{1,0:T(8,128)(2,1)} collective-permute-done((bf16[1024,512]{1,0:T(8,128)(2,1)}, bf16[1024,512]{1,0:T(8,128)(2,1)}, u32[]{:S(2)}, u32[]{:S(2)}) %collective-permute-start.1) | collective-permute-done | bytes 1048608 | tf_op jit(solution)/shard_map/ppermute | solution.py:700
  76.5 17.7 %project.3 = (bf16[1024,1536]{1,0:T(8,128)(2,1)}, bf16[1024,2048]{1,0:T(8,128)(2,1)}, f32[1024,128]{1,0:T(8,128)}) custom-call(s32[1]{0:T(128)} %bitcast.refs_0_, bf16[1024,512]{1,0:T(8,128)(2,1)} %get-tuple-element.102.refs_1_.refs_5_, bf16[1024,512]{1,0:T(8,128)(2,1)} %collective-permute-done.15.refs_2_.refs_6_, ...), custom_call_target="tpu_custom_call" | custom-call | flops 6442450944 | bytes 19529732 | tf_op jit(solution)/shard_map/project/pallas_call | solution.py:38
  94.8 9.8 %attend.3 = (bf16[1024,512]{1,0:T(8,128)(2,1)}, f32[4,8,1024]{2,1,0:T(8,128)}) custom-call(s32[8,1024]{1,0:T(8,128)} %broadcast_in_dim.34.start, bf16[1024,1536]{1,0:T(8,128)(2,1)} %get-tuple-element.103.qkv), custom_call_target="tpu_custom_call" | custom-call | flops 1610612736 | bytes 4358144 | tf_op jit(solution)/shard_map/attend/pallas_call | solution.py:38
  107.0 23.8 %collective-permute-done.19.refs_3_ = bf16[1024,512]{1,0:T(8,128)(2,1)} collective-permute-done((bf16[1024,512]{1,0:T(8,128)(2,1)}, bf16[1024,512]{1,0:T(8,128)(2,1)}, u32[]{:S(2)}, u32[]{:S(2)}) %collective-permute-start.19) | collective-permute-done | bytes 1048608 | tf_op jit(solution)/shard_map/ppermute | solution.py:700
  130.9 17.7 %project.2 = (bf16[1024,1536]{1,0:T(8,128)(2,1)}, bf16[1024,2048]{1,0:T(8,128)(2,1)}, f32[1024,128]{1,0:T(8,128)}) custom-call(s32[1]{0:T(128)} %bitcast.refs_0_, bf16[1024,512]{1,0:T(8,128)(2,1)} %get-tuple-element.93.refs_1_.refs_5_, bf16[1024,512]{1,0:T(8,128)(2,1)} %copy-done.44, bf16[1024,512]{1,0:T(8,128)(2,1)} %collective-permute-done.1.refs_3_.refs_7_, ...), custom_call_target="tpu_custom_call" | custom-call | flops 6442450944 | bytes 19529732 | tf_op jit(solution)/shard_map/project/pallas_call | solution.py:38
  149.2 9.9 %attend.2 = (bf16[1024,512]{1,0:T(8,128)(2,1)}, f32[4,8,1024]{2,1,0:T(8,128)}) custom-call(s32[8,1024]{1,0:T(8,128)} %broadcast_in_dim.30.start, bf16[1024,1536]{1,0:T(8,128)(2,1)} %get-tuple-element.94.qkv), custom_call_target="tpu_custom_call" | custom-call | flops 1610612736 | bytes 4358144 | tf_op jit(solution)/shard_map/attend/pallas_call | solution.py:38
  162.6 40.3 %feed.3 = (f32[1024,512]{1,0:T(8,128)}, bf16[1024,2048]{1,0:T(8,128)(2,1)}, f32[1024,128]{1,0:T(8,128)}, bf16[1024,2048]{1,0:T(8,128)(2,1)}, bf16[1024,2048]{1,0...) custom-call(s32[1]{0:T(128)} %bitcast.refs_0_, ...), custom_call_target="tpu_custom_call" | custom-call | flops 25769803776 | bytes 55246852 | tf_op jit(solution)/shard_map/feed/pallas_call | solution.py:38
  203.5 27.3 %feed_back.2 = (bf16[1024,2048]{1,0:T(8,128)(2,1)}, bf16[1024,2048]{1,0:T(8,128)(2,1)}, f32[8,1024]{1,0:T(8,128)}, f32[8,2048]{1,0:T(8,128)}, f32[8,512]{1,0:T(8...) custom-call(s32[1]{0:T(128)} %bitcast.refs_0_, ...), custom_call_target="tpu_custom_call" | custom-call | flops 17179869184 | bytes 42188804 | tf_op jit(solution)/shard_map/feed_back/pallas_call | solution.py:38
  231.1 40.2 %feed.2 = (f32[1024,512]{1,0:T(8,128)}, bf16[1024,2048]{1,0:T(8,128)(2,1)}, f32[1024,128]{1,0:T(8,128)}, bf16[1024,2048]{1,0:T(8,128)(2,1)}, bf16[1024,2048]{1,0...) custom-call(s32[1]{0:T(128)} %bitcast.refs_0_, ...), custom_call_target="tpu_custom_call" | custom-call | flops 25769803776 | bytes 55246852 | tf_op jit(solution)/shard_map/feed/pallas_call | solution.py:38
  271.4 27.2 %feed_back.3 = (bf16[1024,2048]{1,0:T(8,128)(2,1)}, bf16[1024,2048]{1,0:T(8,128)(2,1)}, f32[8,1024]{1,0:T(8,128)}, f32[8,2048]{1,0:T(8,128)}, f32[8,512]{1,0:T(8...) custom-call(s32[1]{0:T(128)} %bitcast.refs_0_, ...), custom_call_target="tpu_custom_call" | custom-call | flops 17179869184 | bytes 42188804 | tf_op jit(solution)/shard_map/feed_back/pallas_call | solution.py:38
  302.4 2.0 collective-permute-done.30
  305.2 43.1 %collective-permute-done.31 = f32[8,1024]{1,0:T(8,128)S(1)} collective-permute-done((f32[8,1024]{1,0:T(8,128)S(1)}, f32[8,1024]{1,0:T(8,128)S(1)}, u32[]{:S(2)}, u32[]{:S(2)}) %collective-permute-start.31) | collective-permute-done | bytes 32800 | tf_op jit(solution)/shard_map/ppermute | solution.py:700
  349.5 5.9 hidden_back.2
  358.7 22.1 %collective-permute-done.47 = f32[8,1024]{1,0:T(8,128)S(1)} collective-permute-done((f32[8,1024]{1,0:T(8,128)S(1)}, f32[8,1024]{1,0:T(8,128)S(1)}, u32[]{:S(2)}, u32[]{:S(2)}) %collective-permute-start.47) | collective-permute-done | bytes 32800 | tf_op jit(solution)/shard_map/ppermute | solution.py:700
  382.7 6.0 hidden_back.3
  389.7 22.9 %collective-permute-done.49.refs_3_ = bf16[1024,512]{1,0:T(8,128)(2,1)S(1)} collective-permute-done((bf16[1024,512]{1,0:T(8,128)(2,1)}, bf16[1024,512]{1,0:T(8,128)(2,1)S(1)}, u32[]{:S(2)}, u32[]{:S(2)}) %collective-permute-start.49) | collective-permute-done | bytes 1048608 | tf_op jit(solution)/shard_map/ppermute | solution.py:700
  413.6 7.6 attended_back.2
  422.3 7.6 attended_back.3
  429.9 8.8 weight_grad.5
  438.7 12.6 %attend_back.2.refs_1_.refs_4_ = bf16[1024,1536]{1,0:T(8,128)(2,1)} custom-call(s32[8,1024]{1,0:T(8,128)} %broadcast_in_dim.34.start, f32[1024,128]{1,0:T(8,128)} %constant.21.clone.refs_7_.cosine, f32[1024,128]{1,0:T(8,128)} %constant.22.clone.refs_8_.sine, bf16[1024,1536]{1,0:T(8,128)(2,1)} %get-tuple-element.103.qkv, ...), custom_call_target="tpu_custom_call" | custom-call | flops 4026531840 | bytes 8552448 | tf_op jit(solution)/shard_map/attend_back/pallas_call | solution.py:38
  451.4 12.4 %attend_back.3.refs_1_.refs_3_ = bf16[1024,1536]{1,0:T(8,128)(2,1)} custom-call(s32[8,1024]{1,0:T(8,128)} %broadcast_in_dim.30.start, f32[1024,128]{1,0:T(8,128)} %constant.21.clone.refs_7_.cosine, f32[1024,128]{1,0:T(8,128)} %constant.22.clone.refs_8_.sine, bf16[1024,1536]{1,0:T(8,128)(2,1)} %get-tuple-element.94.qkv, ...), custom_call_target="tpu_custom_call" | custom-call | flops 4026531840 | bytes 8552448 | tf_op jit(solution)/shard_map/attend_back/pallas_call | solution.py:38
  463.8 21.5 %weight_grad.4 = bf16[2048,1536]{1,0:T(8,128)(2,1)} custom-call(s32[1]{0:T(128)} %bitcast.refs_0_, bf16[1024,2048]{1,0:T(8,128)(2,1)} %get-tuple-element.141.refs_2_.refs_1_, bf16[1024,2048]{1,0:T(8,128)(2,1)} %get-tuple-element.122.refs_2_, bf16[1024,1536]{1,0:T(8,128)(2,1)} %attend_back.3.refs_1_.refs_3_, bf16[1024,1536]{1,0:T(8,128)(2,1)} %attend_back.2.refs_1_.refs_4_), custom_call_target="tpu_custom_call" | custom-call | flops 12884901888 | bytes 20971520 | tf_op jit(solution)/shard_map/weight_grad/pallas_call | solution.py:668
  485.4 29.7 %weight_grad.7 = bf16[2048,2048]{1,0:T(8,128)(2,1)} custom-call(s32[1]{0:T(128)} %bitcast.refs_0_, bf16[1024,2048]{1,0:T(8,128)(2,1)} %get-tuple-element.167.refs_1_, bf16[1024,2048]{1,0:T(8,128)(2,1)} %get-tuple-element.168.refs_2_, bf16[1024,2048]{1,0:T(8,128)(2,1)} %get-tuple-element.169.refs_3_, bf16[1024,2048]{1,0:T(8,128)(2,1)} %get-tuple-element.170.refs_4_), custom_call_target="tpu_custom_call" | custom-call | flops 17179869184 | bytes 25165824 | tf_op jit(solution)/shard_map/weight_grad/pallas_call | solution.py:668
  515.2 26.5 %weight_grad.6 = bf16[2048,2048]{1,0:T(8,128)(2,1)} custom-call(s32[1]{0:T(128)} %bitcast.refs_0_, bf16[1024,2048]{1,0:T(8,128)(2,1)} %get-tuple-element.131.refs_6_.refs_1_, bf16[1024,2048]{1,0:T(8,128)(2,1)} %get-tuple-element.112.refs_6_.refs_2_, bf16[1024,2048]{1,0:T(8,128)(2,1)} %get-tuple-element.163.refs_3_, bf16[1024,2048]{1,0:T(8,128)(2,1)} %get-tuple-element.164.refs_4_), custom_call_target="tpu_custom_call" | custom-call | flops 17179869184 | bytes 25165824 | tf_op jit(solution)/shard_map/weight_grad/pallas_call | solution.py:668
  542.9 13.5 %project_back.3 = (f32[8,1024]{1,0:T(8,128)}, bf16[1024,512]{1,0:T(8,128)(2,1)}, bf16[1024,512]{1,0:T(8,128)(2,1)}, bf16[1024,512]{1,0:T(8,128)(2,1)}, bf16[1024,512]{1,0:T(8,128)(2,1)}) custom-call(s32[1]{0:T(128)} %bitcast.refs_0_, bf16[1024,1536]{1,0:T(8,128)(2,1)} %attend_back.3.refs_1_.refs_3_, bf16[1024,2048]{1,0:T(8,128)(2,1)} %get-tuple-element.141.refs_2_.refs_1_, ...), custom_call_target="tpu_custom_call" | custom-call | flops 6442450944 | bytes 17989636 | tf_op jit(solution)/shard_map/project_back/pallas_call | solution.py:38
  557.1 13.4 %project_back.2 = (f32[8,1024]{1,0:T(8,128)}, bf16[1024,512]{1,0:T(8,128)(2,1)}, bf16[1024,512]{1,0:T(8,128)(2,1)}, bf16[1024,512]{1,0:T(8,128)(2,1)}, bf16[1024,512]{1,0:T(8,128)(2,1)}) custom-call(s32[1]{0:T(128)} %bitcast.refs_0_, bf16[1024,1536]{1,0:T(8,128)(2,1)} %attend_back.2.refs_1_.refs_4_, bf16[1024,2048]{1,0:T(8,128)(2,1)} %get-tuple-element.122.refs_2_, ...), custom_call_target="tpu_custom_call" | custom-call | flops 6442450944 | bytes 17989636 | tf_op jit(solution)/shard_map/project_back/pallas_call | solution.py:38
  572.7 2.1 collective-permute-start.14
  576.3 22.0 %collective-permute-done.23 = bf16[1024,512]{1,0:T(8,128)(2,1)S(1)} collective-permute-done((bf16[1024,512]{1,0:T(8,128)(2,1)S(1)}, bf16[1024,512]{1,0:T(8,128)(2,1)S(1)}, u32[]{:S(2)}, u32[]{:S(2)}) %collective-permute-start.23) | collective-permute-done | bytes 1048608 | tf_op jit(solution)/shard_map/ppermute | solution.py:700
  598.4 22.4 %collective-permute-done.14 = bf16[1024,512]{1,0:T(8,128)(2,1)S(1)} collective-permute-done((bf16[1024,512]{1,0:T(8,128)(2,1)S(1)}, bf16[1024,512]{1,0:T(8,128)(2,1)S(1)}, u32[]{:S(2)}, u32[]{:S(2)}) %collective-permute-start.14) | collective-permute-done | bytes 1048608 | tf_op jit(solution)/shard_map/ppermute | solution.py:700
  621.0 2.9 add_convert_fusion.6
  624.0 2.0 collective-permute-start.55
  627.5 38.5 %collective-permute-done.55 = f32[8,1024]{1,0:T(8,128)S(1)} collective-permute-done((f32[8,1024]{1,0:T(8,128)S(1)}, f32[8,1024]{1,0:T(8,128)S(1)}, u32[]{:S(2)}, u32[]{:S(2)}) %collective-permute-start.55) | collective-permute-done | bytes 32800 | tf_op jit(solution)/shard_map/ppermute | solution.py:700
  666.9 3.0 collective-permute-done.39
  672.4 14.9 %average_back.2 = (bf16[13,2048,512]{2,1,0:T(8,128)(2,1)}, f32[13,8,128]{2,1,0:T(8,128)}, f32[8,512]{1,0:T(8,128)}, f32[8,512]{1,0:T(8,128)}) custom-call(f32[13]{0:T(128)} %refs_0_.3, bf16[1024,512]{1,0:T(8,128)(2,1)} %get-tuple-element.142.refs_1_, bf16[1024,512]{1,0:T(8,128)(2,1)} %copy-done.7, bf16[1024,512]{1,0:T(8,128)(2,1)} %copy-done.9, ...), custom_call_target="tpu_custom_call" | custom-call | flops 40894464 | bytes 62525492 | tf_op jit(solution)/shard_map/average_back/pallas_call | solution.py:38
  688.7 15.2 %average_back.3 = (bf16[13,2048,512]{2,1,0:T(8,128)(2,1)}, f32[13,8,128]{2,1,0:T(8,128)}, f32[8,512]{1,0:T(8,128)}, f32[8,512]{1,0:T(8,128)}) custom-call(f32[13]{0:T(128)} %refs_0_.3, bf16[1024,512]{1,0:T(8,128)(2,1)} %get-tuple-element.123.refs_1_, bf16[1024,512]{1,0:T(8,128)(2,1)} %copy-done.3, ...), custom_call_target="tpu_custom_call", output_to_operand_aliasing={{0}: (10, {})} | custom-call | flops 40894464 | bytes 89788464 | tf_op jit(solution)/shard_map/average_back/pallas_call | solution.py:38
  705.7 38.0 %all-reduce = (f32[13]{0:T(128)S(1)}, f32[512]{0:T(512)}, f32[512]{0:T(512)}, f32[512]{0:T(512)}, f32[512]{0:T(512)}, /*index=5*/f32[2048]{0:T(1024)}, f32[512]{0:T(512)}) all-reduce(f32[13]{0:T(128)S(1)} %add_reduce_fusion.1, f32[512]{0:T(512)S(1)} %get-tuple-element.193, ...), channel_id=1, replica_groups=mesh['dp'=8,'mp'=4] {'dp'}, use_global_device_ids=true, to_apply=%region_2.0 | all-reduce | flops 4621 | bytes 36968 | tf_op jit(solution)/shard_map/psum | solution.py:876
  743.7 6.5 psum.57
  750.2 1.8 convert_element_type.121
  752.0 2.5 convert_element_type.120
  754.5 26.7 %reduce-scatter.11.cloned.1.call-done = bf16[2048,256]{1,0:T(8,128)(2,1)} async-done(((bf16[2048,2048]{1,0:T(8,128)(2,1)}), bf16[2048,256]{1,0:T(8,128)(2,1)}) %reduce-scatter.11.cloned.1.call-update) | async-done | bytes 1048592 | tf_op jit(solution)/shard_map/reduce_scatter | solution.py:868
  781.2 2.7 convert_element_type.123
  783.9 149.3 %reduce-scatter.9.cloned.1.call-done = bf16[256,2048]{1,0:T(8,128)(2,1)} async-done(((bf16[2048,2048]{1,0:T(8,128)(2,1)}), bf16[256,2048]{1,0:T(8,128)(2,1)}) %reduce-scatter.9.cloned.1.call-update) | async-done | bytes 1048592 | tf_op jit(solution)/shard_map/reduce_scatter | solution.py:869
  933.1 2.8 convert_element_type.122
  (243 shorter events, 48.3 us)
Async XLA Ops:
  7.2 99.2 %all-gather.2.cloned.1.call-start = ((), (), s32[]{:S(2)}) async-start(), calls=%async_computation.4 | async-start | bytes 2359296 | tf_op jit(solution)/shard_map/all_gather | solution.py:733
  18.3 731.9 %reduce-scatter.7.cloned.1.call-start = ((), (), s32[]{:S(2)}) async-start(), calls=%async_computation.6 | async-start | bytes 2359296 | tf_op jit(solution)/shard_map/reduce_scatter | solution.py:870
  26.2 26.4 %collective-permute-start.16 = (bf16[1024,512]{1,0:T(8,128)(2,1)}, bf16[1024,512]{1,0:T(8,128)(2,1)}, u32[]{:S(2)}, u32[]{:S(2)}) collective-permute-start(bf16[1024,512]{1,0:T(8,128)(2,1)} %get-tuple-element.102.refs_1_.refs_5_), channel_id=1, source_target_pairs={{0,2},{1,3},{2,0},{3,1},{4,6},{5,7},{6,4},{7,5},{8,10},{9,11},{10,... | collective-permute-start | bytes 3145736 | tf_op jit(solution)/shard_map/ppermute | solution.py:700
  28.0 25.9 %collective-permute-start.4 = (f32[32,512]{1,0:T(8,128)S(1)}, f32[32,512]{1,0:T(8,128)S(1)}, u32[]{:S(2)}, u32[]{:S(2)}) collective-permute-start(f32[32,512]{1,0:T(8,128)S(1)} %broadcast_bitcast_fusion), channel_id=1, source_target_pairs={{0,2},{1,3},{2,0},{3,1},{4,6},{5,7},{6,4},{7,5},{8,10},{9,11},{10,... | collective-permute-start | bytes 196616 | tf_op jit(solution)/shard_map/ppermute | solution.py:700
  28.4 26.0 %collective-permute-start.3 = (f32[32,512]{1,0:T(8,128)S(1)}, f32[32,512]{1,0:T(8,128)S(1)}, u32[]{:S(2)}, u32[]{:S(2)}) collective-permute-start(f32[32,512]{1,0:T(8,128)S(1)} %broadcast_bitcast_fusion), channel_id=1, source_target_pairs={{0,1},{1,0},{2,3},{3,2},{4,5},{5,4},{6,7},{7,6},{8,9},{9,8},{10,11... | collective-permute-start | bytes 196616 | tf_op jit(solution)/shard_map/ppermute | solution.py:697
  28.4 29.5 %collective-permute-start.15 = (bf16[1024,512]{1,0:T(8,128)(2,1)}, bf16[1024,512]{1,0:T(8,128)(2,1)}, u32[]{:S(2)}, u32[]{:S(2)}) collective-permute-start(bf16[1024,512]{1,0:T(8,128)(2,1)} %get-tuple-element.102.refs_1_.refs_5_), channel_id=1, source_target_pairs={{0,1},{1,0},{2,3},{3,2},{4,5},{5,4},{6,7},{7,6},{8,9},{9,8},{10,11... | collective-permute-start | bytes 3145736 | tf_op jit(solution)/shard_map/ppermute | solution.py:697
  36.7 39.8 %collective-permute-start.1 = (bf16[1024,512]{1,0:T(8,128)(2,1)}, bf16[1024,512]{1,0:T(8,128)(2,1)}, u32[]{:S(2)}, u32[]{:S(2)}) collective-permute-start(bf16[1024,512]{1,0:T(8,128)(2,1)} %get-tuple-element.93.refs_1_.refs_5_), channel_id=1, source_target_pairs={{0,2},{1,3},{2,0},{3,1},{4,6},{5,7},{6,4},{7,5},{8,10},{9,11},{10,... | collective-permute-start | bytes 3145736 | tf_op jit(solution)/shard_map/ppermute | solution.py:700
  52.6 23.9 %collective-permute-start.17 = (bf16[1024,512]{1,0:T(8,128)(2,1)}, bf16[1024,512]{1,0:T(8,128)(2,1)}, u32[]{:S(2)}, u32[]{:S(2)}) collective-permute-start(bf16[1024,512]{1,0:T(8,128)(2,1)} %collective-permute-done.16.refs_3_.refs_7_), channel_id=1, source_target_pairs={{0,1},{1,0},{2,3},{3,2},{4,5},{5,4},{6,7},{7,6},{8,9},{9,8},{10,11... | collective-permute-start | bytes 3145736 | tf_op jit(solution)/shard_map/ppermute | solution.py:697
  54.4 105.3 %collective-permute-start.9 = (bf16[512,2048]{1,0:T(8,128)(2,1)}, bf16[512,2048]{1,0:T(8,128)(2,1)}, u32[]{:S(2)}, u32[]{:S(2)}) collective-permute-start(bf16[512,2048]{1,0:T(8,128)(2,1)} %refs_5_.6), channel_id=1, source_target_pairs={{0,1},{1,0},{2,3},{3,2},{4,5},{5,4},{6,7},{7,6},{8,9},{9,8},{10,11... | collective-permute-start | bytes 6291464 | tf_op jit(solution)/shard_map/ppermute | solution.py:697
  55.4 51.0 %collective-permute-start.41 = (bf16[1024,512]{1,0:T(8,128)(2,1)S(1)}, bf16[1024,512]{1,0:T(8,128)(2,1)}, u32[]{:S(2)}, u32[]{:S(2)}) collective-permute-start(bf16[1024,512]{1,0:T(8,128)(2,1)S(1)} %get-tuple-element.180.refs_1_), channel_id=1, source_target_pairs={{0,2},{1,3},{2,0},{3,1},{4,6},{5,7},{6,4},{7,5},{8,10},{9,11},{10,... | collective-permute-start | bytes 3145736 | tf_op jit(solution)/shard_map/ppermute | solution.py:700
  57.8 48.7 %collective-permute-start = (bf16[1024,512]{1,0:T(8,128)(2,1)}, bf16[1024,512]{1,0:T(8,128)(2,1)S(1)}, u32[]{:S(2)}, u32[]{:S(2)}) collective-permute-start(bf16[1024,512]{1,0:T(8,128)(2,1)} %get-tuple-element.93.refs_1_.refs_5_), channel_id=1, source_target_pairs={{0,1},{1,0},{2,3},{3,2},{4,5},{5,4},{6,7},{7,6},{8,9},{9,8},{10,11... | collective-permute-start | bytes 3145736 | tf_op jit(solution)/shard_map/ppermute | solution.py:697
  76.5 30.5 %collective-permute-start.2 = (bf16[1024,512]{1,0:T(8,128)(2,1)}, bf16[1024,512]{1,0:T(8,128)(2,1)}, u32[]{:S(2)}, u32[]{:S(2)}) collective-permute-start(bf16[1024,512]{1,0:T(8,128)(2,1)} %collective-permute-done.1.refs_3_.refs_7_), channel_id=1, source_target_pairs={{0,1},{1,0},{2,3},{3,2},{4,5},{5,4},{6,7},{7,6},{8,9},{9,8},{10,11... | collective-permute-start | bytes 3145736 | tf_op jit(solution)/shard_map/ppermute | solution.py:697
  104.6 26.3 %collective-permute-start.19 = (bf16[1024,512]{1,0:T(8,128)(2,1)}, bf16[1024,512]{1,0:T(8,128)(2,1)}, u32[]{:S(2)}, u32[]{:S(2)}) collective-permute-start(bf16[1024,512]{1,0:T(8,128)(2,1)} %get-tuple-element.104.refs_1_.refs_2_), channel_id=1, source_target_pairs={{0,2},{1,3},{2,0},{3,1},{4,6},{5,7},{6,4},{7,5},{8,10},{9,11},{10,... | collective-permute-start | bytes 3145736 | tf_op jit(solution)/shard_map/ppermute | solution.py:700
  106.4 53.9 %collective-permute-start.11 = (bf16[512,2048]{1,0:T(8,128)(2,1)}, bf16[512,2048]{1,0:T(8,128)(2,1)}, u32[]{:S(2)}, u32[]{:S(2)}) collective-permute-start(bf16[512,2048]{1,0:T(8,128)(2,1)} %all-gather.2.cloned.1.call-done.refs_11_), channel_id=1, source_target_pairs={{0,1},{1,0},{2,3},{3,2},{4,5},{5,4},{6,7},{7,6},{8,9},{9,8},{10,11... | collective-permute-start | bytes 6291464 | tf_op jit(solution)/shard_map/ppermute | solution.py:697
  106.6 52.5 %collective-permute-start.25 = (bf16[1024,512]{1,0:T(8,128)(2,1)S(1)}, bf16[1024,512]{1,0:T(8,128)(2,1)}, u32[]{:S(2)}, u32[]{:S(2)}) collective-permute-start(bf16[1024,512]{1,0:T(8,128)(2,1)S(1)} %copy-done.16), channel_id=1, source_target_pairs={{0,2},{1,3},{2,0},{3,1},{4,6},{5,7},{6,4},{7,5},{8,10},{9,11},{10,... | collective-permute-start | bytes 3145736 | tf_op jit(solution)/shard_map/ppermute | solution.py:700
  107.0 52.7 %collective-permute-start.18 = (bf16[1024,512]{1,0:T(8,128)(2,1)}, bf16[1024,512]{1,0:T(8,128)(2,1)}, u32[]{:S(2)}, u32[]{:S(2)}) collective-permute-start(bf16[1024,512]{1,0:T(8,128)(2,1)} %get-tuple-element.104.refs_1_.refs_2_), channel_id=1, source_target_pairs={{0,1},{1,0},{2,3},{3,2},{4,5},{5,4},{6,7},{7,6},{8,9},{9,8},{10,11... | collective-permute-start | bytes 3145736 | tf_op jit(solution)/shard_map/ppermute | solution.py:697
  130.9 29.3 %collective-permute-start.20 = (bf16[1024,512]{1,0:T(8,128)(2,1)}, bf16[1024,512]{1,0:T(8,128)(2,1)}, u32[]{:S(2)}, u32[]{:S(2)}) collective-permute-start(bf16[1024,512]{1,0:T(8,128)(2,1)} %collective-permute-done.19.refs_3_), channel_id=1, source_target_pairs={{0,1},{1,0},{2,3},{3,2},{4,5},{5,4},{6,7},{7,6},{8,9},{9,8},{10,11... | collective-permute-start | bytes 3145736 | tf_op jit(solution)/shard_map/ppermute | solution.py:697
  159.1 112.3 %collective-permute-start.40 = (bf16[1024,512]{1,0:T(8,128)(2,1)S(1)}, bf16[1024,512]{1,0:T(8,128)(2,1)}, u32[]{:S(2)}, u32[]{:S(2)}) collective-permute-start(bf16[1024,512]{1,0:T(8,128)(2,1)S(1)} %get-tuple-element.180.refs_1_), channel_id=1, source_target_pairs={{0,1},{1,0},{2,3},{3,2},{4,5},{5,4},{6,7},{7,6},{8,9},{9,8},{10,11... | collective-permute-start | bytes 3145736 | tf_op jit(solution)/shard_map/ppermute | solution.py:697
  159.7 43.3 %collective-permute-start.24 = (bf16[1024,512]{1,0:T(8,128)(2,1)S(1)}, bf16[1024,512]{1,0:T(8,128)(2,1)}, u32[]{:S(2)}, u32[]{:S(2)}) collective-permute-start(bf16[1024,512]{1,0:T(8,128)(2,1)S(1)} %copy-done.16), channel_id=1, source_target_pairs={{0,1},{1,0},{2,3},{3,2},{4,5},{5,4},{6,7},{7,6},{8,9},{9,8},{10,11... | collective-permute-start | bytes 3145736 | tf_op jit(solution)/shard_map/ppermute | solution.py:697
  159.8 111.6 %collective-permute-start.42 = (bf16[1024,512]{1,0:T(8,128)(2,1)}, bf16[1024,512]{1,0:T(8,128)(2,1)}, u32[]{:S(2)}, u32[]{:S(2)}) collective-permute-start(bf16[1024,512]{1,0:T(8,128)(2,1)} %collective-permute-done.41.refs_3_), channel_id=1, source_target_pairs={{0,1},{1,0},{2,3},{3,2},{4,5},{5,4},{6,7},{7,6},{8,9},{9,8},{10,11... | collective-permute-start | bytes 3145736 | tf_op jit(solution)/shard_map/ppermute | solution.py:697
  160.2 43.4 %collective-permute-start.26 = (bf16[1024,512]{1,0:T(8,128)(2,1)}, bf16[1024,512]{1,0:T(8,128)(2,1)}, u32[]{:S(2)}, u32[]{:S(2)}) collective-permute-start(bf16[1024,512]{1,0:T(8,128)(2,1)} %collective-permute-done.25.refs_3_), channel_id=1, source_target_pairs={{0,1},{1,0},{2,3},{3,2},{4,5},{5,4},{6,7},{7,6},{8,9},{9,8},{10,11... | collective-permute-start | bytes 3145736 | tf_op jit(solution)/shard_map/ppermute | solution.py:697
  160.3 42.9 %collective-permute-start.7 = (bf16[1024,512]{1,0:T(8,128)(2,1)}, bf16[1024,512]{1,0:T(8,128)(2,1)}, u32[]{:S(2)}, u32[]{:S(2)}) collective-permute-start(bf16[1024,512]{1,0:T(8,128)(2,1)} %get-tuple-element.95.refs_1_), channel_id=1, source_target_pairs={{0,2},{1,3},{2,0},{3,1},{4,6},{5,7},{6,4},{7,5},{8,10},{9,11},{10,... | collective-permute-start | bytes 3145736 | tf_op jit(solution)/shard_map/ppermute | solution.py:700
  203.0 28.2 %collective-permute-start.6 = (bf16[1024,512]{1,0:T(8,128)(2,1)S(1)}, bf16[1024,512]{1,0:T(8,128)(2,1)}, u32[]{:S(2)}, u32[]{:S(2)}) collective-permute-start(bf16[1024,512]{1,0:T(8,128)(2,1)S(1)} %copy-done.43), channel_id=1, source_target_pairs={{0,1},{1,0},{2,3},{3,2},{4,5},{5,4},{6,7},{7,6},{8,9},{9,8},{10,11... | collective-permute-start | bytes 3145736 | tf_op jit(solution)/shard_map/ppermute | solution.py:697
  203.2 27.9 %collective-permute-start.8 = (bf16[1024,512]{1,0:T(8,128)(2,1)}, bf16[1024,512]{1,0:T(8,128)(2,1)}, u32[]{:S(2)}, u32[]{:S(2)}) collective-permute-start(bf16[1024,512]{1,0:T(8,128)(2,1)} %collective-permute-done.7.refs_3_), channel_id=1, source_target_pairs={{0,1},{1,0},{2,3},{3,2},{4,5},{5,4},{6,7},{7,6},{8,9},{9,8},{10,11... | collective-permute-start | bytes 3145736 | tf_op jit(solution)/shard_map/ppermute | solution.py:697
  230.9 68.6 %collective-permute-start.28 = (bf16[1024,512]{1,0:T(8,128)(2,1)}, bf16[1024,512]{1,0:T(8,128)(2,1)S(1)}, u32[]{:S(2)}, u32[]{:S(2)}) collective-permute-start(bf16[1024,512]{1,0:T(8,128)(2,1)} %get-tuple-element.116), channel_id=1, source_target_pairs={{0,1},{1,0},{2,3},{3,2},{4,5},{5,4},{6,7},{7,6},{8,9},{9,8},{10,11... | collective-permute-start | bytes 3145736 | tf_op jit(solution)/shard_map/ppermute | solution.py:697
  299.0 49.9 %collective-permute-start.27 = (bf16[1024,512]{1,0:T(8,128)(2,1)}, bf16[1024,512]{1,0:T(8,128)(2,1)}, u32[]{:S(2)}, u32[]{:S(2)}) collective-permute-start(bf16[1024,512]{1,0:T(8,128)(2,1)} %get-tuple-element.114), channel_id=1, source_target_pairs={{0,1},{1,0},{2,3},{3,2},{4,5},{5,4},{6,7},{7,6},{8,9},{9,8},{10,11... | collective-permute-start | bytes 3145736 | tf_op jit(solution)/shard_map/ppermute | solution.py:697
  299.2 82.2 %collective-permute-start.43 = (bf16[1024,512]{1,0:T(8,128)(2,1)}, bf16[1024,512]{1,0:T(8,128)(2,1)S(1)}, u32[]{:S(2)}, u32[]{:S(2)}) collective-permute-start(bf16[1024,512]{1,0:T(8,128)(2,1)} %get-tuple-element.133), channel_id=1, source_target_pairs={{0,1},{1,0},{2,3},{3,2},{4,5},{5,4},{6,7},{7,6},{8,9},{9,8},{10,11... | collective-permute-start | bytes 3145736 | tf_op jit(solution)/shard_map/ppermute | solution.py:697
  299.8 49.1 %collective-permute-start.29 = (bf16[1024,512]{1,0:T(8,128)(2,1)S(1)}, bf16[1024,512]{1,0:T(8,128)(2,1)}, u32[]{:S(2)}, u32[]{:S(2)}) collective-permute-start(bf16[1024,512]{1,0:T(8,128)(2,1)S(1)} %add_convert_fusion.3), channel_id=1, source_target_pairs={{0,2},{1,3},{2,0},{3,1},{4,6},{5,7},{6,4},{7,5},{8,10},{9,11},{10,... | collective-permute-start | bytes 3145736 | tf_op jit(solution)/shard_map/ppermute | solution.py:700
  301.9 79.5 %collective-permute-start.45 = (bf16[1024,512]{1,0:T(8,128)(2,1)S(1)}, bf16[1024,512]{1,0:T(8,128)(2,1)S(1)}, u32[]{:S(2)}, u32[]{:S(2)}) collective-permute-start(bf16[1024,512]{1,0:T(8,128)(2,1)S(1)} %add_convert_fusion.1), channel_id=1, source_target_pairs={{0,2},{1,3},{2,0},{3,1},{4,6},{5,7},{6,4},{7,5},{8,10},{9,11},{10,... | collective-permute-start | bytes 3145736 | tf_op jit(solution)/shard_map/ppermute | solution.py:700
  304.4 43.9 %collective-permute-start.31 = (f32[8,1024]{1,0:T(8,128)S(1)}, f32[8,1024]{1,0:T(8,128)S(1)}, u32[]{:S(2)}, u32[]{:S(2)}) collective-permute-start(f32[8,1024]{1,0:T(8,128)S(1)} %add.135), channel_id=1, source_target_pairs={{0,2},{1,3},{2,0},{3,1},{4,6},{5,7},{6,4},{7,5},{8,10},{9,11},{10,... | collective-permute-start | bytes 98312 | tf_op jit(solution)/shard_map/ppermute | solution.py:700
  355.4 33.7 %collective-permute-start.33 = (bf16[1024,512]{1,0:T(8,128)(2,1)}, bf16[1024,512]{1,0:T(8,128)(2,1)}, u32[]{:S(2)}, u32[]{:S(2)}) collective-permute-start(bf16[1024,512]{1,0:T(8,128)(2,1)} %get-tuple-element.119.refs_1_), channel_id=1, source_target_pairs={{0,2},{1,3},{2,0},{3,1},{4,6},{5,7},{6,4},{7,5},{8,10},{9,11},{10,... | collective-permute-start | bytes 3145736 | tf_op jit(solution)/shard_map/ppermute | solution.py:700
  389.1 24.5 %collective-permute-start.34 = (bf16[1024,512]{1,0:T(8,128)(2,1)}, bf16[1024,512]{1,0:T(8,128)(2,1)}, u32[]{:S(2)}, u32[]{:S(2)}) collective-permute-start(bf16[1024,512]{1,0:T(8,128)(2,1)} %collective-permute-done.33.refs_3_), channel_id=1, source_target_pairs={{0,1},{1,0},{2,3},{3,2},{4,5},{5,4},{6,7},{7,6},{8,9},{9,8},{10,11... | collective-permute-start | bytes 3145736 | tf_op jit(solution)/shard_map/ppermute | solution.py:697
  389.6 31.7 %collective-permute-start.48 = (bf16[1024,512]{1,0:T(8,128)(2,1)}, bf16[1024,512]{1,0:T(8,128)(2,1)S(1)}, u32[]{:S(2)}, u32[]{:S(2)}) collective-permute-start(bf16[1024,512]{1,0:T(8,128)(2,1)} %get-tuple-element.138.refs_1_), channel_id=1, source_target_pairs={{0,1},{1,0},{2,3},{3,2},{4,5},{5,4},{6,7},{7,6},{8,9},{9,8},{10,11... | collective-permute-start | bytes 3145736 | tf_op jit(solution)/shard_map/ppermute | solution.py:697
  438.7 313.3 %reduce-scatter.5.cloned.1.call-start = ((), (), s32[]{:S(2)}) async-start(), calls=%async_computation.5 | async-start | bytes 7077888 | tf_op jit(solution)/shard_map/reduce_scatter | solution.py:871
  485.3 295.8 %reduce-scatter.11.cloned.1.call-start = ((), (), s32[]{:S(2)}) async-start(), calls=%async_computation.8 | async-start | bytes 9437184 | tf_op jit(solution)/shard_map/reduce_scatter | solution.py:868
  515.2 418.0 %reduce-scatter.9.cloned.1.call-start = ((), (), s32[]{:S(2)}) async-start(), calls=%async_computation.7 | async-start | bytes 9437184 | tf_op jit(solution)/shard_map/reduce_scatter | solution.py:869
  541.7 33.9 %collective-permute-start.21 = (bf16[1024,512]{1,0:T(8,128)(2,1)}, bf16[1024,512]{1,0:T(8,128)(2,1)}, u32[]{:S(2)}, u32[]{:S(2)}) collective-permute-start(bf16[1024,512]{1,0:T(8,128)(2,1)} %get-tuple-element.108), channel_id=1, source_target_pairs={{0,1},{1,0},{2,3},{3,2},{4,5},{5,4},{6,7},{7,6},{8,9},{9,8},{10,11... | collective-permute-start | bytes 3145736 | tf_op jit(solution)/shard_map/ppermute | solution.py:697
  542.4 28.1 %collective-permute-start.22 = (bf16[1024,512]{1,0:T(8,128)(2,1)}, bf16[1024,512]{1,0:T(8,128)(2,1)}, u32[]{:S(2)}, u32[]{:S(2)}) collective-permute-start(bf16[1024,512]{1,0:T(8,128)(2,1)} %get-tuple-element.110), channel_id=1, source_target_pairs={{0,1},{1,0},{2,3},{3,2},{4,5},{5,4},{6,7},{7,6},{8,9},{9,8},{10,11... | collective-permute-start | bytes 3145736 | tf_op jit(solution)/shard_map/ppermute | solution.py:697
  542.4 33.8 %collective-permute-start.12 = (bf16[1024,512]{1,0:T(8,128)(2,1)}, bf16[1024,512]{1,0:T(8,128)(2,1)}, u32[]{:S(2)}, u32[]{:S(2)}) collective-permute-start(bf16[1024,512]{1,0:T(8,128)(2,1)} %get-tuple-element.99), channel_id=1, source_target_pairs={{0,1},{1,0},{2,3},{3,2},{4,5},{5,4},{6,7},{7,6},{8,9},{9,8},{10,11... | collective-permute-start | bytes 3145736 | tf_op jit(solution)/shard_map/ppermute | solution.py:697
  542.9 29.4 %collective-permute-start.13 = (bf16[1024,512]{1,0:T(8,128)(2,1)}, bf16[1024,512]{1,0:T(8,128)(2,1)S(1)}, u32[]{:S(2)}, u32[]{:S(2)}) collective-permute-start(bf16[1024,512]{1,0:T(8,128)(2,1)} %get-tuple-element.101), channel_id=1, source_target_pairs={{0,1},{1,0},{2,3},{3,2},{4,5},{5,4},{6,7},{7,6},{8,9},{9,8},{10,11... | collective-permute-start | bytes 3145736 | tf_op jit(solution)/shard_map/ppermute | solution.py:697
  572.3 26.0 %collective-permute-start.23 = (bf16[1024,512]{1,0:T(8,128)(2,1)S(1)}, bf16[1024,512]{1,0:T(8,128)(2,1)S(1)}, u32[]{:S(2)}, u32[]{:S(2)}) collective-permute-start(bf16[1024,512]{1,0:T(8,128)(2,1)S(1)} %add_convert_fusion.5), channel_id=1, source_target_pairs={{0,2},{1,3},{2,0},{3,1},{4,6},{5,7},{6,4},{7,5},{8,10},{9,11},{10,... | collective-permute-start | bytes 3145736 | tf_op jit(solution)/shard_map/ppermute | solution.py:700
  572.7 48.1 %collective-permute-start.14 = (bf16[1024,512]{1,0:T(8,128)(2,1)S(1)}, bf16[1024,512]{1,0:T(8,128)(2,1)S(1)}, u32[]{:S(2)}, u32[]{:S(2)}) collective-permute-start(bf16[1024,512]{1,0:T(8,128)(2,1)S(1)} %add_convert_fusion.7), channel_id=1, source_target_pairs={{0,2},{1,3},{2,0},{3,1},{4,6},{5,7},{6,4},{7,5},{8,10},{9,11},{10,... | collective-permute-start | bytes 3145736 | tf_op jit(solution)/shard_map/ppermute | solution.py:700
  575.2 45.7 %collective-permute-start.54 = (f32[8,1024]{1,0:T(8,128)S(1)}, f32[8,1024]{1,0:T(8,128)S(1)}, u32[]{:S(2)}, u32[]{:S(2)}) collective-permute-start(f32[8,1024]{1,0:T(8,128)S(1)} %copy-done.24), channel_id=1, source_target_pairs={{0,1},{1,0},{2,3},{3,2},{4,5},{5,4},{6,7},{7,6},{8,9},{9,8},{10,11... | collective-permute-start | bytes 98312 | tf_op jit(solution)/shard_map/ppermute | solution.py:697
  575.7 94.8 %collective-permute-start.51 = (bf16[1024,512]{1,0:T(8,128)(2,1)S(1)}, bf16[1024,512]{1,0:T(8,128)(2,1)S(1)}, u32[]{:S(2)}, u32[]{:S(2)}) collective-permute-start(bf16[1024,512]{1,0:T(8,128)(2,1)S(1)} %copy-done.45), channel_id=1, source_target_pairs={{0,1},{1,0},{2,3},{3,2},{4,5},{5,4},{6,7},{7,6},{8,9},{9,8},{10,11... | collective-permute-start | bytes 3145736 | tf_op jit(solution)/shard_map/ppermute | solution.py:697
  576.2 111.1 %collective-permute-start.35 = (bf16[1024,512]{1,0:T(8,128)(2,1)}, bf16[1024,512]{1,0:T(8,128)(2,1)S(1)}, u32[]{:S(2)}, u32[]{:S(2)}) collective-permute-start(bf16[1024,512]{1,0:T(8,128)(2,1)} %get-tuple-element.124), channel_id=1, source_target_pairs={{0,1},{1,0},{2,3},{3,2},{4,5},{5,4},{6,7},{7,6},{8,9},{9,8},{10,11... | collective-permute-start | bytes 3145736 | tf_op jit(solution)/shard_map/ppermute | solution.py:697
  598.3 72.2 %collective-permute-start.53 = (bf16[1024,512]{1,0:T(8,128)(2,1)S(1)}, bf16[1024,512]{1,0:T(8,128)(2,1)S(1)}, u32[]{:S(2)}, u32[]{:S(2)}) collective-permute-start(bf16[1024,512]{1,0:T(8,128)(2,1)S(1)} %add_convert_fusion), channel_id=1, source_target_pairs={{0,2},{1,3},{2,0},{3,1},{4,6},{5,7},{6,4},{7,5},{8,10},{9,11},{10,... | collective-permute-start | bytes 3145736 | tf_op jit(solution)/shard_map/ppermute | solution.py:700
  620.8 66.6 %collective-permute-start.37 = (bf16[1024,512]{1,0:T(8,128)(2,1)S(1)}, bf16[1024,512]{1,0:T(8,128)(2,1)S(1)}, u32[]{:S(2)}, u32[]{:S(2)}) collective-permute-start(bf16[1024,512]{1,0:T(8,128)(2,1)S(1)} %add_convert_fusion.2), channel_id=1, source_target_pairs={{0,2},{1,3},{2,0},{3,1},{4,6},{5,7},{6,4},{7,5},{8,10},{9,11},{10,... | collective-permute-start | bytes 3145736 | tf_op jit(solution)/shard_map/ppermute | solution.py:700
  624.0 42.0 %collective-permute-start.55 = (f32[8,1024]{1,0:T(8,128)S(1)}, f32[8,1024]{1,0:T(8,128)S(1)}, u32[]{:S(2)}, u32[]{:S(2)}) collective-permute-start(f32[8,1024]{1,0:T(8,128)S(1)} %add.144), channel_id=1, source_target_pairs={{0,2},{1,3},{2,0},{3,1},{4,6},{5,7},{6,4},{7,5},{8,10},{9,11},{10,... | collective-permute-start | bytes 98312 | tf_op jit(solution)/shard_map/ppermute | solution.py:700
  (63 other events, 1119.4 us)
Sparse Core Ops, SparseCore 0:
  18.4 50.7 all-gather.1
  438.8 68.5 reduce-scatter.6
  511.0 117.0 reduce-scatter.4
  631.6 149.5 reduce-scatter.10
  785.1 147.9 reduce-scatter.8

commit v2 on v1

--- a/solution.py
+++ b/solution.py
@@ -32,21 +32,39 @@
     return lax.dot_general(a, b, (((0,), (0,)), ((), ())), preferred_element_type=F32)
 
 
-def call(name, body, grid, args, in_specs, outs, out_specs, scratch=(), flops=0, trans=0, **kw):
+class Order:
+    last = None
+
+
+def call(
+    name, body, grid, args, in_specs, outs, out_specs, scratch=(), flops=0, prefetch=0, after=(), aliases=None
+):
     moved = sum(a.size * a.dtype.itemsize for a in args)
     moved += sum(math.prod(o.shape) * o.dtype.itemsize for o in outs)
-    return pl.pallas_call(
-        body,
-        grid=grid,
-        in_specs=in_specs,
-        out_specs=out_specs,
+    count = len(args)
+    extra = [*after] + ([] if Order.last is None else [Order.last])
+
+    def without_extra(*refs):
+        body(*refs[:count], *refs[count + len(extra) :])
+
+    got = pl.pallas_call(
+        without_extra,
+        grid_spec=pltpu.PrefetchScalarGridSpec(
+            num_scalar_prefetch=prefetch,
+            grid=grid,
+            in_specs=list(in_specs) + [ANY] * len(extra),
+            out_specs=out_specs,
+            scratch_shapes=list(scratch),
+        ),
         out_shape=outs,
-        scratch_shapes=list(scratch),
+        input_output_aliases=aliases or {},
         compiler_params=pltpu.CompilerParams(vmem_limit_bytes=60 * MIB),
-        cost_estimate=pl.CostEstimate(flops=flops, bytes_accessed=moved, transcendentals=trans),
+        cost_estimate=pl.CostEstimate(flops=flops, bytes_accessed=moved, transcendentals=0),
         name=name,
-        **kw,
-    )(*args)
+    )(*args, *extra)
+    fresh = [v for i, v in enumerate(got) if i not in (aliases or {}).values()]
+    Order.last = min(fresh or got, key=lambda v: v.size)
+    return got
 
 
 def shape(dims, dtype):
@@ -57,6 +75,21 @@
 ANY = pl.BlockSpec(memory_space=pl.ANY)
 
 
+def gate(arrays, after):
+    arrays = list(arrays)
+    return call(
+        "gate",
+        lambda *refs: None,
+        (1,),
+        arrays,
+        [ANY] * len(arrays),
+        [shape(a.shape, a.dtype) for a in arrays],
+        [ANY] * len(arrays),
+        after=after,
+        aliases={i: i for i in range(len(arrays))},
+    )
+
+
 def rows_of(block):
     return pl.BlockSpec(block, lambda i: (i, 0))
 
@@ -67,6 +100,10 @@
 
 def fixed(block):
     return pl.BlockSpec(block, lambda i: (0,) * len(block))
+
+
+def place_of(me, j, width):
+    return pl.ds(pl.multiple_of((me ^ j) * width, width), width)
 
 
 def start_all(copies):
@@ -86,7 +123,7 @@
 def row_blocks(me, n, width, source, target, sems, base):
     return [
         pltpu.make_async_copy(
-            source.at[pl.ds(pl.multiple_of((me ^ j) * width, width), width), :],
+            source.at[place_of(me, j, width), :],
             target.at[pl.ds(j * width, width), :],
             sems.at[base + j],
         )
@@ -97,7 +134,7 @@
 def col_blocks(me, n, width, source, target, sems, base):
     return [
         pltpu.make_async_copy(
-            source.at[:, pl.ds(pl.multiple_of((me ^ j) * width, width), width)],
+            source.at[:, place_of(me, j, width)],
             target.at[:, pl.ds(j * width, width)],
             sems.at[base + j],
         )
@@ -153,7 +190,11 @@
     gain, bias, cosine, sine, weight, qkv, normed, stat, held, sems = refs[n:]
     width = xs[0].shape[1]
     full = n * width
-    copies = row_blocks(me[0], n, width, weight, held, sems, 0)
+    heads = held.shape[1] // (3 * HEAD)
+    copies = []
+    for h in range(heads):
+        part = pl.ds(3 * h * HEAD, 3 * HEAD)
+        copies.append(pltpu.make_async_copy(weight.at[:, part], held.at[:, part], sems.at[h]))
     start_all(copies)
     total = square = 0.0
     for x in xs:
@@ -165,11 +206,11 @@
     stat[...] = stat_columns(mean, inv)
     for j, x in enumerate(xs):
         part = slice(j * width, (j + 1) * width)
-        normed[:, part] = (
+        normed[:, place_of(me[0], j, width)] = (
             (x[...].astype(F32) - mean) * inv * gain[0:1, part] + bias[0:1, part]
         ).astype(BF16)
-    wait_all(copies)
-    for h in range(held.shape[1] // (3 * HEAD)):
+    for h in range(heads):
+        wait_all(copies[h : h + 1])
         base = 3 * h * HEAD
         out = dot_nn(normed[...], held[:, base : base + 3 * HEAD])
         for s in range(2):
@@ -195,7 +236,7 @@
         + [ANY],
         [shape((length, out), BF16), shape((length, full), BF16), shape((length, 128), F32)],
         [rows_of((tile, out)), rows_of((tile, full)), rows_of((tile, 128))],
-        scratch=[pltpu.VMEM((full, out), BF16), pltpu.SemaphoreType.DMA((n,))],
+        scratch=[pltpu.VMEM((full, out), BF16), pltpu.SemaphoreType.DMA((out // (3 * HEAD),))],
         flops=2 * length * full * out,
     )
 
@@ -304,23 +345,29 @@
     full = n * width
     inner = up_held.shape[1]
     out_copies = []
-    for k in range(n):
-        for j in range(n):
+    for j in range(n):
+        for k in range(n):
             out_copies.append(
                 pltpu.make_async_copy(
-                    outs_w[k].at[:, pl.ds(pl.multiple_of((me[0] ^ j) * width, width), width)],
+                    outs_w[k].at[:, place_of(me[0], j, width)],
                     out_held.at[pl.ds(k * width, width), pl.ds(j * width, width)],
                     sems.at[k * n + j],
                 )
             )
-    up_copies = row_blocks(me[0], n, width, up_weight, up_held, sems, n * n)
-    down_copies = col_blocks(me[0], n, width, down_weight, down_held, sems, n * n + n)
+    step = divisor(inner, 512)
+    up_copies = []
+    for c in range(inner // step):
+        part = pl.ds(c * step, step)
+        up_copies.append(
+            pltpu.make_async_copy(up_weight.at[:, part], up_held.at[:, part], sems.at[n * n + n + c])
+        )
+    down_copies = col_blocks(me[0], n, width, down_weight, down_held, sems, n * n)
     start_all(out_copies + up_copies + down_copies)
     for j in range(n):
         joined[:, j * width : (j + 1) * width] = attended[j][...]
-    wait_all(out_copies)
     total = square = 0.0
     for j in range(n):
+        wait_all(out_copies[j * n : (j + 1) * n])
         part = slice(j * width, (j + 1) * width)
         base = own[...] if j == 0 else xs[j][...].astype(F32)
         value = base + dot_nn(joined[...], out_held[:, part])
@@ -334,19 +381,18 @@
     stat[...] = stat_columns(mean, inv)
     for j in range(n):
         part = slice(j * width, (j + 1) * width)
-        normed[:, part] = (
+        normed[:, place_of(me[0], j, width)] = (
             (whole[:, part] - mean) * inv * gain[0:1, part] + bias[0:1, part]
         ).astype(BF16)
-    wait_all(up_copies)
-    step = min(512, inner)
     for c in range(inner // step):
+        wait_all(up_copies[c : c + 1])
         part = slice(c * step, (c + 1) * step)
         up = dot_nn(normed[...], up_held[:, part]) + up_bias[0:1, part]
         half = 0.5 * (1.0 + lax.erf(up * SQRT_HALF))
         activated[:, part] = (up * half).astype(BF16)
         slope[:, part] = (half + up * INV_ROOT_TWO_PI * jnp.exp(-0.5 * up * up)).astype(BF16)
-    wait_all(down_copies)
     for j in range(n):
+        wait_all(down_copies[j : j + 1])
         parts[j][...] = dot_nn(
             activated[...], down_held[:, j * width : (j + 1) * width]
         ).astype(BF16)
@@ -390,7 +436,7 @@
             pltpu.VMEM((inner, full), BF16),
             pltpu.VMEM((tile, full), BF16),
             pltpu.VMEM((tile, full), F32),
-            pltpu.SemaphoreType.DMA((n * n + 2 * n,)),
+            pltpu.SemaphoreType.DMA((n * n + n + inner // divisor(inner, 512),)),
         ],
         flops=2 * length * full * (full + 2 * inner),
     )
@@ -401,78 +447,92 @@
     return stat_columns(total, weighted).T[0:8, :]
 
 
+def join_body(n, me, *refs):
+    blocks, whole, sums = refs[:n], refs[n], refs[n + 1]
+    width = blocks[0].shape[1]
+    for j in range(n):
+        whole[:, place_of(me[0], j, width)] = blocks[j][...]
+    accumulate(sums, fold_rows(blocks[0][...].astype(F32)))
+
+
+def join(me, blocks):
+    n, (length, width) = len(blocks), blocks[0].shape
+    tile = min(256, length)
+    return call(
+        "join",
+        lambda *refs: join_body(n, *refs),
+        (length // tile,),
+        (me, *blocks),
+        [SMEM] + [rows_of((tile, width))] * n,
+        [shape((length, n * width), BF16), shape((8, width), F32)],
+        [rows_of((tile, n * width)), fixed((8, width))],
+    )
+
+
 def feed_back_body(n, me, *refs):
-    cots = refs[:n]
-    slope, normed, gain, bias, up_weight, down_weight = refs[n : n + 6]
-    cot_full, up_grad, sums, up_bias_sum, down_bias_sum = refs[n + 6 : n + 11]
-    parts = refs[n + 11 : 2 * n + 11]
-    up_held, down_held, sems = refs[2 * n + 11 :]
-    width = cots[0].shape[1]
+    cot, slope, normed, gain, bias, up_weight, down_weight = refs[:7]
+    up_grad, sums, up_bias_sum = refs[7:10]
+    parts = refs[10 : n + 10]
+    up_held, down_held, sems = refs[n + 10 :]
+    width = parts[0].shape[1]
     inner = up_held.shape[1]
-    down_copies = col_blocks(me[0], n, width, down_weight, down_held, sems, 0)
-    up_copies = row_blocks(me[0], n, width, up_weight, up_held, sems, n)
+    step = divisor(inner, 512)
+    steps = inner // step
+    down_copies = []
+    for c in range(steps):
+        part = pl.ds(c * step, step)
+        down_copies.append(
+            pltpu.make_async_copy(down_weight.at[part, :], down_held.at[part, :], sems.at[n + c])
+        )
+    up_copies = row_blocks(me[0], n, width, up_weight, up_held, sems, 0)
     start_all(down_copies + up_copies)
-    for j in range(n):
-        cot_full[:, j * width : (j + 1) * width] = cots[j][...]
-    accumulate(down_bias_sum, fold_rows(cots[0][...].astype(F32)))
-    wait_all(down_copies)
-    step = min(512, inner)
-    for c in range(inner // step):
+    bias_parts = []
+    for c in range(steps):
+        wait_all(down_copies[c : c + 1])
         part = slice(c * step, (c + 1) * step)
-        value = dot_nt(cot_full[...], down_held[part, :]) * slope[:, part].astype(F32)
-        up_grad[:, part] = value.astype(BF16)
-    accumulate(up_bias_sum, fold_rows(up_grad[...].astype(F32)))
-    wait_all(up_copies)
+        value = dot_nt(cot[...], down_held[part, :]) * slope[:, part].astype(F32)
+        low = value.astype(BF16)
+        up_grad[:, part] = low
+        bias_parts.append(fold_rows(low.astype(F32)))
+    accumulate(up_bias_sum, jnp.concatenate(bias_parts, 1))
     total = weighted = 0.0
     for j in range(n):
+        wait_all(up_copies[j : j + 1])
         part = slice(j * width, (j + 1) * width)
         value = dot_nt(up_grad[...], up_held[part, :])
         parts[j][...] = value.astype(BF16)
         total += jnp.sum(value * gain[0:1, part], 1, keepdims=True)
-        weighted += jnp.sum(
-            value * (normed[:, part].astype(F32) - bias[0:1, part]), 1, keepdims=True
-        )
+        there = normed[:, place_of(me[0], j, width)].astype(F32)
+        weighted += jnp.sum(value * (there - bias[0:1, part]), 1, keepdims=True)
     sums[...] = row_stats(total, weighted)
 
 
-def feed_back(me, cots, slope, normed, gain, bias, up_weight, down_weight):
-    n, (length, width) = len(cots), cots[0].shape
-    full, inner = up_weight.shape
+def feed_back(me, n, cot, slope, normed, gain, bias, up_weight, down_weight):
+    length, full = cot.shape
+    width = full // n
+    inner = up_weight.shape[1]
     tile = min(256, length)
     got = call(
         "feed_back",
         lambda *refs: feed_back_body(n, *refs),
         (length // tile,),
-        (me, *cots, slope, normed, gain, bias, up_weight, down_weight),
+        (me, cot, slope, normed, gain, bias, up_weight, down_weight),
         [SMEM]
-        + [rows_of((tile, width))] * n
-        + [rows_of((tile, inner)), rows_of((tile, full))]
+        + [rows_of((tile, full)), rows_of((tile, inner)), rows_of((tile, full))]
         + [fixed((8, full))] * 2
         + [ANY] * 2,
-        [
-            shape((length, full), BF16),
-            shape((length, inner), BF16),
-            shape((8, length), F32),
-            shape((8, inner), F32),
-            shape((8, width), F32),
-        ]
+        [shape((length, inner), BF16), shape((8, length), F32), shape((8, inner), F32)]
         + [shape((length, width), BF16)] * n,
-        [
-            rows_of((tile, full)),
-            rows_of((tile, inner)),
-            cols_of((8, tile)),
-            fixed((8, inner)),
-            fixed((8, width)),
-        ]
+        [rows_of((tile, inner)), cols_of((8, tile)), fixed((8, inner))]
         + [rows_of((tile, width))] * n,
         scratch=[
             pltpu.VMEM((full, inner), BF16),
             pltpu.VMEM((inner, full), BF16),
-            pltpu.SemaphoreType.DMA((2 * n,)),
+            pltpu.SemaphoreType.DMA((n + inner // divisor(inner, 512),)),
         ],
         flops=4 * length * full * inner,
     )
-    return (*got[:5], got[5:])
+    return (*got[:3], got[3:])
 
 
 def norm_back(refs, n_parts, source, stat, sums, gain, full):
@@ -524,14 +584,11 @@
 
 def attended_back_body(n, me, *refs):
     grads = refs[:n]
-    weight, joined, out, held, sems = refs[n:]
+    weight, joined, out = refs[n:]
     width = grads[0].shape[1]
-    copies = col_blocks(me[0], n, width, weight, held, sems, 0)
-    start_all(copies)
     for j in range(n):
-        joined[:, j * width : (j + 1) * width] = grads[j][...]
-    wait_all(copies)
-    out[...] = dot_nt(joined[...], held[...]).astype(BF16)
+        joined[:, place_of(me[0], j, width)] = grads[j][...]
+    out[...] = dot_nt(joined[...], weight[...]).astype(BF16)
 
 
 def attended_back(me, grads, weight):
@@ -543,10 +600,9 @@
         lambda *refs: attended_back_body(n, *refs),
         (length // tile,),
         (me, *grads, weight),
-        [SMEM] + [rows_of((tile, width))] * n + [ANY],
+        [SMEM] + [rows_of((tile, width))] * n + [fixed((rows, full))],
         [shape((length, full), BF16), shape((length, rows), BF16)],
         [rows_of((tile, full)), rows_of((tile, rows))],
-        scratch=[pltpu.VMEM((rows, full), BF16), pltpu.SemaphoreType.DMA((n,))],
         flops=2 * length * full * rows,
     )
 
@@ -557,16 +613,15 @@
     width = parts[0].shape[1]
     copies = row_blocks(me[0], n, width, weight, held, sems, 0)
     start_all(copies)
-    wait_all(copies)
     total = weighted = 0.0
     for j in range(n):
+        wait_all(copies[j : j + 1])
         part = slice(j * width, (j + 1) * width)
         value = dot_nt(grad[...], held[part, :])
         parts[j][...] = value.astype(BF16)
         total += jnp.sum(value * gain[0:1, part], 1, keepdims=True)
-        weighted += jnp.sum(
-            value * (normed[:, part].astype(F32) - bias[0:1, part]), 1, keepdims=True
-        )
+        there = normed[:, place_of(me[0], j, width)].astype(F32)
+        weighted += jnp.sum(value * (there - bias[0:1, part]), 1, keepdims=True)
     sums[...] = row_stats(total, weighted)
 
 
@@ -622,7 +677,7 @@
     )
     more = {}
     if made is not None:
-        more = {"input_output_aliases": {len(args): 0}}
+        more = {"aliases": {len(args): 0}}
         args, specs = (*args, made), specs + [ANY]
     return call(
         "average_back",
@@ -637,7 +692,11 @@
     )
 
 
-def weight_body(rows, me, *refs):
+def divisor(size, most):
+    return max(d for d in range(128, most + 1, 128) if size % d == 0) if size > 128 else size
+
+
+def weight_body(rows, *refs):
     out = refs[-1]
     total = dot_tn(refs[0][...], refs[rows][...])
     for r in range(1, rows):
@@ -645,44 +704,207 @@
     out[...] = total.astype(BF16)
 
 
-def divisor(size, most):
-    return max(d for d in range(128, most + 1, 128) if size % d == 0)
-
-
-def weight_grad(me, lefts, rights, width, turned):
+def weight_grad(lefts, rights):
     rows, (length, high), wide = len(lefts), lefts[0].shape, rights[0].shape[1]
     tall, across = divisor(high, 512), divisor(wide, 1024)
-    if turned == 0:
-        tall = min(tall, width)
-    if turned == 1:
-        across = min(across, width)
-    per = width // (tall if turned == 0 else across)
-
-    def place(i, j, me):
-        if turned == 0:
-            i = (me[0] ^ (i // per)) * per + i % per
-        if turned == 1:
-            j = (me[0] ^ (j // per)) * per + j % per
-        return i, j
-
-    return pl.pallas_call(
+    return call(
+        "weight_grad",
         lambda *refs: weight_body(rows, *refs),
-        grid_spec=pltpu.PrefetchScalarGridSpec(
-            num_scalar_prefetch=1,
-            grid=(high // tall, wide // across),
-            in_specs=[pl.BlockSpec((length, tall), lambda i, j, me: (0, i))] * rows
-            + [pl.BlockSpec((length, across), lambda i, j, me: (0, j))] * rows,
-            out_specs=pl.BlockSpec((tall, across), place),
-        ),
-        out_shape=shape((high, wide), BF16),
-        compiler_params=pltpu.CompilerParams(vmem_limit_bytes=60 * MIB),
-        cost_estimate=pl.CostEstimate(
-            flops=2 * rows * length * high * wide,
-            bytes_accessed=2 * (rows * length * (high + wide) + high * wide),
-            transcendentals=0,
-        ),
-        name="weight_grad",
-    )(me, *lefts, *rights)
+        (high // tall, wide // across),
+        (*lefts, *rights),
+        [pl.BlockSpec((length, tall), lambda i, j: (0, i))] * rows
+        + [pl.BlockSpec((length, across), lambda i, j: (0, j))] * rows,
+        [shape((high, wide), BF16)],
+        [pl.BlockSpec((tall, across), lambda i, j: (i, j))],
+        flops=2 * rows * length * high * wide,
+    )[0]
+
+
+def tall_blocks_body(rows, count, group, *refs):
+    lefts, rights = refs[: rows * count], refs[rows * count : rows * count + rows]
+    out, turned = refs[-2:]
+    high = lefts[0].shape[1]
+    length = lefts[0].shape[0]
+
+    @pl.when(pl.program_id(0) == 0)
+    def _():
+        for k in range(count):
+            for r in range(rows):
+                turned[k * high : (k + 1) * high, r * length : (r + 1) * length] = lefts[
+                    k * rows + r
+                ][...].T
+
+    total = 0.0
+    for r in range(rows):
+        total += dot_nn(turned[:, r * length : (r + 1) * length], rights[r][...])
+    out[...] = total.astype(BF16).reshape(out.shape)
+
+
+def wide_blocks_body(rows, count, group, *refs):
+    lefts, rights = refs[:rows], refs[rows : rows + rows * count]
+    out = refs[-1]
+    turned = [left[...].T for left in lefts]
+    for k in range(count):
+        total = 0.0
+        for r in range(rows):
+            total += dot_nn(turned[r], rights[k * rows + r][...])
+        out[k] = total.astype(BF16)
+
+
+class Spread:
+    def __init__(self, lefts, rights, dim, bits, part=(0, 1)):
+        self.lefts, self.rights, self.dim, self.bits, self.part = lefts, rights, dim, list(bits), part
+        self.groups = lax.axis_size("dp")
+        self.block = (lefts, rights)[dim][0].shape[1] // self.groups
+        order = [0]
+        for bit in reversed(self.bits):
+            order = order + [e | bit for e in order]
+        self.order = order
+
+    def blocks(self, half):
+        count = self.groups // 2
+        which = self.order[half * count : (half + 1) * count]
+        rows, length = len(self.lefts), self.lefts[0].shape[0]
+        group = lax.axis_index("dp").astype(jnp.int32)[None]
+        size, (index, pieces) = self.block, self.part
+        stay = [
+            pl.BlockSpec((length, size), lambda i, group, e=e: (0, group[0] ^ e))
+            for e in which
+            for _ in range(rows)
+        ]
+        other = self.rights if self.dim == 0 else self.lefts
+        extent = other[0].shape[1] // pieces
+        tile = divisor(extent, 512)
+        steps = extent // tile
+        move = [pl.BlockSpec((length, tile), lambda i, group: (0, index * steps + i))] * rows
+        if self.dim == 0:
+            args = (*(list(self.lefts) * count), *self.rights)
+            specs = stay + move
+            out, spec = (count, size, extent), pl.BlockSpec((count, size, tile), lambda i, group: (0, 0, i))
+            body, scratch = tall_blocks_body, [pltpu.VMEM((count * size, rows * length), BF16)]
+        else:
+            args = (*self.lefts, *(list(self.rights) * count))
+            specs = move + stay
+            out, spec = (count, extent, size), pl.BlockSpec((count, tile, size), lambda i, group: (0, i, 0))
+            body, scratch = wide_blocks_body, []
+        return call(
+            "weight_blocks",
+            lambda *refs: body(rows, count, *refs),
+            (steps,),
+            (group, *args),
+            specs,
+            [shape(out, BF16)],
+            [spec],
+            scratch=scratch,
+            flops=2 * rows * length * count * size * extent,
+            prefetch=1,
+        )[0]
+
+    def send(self, value, step):
+        bit = self.bits[step]
+        return lax.ppermute(value, "dp", [(i, i ^ bit) for i in range(self.groups)])
+
+    def first(self):
+        self.coming = self.send(self.blocks(1), 0)
+        self.step = 1
+
+    def keep(self):
+        self.held = self.blocks(0)
+
+    def next(self):
+        self.held, out = fold(self.held, self.coming)
+        self.coming = self.send(out, self.step)
+        self.step += 1
+
+    def finish(self):
+        return fold_last(self.held, self.coming)
+
+
+def fold_body(held, came, keep, send):
+    half = keep.shape[0]
+    keep[...] = (held[:half].astype(F32) + came[:half].astype(F32)).astype(BF16)
+    send[...] = (held[half:].astype(F32) + came[half:].astype(F32)).astype(BF16)
+
+
+def fold(held, came):
+    count, high, wide = held.shape
+    tile = max(16, high // 4)
+    full = pl.BlockSpec((count, tile, wide), lambda i: (0, i, 0))
+    half = pl.BlockSpec((count // 2, tile, wide), lambda i: (0, i, 0))
+    return call(
+        "fold",
+        fold_body,
+        (high // tile,),
+        (held, came),
+        [full, full],
+        [shape((count // 2, high, wide), BF16)] * 2,
+        [half, half],
+    )
+
+
+def fold_last_body(held, came, out):
+    out[...] = held[0].astype(F32) + came[0].astype(F32)
+
+
+def fold_last(held, came):
+    _, high, wide = held.shape
+    tile = max(16, high // 4)
+    spec = pl.BlockSpec((1, tile, wide), lambda i: (0, i, 0))
+    return call(
+        "fold_last",
+        fold_last_body,
+        (high // tile,),
+        (held, came),
+        [spec, spec],
+        [shape((high, wide), F32)],
+        [rows_of((tile, wide))],
+    )[0]
+
+
+def add_body(left, right, out):
+    out[...] = (left[...].astype(F32) + right[...].astype(F32)).astype(BF16)
+
+
+def add(left, right):
+    length, width = left.shape
+    tile = min(512, length)
+    return call(
+        "add",
+        add_body,
+        (length // tile,),
+        (left, right),
+        [rows_of((tile, width))] * 2,
+        [shape((length, width), BF16)],
+        [rows_of((tile, width))],
+    )[0]
+
+
+def output_body(k, *refs):
+    parts, hidden, bias, out = refs[:k], refs[k], refs[k + 1], refs[-1]
+    total = bias[0:1, :]
+    for part in parts:
+        total = total + part[...].astype(F32)
+    out[...] = (hidden[...] + total).astype(BF16)
+
+
+def output(parts, hidden, bias, row, rows, made):
+    k, (length, width) = len(parts), hidden.shape
+    tile = min(512, length)
+    steps = length // tile
+    args = (*parts, hidden, bias)
+    specs = [rows_of((tile, width))] * (k + 1) + [fixed((8, width))]
+    if made is not None:
+        args, specs = (*args, made), specs + [ANY]
+    return call(
+        "output",
+        lambda *refs: output_body(k, *refs),
+        (steps,),
+        args,
+        specs,
+        [shape((rows * length, width), BF16)],
+        [pl.BlockSpec((tile, width), lambda i: (row * steps + i, 0))],
+        aliases=None if made is None else {k + 2: 0},
+    )[0]
 
 
 class Ring:
@@ -709,11 +931,15 @@
             lax.dynamic_index_in_dim(every, self.me ^ j, 0, keepdims=False) for j in range(self.n)
         ]
 
+    def scatter_start(self, parts):
+        if self.pairs:
+            other, mine = self.over_core(parts[3]), self.over_core(parts[1])
+            return (parts[0], mine, parts[2], other)
+        return parts
+
     def scatter(self, parts):
         if self.pairs:
-            mine, other = self.over_core(parts[1]), self.over_core(parts[3])
-            chip_sum = (parts[2].astype(F32) + other.astype(F32)).astype(BF16)
-            return [parts[0], mine, self.over_chip(chip_sum)]
+            return [parts[0], parts[1], self.over_chip(add(parts[2], parts[3]))]
         stacked = jnp.stack([part.astype(F32) for part in parts])
         ordered = jnp.take(stacked, self.me ^ jnp.arange(self.n), axis=0)
         return [lax.psum_scatter(ordered, "mp", scatter_dimension=0, tiled=False)]
@@ -733,6 +959,20 @@
             across = lax.all_gather(self.over_chip(piece), "dp", axis=0, tiled=True)
             return [weight, self.over_core(weight), across, self.over_core(across)]
         return self.gather(weight)
+
+
+def dp_total(vectors):
+    groups = lax.axis_size("dp")
+    sizes = [v.size for v in vectors]
+    packed = jnp.concatenate(vectors)
+    packed = jnp.pad(packed, (0, -packed.size % 1024)).reshape(-1, 128)
+    bit = 1
+    while bit < groups:
+        packed = packed + lax.ppermute(packed, "dp", [(i, i ^ bit) for i in range(groups)])
+        bit *= 2
+    packed = packed.reshape(-1)
+    ends = np.cumsum(sizes)
+    return [packed[end - size : end] for end, size in zip(ends, sizes)]
 
 
 def tables_of(length):
@@ -779,14 +1019,21 @@
     own1, own2 = gain1[:, :width], gain2[:, :width]
     up_bias8 = jnp.broadcast_to(up_bias[None], (8, up_bias.shape[0]))
 
+    down_bias8 = jnp.broadcast_to(down_bias[None], (8, width))
+    groups = lax.axis_size("dp")
+    spread = full % (128 * groups) == 0
+
+    Order.last = None
+    out_w = ring.out_blocks(out_weight)
+    cot_rows = [lax.slice_in_dim(cotangent, r * length, (r + 1) * length) for r in rows]
+
     wide, low = zip(*[average(depth_weights, history, r, length) for r in rows])
-    xs = [ring.gather(low[r]) for r in rows]
-    cots = [
-        ring.gather(lax.slice_in_dim(cotangent, r * length, (r + 1) * length)) for r in rows
-    ]
-    out_w = ring.out_blocks(out_weight)
-
-    qkv, normed1, stat1, attended, logs = [], [], [], [], []
+    qkv, normed1, stat1, attended, logs, xs, heads = [], [], [], [], [], [], []
+    waits = []
+    for r in rows:
+        block = low[r] if r == 0 else gate([low[r]], waits)[0]
+        xs.append(ring.gather(block))
+        waits = xs[r][1:]
     for r in rows:
         got = project(me, xs[r], gain1, bias1, tables, qkv_weight)
         qkv.append(got[0])
@@ -795,10 +1042,11 @@
         got = attend(starts[r], qkv[r])
         attended.append(got[0])
         logs.append(got[1])
-    heads = [ring.gather(attended[r]) for r in rows]
-
-    hidden, normed2, stat2, activated, slope, outputs = [], [], [], [], [], []
+        heads.append(ring.gather(attended[r]))
+
+    hidden, normed2, stat2, activated, slope, branch, cots = [], [], [], [], [], [], []
     for r in rows:
+        cots.append(ring.gather(gate([cot_rows[r]], heads[r][1:] if r == 0 else [])[0]))
         got = feed(
             me, heads[r], xs[r], out_w, wide[r], gain2, bias2, up_bias8, up_weight, down_weight
         )
@@ -807,24 +1055,44 @@
         stat2.append(got[2])
         activated.append(got[3])
         slope.append(got[4])
-        branch = ring.scatter(got[5])
-        mlp = sum(part.astype(F32) for part in branch)
-        outputs.append((got[0] + (mlp + down_bias)).astype(BF16))
-
-    cot_full, up_grad, parts2, sums2, up_bias_sum, down_bias_sum = [], [], [], [], 0.0, 0.0
+        branch.append(ring.scatter_start(got[5]))
+
+    up_grad, parts2, sums2, up_bias_sum, down_bias_sum = [], [], [], 0.0, 0.0
+    cot_full = []
+    branch[0] = ring.scatter(branch[0])
+    for r in rows:
+        got = join(me, cots[r])
+        cot_full.append(got[0])
+        down_bias_sum += got[1]
+    down = Spread(activated, cot_full, 1, (1, 2, 4)) if spread else None
+    if spread:
+        down.first()
+    for r in rows:
+        if r > 0:
+            branch[r] = ring.scatter(branch[r])
     for r in rows:
         got = feed_back(
-            me, cots[r], slope[r], normed2[r], gain2, bias2, up_weight, down_weight
+            me, n, cot_full[r], slope[r], normed2[r], gain2, bias2, up_weight, down_weight
         )
-        cot_full.append(got[0])
-        up_grad.append(got[1])
-        sums2.append(ring.total(got[2]))
-        up_bias_sum += got[3]
-        down_bias_sum += got[4]
-        parts2.append(ring.scatter(got[5]))
-
-    down_part = weight_grad(me, activated, cot_full, width, 1)
-    up_part = weight_grad(me, normed2, up_grad, width, 0)
+        up_grad.append(got[0])
+        sums2.append(ring.total(got[1]))
+        up_bias_sum += got[2]
+        parts2.append(ring.scatter_start(got[3]))
+        if r == 0 and spread:
+            down.keep()
+        if r == 0:
+            parts2[r] = ring.scatter(parts2[r])
+    up = []
+    if spread:
+        up = [
+            Spread(normed2, up_grad, 0, (1, 2, 4), (0, 2)),
+            Spread(normed2, up_grad, 0, (2, 4, 1), (1, 2)),
+        ]
+        up[1].first()
+        up[0].first()
+    for r in rows:
+        if r > 0:
+            parts2[r] = ring.scatter(parts2[r])
 
     hidden_grad, gain2_sum, bias2_sum, grads = [], 0.0, 0.0, []
     for r in rows:
@@ -833,18 +1101,46 @@
         gain2_sum += got[2]
         bias2_sum += got[3]
         grads.append(ring.gather(got[1]))
+        if r == 0 and spread:
+            up[1].keep()
+            up[0].keep()
+    if spread:
+        down.next()
 
     grad_full, qkv_grad, parts1, sums1 = [], [], [], []
     for r in rows:
         got = attended_back(me, grads[r], out_weight)
+        if r == 1:
+            parts1[0] = ring.scatter(parts1[0])
         grad_full.append(got[0])
         qkv_grad.append(attend_back(starts[r], tables, qkv[r], got[1], logs[r]))
+        if r == 1 and spread:
+            up[1].next()
+            down.next()
         sums, parts = project_back(me, n, qkv_grad[r], normed1[r], gain1, bias1, qkv_weight)
         sums1.append(ring.total(sums))
-        parts1.append(ring.scatter(parts))
-
-    out_part = weight_grad(me, attended, grad_full, width, 1)
-    qkv_part = weight_grad(me, normed1, qkv_grad, width, 0)
+        parts1.append(ring.scatter_start(parts))
+
+    if spread:
+        qkv_w = [
+            Spread(normed1, qkv_grad, 0, (1, 2, 4), (0, 2)),
+            Spread(normed1, qkv_grad, 0, (2, 4, 1), (1, 2)),
+        ]
+        out = Spread(attended, grad_full, 1, (2, 4, 1))
+        qkv_w[0].first()
+        qkv_w[1].first()
+    for r in rows:
+        if r > 0 or row_count == 1:
+            parts1[r] = ring.scatter(parts1[r])
+    made = None
+    if spread:
+        out.first()
+        qkv_w[0].keep()
+        qkv_w[1].keep()
+        out.keep()
+        up[0].next()
+    for r in rows:
+        made = output(branch[r], hidden[r], down_bias8, r, row_count, made)
 
     grad_history, depth_sum, gain1_sum, bias1_sum = None, 0.0, 0.0, 0.0
     for r in rows:
@@ -864,21 +1160,40 @@
         depth_sum += got[1]
         gain1_sum += got[2]
         bias1_sum += got[3]
-
-    down_total = lax.psum_scatter(down_part, "dp", scatter_dimension=1, tiled=True).astype(F32)
-    up_total = lax.psum_scatter(up_part, "dp", scatter_dimension=0, tiled=True).astype(F32)
-    out_total = lax.psum_scatter(out_part, "dp", scatter_dimension=1, tiled=True).astype(F32)
-    qkv_total = lax.psum_scatter(qkv_part, "dp", scatter_dimension=0, tiled=True).astype(F32)
-
-    early = lax.psum(
-        tuple(jnp.sum(v, 0) for v in (up_bias_sum, down_bias_sum, gain2_sum, bias2_sum)), "dp"
-    )
-    late = lax.psum(
-        (jnp.sum(gain1_sum, 0), jnp.sum(bias1_sum, 0), jnp.sum(depth_sum, (1, 2))), "dp"
-    )
-    depth_grad = lax.psum(late[2], "mp")
+        if r == 0 and spread:
+            up[1].next()
+            up[0].next()
+
+    if spread:
+        down_total = down.finish()
+        qkv_w[0].next()
+        qkv_w[1].next()
+        out.next()
+        up_total = [up[0].finish(), up[1].finish()]
+        qkv_w[0].next()
+        qkv_w[1].next()
+        out.next()
+        out_total = out.finish()
+        qkv_total = [qkv_w[0].finish(), qkv_w[1].finish()]
+        up_total, qkv_total = jnp.concatenate(up_total, 1), jnp.concatenate(qkv_total, 1)
+    else:
+        down_total, up_total, out_total, qkv_total = (
+            lax.psum_scatter(
+                weight_grad(*pair), "dp", scatter_dimension=dim, tiled=True
+            ).astype(F32)
+            for pair, dim in (
+                ((activated, cot_full), 1),
+                ((normed2, up_grad), 0),
+                ((attended, grad_full), 1),
+                ((normed1, qkv_grad), 0),
+            )
+        )
+
+    early = dp_total([jnp.sum(v, 0) for v in (up_bias_sum, down_bias_sum, gain2_sum, bias2_sum)])
+    late = dp_total([jnp.sum(gain1_sum, 0), jnp.sum(bias1_sum, 0), jnp.sum(depth_sum, (1, 2))])
+    depth_grad = ring.total(late[2])
     return (
-        jnp.concatenate(outputs),
+        made,
         grad_history,
         depth_grad,
         late[0],

time: 953 us -> 970 us (1.018)
  Pallas kernels: 402 us -> 558 us
  waiting for transfers between devices: 418 us -> 294 us
  blocking collectives: 44.5 us -> 0 us
  starting transfers between devices: 28.9 us -> 56.9 us
  local copies, waits for them, and re-layouts: 12.7 us -> 26.4 us
  other arithmetic: 22.7 us -> 10 us
    reduce_scatter x4 -> x0, waiting for transfers between devices: 176 us -> none  [the longest x1 149 us: local(): lax.psum_scatter(up_part, 'dp', scatter_dimension=0, tiled=True).astype(F32)]
    pallas_call x24 -> x63, Pallas kernels: 402 us -> 558 us  [call(): pl.pallas_call(without_extra, grid_spec=pltpu.PrefetchScalarGridSpec(num_...]
    ppermute x0 -> x24, waiting for transfers between devices: none -> 119 us  [the longest x18 64.1 us: send(): return lax.ppermute(value, 'dp', [(i, i ^ bit) for i in range(self.groups)])]
    ppermute x20 -> x21, waiting for transfers between devices: 236 us -> 168 us  [over_chip(): return lax.ppermute(value, 'mp', self.chip)]
    psum x2 -> x0, blocking collectives: 44.5 us -> none  [the longest x1 38 us: local(): lax.psum((jnp.sum(gain1_sum, 0), jnp.sum(bias1_sum, 0), jnp.sum(depth_sum...]
    ppermute x0 -> x24, starting transfers between devices: none -> 27.5 us  [the longest x18 22 us: send(): return lax.ppermute(value, 'dp', [(i, i ^ bit) for i in range(self.groups)])]
    convert_element_type x11 -> x0, other arithmetic: 15.8 us -> none  [the longest x6 3.15 us: scatter(): chip_sum = (parts[2].astype(F32) + other.astype(F32)).astype(BF16)]
    unnamed x100 -> x121, local copies, waits for them, and re-layouts: 6.73 us -> 17.9 us
  transfers between devices with their start and end apart: 61 -> 83, of which waited for: 18 -> 20; matrix products, arithmetic and copies ran while one was open for 3% -> 2% of each run, Pallas kernels for 41% -> 53%
where the time goes in v2:
time: 970 us; the launch traced here: 961 us
  Pallas kernels  558 us (58%)
  waiting for transfers between devices  294 us (30%)
  starting transfers between devices  56.9 us (6%)
  local copies, waits for them, and re-layouts  26.4 us (3%)
  between operations  15.3 us (2%)
  other arithmetic  10 us (1%)
    pallas_call x63, Pallas kernels, call(): pl.pallas_call(without_extra, grid_spec=pltpu.PrefetchScalarGridSpec(num_...  558 us
    ppermute x21, waiting for transfers between devices, over_chip(): return lax.ppermute(value, 'mp', self.chip)  168 us
    ppermute x18, waiting for transfers between devices, send(): return lax.ppermute(value, 'dp', [(i, i ^ bit) for i in range(self.groups)])  64.1 us
    ppermute x6, waiting for transfers between devices, dp_total(): lax.ppermute(packed, 'dp', [(i, i ^ bit) for i in range(groups)])  55 us
    ppermute x21, starting transfers between devices, over_chip(): return lax.ppermute(value, 'mp', self.chip)  22.4 us
    ppermute x18, starting transfers between devices, send(): return lax.ppermute(value, 'dp', [(i, i ^ bit) for i in range(self.groups)])  22 us
  transfers between devices with their start and end apart: 83, of which 20 were waited for; matrix products, arithmetic and copies ran while one was open for 2% of the time, Pallas kernels for 53%

profile of v2, /device:TPU:0, one launch (start us, length us, event | category | flops | bytes accessed | tf_op | source)
XLA Modules:
  0.0 961.0 jit_solution(11013065378087829044)
XLA Ops:
  7.3 7.8 average.2
  19.1 27.9 %collective-permute-done.13 = bf16[64,2048]{1,0:T(8,128)(2,1)S(1)} collective-permute-done((bf16[64,2048]{1,0:T(8,128)(2,1)S(1)}, bf16[64,2048]{1,0:T(8,128)(2,1)S(1)}, u32[]{:S(2)}, u32[]{:S(2)}) %collective-permute-start.13) | collective-permute-done | bytes 262176 | tf_op jit(solution)/shard_map/ppermute | solution.py:922
  52.8 8.0 average.3
  64.8 19.8 %project.2 = (bf16[1024,1536]{1,0:T(8,128)(2,1)}, bf16[1024,2048]{1,0:T(8,128)(2,1)}, f32[1024,128]{1,0:T(8,128)}) custom-call(s32[1]{0:T(128)} %bitcast.refs_0_, bf16[1024,512]{1,0:T(8,128)(2,1)} %get-tuple-element.119.refs_1_.refs_5_, bf16[1024,512]{1,0:T(8,128)(2,1)} %copy-done.11, bf16[1024,512]{1,0:T(8,128)(2,1)} %copy-done.10, ...), custom_call_target="tpu_custom_call" | custom-call | flops 6442450944 | bytes 19529732 | tf_op jit(solution)/shard_map/project/pallas_call | solution.py:50
  85.2 9.7 %attend.2 = (bf16[1024,512]{1,0:T(8,128)(2,1)}, f32[4,8,1024]{2,1,0:T(8,128)}) custom-call(s32[8,1024]{1,0:T(8,128)} %broadcast_in_dim.23.refs_0_, bf16[1024,1536]{1,0:T(8,128)(2,1)} %get-tuple-element.121.refs_1_.refs_3_, f32[1024,128]{1,0:T(8,128)} %get-tuple-element.122.refs_2_.refs_5_), custom_call_target="tpu_custom_call" | custom-call | flops 1610612736 | bytes 4358144 | tf_op jit(solution)/shard_map/attend/pallas_call | solution.py:50
  99.2 21.4 %collective-permute-done.16.refs_2_.refs_3_ = bf16[1024,512]{1,0:T(8,128)(2,1)} collective-permute-done((bf16[1024,512]{1,0:T(8,128)(2,1)}, bf16[1024,512]{1,0:T(8,128)(2,1)}, u32[]{:S(2)}, u32[]{:S(2)}) %collective-permute-start.16) | collective-permute-done | bytes 1048608 | tf_op jit(solution)/shard_map/ppermute | solution.py:922
  121.6 20.1 %project.3 = (bf16[1024,1536]{1,0:T(8,128)(2,1)}, bf16[1024,2048]{1,0:T(8,128)(2,1)}, f32[1024,128]{1,0:T(8,128)}) custom-call(s32[1]{0:T(128)} %bitcast.refs_0_, bf16[1024,512]{1,0:T(8,128)(2,1)} %gate.3.refs_10_.refs_1_.refs_5_, bf16[1024,512]{1,0:T(8,128)(2,1)} %copy-done.58, bf16[1024,512]{1,0:T(8,128)(2,1)} %copy-done.57, bf16[1024,512]{1,0:T(8,128)(2,1)} %copy-done.59, ...), custom_call_target="tpu_custom_call" | custom-call | flops 6442450944 | bytes 19529732 | tf_op jit(solution)/shard_map/project/pallas_call | solution.py:50
  142.3 9.9 %attend.3 = (bf16[1024,512]{1,0:T(8,128)(2,1)}, f32[4,8,1024]{2,1,0:T(8,128)}) custom-call(s32[8,1024]{1,0:T(8,128)} %broadcast_in_dim.20.refs_0_, bf16[1024,1536]{1,0:T(8,128)(2,1)} %get-tuple-element.124.refs_1_.refs_3_, f32[1024,128]{1,0:T(8,128)} %get-tuple-element.125.refs_2_.refs_5_), custom_call_target="tpu_custom_call" | custom-call | flops 1610612736 | bytes 4358144 | tf_op jit(solution)/shard_map/attend/pallas_call | solution.py:50
  155.9 22.6 %collective-permute-done.10.refs_3_ = bf16[1024,512]{1,0:T(8,128)(2,1)} collective-permute-done((bf16[1024,512]{1,0:T(8,128)(2,1)}, bf16[1024,512]{1,0:T(8,128)(2,1)}, u32[]{:S(2)}, u32[]{:S(2)}) %collective-permute-start.10) | collective-permute-done | bytes 1048608 | tf_op jit(solution)/shard_map/ppermute | solution.py:922
  179.2 46.4 %feed.2 = (f32[1024,512]{1,0:T(8,128)}, bf16[1024,2048]{1,0:T(8,128)(2,1)}, f32[1024,128]{1,0:T(8,128)}, bf16[1024,2048]{1,0:T(8,128)(2,1)}, bf16[1024,2048]{1,0...) custom-call(s32[1]{0:T(128)} %bitcast.refs_0_, ...), custom_call_target="tpu_custom_call" | custom-call | flops 25769803776 | bytes 55246852 | tf_op jit(solution)/shard_map/feed/pallas_call | solution.py:50
  227.9 23.5 %collective-permute-done.25.refs_3_ = bf16[1024,512]{1,0:T(8,128)(2,1)S(1)} collective-permute-done((bf16[1024,512]{1,0:T(8,128)(2,1)}, bf16[1024,512]{1,0:T(8,128)(2,1)S(1)}, u32[]{:S(2)}, u32[]{:S(2)}) %collective-permute-start.25) | collective-permute-done | bytes 1048608 | tf_op jit(solution)/shard_map/ppermute | solution.py:922
  251.4 46.2 %feed.3 = (f32[1024,512]{1,0:T(8,128)}, bf16[1024,2048]{1,0:T(8,128)(2,1)}, f32[1024,128]{1,0:T(8,128)}, bf16[1024,2048]{1,0:T(8,128)(2,1)}, bf16[1024,2048]{1,0...) custom-call(s32[1]{0:T(128)} %bitcast.refs_0_, ...), custom_call_target="tpu_custom_call" | custom-call | flops 25769803776 | bytes 55246852 | tf_op jit(solution)/shard_map/feed/pallas_call | solution.py:50
  310.9 13.5 %weight_blocks.12.refs_2_ = bf16[4,2048,256]{2,1,0:T(8,128)(2,1)} custom-call(s32[1]{0:T(128)} %bitcast.8.refs_0_, bf16[1024,2048]{1,0:T(8,128)(2,1)} %get-tuple-element.134.refs_1_, bf16[1024,2048]{1,0:T(8,128)(2,1)} %get-tuple-element.135.refs_2_, bf16[1024,2048]{1,0:T(8,128)(2,1)} %get-tuple-element.139.refs_3_.refs_5_.refs_7_.refs_9_.refs_1_, ...), custom_call_target="tpu_custom_call" | custom-call | flops 8589934592 | bytes 46137348 | tf_op jit(solution)/shard_map/weight_blocks/pallas_call | solution.py:50
  326.9 30.9 %feed_back.2 = (bf16[1024,2048]{1,0:T(8,128)(2,1)}, f32[8,1024]{1,0:T(8,128)}, f32[8,2048]{1,0:T(8,128)}, bf16[1024,512]{1,0:T(8,128)(2,1)}, bf16[1024,512]{1,0:...) custom-call(s32[1]{0:T(128)} %bitcast.refs_0_, ...), custom_call_target="tpu_custom_call" | custom-call | flops 17179869184 | bytes 37978116 | tf_op jit(solution)/shard_map/feed_back/pallas_call | solution.py:50
  359.6 13.5 %weight_blocks.13.refs_2_.refs_0_ = bf16[4,2048,256]{2,1,0:T(8,128)(2,1)} custom-call(s32[1]{0:T(128)} %bitcast.8.refs_0_, bf16[1024,2048]{1,0:T(8,128)(2,1)} %get-tuple-element.134.refs_1_, bf16[1024,2048]{1,0:T(8,128)(2,1)} %get-tuple-element.135.refs_2_, bf16[1024,2048]{1,0:T(8,128)(2,1)} %get-tuple-element.139.refs_3_.refs_5_.refs_7_.refs_9_.refs_1_, ...), custom_call_target="tpu_custom_call" | custom-call | flops 8589934592 | bytes 46137348 | tf_op jit(solution)/shard_map/weight_blocks/pallas_call | solution.py:50
  376.5 31.2 %feed_back.3 = (bf16[1024,2048]{1,0:T(8,128)(2,1)}, f32[8,1024]{1,0:T(8,128)}, f32[8,2048]{1,0:T(8,128)}, bf16[1024,512]{1,0:T(8,128)(2,1)}, bf16[1024,512]{1,0:...) custom-call(s32[1]{0:T(128)} %bitcast.refs_0_, ...), custom_call_target="tpu_custom_call" | custom-call | flops 17179869184 | bytes 37978116 | tf_op jit(solution)/shard_map/feed_back/pallas_call | solution.py:50
  412.3 9.8 %weight_blocks.14.refs_11_ = bf16[4,256,1024]{2,1,0:T(8,128)(2,1)} custom-call(s32[1]{0:T(128)} %bitcast.8.refs_0_, bf16[1024,2048]{1,0:T(8,128)(2,1)} %get-tuple-element.147.refs_3_.refs_1_.refs_5_.refs_7_, bf16[1024,2048]{1,0:T(8,128)(2,1)} %get-tuple-element.148.refs_3_.refs_2_.refs_4_.refs_6_.refs_8_, ...), custom_call_target="tpu_custom_call" | custom-call | flops 4294967296 | bytes 44040196 | tf_op jit(solution)/shard_map/weight_blocks/pallas_call | solution.py:50
  422.2 9.9 %weight_blocks.15.refs_2_ = bf16[4,256,1024]{2,1,0:T(8,128)(2,1)} custom-call(s32[1]{0:T(128)} %bitcast.8.refs_0_, bf16[1024,2048]{1,0:T(8,128)(2,1)} %get-tuple-element.147.refs_3_.refs_1_.refs_5_.refs_7_, bf16[1024,2048]{1,0:T(8,128)(2,1)} %get-tuple-element.148.refs_3_.refs_2_.refs_4_.refs_6_.refs_8_, ...), custom_call_target="tpu_custom_call" | custom-call | flops 4294967296 | bytes 44040196 | tf_op jit(solution)/shard_map/weight_blocks/pallas_call | solution.py:50
  437.8 6.0 hidden_back.2
  447.1 36.9 %collective-permute-done.44 = f32[8,1024]{1,0:T(8,128)S(1)} collective-permute-done((f32[8,1024]{1,0:T(8,128)S(1)}, f32[8,1024]{1,0:T(8,128)S(1)}, u32[]{:S(2)}, u32[]{:S(2)}) %collective-permute-start.44) | collective-permute-done | bytes 32800 | tf_op jit(solution)/shard_map/ppermute | solution.py:922
  484.7 9.8 %weight_blocks.16.refs_11_.refs_0_ = bf16[4,256,1024]{2,1,0:T(8,128)(2,1)} custom-call(s32[1]{0:T(128)} %bitcast.8.refs_0_, bf16[1024,2048]{1,0:T(8,128)(2,1)} %get-tuple-element.147.refs_3_.refs_1_.refs_5_.refs_7_, bf16[1024,2048]{1,0:T(8,128)(2,1)} %get-tuple-element.148.refs_3_.refs_2_.refs_4_.refs_6_.refs_8_, ...), custom_call_target="tpu_custom_call" | custom-call | flops 4294967296 | bytes 44040196 | tf_op jit(solution)/shard_map/weight_blocks/pallas_call | solution.py:50
  494.5 9.9 %weight_blocks.17.refs_8_.refs_0_ = bf16[4,256,1024]{2,1,0:T(8,128)(2,1)} custom-call(s32[1]{0:T(128)} %bitcast.8.refs_0_, bf16[1024,2048]{1,0:T(8,128)(2,1)} %get-tuple-element.147.refs_3_.refs_1_.refs_5_.refs_7_, bf16[1024,2048]{1,0:T(8,128)(2,1)} %get-tuple-element.148.refs_3_.refs_2_.refs_4_.refs_6_.refs_8_, ...), custom_call_target="tpu_custom_call" | custom-call | flops 4294967296 | bytes 44040196 | tf_op jit(solution)/shard_map/weight_blocks/pallas_call | solution.py:50
  505.7 6.1 hidden_back.3
  514.8 21.8 %collective-permute-done.46.refs_3_ = bf16[1024,512]{1,0:T(8,128)(2,1)} collective-permute-done((bf16[1024,512]{1,0:T(8,128)(2,1)}, bf16[1024,512]{1,0:T(8,128)(2,1)}, u32[]{:S(2)}, u32[]{:S(2)}) %collective-permute-start.46) | collective-permute-done | bytes 1048608 | tf_op jit(solution)/shard_map/ppermute | solution.py:922
  537.2 6.0 fold.12
  544.8 6.8 attended_back.2
  551.6 12.6 %attend_back.2.refs_1_.refs_6_.refs_9_ = bf16[1024,1536]{1,0:T(8,128)(2,1)} custom-call(s32[8,1024]{1,0:T(8,128)} %broadcast_in_dim.23.refs_0_, f32[1024,128]{1,0:T(8,128)} %constant.22.clone.refs_7_.refs_1_, f32[1024,128]{1,0:T(8,128)} %constant.23.clone.refs_8_.refs_2_, bf16[1024,1536]{1,0:T(8,128)(2,1)} %get-tuple-element.121.refs_1_.refs_3_, ...), custom_call_target="tpu_custom_call" | custom-call | flops 4026531840 | bytes 8552448 | tf_op jit(solution)/shard_map/attend_back/pallas_call | solution.py:50
  564.2 15.1 %project_back.2 = (f32[8,1024]{1,0:T(8,128)}, bf16[1024,512]{1,0:T(8,128)(2,1)}, bf16[1024,512]{1,0:T(8,128)(2,1)}, bf16[1024,512]{1,0:T(8,128)(2,1)}, bf16[1024,512]{1,0:T(8,128)(2,1)}) custom-call(s32[1]{0:T(128)} %bitcast.refs_0_, bf16[1024,1536]{1,0:T(8,128)(2,1)} %attend_back.2.refs_1_.refs_6_.refs_9_, ...), custom_call_target="tpu_custom_call" | custom-call | flops 6442450944 | bytes 17989636 | tf_op jit(solution)/shard_map/project_back/pallas_call | solution.py:50
  579.8 6.8 attended_back.3
  590.0 12.4 %attend_back.3.refs_2_.refs_1_.refs_10_ = bf16[1024,1536]{1,0:T(8,128)(2,1)} custom-call(s32[8,1024]{1,0:T(8,128)} %broadcast_in_dim.20.refs_0_, f32[1024,128]{1,0:T(8,128)} %constant.22.clone.refs_7_.refs_1_, f32[1024,128]{1,0:T(8,128)} %constant.23.clone.refs_8_.refs_2_, bf16[1024,1536]{1,0:T(8,128)(2,1)} %get-tuple-element.124.refs_1_.refs_3_, ...), custom_call_target="tpu_custom_call" | custom-call | flops 4026531840 | bytes 8552448 | tf_op jit(solution)/shard_map/attend_back/pallas_call | solution.py:50
  611.0 15.2 %project_back.3 = (f32[8,1024]{1,0:T(8,128)}, bf16[1024,512]{1,0:T(8,128)(2,1)}, bf16[1024,512]{1,0:T(8,128)(2,1)}, bf16[1024,512]{1,0:T(8,128)(2,1)}, bf16[1024,512]{1,0:T(8,128)(2,1)}) custom-call(s32[1]{0:T(128)} %bitcast.refs_0_, bf16[1024,1536]{1,0:T(8,128)(2,1)} %attend_back.3.refs_2_.refs_1_.refs_10_, ...), custom_call_target="tpu_custom_call" | custom-call | flops 6442450944 | bytes 17989636 | tf_op jit(solution)/shard_map/project_back/pallas_call | solution.py:50
  627.5 9.8 %weight_blocks.18.refs_11_ = bf16[4,256,768]{2,1,0:T(8,128)(2,1)} custom-call(s32[1]{0:T(128)} %bitcast.8.refs_0_, bf16[1024,2048]{1,0:T(8,128)(2,1)} %get-tuple-element.170.refs_2_.refs_1_.refs_3_.refs_5_.refs_7_, bf16[1024,2048]{1,0:T(8,128)(2,1)} %get-tuple-element.173.refs_2_.refs_4_.refs_6_.refs_8_, ...), custom_call_target="tpu_custom_call" | custom-call | flops 3221225472 | bytes 41418756 | tf_op jit(solution)/shard_map/weight_blocks/pallas_call | solution.py:50
  637.3 9.6 %weight_blocks.19.refs_2_ = bf16[4,256,768]{2,1,0:T(8,128)(2,1)} custom-call(s32[1]{0:T(128)} %bitcast.8.refs_0_, bf16[1024,2048]{1,0:T(8,128)(2,1)} %get-tuple-element.170.refs_2_.refs_1_.refs_3_.refs_5_.refs_7_, bf16[1024,2048]{1,0:T(8,128)(2,1)} %get-tuple-element.173.refs_2_.refs_4_.refs_6_.refs_8_, ...), custom_call_target="tpu_custom_call" | custom-call | flops 3221225472 | bytes 41418756 | tf_op jit(solution)/shard_map/weight_blocks/pallas_call | solution.py:50
  650.9 6.2 weight_blocks.20.refs_11_
  657.1 9.6 %weight_blocks.21.refs_11_.refs_0_ = bf16[4,256,768]{2,1,0:T(8,128)(2,1)} custom-call(s32[1]{0:T(128)} %bitcast.8.refs_0_, bf16[1024,2048]{1,0:T(8,128)(2,1)} %get-tuple-element.170.refs_2_.refs_1_.refs_3_.refs_5_.refs_7_, bf16[1024,2048]{1,0:T(8,128)(2,1)} %get-tuple-element.173.refs_2_.refs_4_.refs_6_.refs_8_, ...), custom_call_target="tpu_custom_call" | custom-call | flops 3221225472 | bytes 41418756 | tf_op jit(solution)/shard_map/weight_blocks/pallas_call | solution.py:50
  670.3 9.5 weight_blocks.22.refs_11_.refs_0_
  680.0 6.2 weight_blocks.23.refs_2_.refs_0_
  686.2 4.8 fold.15
  693.0 5.0 collective-permute-done.59
  701.3 15.5 %collective-permute-done.61.refs_1_ = bf16[2,256,1024]{2,1,0:T(8,128)(2,1)} collective-permute-done((bf16[2,256,1024]{2,1,0:T(8,128)(2,1)}, bf16[2,256,1024]{2,1,0:T(8,128)(2,1)}, u32[]{:S(2)}, u32[]{:S(2)}) %collective-permute-start.61) | collective-permute-done | bytes 1048608 | tf_op jit(solution)/shard_map/ppermute | solution.py:805
  718.4 7.0 collective-permute-done.55
  726.2 13.0 %collective-permute-done.60.refs_1_ = bf16[2,256,1024]{2,1,0:T(8,128)(2,1)} collective-permute-done((bf16[2,256,1024]{2,1,0:T(8,128)(2,1)}, bf16[2,256,1024]{2,1,0:T(8,128)(2,1)}, u32[]{:S(2)}, u32[]{:S(2)}) %collective-permute-start.60) | collective-permute-done | bytes 1048608 | tf_op jit(solution)/shard_map/ppermute | solution.py:805
  751.9 14.7 %average_back.2 = (bf16[13,2048,512]{2,1,0:T(8,128)(2,1)}, f32[13,8,128]{2,1,0:T(8,128)}, f32[8,512]{1,0:T(8,128)}, f32[8,512]{1,0:T(8,128)}) custom-call(f32[13]{0:T(128)} %refs_0_.7, bf16[1024,512]{1,0:T(8,128)(2,1)} %get-tuple-element.187.refs_1_, bf16[1024,512]{1,0:T(8,128)(2,1)} %collective-permute-done.56.refs_2_, ...), custom_call_target="tpu_custom_call" | custom-call | flops 40894464 | bytes 62525492 | tf_op jit(solution)/shard_map/average_back/pallas_call | solution.py:50
  775.7 14.8 %average_back.3 = (bf16[13,2048,512]{2,1,0:T(8,128)(2,1)}, f32[13,8,128]{2,1,0:T(8,128)}, f32[8,512]{1,0:T(8,128)}, f32[8,512]{1,0:T(8,128)}) custom-call(f32[13]{0:T(128)} %refs_0_.7, bf16[1024,512]{1,0:T(8,128)(2,1)} %get-tuple-element.184.refs_1_, bf16[1024,512]{1,0:T(8,128)(2,1)} %collective-permute-done.52.refs_2_, ...), custom_call_target="tpu_custom_call", output_to_operand_aliasing={{0}: (10, {})} | custom-call | flops 40894464 | bytes 89788464 | tf_op jit(solution)/shard_map/average_back/pallas_call | solution.py:50
  797.7 20.1 %collective-permute-done.80 = f32[32,128]{1,0:T(8,128)S(1)} collective-permute-done((f32[32,128]{1,0:T(8,128)S(1)}, f32[32,128]{1,0:T(8,128)S(1)}, u32[]{:S(2)}, u32[]{:S(2)}) %collective-permute-start.80) | collective-permute-done | bytes 16416 | tf_op jit(solution)/shard_map/ppermute | solution.py:971
  836.7 32.3 %collective-permute-done.64 = f32[16,128]{1,0:T(8,128)S(1)} collective-permute-done((f32[16,128]{1,0:T(8,128)S(1)}, f32[16,128]{1,0:T(8,128)S(1)}, u32[]{:S(2)}, u32[]{:S(2)}) %collective-permute-start.64) | collective-permute-done | bytes 8224 | tf_op jit(solution)/shard_map/ppermute | solution.py:971
  876.9 27.9 %collective-permute-done.71.refs_1_ = bf16[1,256,1024]{2,1,0:T(8,128)(2,1)S(1)} collective-permute-done((bf16[1,256,1024]{2,1,0:T(8,128)(2,1)}, bf16[1,256,1024]{2,1,0:T(8,128)(2,1)S(1)}, u32[]{:S(2)}, u32[]{:S(2)}) %collective-permute-start.71) | collective-permute-done | bytes 524320 | tf_op jit(solution)/shard_map/ppermute | solution.py:805
  931.6 7.7 collective-permute-done.77.refs_1_
  (346 shorter events, 194.0 us)
Async XLA Ops:
  7.2 91.5 %all-gather.2.cloned.1.call-start = ((), (), s32[]{:S(2)}) async-start(), calls=%async_computation | async-start | bytes 2359296 | tf_op jit(solution)/shard_map/all_gather | solution.py:959
  15.1 32.8 %collective-permute-start.1 = (bf16[1024,512]{1,0:T(8,128)(2,1)}, bf16[1024,512]{1,0:T(8,128)(2,1)S(1)}, u32[]{:S(2)}, u32[]{:S(2)}) collective-permute-start(bf16[1024,512]{1,0:T(8,128)(2,1)} %get-tuple-element.119.refs_1_.refs_5_), channel_id=1, source_target_pairs={{0,2},{1,3},{2,0},{3,1},{4,6},{5,7},{6,4},{7,5},{8,10},{9,11},{10,... | collective-permute-start | bytes 3145736 | tf_op jit(solution)/shard_map/ppermute | solution.py:922
  62.1 33.1 %collective-permute-start.4 = (bf16[1024,512]{1,0:T(8,128)(2,1)}, bf16[1024,512]{1,0:T(8,128)(2,1)S(1)}, u32[]{:S(2)}, u32[]{:S(2)}) collective-permute-start(bf16[1024,512]{1,0:T(8,128)(2,1)} %gate.3.refs_10_.refs_1_.refs_5_), channel_id=1, source_target_pairs={{0,2},{1,3},{2,0},{3,1},{4,6},{5,7},{6,4},{7,5},{8,10},{9,11},{10,... | collective-permute-start | bytes 3145736 | tf_op jit(solution)/shard_map/ppermute | solution.py:922
  64.6 34.1 %collective-permute-start.3 = (bf16[1024,512]{1,0:T(8,128)(2,1)}, bf16[1024,512]{1,0:T(8,128)(2,1)S(1)}, u32[]{:S(2)}, u32[]{:S(2)}) collective-permute-start(bf16[1024,512]{1,0:T(8,128)(2,1)} %gate.3.refs_10_.refs_1_.refs_5_), channel_id=1, source_target_pairs={{0,1},{1,0},{2,3},{3,2},{4,5},{5,4},{6,7},{7,6},{8,9},{9,8},{10,11... | collective-permute-start | bytes 3145736 | tf_op jit(solution)/shard_map/ppermute | solution.py:919
  95.3 83.2 %collective-permute-start.12 = (bf16[512,2048]{1,0:T(8,128)(2,1)}, bf16[512,2048]{1,0:T(8,128)(2,1)}, u32[]{:S(2)}, u32[]{:S(2)}) collective-permute-start(bf16[512,2048]{1,0:T(8,128)(2,1)} %refs_5_.6), channel_id=1, source_target_pairs={{0,1},{1,0},{2,3},{3,2},{4,5},{5,4},{6,7},{7,6},{8,9},{9,8},{10,11... | collective-permute-start | bytes 6291464 | tf_op jit(solution)/shard_map/ppermute | solution.py:919
  98.7 79.8 %collective-permute-start.14 = (bf16[512,2048]{1,0:T(8,128)(2,1)}, bf16[512,2048]{1,0:T(8,128)(2,1)}, u32[]{:S(2)}, u32[]{:S(2)}) collective-permute-start(bf16[512,2048]{1,0:T(8,128)(2,1)} %all-gather.2.cloned.1.call-done.refs_11_), channel_id=1, source_target_pairs={{0,1},{1,0},{2,3},{3,2},{4,5},{5,4},{6,7},{7,6},{8,9},{9,8},{10,11... | collective-permute-start | bytes 6291464 | tf_op jit(solution)/shard_map/ppermute | solution.py:919
  98.7 55.3 %collective-permute-start.15 = (bf16[1024,512]{1,0:T(8,128)(2,1)}, bf16[1024,512]{1,0:T(8,128)(2,1)}, u32[]{:S(2)}, u32[]{:S(2)}) collective-permute-start(bf16[1024,512]{1,0:T(8,128)(2,1)} %get-tuple-element.127.refs_1_), channel_id=1, source_target_pairs={{0,1},{1,0},{2,3},{3,2},{4,5},{5,4},{6,7},{7,6},{8,9},{9,8},{10,11... | collective-permute-start | bytes 3145736 | tf_op jit(solution)/shard_map/ppermute | solution.py:919
  120.6 33.7 %collective-permute-start.17 = (bf16[1024,512]{1,0:T(8,128)(2,1)}, bf16[1024,512]{1,0:T(8,128)(2,1)}, u32[]{:S(2)}, u32[]{:S(2)}) collective-permute-start(bf16[1024,512]{1,0:T(8,128)(2,1)} %collective-permute-done.16.refs_2_.refs_3_), channel_id=1, source_target_pairs={{0,1},{1,0},{2,3},{3,2},{4,5},{5,4},{6,7},{7,6},{8,9},{9,8},{10,11... | collective-permute-start | bytes 3145736 | tf_op jit(solution)/shard_map/ppermute | solution.py:919
  154.0 73.3 %collective-permute-start.9 = (bf16[1024,512]{1,0:T(8,128)(2,1)S(1)}, bf16[1024,512]{1,0:T(8,128)(2,1)}, u32[]{:S(2)}, u32[]{:S(2)}) collective-permute-start(bf16[1024,512]{1,0:T(8,128)(2,1)S(1)} %copy-done.8), channel_id=1, source_target_pairs={{0,1},{1,0},{2,3},{3,2},{4,5},{5,4},{6,7},{7,6},{8,9},{9,8},{10,11... | collective-permute-start | bytes 3145736 | tf_op jit(solution)/shard_map/ppermute | solution.py:919
  154.3 72.9 %collective-permute-start.21 = (bf16[1024,512]{1,0:T(8,128)(2,1)}, bf16[1024,512]{1,0:T(8,128)(2,1)}, u32[]{:S(2)}, u32[]{:S(2)}) collective-permute-start(bf16[1024,512]{1,0:T(8,128)(2,1)} %gate.4.refs_19_.refs_1_), channel_id=1, source_target_pairs={{0,2},{1,3},{2,0},{3,1},{4,6},{5,7},{6,4},{7,5},{8,10},{9,11},{10,... | collective-permute-start | bytes 3145736 | tf_op jit(solution)/shard_map/ppermute | solution.py:922
  178.5 49.3 %collective-permute-start.11 = (bf16[1024,512]{1,0:T(8,128)(2,1)}, bf16[1024,512]{1,0:T(8,128)(2,1)}, u32[]{:S(2)}, u32[]{:S(2)}) collective-permute-start(bf16[1024,512]{1,0:T(8,128)(2,1)} %collective-permute-done.10.refs_3_), channel_id=1, source_target_pairs={{0,1},{1,0},{2,3},{3,2},{4,5},{5,4},{6,7},{7,6},{8,9},{9,8},{10,11... | collective-permute-start | bytes 3145736 | tf_op jit(solution)/shard_map/ppermute | solution.py:919
  226.8 73.7 %collective-permute-start.20 = (bf16[1024,512]{1,0:T(8,128)(2,1)S(1)}, bf16[1024,512]{1,0:T(8,128)(2,1)}, u32[]{:S(2)}, u32[]{:S(2)}) collective-permute-start(bf16[1024,512]{1,0:T(8,128)(2,1)S(1)} %copy-done.3), channel_id=1, source_target_pairs={{0,1},{1,0},{2,3},{3,2},{4,5},{5,4},{6,7},{7,6},{8,9},{9,8},{10,11... | collective-permute-start | bytes 3145736 | tf_op jit(solution)/shard_map/ppermute | solution.py:919
  227.3 73.2 %collective-permute-start.22 = (bf16[1024,512]{1,0:T(8,128)(2,1)}, bf16[1024,512]{1,0:T(8,128)(2,1)}, u32[]{:S(2)}, u32[]{:S(2)}) collective-permute-start(bf16[1024,512]{1,0:T(8,128)(2,1)} %collective-permute-done.21.refs_3_), channel_id=1, source_target_pairs={{0,1},{1,0},{2,3},{3,2},{4,5},{5,4},{6,7},{7,6},{8,9},{9,8},{10,11... | collective-permute-start | bytes 3145736 | tf_op jit(solution)/shard_map/ppermute | solution.py:919
  227.3 77.9 %collective-permute-start.24 = (bf16[1024,512]{1,0:T(8,128)(2,1)}, bf16[1024,512]{1,0:T(8,128)(2,1)S(1)}, u32[]{:S(2)}, u32[]{:S(2)}) collective-permute-start(bf16[1024,512]{1,0:T(8,128)(2,1)} %gate.5.refs_19_.refs_1_), channel_id=1, source_target_pairs={{0,1},{1,0},{2,3},{3,2},{4,5},{5,4},{6,7},{7,6},{8,9},{9,8},{10,11... | collective-permute-start | bytes 3145736 | tf_op jit(solution)/shard_map/ppermute | solution.py:919
  227.8 69.8 %collective-permute-start.23 = (bf16[1024,512]{1,0:T(8,128)(2,1)}, bf16[1024,512]{1,0:T(8,128)(2,1)}, u32[]{:S(2)}, u32[]{:S(2)}) collective-permute-start(bf16[1024,512]{1,0:T(8,128)(2,1)} %get-tuple-element.137), channel_id=1, source_target_pairs={{0,1},{1,0},{2,3},{3,2},{4,5},{5,4},{6,7},{7,6},{8,9},{9,8},{10,11... | collective-permute-start | bytes 3145736 | tf_op jit(solution)/shard_map/ppermute | solution.py:919
  251.4 53.8 %collective-permute-start.26 = (bf16[1024,512]{1,0:T(8,128)(2,1)S(1)}, bf16[1024,512]{1,0:T(8,128)(2,1)}, u32[]{:S(2)}, u32[]{:S(2)}) collective-permute-start(bf16[1024,512]{1,0:T(8,128)(2,1)S(1)} %collective-permute-done.25.refs_3_), channel_id=1, source_target_pairs={{0,1},{1,0},{2,3},{3,2},{4,5},{5,4},{6,7},{7,6},{8,9},{9,8},{10,11... | collective-permute-start | bytes 3145736 | tf_op jit(solution)/shard_map/ppermute | solution.py:919
  358.1 178.6 %collective-permute-start.40 = (bf16[4,2048,256]{2,1,0:T(8,128)(2,1)}, bf16[4,2048,256]{2,1,0:T(8,128)(2,1)}, u32[]{:S(2)}, u32[]{:S(2)}) collective-permute-start(bf16[4,2048,256]{2,1,0:T(8,128)(2,1)} %weight_blocks.12.refs_2_), channel_id=1, source_target_pairs={{0,4},{4,0},{8,12},{12,8},{16,20},{20,16},{24,28},{28,24},{1,5},{5... | collective-permute-start | bytes 12582920 | tf_op jit(solution)/shard_map/ppermute | solution.py:805
  407.9 29.2 %collective-permute-start.31 = (bf16[1024,512]{1,0:T(8,128)(2,1)}, bf16[1024,512]{1,0:T(8,128)(2,1)}, u32[]{:S(2)}, u32[]{:S(2)}) collective-permute-start(bf16[1024,512]{1,0:T(8,128)(2,1)} %get-tuple-element.157), channel_id=1, source_target_pairs={{0,1},{1,0},{2,3},{3,2},{4,5},{5,4},{6,7},{7,6},{8,9},{9,8},{10,11... | collective-permute-start | bytes 3145736 | tf_op jit(solution)/shard_map/ppermute | solution.py:919
  432.1 72.3 %collective-permute-start.41 = (bf16[1024,512]{1,0:T(8,128)(2,1)}, bf16[1024,512]{1,0:T(8,128)(2,1)S(1)}, u32[]{:S(2)}, u32[]{:S(2)}) collective-permute-start(bf16[1024,512]{1,0:T(8,128)(2,1)} %get-tuple-element.164), channel_id=1, source_target_pairs={{0,1},{1,0},{2,3},{3,2},{4,5},{5,4},{6,7},{7,6},{8,9},{9,8},{10,11... | collective-permute-start | bytes 3145736 | tf_op jit(solution)/shard_map/ppermute | solution.py:919
  435.5 68.9 %collective-permute-start.42 = (bf16[1024,512]{1,0:T(8,128)(2,1)}, bf16[1024,512]{1,0:T(8,128)(2,1)S(1)}, u32[]{:S(2)}, u32[]{:S(2)}) collective-permute-start(bf16[1024,512]{1,0:T(8,128)(2,1)} %add.125.refs_8_), channel_id=1, source_target_pairs={{0,2},{1,3},{2,0},{3,1},{4,6},{5,7},{6,4},{7,5},{8,10},{9,11},{10,... | collective-permute-start | bytes 3145736 | tf_op jit(solution)/shard_map/ppermute | solution.py:922
  443.8 68.9 %collective-permute-start.38 = (bf16[1024,512]{1,0:T(8,128)(2,1)}, bf16[1024,512]{1,0:T(8,128)(2,1)}, u32[]{:S(2)}, u32[]{:S(2)}) collective-permute-start(bf16[1024,512]{1,0:T(8,128)(2,1)} %get-tuple-element.162.refs_1_), channel_id=1, source_target_pairs={{0,2},{1,3},{2,0},{3,1},{4,6},{5,7},{6,4},{7,5},{8,10},{9,11},{10,... | collective-permute-start | bytes 3145736 | tf_op jit(solution)/shard_map/ppermute | solution.py:922
  446.1 38.0 %collective-permute-start.44 = (f32[8,1024]{1,0:T(8,128)S(1)}, f32[8,1024]{1,0:T(8,128)S(1)}, u32[]{:S(2)}, u32[]{:S(2)}) collective-permute-start(f32[8,1024]{1,0:T(8,128)S(1)} %add.85), channel_id=1, source_target_pairs={{0,2},{1,3},{2,0},{3,1},{4,6},{5,7},{6,4},{7,5},{8,10},{9,11},{10,... | collective-permute-start | bytes 98312 | tf_op jit(solution)/shard_map/ppermute | solution.py:922
  512.7 30.5 %collective-permute-start.37 = (bf16[1024,512]{1,0:T(8,128)(2,1)S(1)}, bf16[1024,512]{1,0:T(8,128)(2,1)}, u32[]{:S(2)}, u32[]{:S(2)}) collective-permute-start(bf16[1024,512]{1,0:T(8,128)(2,1)S(1)} %copy-done.13), channel_id=1, source_target_pairs={{0,1},{1,0},{2,3},{3,2},{4,5},{5,4},{6,7},{7,6},{8,9},{9,8},{10,11... | collective-permute-start | bytes 3145736 | tf_op jit(solution)/shard_map/ppermute | solution.py:919
  512.7 32.0 %collective-permute-start.39 = (bf16[1024,512]{1,0:T(8,128)(2,1)}, bf16[1024,512]{1,0:T(8,128)(2,1)}, u32[]{:S(2)}, u32[]{:S(2)}) collective-permute-start(bf16[1024,512]{1,0:T(8,128)(2,1)} %collective-permute-done.38.refs_3_), channel_id=1, source_target_pairs={{0,1},{1,0},{2,3},{3,2},{4,5},{5,4},{6,7},{7,6},{8,9},{9,8},{10,11... | collective-permute-start | bytes 3145736 | tf_op jit(solution)/shard_map/ppermute | solution.py:919
  513.2 89.2 %collective-permute-start.50 = (bf16[4,256,1024]{2,1,0:T(8,128)(2,1)S(1)}, bf16[4,256,1024]{2,1,0:T(8,128)(2,1)}, u32[]{:S(2)}, u32[]{:S(2)}) collective-permute-start(bf16[4,256,1024]{2,1,0:T(8,128)(2,1)S(1)} %copy-done.4), channel_id=1, source_target_pairs={{0,8},{4,12},{8,0},{12,4},{16,24},{20,28},{24,16},{28,20},{1,9},{5... | collective-permute-start | bytes 6291464 | tf_op jit(solution)/shard_map/ppermute | solution.py:805
  536.7 42.7 %collective-permute-start.45 = (bf16[1024,512]{1,0:T(8,128)(2,1)}, bf16[1024,512]{1,0:T(8,128)(2,1)}, u32[]{:S(2)}, u32[]{:S(2)}) collective-permute-start(bf16[1024,512]{1,0:T(8,128)(2,1)} %get-tuple-element.168.refs_1_), channel_id=1, source_target_pairs={{0,1},{1,0},{2,3},{3,2},{4,5},{5,4},{6,7},{7,6},{8,9},{9,8},{10,11... | collective-permute-start | bytes 3145736 | tf_op jit(solution)/shard_map/ppermute | solution.py:919
  536.7 43.1 %collective-permute-start.47 = (bf16[1024,512]{1,0:T(8,128)(2,1)}, bf16[1024,512]{1,0:T(8,128)(2,1)}, u32[]{:S(2)}, u32[]{:S(2)}) collective-permute-start(bf16[1024,512]{1,0:T(8,128)(2,1)} %collective-permute-done.46.refs_3_), channel_id=1, source_target_pairs={{0,1},{1,0},{2,3},{3,2},{4,5},{5,4},{6,7},{7,6},{8,9},{9,8},{10,11... | collective-permute-start | bytes 3145736 | tf_op jit(solution)/shard_map/ppermute | solution.py:919
  543.2 63.6 %collective-permute-start.49 = (bf16[2,2048,256]{2,1,0:T(8,128)(2,1)}, bf16[2,2048,256]{2,1,0:T(8,128)(2,1)}, u32[]{:S(2)}, u32[]{:S(2)}) collective-permute-start(bf16[2,2048,256]{2,1,0:T(8,128)(2,1)} %get-tuple-element.177), channel_id=1, source_target_pairs={{0,8},{4,12},{8,0},{12,4},{16,24},{20,28},{24,16},{28,20},{1,9},{5... | collective-permute-start | bytes 6291464 | tf_op jit(solution)/shard_map/ppermute | solution.py:805
  579.4 100.5 %collective-permute-start.36 = (bf16[4,256,1024]{2,1,0:T(8,128)(2,1)}, bf16[4,256,1024]{2,1,0:T(8,128)(2,1)}, u32[]{:S(2)}, u32[]{:S(2)}) collective-permute-start(bf16[4,256,1024]{2,1,0:T(8,128)(2,1)} %weight_blocks.15.refs_2_), channel_id=1, source_target_pairs={{0,4},{4,0},{8,12},{12,8},{16,20},{20,16},{24,28},{28,24},{1,5},{5... | collective-permute-start | bytes 6291464 | tf_op jit(solution)/shard_map/ppermute | solution.py:805
  626.8 39.9 %collective-permute-start.18 = (bf16[1024,512]{1,0:T(8,128)(2,1)}, bf16[1024,512]{1,0:T(8,128)(2,1)S(1)}, u32[]{:S(2)}, u32[]{:S(2)}) collective-permute-start(bf16[1024,512]{1,0:T(8,128)(2,1)} %get-tuple-element.131), channel_id=1, source_target_pairs={{0,1},{1,0},{2,3},{3,2},{4,5},{5,4},{6,7},{7,6},{8,9},{9,8},{10,11... | collective-permute-start | bytes 3145736 | tf_op jit(solution)/shard_map/ppermute | solution.py:919
  626.9 40.8 %collective-permute-start.29 = (bf16[1024,512]{1,0:T(8,128)(2,1)S(1)}, bf16[1024,512]{1,0:T(8,128)(2,1)}, u32[]{:S(2)}, u32[]{:S(2)}) collective-permute-start(bf16[1024,512]{1,0:T(8,128)(2,1)S(1)} %copy-done.9), channel_id=1, source_target_pairs={{0,2},{1,3},{2,0},{3,1},{4,6},{5,7},{6,4},{7,5},{8,10},{9,11},{10,... | collective-permute-start | bytes 3145736 | tf_op jit(solution)/shard_map/ppermute | solution.py:922
  646.9 44.9 %collective-permute-start.27 = (bf16[1024,512]{1,0:T(8,128)(2,1)}, bf16[1024,512]{1,0:T(8,128)(2,1)}, u32[]{:S(2)}, u32[]{:S(2)}) collective-permute-start(bf16[1024,512]{1,0:T(8,128)(2,1)} %add.123.refs_8_), channel_id=1, source_target_pairs={{0,2},{1,3},{2,0},{3,1},{4,6},{5,7},{6,4},{7,5},{8,10},{9,11},{10,... | collective-permute-start | bytes 3145736 | tf_op jit(solution)/shard_map/ppermute | solution.py:922
  650.9 47.1 %collective-permute-start.56 = (bf16[1024,512]{1,0:T(8,128)(2,1)}, bf16[1024,512]{1,0:T(8,128)(2,1)}, u32[]{:S(2)}, u32[]{:S(2)}) collective-permute-start(bf16[1024,512]{1,0:T(8,128)(2,1)} %get-tuple-element.188), channel_id=1, source_target_pairs={{0,1},{1,0},{2,3},{3,2},{4,5},{5,4},{6,7},{7,6},{8,9},{9,8},{10,11... | collective-permute-start | bytes 3145736 | tf_op jit(solution)/shard_map/ppermute | solution.py:919
  666.7 33.1 %collective-permute-start.57 = (bf16[1024,512]{1,0:T(8,128)(2,1)}, bf16[1024,512]{1,0:T(8,128)(2,1)}, u32[]{:S(2)}, u32[]{:S(2)}) collective-permute-start(bf16[1024,512]{1,0:T(8,128)(2,1)} %add.126.refs_6_), channel_id=1, source_target_pairs={{0,2},{1,3},{2,0},{3,1},{4,6},{5,7},{6,4},{7,5},{8,10},{9,11},{10,... | collective-permute-start | bytes 3145736 | tf_op jit(solution)/shard_map/ppermute | solution.py:922
  667.8 49.0 %collective-permute-start.61 = (bf16[2,256,1024]{2,1,0:T(8,128)(2,1)}, bf16[2,256,1024]{2,1,0:T(8,128)(2,1)}, u32[]{:S(2)}, u32[]{:S(2)}) collective-permute-start(bf16[2,256,1024]{2,1,0:T(8,128)(2,1)} %get-tuple-element.192), channel_id=1, source_target_pairs={{0,16},{4,20},{8,24},{12,28},{16,0},{20,4},{24,8},{28,12},{1,17},{... | collective-permute-start | bytes 3145736 | tf_op jit(solution)/shard_map/ppermute | solution.py:805
  691.0 48.2 %collective-permute-start.60 = (bf16[2,256,1024]{2,1,0:T(8,128)(2,1)}, bf16[2,256,1024]{2,1,0:T(8,128)(2,1)}, u32[]{:S(2)}, u32[]{:S(2)}) collective-permute-start(bf16[2,256,1024]{2,1,0:T(8,128)(2,1)} %get-tuple-element.191), channel_id=1, source_target_pairs={{0,8},{4,12},{8,0},{12,4},{16,24},{20,28},{24,16},{28,20},{1,9},{5... | collective-permute-start | bytes 3145736 | tf_op jit(solution)/shard_map/ppermute | solution.py:805
  698.0 75.7 %collective-permute-start.52 = (bf16[1024,512]{1,0:T(8,128)(2,1)}, bf16[1024,512]{1,0:T(8,128)(2,1)}, u32[]{:S(2)}, u32[]{:S(2)}) collective-permute-start(bf16[1024,512]{1,0:T(8,128)(2,1)} %get-tuple-element.185), channel_id=1, source_target_pairs={{0,1},{1,0},{2,3},{3,2},{4,5},{5,4},{6,7},{7,6},{8,9},{9,8},{10,11... | collective-permute-start | bytes 3145736 | tf_op jit(solution)/shard_map/ppermute | solution.py:919
  699.2 76.1 %collective-permute-start.53 = (bf16[1024,512]{1,0:T(8,128)(2,1)}, bf16[1024,512]{1,0:T(8,128)(2,1)}, u32[]{:S(2)}, u32[]{:S(2)}) collective-permute-start(bf16[1024,512]{1,0:T(8,128)(2,1)} %add.127.refs_11_), channel_id=1, source_target_pairs={{0,2},{1,3},{2,0},{3,1},{4,6},{5,7},{6,4},{7,5},{8,10},{9,11},{10,... | collective-permute-start | bytes 3145736 | tf_op jit(solution)/shard_map/ppermute | solution.py:922
  716.8 105.8 %collective-permute-start.67 = (bf16[4,256,768]{2,1,0:T(8,128)(2,1)S(1)}, bf16[4,256,768]{2,1,0:T(8,128)(2,1)}, u32[]{:S(2)}, u32[]{:S(2)}) collective-permute-start(bf16[4,256,768]{2,1,0:T(8,128)(2,1)S(1)} %copy-done.6), channel_id=1, source_target_pairs={{0,4},{4,0},{8,12},{12,8},{16,20},{20,16},{24,28},{28,24},{1,5},{5... | collective-permute-start | bytes 4718600 | tf_op jit(solution)/shard_map/ppermute | solution.py:805
  725.4 102.5 %collective-permute-start.73 = (bf16[4,256,768]{2,1,0:T(8,128)(2,1)S(1)}, bf16[4,256,768]{2,1,0:T(8,128)(2,1)}, u32[]{:S(2)}, u32[]{:S(2)}) collective-permute-start(bf16[4,256,768]{2,1,0:T(8,128)(2,1)S(1)} %copy-done.7), channel_id=1, source_target_pairs={{0,8},{4,12},{8,0},{12,4},{16,24},{20,28},{24,16},{28,20},{1,9},{5... | collective-permute-start | bytes 4718600 | tf_op jit(solution)/shard_map/ppermute | solution.py:805
  739.2 78.7 %collective-permute-start.68 = (bf16[1,2048,256]{2,1,0:T(8,128)(2,1)}, bf16[1,2048,256]{2,1,0:T(8,128)(2,1)}, u32[]{:S(2)}, u32[]{:S(2)}) collective-permute-start(bf16[1,2048,256]{2,1,0:T(8,128)(2,1)} %get-tuple-element.202), channel_id=1, source_target_pairs={{0,16},{4,20},{8,24},{12,28},{16,0},{20,4},{24,8},{28,12},{1,17},{... | collective-permute-start | bytes 3145736 | tf_op jit(solution)/shard_map/ppermute | solution.py:805
  775.3 94.4 %collective-permute-start.72 = (bf16[4,512,256]{2,1,0:T(8,128)(2,1)}, bf16[4,512,256]{2,1,0:T(8,128)(2,1)}, u32[]{:S(2)}, u32[]{:S(2)}) collective-permute-start(bf16[4,512,256]{2,1,0:T(8,128)(2,1)} %weight_blocks.20.refs_11_), channel_id=1, source_target_pairs={{0,8},{4,12},{8,0},{12,4},{16,24},{20,28},{24,16},{28,20},{1,9},{5... | collective-permute-start | bytes 3145736 | tf_op jit(solution)/shard_map/ppermute | solution.py:805
  826.7 87.2 %collective-permute-start.69 = (bf16[2,256,768]{2,1,0:T(8,128)(2,1)}, bf16[2,256,768]{2,1,0:T(8,128)(2,1)S(1)}, u32[]{:S(2)}, u32[]{:S(2)}) collective-permute-start(bf16[2,256,768]{2,1,0:T(8,128)(2,1)} %get-tuple-element.204), channel_id=1, source_target_pairs={{0,8},{4,12},{8,0},{12,4},{16,24},{20,28},{24,16},{28,20},{1,9},{5... | collective-permute-start | bytes 2359304 | tf_op jit(solution)/shard_map/ppermute | solution.py:805
  831.9 86.6 %collective-permute-start.76 = (bf16[2,256,768]{2,1,0:T(8,128)(2,1)}, bf16[2,256,768]{2,1,0:T(8,128)(2,1)S(1)}, u32[]{:S(2)}, u32[]{:S(2)}) collective-permute-start(bf16[2,256,768]{2,1,0:T(8,128)(2,1)} %get-tuple-element.212), channel_id=1, source_target_pairs={{0,16},{4,20},{8,24},{12,28},{16,0},{20,4},{24,8},{28,12},{1,17},{... | collective-permute-start | bytes 2359304 | tf_op jit(solution)/shard_map/ppermute | solution.py:805
  834.8 34.3 %collective-permute-start.64 = (f32[16,128]{1,0:T(8,128)S(1)}, f32[16,128]{1,0:T(8,128)S(1)}, u32[]{:S(2)}, u32[]{:S(2)}) collective-permute-start(f32[16,128]{1,0:T(8,128)S(1)} %fusion.8), channel_id=1, source_target_pairs={{0,16},{4,20},{8,24},{12,28},{16,0},{20,4},{24,8},{28,12},{1,17},{... | collective-permute-start | bytes 24584 | tf_op jit(solution)/shard_map/ppermute | solution.py:971
  834.9 74.7 %collective-permute-start.70 = (bf16[1,256,1024]{2,1,0:T(8,128)(2,1)}, bf16[1,256,1024]{2,1,0:T(8,128)(2,1)S(1)}, u32[]{:S(2)}, u32[]{:S(2)}) collective-permute-start(bf16[1,256,1024]{2,1,0:T(8,128)(2,1)} %get-tuple-element.205), channel_id=1, source_target_pairs={{0,4},{4,0},{8,12},{12,8},{16,20},{20,16},{24,28},{28,24},{1,5},{5... | collective-permute-start | bytes 1572872 | tf_op jit(solution)/shard_map/ppermute | solution.py:805
  869.1 35.7 %collective-permute-start.71 = (bf16[1,256,1024]{2,1,0:T(8,128)(2,1)}, bf16[1,256,1024]{2,1,0:T(8,128)(2,1)S(1)}, u32[]{:S(2)}, u32[]{:S(2)}) collective-permute-start(bf16[1,256,1024]{2,1,0:T(8,128)(2,1)} %get-tuple-element.206), channel_id=1, source_target_pairs={{0,16},{4,20},{8,24},{12,28},{16,0},{20,4},{24,8},{28,12},{1,17},{... | collective-permute-start | bytes 1572872 | tf_op jit(solution)/shard_map/ppermute | solution.py:805
  873.4 52.3 %collective-permute-start.75 = (bf16[2,512,256]{2,1,0:T(8,128)(2,1)}, bf16[2,512,256]{2,1,0:T(8,128)(2,1)S(1)}, u32[]{:S(2)}, u32[]{:S(2)}) collective-permute-start(bf16[2,512,256]{2,1,0:T(8,128)(2,1)} %get-tuple-element.211), channel_id=1, source_target_pairs={{0,16},{4,20},{8,24},{12,28},{16,0},{20,4},{24,8},{28,12},{1,17},{... | collective-permute-start | bytes 1572872 | tf_op jit(solution)/shard_map/ppermute | solution.py:805
  (95 other events, 1618.1 us)
Sparse Core Ops, SparseCore 0:
  47.9 50.7 all-gather.1

commit v3 on v2

v3 whole, which is shorter than its diff:
```python
import math

import jax
import jax.numpy as jnp
import numpy as np
from jax import lax
from jax.experimental import pallas as pl
from jax.experimental.pallas import tpu as pltpu
from jax.sharding import PartitionSpec as P

HEAD = 128
MAX_DOC = 512
EPSILON = 1e-05
SQRT_HALF = 0.7071067811865476
INV_ROOT_TWO_PI = 0.3989422804014327
LOG2E = 1.4426950408889634
SCALE = HEAD ** (-0.5)
MIB = 2**20
BF16 = jnp.bfloat16
F32 = jnp.float32


def dot_nn(a, b):
    return jnp.dot(a, b, preferred_element_type=F32)


def dot_nt(a, b):
    return lax.dot_general(a, b, (((1,), (1,)), ((), ())), preferred_element_type=F32)


def dot_tn(a, b):
    return lax.dot_general(a, b, (((0,), (0,)), ((), ())), preferred_element_type=F32)


class Order:
    last = None


def call(
    name, body, grid, args, in_specs, outs, out_specs, scratch=(), prefetch=0, after=(), aliases=None
):
    count = len(args)
    extra = [*after]
    if Order.last is not None and not any(Order.last is a for a in args):
        extra.append(Order.last)

    def without_extra(*refs):
        body(*refs[:count], *refs[count + len(extra) :])

    got = pl.pallas_call(
        without_extra,
        grid_spec=pltpu.PrefetchScalarGridSpec(
            num_scalar_prefetch=prefetch,
            grid=grid,
            in_specs=list(in_specs) + [ANY] * len(extra),
            out_specs=out_specs,
            scratch_shapes=list(scratch),
        ),
        out_shape=outs,
        input_output_aliases=aliases or {},
        compiler_params=pltpu.CompilerParams(vmem_limit_bytes=60 * MIB),
        cost_estimate=pl.CostEstimate(flops=1, bytes_accessed=1, transcendentals=0),
        name=name,
    )(*args, *extra)
    fresh = [v for i, v in enumerate(got) if i not in (aliases or {}).values()]
    Order.last = min(fresh or got, key=lambda v: v.size)
    return got


def shape(dims, dtype):
    return jax.ShapeDtypeStruct(dims, dtype)


SMEM = pl.BlockSpec(memory_space=pltpu.SMEM)
ANY = pl.BlockSpec(memory_space=pl.ANY)


def gate(arrays, after=()):
    arrays = list(arrays)
    return call(
        "gate",
        lambda *refs: None,
        (1,),
        arrays,
        [ANY] * len(arrays),
        [shape(a.shape, a.dtype) for a in arrays],
        [ANY] * len(arrays),
        after=after,
        aliases={i: i for i in range(len(arrays))},
    )


def rows_of(block):
    return pl.BlockSpec(block, lambda i: (i, 0))


def cols_of(block):
    return pl.BlockSpec(block, lambda i: (0, i))


def fixed(block):
    return pl.BlockSpec(block, lambda i: (0,) * len(block))


def place_of(me, j, width):
    return pl.ds(pl.multiple_of((me ^ j) * width, width), width)


def with_weights(copies, work):
    @pl.when(pl.program_id(0) == 0)
    def _():
        for one in copies:
            one.start()

        def wait(some):
            for one in some:
                one.wait()

        work(wait)

    @pl.when(pl.program_id(0) != 0)
    def _():
        work(lambda some: None)


def row_blocks(me, n, width, source, target, sems, base):
    return [
        pltpu.make_async_copy(
            source.at[place_of(me, j, width), :],
            target.at[pl.ds(j * width, width), :],
            sems.at[base + j],
        )
        for j in range(n)
    ]


def col_blocks(me, n, width, source, target, sems, base):
    return [
        pltpu.make_async_copy(
            source.at[:, place_of(me, j, width)],
            target.at[:, pl.ds(j * width, width)],
            sems.at[base + j],
        )
        for j in range(n)
    ]


def stat_columns(first, second):
    lane = lax.broadcasted_iota(jnp.int32, (first.shape[0], 128), 1)
    return jnp.where(lane == 0, first, jnp.where(lane == 1, second, 0.0))


def fold_rows(values):
    return jnp.sum(values.reshape(values.shape[0] // 8, 8, values.shape[1]), 0)


def accumulate(ref, value):
    @pl.when(pl.program_id(0) == 0)
    def _():
        ref[...] = value

    @pl.when(pl.program_id(0) != 0)
    def _():
        ref[...] += value


def average_body(weights, history, wide, low):
    total = weights[0] * history[0].astype(F32)
    for j in range(1, history.shape[0]):
        total += weights[j] * history[j].astype(F32)
    wide[...] = total
    low[...] = total.astype(BF16)


def average(weights, history, row, length):
    count, _, width = history.shape
    tile = min(256, length)
    steps = length // tile
    return call(
        "average",
        average_body,
        (steps,),
        (weights, history),
        [SMEM, pl.BlockSpec((count, tile, width), lambda i: (0, row * steps + i, 0))],
        [shape((length, width), F32), shape((length, width), BF16)],
        [rows_of((tile, width))] * 2,
    )


def project_body(n, me, *refs):
    xs = refs[:n]
    gain, bias, cosine, sine, weight, qkv, normed, stat, held, joined, sems = refs[n:]
    width = xs[0].shape[1]
    full = n * width
    heads = held.shape[1] // (3 * HEAD)
    tile = xs[0].shape[0]
    sub = min(256, tile)
    copies = row_blocks(me[0], n, width, weight, held, sems, 0)

    def work(wait):
        for t in range(tile // sub):
            rows = slice(t * sub, (t + 1) * sub)
            total = square = 0.0
            for x in xs:
                value = x[rows, :].astype(F32)
                total += jnp.sum(value, 1, keepdims=True)
                square += jnp.sum(value * value, 1, keepdims=True)
            mean = total / full
            inv = lax.rsqrt(square / full - mean * mean + EPSILON)
            stat[rows, :] = stat_columns(mean, inv)
            for j, x in enumerate(xs):
                part = slice(j * width, (j + 1) * width)
                value = (x[rows, :].astype(F32) - mean) * inv * gain[0:1, part] + bias[0:1, part]
                joined[rows, part] = value.astype(BF16)
                normed[rows, place_of(me[0], j, width)] = value.astype(BF16)
            if t == 0:
                wait(copies)
            for h in range(heads):
                base = 3 * h * HEAD
                out = dot_nn(joined[rows, :], held[:, base : base + 3 * HEAD])
                for s in range(2):
                    v = out[:, s * HEAD : (s + 1) * HEAD]
                    turned = v * cosine[rows, :] + pltpu.roll(v, HEAD // 2, 1) * sine[rows, :]
                    qkv[rows, base + s * HEAD : base + (s + 1) * HEAD] = turned.astype(BF16)
                qkv[rows, base + 2 * HEAD : base + 3 * HEAD] = out[:, 2 * HEAD :].astype(BF16)

    with_weights(copies, work)


def project(me, xs, gain, bias, tables, weight):
    n, (length, width) = len(xs), xs[0].shape
    full, out = weight.shape
    tile = min(512, length)
    return call(
        "project",
        lambda *refs: project_body(n, *refs),
        (length // tile,),
        (me, *xs, gain, bias, *tables, weight),
        [SMEM]
        + [rows_of((tile, width))] * n
        + [fixed((8, full))] * 2
        + [rows_of((tile, HEAD))] * 2
        + [ANY],
        [shape((length, out), BF16), shape((length, full), BF16), shape((length, 128), F32)],
        [rows_of((tile, out)), rows_of((tile, full)), rows_of((tile, 128))],
        scratch=[
            pltpu.VMEM((full, out), BF16),
            pltpu.VMEM((tile, full), BF16),
            pltpu.SemaphoreType.DMA((n,)),
        ],
    )


def windows(length):
    block = min(256, length)
    for i in range(length // block):
        low = max(0, i * block - (MAX_DOC - 1)) // block * block
        yield slice(i * block, (i + 1) * block), slice(low, (i + 1) * block)


def score_mask(start, q_part, k_part):
    dims = (k_part.stop - k_part.start, q_part.stop - q_part.start)
    k_pos = lax.broadcasted_iota(jnp.int32, dims, 0) + k_part.start
    q_pos = lax.broadcasted_iota(jnp.int32, dims, 1) + q_part.start
    return (k_pos >= start[0:1, q_part]) & (k_pos <= q_pos)


def attend_body(start, qkv, out, logs):
    length = qkv.shape[0]
    value_t = qkv[:, 2 * HEAD :].T
    for q_part, k_part in windows(length):
        query, key = qkv[q_part, :HEAD], qkv[k_part, HEAD : 2 * HEAD]
        scores = dot_nt(key, query) * (SCALE * LOG2E)
        scores = jnp.where(score_mask(start, q_part, k_part), scores, -1e30)
        top = jnp.max(scores, 0, keepdims=True)
        probs = jnp.exp2(scores - top)
        total = jnp.sum(probs, 0, keepdims=True)
        logs[0, :, q_part] = jnp.broadcast_to(top + jnp.log2(total), (8, q_part.stop - q_part.start))
        got = dot_nn(value_t[:, k_part], probs.astype(BF16)) / total
        out[q_part, :] = got.T.astype(BF16)


def attend(start, qkv):
    length, width = qkv.shape
    heads = width // (3 * HEAD)
    return call(
        "attend",
        attend_body,
        (heads,),
        (start, qkv),
        [fixed((8, length)), cols_of((length, 3 * HEAD))],
        [shape((length, heads * HEAD), BF16), shape((heads, 8, length), F32)],
        [cols_of((length, HEAD)), pl.BlockSpec((1, 8, length), lambda i: (i, 0, 0))],
    )


def attend_back_body(start, cosine, sine, qkv, grad, logs, out, key_sum, value_sum):
    length = qkv.shape[0]
    key_t = qkv[:, HEAD : 2 * HEAD].T
    key_sum[...] = jnp.zeros_like(key_sum)
    value_sum[...] = jnp.zeros_like(value_sum)

    def turn_back(v, part):
        return (
            v * cosine[part, :] - pltpu.roll(v, HEAD // 2, 1) * sine[part, :]
        ).astype(BF16)

    for q_part, k_part in windows(length):
        query, key = qkv[q_part, :HEAD], qkv[k_part, HEAD : 2 * HEAD]
        value, g = qkv[k_part, 2 * HEAD :], grad[q_part, :]
        scores = dot_nt(key, query) * (SCALE * LOG2E) - logs[0, 0:1, q_part]
        probs = jnp.exp2(jnp.where(score_mask(start, q_part, k_part), scores, -1e30))
        prob_grad = dot_nt(value, g)
        mean = jnp.sum(prob_grad * probs, 0, keepdims=True)
        score_grad = (probs * (prob_grad - mean)).astype(BF16)
        value_sum[k_part, :] += dot_nn(probs.astype(BF16), g)
        key_sum[k_part, :] += dot_nn(score_grad, query)
        query_grad = dot_nn(key_t[:, k_part], score_grad) * SCALE
        out[q_part, :HEAD] = turn_back(query_grad.T, q_part)
    for q_part, _ in windows(length):
        out[q_part, HEAD : 2 * HEAD] = turn_back(key_sum[q_part, :] * SCALE, q_part)
        out[q_part, 2 * HEAD :] = value_sum[q_part, :].astype(BF16)


def attend_back(start, tables, qkv, grad, logs):
    length, width = qkv.shape
    heads = width // (3 * HEAD)
    return call(
        "attend_back",
        attend_back_body,
        (heads,),
        (start, *tables, qkv, grad, logs),
        [fixed((8, length))]
        + [fixed((length, HEAD))] * 2
        + [
            cols_of((length, 3 * HEAD)),
            cols_of((length, HEAD)),
            pl.BlockSpec((1, 8, length), lambda i: (i, 0, 0)),
        ],
        [shape((length, width), BF16)],
        [cols_of((length, 3 * HEAD))],
        scratch=[pltpu.VMEM((length, HEAD), F32)] * 2,
    )[0]


def feed_body(n, beside, me, *refs):
    attended, xs, outs_w = refs[:n], refs[n : 2 * n], refs[2 * n : 3 * n]
    own, gain, bias, up_bias, up_weight, down_weight = refs[3 * n : 3 * n + 6]
    extra = refs[3 * n + 6 : 3 * n + 6 + beside]
    refs = refs[3 * n + 6 + beside :]
    hidden, normed, stat, activated, slope = refs[:5]
    parts = refs[5 : n + 5]
    refs = refs[n + 5 :]
    if beside:
        put_beside(me, extra, *refs[:2])
        refs = refs[2:]
    out_held, up_held, down_held, joined, whole, sems = refs
    width = xs[0].shape[1]
    full = n * width
    inner = up_held.shape[1]
    out_copies = []
    for j in range(n):
        for k in range(n):
            out_copies.append(
                pltpu.make_async_copy(
                    outs_w[k].at[:, place_of(me[0], j, width)],
                    out_held.at[pl.ds(k * width, width), pl.ds(j * width, width)],
                    sems.at[j * n + k],
                )
            )
    up_copies = row_blocks(me[0], n, width, up_weight, up_held, sems, n * n)
    down_copies = col_blocks(me[0], n, width, down_weight, down_held, sems, n * n + n)

    def work(wait):
        for j in range(n):
            joined[:, j * width : (j + 1) * width] = attended[j][...]
        total = square = 0.0
        for j in range(n):
            wait(out_copies[j * n : (j + 1) * n])
            part = slice(j * width, (j + 1) * width)
            base = own[...] if j == 0 else xs[j][...].astype(F32)
            value = base + dot_nn(joined[...], out_held[:, part])
            whole[:, part] = value
            if j == 0:
                hidden[...] = value
            total += jnp.sum(value, 1, keepdims=True)
            square += jnp.sum(value * value, 1, keepdims=True)
        mean = total / full
        inv = lax.rsqrt(square / full - mean * mean + EPSILON)
        stat[...] = stat_columns(mean, inv)
        for j in range(n):
            part = slice(j * width, (j + 1) * width)
            value = ((whole[:, part] - mean) * inv * gain[0:1, part] + bias[0:1, part]).astype(BF16)
            joined[:, part] = value
            normed[:, place_of(me[0], j, width)] = value
        wait(up_copies)
        step = divisor(inner, 512)
        for c in range(inner // step):
            part = slice(c * step, (c + 1) * step)
            up = dot_nn(joined[...], up_held[:, part]) + up_bias[0:1, part]
            half = 0.5 * (1.0 + lax.erf(up * SQRT_HALF))
            activated[:, part] = (up * half).astype(BF16)
            slope[:, part] = (half + up * INV_ROOT_TWO_PI * jnp.exp(-0.5 * up * up)).astype(BF16)
        wait(down_copies)
        for j in range(n):
            parts[j][...] = dot_nn(
                activated[...], down_held[:, j * width : (j + 1) * width]
            ).astype(BF16)

    with_weights(out_copies + up_copies + down_copies, work)


def put_beside(me, blocks, whole, sums):
    width = blocks[0].shape[1]
    for j, block in enumerate(blocks):
        whole[:, place_of(me[0], j, width)] = block[...]
    accumulate(sums, fold_rows(blocks[0][...].astype(F32)))


def feed(me, attended, xs, outs_w, own, gain, bias, up_bias, up_weight, down_weight, beside=()):
    n, (length, width) = len(xs), own.shape
    full, inner = up_weight.shape
    tile = min(256, length)
    got = call(
        "feed",
        lambda *refs: feed_body(n, len(beside), *refs),
        (length // tile,),
        (me, *attended, *xs, *outs_w, own, gain, bias, up_bias, up_weight, down_weight, *beside),
        [SMEM]
        + [rows_of((tile, width))] * (2 * n)
        + [ANY] * n
        + [rows_of((tile, width))]
        + [fixed((8, full))] * 2
        + [fixed((8, inner))]
        + [ANY] * 2
        + [rows_of((tile, width))] * len(beside),
        [
            shape((length, width), F32),
            shape((length, full), BF16),
            shape((length, 128), F32),
            shape((length, inner), BF16),
            shape((length, inner), BF16),
        ]
        + [shape((length, width), BF16)] * n
        + ([shape((length, full), BF16), shape((8, width), F32)] if beside else []),
        [
            rows_of((tile, width)),
            rows_of((tile, full)),
            rows_of((tile, 128)),
            rows_of((tile, inner)),
            rows_of((tile, inner)),
        ]
        + [rows_of((tile, width))] * n
        + ([rows_of((tile, full)), fixed((8, width))] if beside else []),
        scratch=[
            pltpu.VMEM((full, full), BF16),
            pltpu.VMEM((full, inner), BF16),
            pltpu.VMEM((inner, full), BF16),
            pltpu.VMEM((tile, full), BF16),
            pltpu.VMEM((tile, full), F32),
            pltpu.SemaphoreType.DMA((n * n + 2 * n,)),
        ],
    )
    return (*got[:5], got[5 : n + 5], got[n + 5 :])


def row_stats(total, weighted):
    return stat_columns(total, weighted).T[0:8, :]


def beside(me, blocks):
    n, (length, width) = len(blocks), blocks[0].shape
    tile = min(256, length)
    return call(
        "beside",
        lambda me, *refs: put_beside(me, refs[:n], *refs[n:]),
        (length // tile,),
        (me, *blocks),
        [SMEM] + [rows_of((tile, width))] * n,
        [shape((length, n * width), BF16), shape((8, width), F32)],
        [rows_of((tile, n * width)), fixed((8, width))],
    )


def feed_back_body(n, beside, joined_in, me, *refs):
    cots, refs = refs[:joined_in], refs[joined_in:]
    slope, normed, gain, bias, up_weight, down_weight = refs[:6]
    extra, refs = refs[6 : 6 + beside], refs[6 + beside :]
    up_grad, sums, up_bias_sum = refs[:3]
    parts, refs = refs[3 : n + 3], refs[n + 3 :]
    if beside:
        put_beside(me, extra, *refs[:2])
        refs = refs[2:]
    up_held, down_held, sems = refs
    width = parts[0].shape[1]
    inner = up_held.shape[1]
    step = divisor(inner, 512)
    down_copies = [pltpu.make_async_copy(down_weight, down_held, sems.at[n])]
    up_copies = row_blocks(me[0], n, width, up_weight, up_held, sems, 0)
    cot = cots[0]

    def work(wait):
        wait(down_copies)
        bias_parts = []
        for c in range(inner // step):
            part = slice(c * step, (c + 1) * step)
            value = dot_nt(cot[...], down_held[part, :]) * slope[:, part].astype(F32)
            low = value.astype(BF16)
            up_grad[:, part] = low
            bias_parts.append(fold_rows(low.astype(F32)))
        accumulate(up_bias_sum, jnp.concatenate(bias_parts, 1))
        total = weighted = 0.0
        wait(up_copies)
        for j in range(n):
            part = slice(j * width, (j + 1) * width)
            value = dot_nt(up_grad[...], up_held[part, :])
            parts[j][...] = value.astype(BF16)
            total += jnp.sum(value * gain[0:1, part], 1, keepdims=True)
            there = normed[:, place_of(me[0], j, width)].astype(F32)
            weighted += jnp.sum(value * (there - bias[0:1, part]), 1, keepdims=True)
        sums[...] = row_stats(total, weighted)

    with_weights(down_copies + up_copies, work)


def feed_back(me, n, cot, slope, normed, gain, bias, up_weight, down_weight, beside=()):
    length, full = cot.shape
    width = full // n
    inner = up_weight.shape[1]
    tile = min(256, length)
    got = call(
        "feed_back",
        lambda *refs: feed_back_body(n, len(beside), 1, *refs),
        (length // tile,),
        (me, cot, slope, normed, gain, bias, up_weight, down_weight, *beside),
        [SMEM]
        + [rows_of((tile, full)), rows_of((tile, inner)), rows_of((tile, full))]
        + [fixed((8, full))] * 2
        + [ANY] * 2
        + [rows_of((tile, width))] * len(beside),
        [shape((length, inner), BF16), shape((8, length), F32), shape((8, inner), F32)]
        + [shape((length, width), BF16)] * n
        + ([shape((length, full), BF16), shape((8, width), F32)] if beside else []),
        [rows_of((tile, inner)), cols_of((8, tile)), fixed((8, inner))]
        + [rows_of((tile, width))] * n
        + ([rows_of((tile, full)), fixed((8, width))] if beside else []),
        scratch=[
            pltpu.VMEM((full, inner), BF16),
            pltpu.VMEM((inner, full), BF16),
            pltpu.SemaphoreType.DMA((n + 1,)),
        ],
    )
    return (*got[:3], got[3 : n + 3], got[n + 3 :])


def norm_back(refs, n_parts, source, stat, sums, gain, full):
    grad = refs[0][...].astype(F32)
    for ref in refs[1:n_parts]:
        grad += ref[...].astype(F32)
    columns = sum(one[...] for one in sums).T
    mean, inv = stat[:, 0:1], stat[:, 1:2]
    scaled = (source[...] - mean) * inv
    back = inv * (
        grad * gain[0:1, :] - columns[:, 0:1] * (1.0 / full) - scaled * (columns[:, 1:2] * (1.0 / full))
    )
    return back, fold_rows(grad * scaled), fold_rows(grad)


def hidden_back_body(k, m, full, *refs):
    parts, sums = refs[:k], refs[k : k + m]
    cot, hidden, stat, gain, wide, low, gain_sum, bias_sum = refs[k + m :]
    back, gain_part, bias_part = norm_back(parts, k, hidden, stat, sums, gain, full)
    value = cot[...].astype(F32) + back
    wide[...] = value
    low[...] = value.astype(BF16)
    accumulate(gain_sum, gain_part)
    accumulate(bias_sum, bias_part)


def hidden_back(parts, cotangent, row, hidden, stat, sums, gain, full):
    k, m, (length, width) = len(parts), len(sums), hidden.shape
    tile = min(256, length)
    steps = length // tile
    return call(
        "hidden_back",
        lambda *refs: hidden_back_body(k, m, full, *refs),
        (steps,),
        (*parts, *sums, cotangent, hidden, stat, gain),
        [rows_of((tile, width))] * k
        + [cols_of((8, tile))] * m
        + [
            pl.BlockSpec((tile, width), lambda i: (row * steps + i, 0)),
            rows_of((tile, width)),
            rows_of((tile, 128)),
            fixed((8, width)),
        ],
        [shape((length, width), F32), shape((length, width), BF16)] + [shape((8, width), F32)] * 2,
        [rows_of((tile, width))] * 2 + [fixed((8, width))] * 2,
    )


def attended_back_body(n, me, *refs):
    grads = refs[:n]
    weight, joined, out = refs[n:]
    width = grads[0].shape[1]
    for j in range(n):
        joined[:, place_of(me[0], j, width)] = grads[j][...]
    out[...] = dot_nt(joined[...], weight[...]).astype(BF16)


def attended_back(me, grads, weight):
    n, (length, width) = len(grads), grads[0].shape
    rows, full = weight.shape
    tile = min(256, length)
    return call(
        "attended_back",
        lambda *refs: attended_back_body(n, *refs),
        (length // tile,),
        (me, *grads, weight),
        [SMEM] + [rows_of((tile, width))] * n + [fixed((rows, full))],
        [shape((length, full), BF16), shape((length, rows), BF16)],
        [rows_of((tile, full)), rows_of((tile, rows))],
    )


def project_back_body(n, me, grad, normed, gain, bias, weight, sums, *refs):
    parts = refs[:n]
    held, sems = refs[n:]
    width = parts[0].shape[1]
    copies = row_blocks(me[0], n, width, weight, held, sems, 0)

    def work(wait):
        total = weighted = 0.0
        for j in range(n):
            wait(copies[j : j + 1])
            part = slice(j * width, (j + 1) * width)
            value = dot_nt(grad[...], held[part, :])
            parts[j][...] = value.astype(BF16)
            total += jnp.sum(value * gain[0:1, part], 1, keepdims=True)
            there = normed[:, place_of(me[0], j, width)].astype(F32)
            weighted += jnp.sum(value * (there - bias[0:1, part]), 1, keepdims=True)
        sums[...] = row_stats(total, weighted)

    with_weights(copies, work)


def project_back(me, n, grad, normed, gain, bias, weight):
    length, out = grad.shape
    full = weight.shape[0]
    width = full // n
    tile = min(256, length)
    got = call(
        "project_back",
        lambda *refs: project_back_body(n, *refs),
        (length // tile,),
        (me, grad, normed, gain, bias, weight),
        [SMEM, rows_of((tile, out)), rows_of((tile, full))] + [fixed((8, full))] * 2 + [ANY],
        [shape((8, length), F32)] + [shape((length, width), BF16)] * n,
        [cols_of((8, tile))] + [rows_of((tile, width))] * n,
        scratch=[pltpu.VMEM((full, out), BF16), pltpu.SemaphoreType.DMA((n,))],
    )
    return got[0], got[1:]


def average_back_body(k, m, full, count, *refs):
    weights, parts, sums = refs[0], refs[1 : k + 1], refs[k + 1 : k + m + 1]
    source, stat, gain, hidden_grad, history = refs[k + m + 1 : k + m + 6]
    grad_history, depth_sum, gain_sum, bias_sum = refs[-4:]
    back, gain_part, bias_part = norm_back(parts, k, source, stat, sums, gain, full)
    value = hidden_grad[...] + back
    accumulate(gain_sum, gain_part)
    accumulate(bias_sum, bias_part)
    lanes = value.shape[1] // 128
    for j in range(count):
        grad_history[j] = (weights[j] * value).astype(BF16)
        product = fold_rows(value * history[j].astype(F32))
        folded = product[:, 0:128]
        for c in range(1, lanes):
            folded += product[:, c * 128 : (c + 1) * 128]
        accumulate(depth_sum.at[j], folded)


def average_back(weights, parts, source, stat, sums, gain, hidden_grad, history, row, made):
    k, m, (length, width) = len(parts), len(sums), source.shape
    count = history.shape[0]
    tile = min(256, length)
    steps = length // tile
    full = gain[1]
    block = pl.BlockSpec((count, tile, width), lambda i: (0, row * steps + i, 0))
    args = (weights, *parts, *sums, source, stat, gain[0], hidden_grad, history)
    specs = (
        [SMEM]
        + [rows_of((tile, width))] * k
        + [cols_of((8, tile))] * m
        + [rows_of((tile, width)), rows_of((tile, 128)), fixed((8, width)), rows_of((tile, width)), block]
    )
    more = {}
    if made is not None:
        more = {"aliases": {len(args): 0}}
        args, specs = (*args, made), specs + [ANY]
    return call(
        "average_back",
        lambda *refs: average_back_body(k, m, full, count, *refs),
        (steps,),
        args,
        specs,
        [shape(history.shape, BF16), shape((count, 8, 128), F32)] + [shape((8, width), F32)] * 2,
        [block, fixed((count, 8, 128))] + [fixed((8, width))] * 2,
        **more,
    )


def divisor(size, most):
    return max(d for d in range(128, most + 1, 128) if size % d == 0) if size > 128 else size


def weight_body(rows, *refs):
    out = refs[-1]
    total = dot_tn(refs[0][...], refs[rows][...])
    for r in range(1, rows):
        total += dot_tn(refs[r][...], refs[rows + r][...])
    out[...] = total.astype(BF16)


def weight_grad(lefts, rights):
    rows, (length, high), wide = len(lefts), lefts[0].shape, rights[0].shape[1]
    tall, across = divisor(high, 512), divisor(wide, 1024)
    return call(
        "weight_grad",
        lambda *refs: weight_body(rows, *refs),
        (high // tall, wide // across),
        (*lefts, *rights),
        [pl.BlockSpec((length, tall), lambda i, j: (0, i))] * rows
        + [pl.BlockSpec((length, across), lambda i, j: (0, j))] * rows,
        [shape((high, wide), BF16)],
        [pl.BlockSpec((tall, across), lambda i, j: (i, j))],
    )[0]


def put_blocks(came, outs, k, value):
    if came is not None:
        value = value + came[k].astype(F32)
    per = outs[0].shape[0]
    outs[k // per][k % per] = value.astype(BF16)


def tall_blocks_body(rows, count, fused, group, *refs):
    lefts, rights = refs[: rows * count], refs[rows * count : rows * count + rows]
    refs = refs[rows * count + rows :]
    came, outs, turned = refs[0] if fused else None, refs[fused:-1], refs[-1]
    length, high = lefts[0].shape

    @pl.when(pl.program_id(0) == 0)
    def _():
        for k in range(count):
            for r in range(rows):
                turned[k * high : (k + 1) * high, r * length : (r + 1) * length] = lefts[
                    k * rows + r
                ][...].T

    for k in range(count):
        total = 0.0
        for r in range(rows):
            total += dot_nn(
                turned[k * high : (k + 1) * high, r * length : (r + 1) * length], rights[r][...]
            )
        put_blocks(came, outs, k, total)


def wide_blocks_body(rows, count, fused, group, *refs):
    lefts, rights = refs[:rows], refs[rows : rows + rows * count]
    refs = refs[rows + rows * count :]
    came, outs = refs[0] if fused else None, refs[fused:]
    turned = [left[...].T for left in lefts]
    for k in range(count):
        total = 0.0
        for r in range(rows):
            total += dot_nn(turned[r], rights[k * rows + r][...])
        put_blocks(came, outs, k, total)


class Spread:
    def __init__(self, lefts, rights, dim, bits, part=(0, 1)):
        self.lefts, self.rights, self.dim, self.bits, self.part = lefts, rights, dim, list(bits), part
        self.groups = lax.axis_size("dp")
        self.block = (lefts, rights)[dim][0].shape[1] // self.groups
        order = [0]
        for bit in reversed(self.bits):
            order = order + [e | bit for e in order]
        self.order = order

    def blocks(self, half, came=None):
        count = self.groups // 2
        which = self.order[half * count : (half + 1) * count]
        rows, length = len(self.lefts), self.lefts[0].shape[0]
        group = lax.axis_index("dp").astype(jnp.int32)[None]
        size, (index, pieces) = self.block, self.part
        stay = [
            pl.BlockSpec((length, size), lambda i, group, e=e: (0, group[0] ^ e))
            for e in which
            for _ in range(rows)
        ]
        other = self.rights if self.dim == 0 else self.lefts
        extent = other[0].shape[1] // pieces
        tile = divisor(extent, 512)
        steps = extent // tile
        move = [pl.BlockSpec((length, tile), lambda i, group: (0, index * steps + i))] * rows

        def blocked(number):
            if self.dim == 0:
                return (
                    shape((number, size, extent), BF16),
                    pl.BlockSpec((number, size, tile), lambda i, group: (0, 0, i)),
                )
            return (
                shape((number, extent, size), BF16),
                pl.BlockSpec((number, tile, size), lambda i, group: (0, i, 0)),
            )

        if self.dim == 0:
            args = (*(list(self.lefts) * count), *self.rights)
            specs = stay + move
            body, scratch = tall_blocks_body, [pltpu.VMEM((count * size, rows * length), BF16)]
        else:
            args = (*self.lefts, *(list(self.rights) * count))
            specs = move + stay
            body, scratch = wide_blocks_body, []
        outs = [blocked(count)]
        if came is not None:
            args, specs = (*args, came), specs + [blocked(count)[1]]
            outs = [blocked(count // 2)] * 2
        return call(
            "weight_blocks",
            lambda *refs: body(rows, count, came is not None, *refs),
            (steps,),
            (group, *args),
            specs,
            [one[0] for one in outs],
            [one[1] for one in outs],
            scratch=scratch,
            prefetch=1,
        )

    def send(self, value):
        bit = self.bits[self.step]
        self.step += 1
        self.coming = lax.ppermute(value, "dp", [(i, i ^ bit) for i in range(self.groups)])

    def first(self):
        self.step = 0
        self.send(self.blocks(1)[0])

    def keep(self):
        self.held = self.blocks(0)[0]

    def keep_added(self):
        self.held, out = self.blocks(0, self.coming)
        self.send(out)


def fold_body(count, *refs):
    for i in range(count):
        held, came, keep, send = refs[2 * i], refs[2 * i + 1], refs[2 * count + 2 * i], refs[2 * count + 2 * i + 1]
        half = keep.shape[0]
        keep[...] = (held[:half].astype(F32) + came[:half].astype(F32)).astype(BF16)
        send[...] = (held[half:].astype(F32) + came[half:].astype(F32)).astype(BF16)


def advance(*spreads):
    steps = 4
    args, specs, outs, out_specs = [], [], [], []
    for one in spreads:
        count, high, wide = one.held.shape
        args += [one.held, one.coming]
        specs += [pl.BlockSpec((count, high // steps, wide), lambda i: (0, i, 0))] * 2
        outs += [shape((count // 2, high, wide), BF16)] * 2
        out_specs += [pl.BlockSpec((count // 2, high // steps, wide), lambda i: (0, i, 0))] * 2
    got = call("fold", lambda *refs: fold_body(len(spreads), *refs), (steps,), args, specs, outs, out_specs)
    for i, one in enumerate(spreads):
        one.held = got[2 * i]
        one.send(got[2 * i + 1])


def finish_body(groups, *refs):
    outs = refs[len(refs) - len(groups) :]
    at = 0
    for out, group in zip(outs, groups):
        for first, wide in group:
            total = refs[at][0].astype(F32) + refs[at + 1][0].astype(F32)
            out[:, first : first + wide] = total
            at += 2


def finish(*groups):
    steps = 4
    args, specs, outs, out_specs, places = [], [], [], [], []
    for group in groups:
        first, place = 0, []
        for one in group:
            _, high, wide = one.held.shape
            args += [one.held, one.coming]
            specs += [pl.BlockSpec((1, high // steps, wide), lambda i: (0, i, 0))] * 2
            place.append((first, wide))
            first += wide
        outs.append(shape((high, first), F32))
        out_specs.append(rows_of((high // steps, first)))
        places.append(place)
    return call("finish", lambda *refs: finish_body(places, *refs), (steps,), args, specs, outs, out_specs)


def add_body(*refs):
    count = len(refs) // 3
    for left, right, out in zip(refs[:count], refs[count : 2 * count], refs[2 * count :]):
        out[...] = (left[...].astype(F32) + right[...].astype(F32)).astype(out.dtype)


def add(lefts, rights):
    steps = 2

    def spec(v):
        if v.dtype == BF16:
            return rows_of((v.shape[0] // steps, v.shape[1]))
        return cols_of((v.shape[0], v.shape[1] // steps))

    specs = [spec(v) for v in lefts]
    return call(
        "add", add_body, (steps,), (*lefts, *rights), specs * 2, [shape(v.shape, v.dtype) for v in lefts], specs
    )


def output_body(rows, steps, *refs):
    bias, out = refs[-2:]
    per = (len(refs) - 2) // rows
    for r in range(rows):

        @pl.when(pl.program_id(0) // steps == r)
        def _(r=r):
            total = bias[0:1, :]
            for part in refs[r * per + 1 : (r + 1) * per]:
                total = total + part[...].astype(F32)
            out[...] = (refs[r * per][...] + total).astype(BF16)


def output(parts, hidden, bias):
    rows, (length, width) = len(hidden), hidden[0].shape
    tile = min(512, length)
    steps = length // tile
    args, specs = [], []
    for r in range(rows):
        args += [hidden[r], *parts[r]]
        specs += [
            pl.BlockSpec((tile, width), lambda i, r=r: (jnp.clip(i - r * steps, 0, steps - 1), 0))
        ] * (1 + len(parts[r]))
    return call(
        "output",
        lambda *refs: output_body(rows, steps, *refs),
        (rows * steps,),
        (*args, bias),
        specs + [fixed((8, width))],
        [shape((rows * length, width), BF16)],
        [rows_of((tile, width))],
    )[0]


class Ring:
    def __init__(self):
        self.n = lax.axis_size("mp")
        self.me = lax.axis_index("mp").astype(jnp.int32)
        self.pairs = self.n == 4
        self.core = [(i, i ^ 1) for i in range(self.n)]
        self.chip = [(i, i ^ 2) for i in range(self.n)]

    def over_core(self, value):
        return lax.ppermute(value, "mp", self.core)

    def over_chip(self, value):
        return lax.ppermute(value, "mp", self.chip)

    def gather_start(self, block):
        if self.pairs:
            return [block, self.over_chip(block)]
        every = lax.all_gather(block, "mp")
        return [
            lax.dynamic_index_in_dim(every, self.me ^ j, 0, keepdims=False) for j in range(self.n)
        ]

    def gather_end(self, blocks, held=True):
        if self.pairs:
            block, across = gate(blocks) if held else blocks
            return [block, self.over_core(block), across, self.over_core(across)]
        return blocks

    def gather(self, block):
        return self.gather_end(self.gather_start(block), False)

    def scatter_start(self, parts, sums=None):
        extra = [] if sums is None else [sums]
        if self.pairs:
            sent = [parts[3], *extra, parts[1]]
            return [parts[2], *extra, parts[0]], [self.over_core(v) for v in sent]
        stacked = jnp.stack([part.astype(F32) for part in parts])
        ordered = jnp.take(stacked, self.me ^ jnp.arange(self.n), axis=0)
        total = lax.psum_scatter(ordered, "mp", scatter_dimension=0, tiled=False)
        return [total], [lax.psum(v, "mp") for v in extra]

    def scatter_end(self, state):
        if not self.pairs:
            return state
        got = add(*state)
        sums = list(got[1:-1])
        return [got[-1], self.over_chip(got[0])], sums + [self.over_chip(v) for v in sums]

    def total(self, value):
        if self.pairs:
            value = value + self.over_core(value)
            return value + self.over_chip(value)
        return lax.psum(value, "mp")

    def out_start(self, weight):
        rows, groups = weight.shape[0], lax.axis_size("dp")
        if self.pairs and rows % (16 * groups) == 0:
            size = rows // groups
            piece = lax.dynamic_slice_in_dim(weight, lax.axis_index("dp") * size, size, 0)
            return self.over_chip(piece)
        return None

    def out_middle(self, piece):
        return None if piece is None else lax.all_gather(gate([piece])[0], "dp", axis=0, tiled=True)

    def out_end(self, weight, across):
        if across is None:
            return lambda: self.gather(weight)
        sent = [self.over_core(weight), self.over_core(across)]

        def end():
            sibling, far = gate(sent)
            return [weight, sibling, across, far]

        return end


def dp_total(vectors):
    groups = lax.axis_size("dp")
    sizes = [v.size for v in vectors]
    packed = jnp.concatenate(vectors)
    packed = jnp.pad(packed, (0, -packed.size % 1024)).reshape(-1, 128)
    bit = 1
    while bit < groups:
        packed = packed + lax.ppermute(packed, "dp", [(i, i ^ bit) for i in range(groups)])
        bit *= 2
    packed = packed.reshape(-1)
    ends = np.cumsum(sizes)
    return [packed[end - size : end] for end, size in zip(ends, sizes)]


def tables_of(length):
    half = HEAD // 2
    rate = np.exp(np.arange(half, dtype=np.float64) * (-math.log(10000.0) / half))
    angle = np.arange(length, dtype=np.float64)[:, None] * rate[None, :]
    cosine, sine = np.cos(angle), np.sin(angle)
    return (
        jnp.asarray(np.concatenate([cosine, cosine], 1), F32),
        jnp.asarray(np.concatenate([-sine, sine], 1), F32),
    )


def local(
    history,
    depth_weights,
    segment_ids,
    first_gain,
    first_bias,
    qkv_weight,
    out_weight,
    second_gain,
    second_bias,
    up_weight,
    up_bias,
    down_weight,
    down_bias,
    cotangent,
):
    ring = Ring()
    n = ring.n
    me = ring.me[None]
    width = history.shape[2]
    full = n * width
    row_count, length = segment_ids.shape
    rows = range(row_count)
    tables = tables_of(length)
    earlier = (segment_ids[:, None, :] < segment_ids[:, :, None]).astype(jnp.int32)
    starts = jnp.broadcast_to(jnp.sum(earlier, -1)[:, None, :], (row_count, 8, length))

    vectors = jnp.stack([first_gain, first_bias, second_gain, second_bias])
    vectors = jnp.concatenate(ring.gather(jnp.repeat(vectors, 8, 0)), 1)
    gain1, bias1, gain2, bias2 = (vectors[8 * i : 8 * i + 8] for i in range(4))
    own1, own2 = gain1[:, :width], gain2[:, :width]
    up_bias8 = jnp.broadcast_to(up_bias[None], (8, up_bias.shape[0]))

    down_bias8 = jnp.broadcast_to(down_bias[None], (8, width))
    groups = lax.axis_size("dp")
    spread = full % (128 * groups) == 0 and groups >= 4
    last = row_count - 1

    Order.last = None
    piece = ring.out_start(out_weight)
    cot_rows = [lax.slice_in_dim(cotangent, r * length, (r + 1) * length) for r in rows]
    none = [None] * row_count
    wide, xs, qkv, normed1, stat1 = list(none), list(none), list(none), list(none), list(none)
    attended, logs, heads, cots, cot_full = list(none), list(none), list(none), list(none), list(none)
    hidden, normed2, stat2, activated, slope = (list(none) for _ in range(5))
    branch, up_grad, parts2, parts1 = list(none), list(none), list(none), list(none)
    hidden_grad, grads, grad_full, qkv_grad = list(none), list(none), list(none), list(none)
    up_bias_sum = down_bias_sum = gain2_sum = bias2_sum = 0.0

    low = list(none)
    for r in rows:
        wide[r], low[r] = average(depth_weights, history, r, length)
        if r == 0:
            xs[0] = ring.gather_start(low[0])
    across = ring.out_middle(piece)
    for r in rows:
        if r > 0:
            xs[r] = ring.gather_start(gate([low[r]], xs[r - 1][1:2])[0])
        if r == min(1, last):
            xs[0] = ring.gather_end(xs[0])
    out_w = ring.out_end(out_weight, across)
    for r in rows:
        if r > 0:
            xs[r] = ring.gather_end(xs[r])
        got = project(me, xs[r], gain1, bias1, tables, qkv_weight)
        qkv[r], normed1[r], stat1[r] = got
        if r > 0:
            heads[r - 1] = ring.gather_end(heads[r - 1])
        if r == last:
            out_w = out_w()
        attended[r], logs[r] = attend(starts[r], qkv[r])
        heads[r] = ring.gather_start(attended[r])

    for r in rows:
        cots[r] = ring.gather_start(gate([cot_rows[r]])[0])
        if r == last:
            heads[r] = ring.gather_end(heads[r])
        if r > 0:
            cots[r - 1] = ring.gather_end(cots[r - 1])
        got = feed(
            me,
            heads[r],
            xs[r],
            out_w,
            wide[r],
            gain2,
            bias2,
            up_bias8,
            up_weight,
            down_weight,
            cots[r - 1] if r > 0 else (),
        )
        hidden[r], normed2[r], stat2[r], activated[r], slope[r], parts, joined = got
        branch[r] = ring.scatter_start(parts)
        if r > 0:
            cot_full[r - 1], sums = joined
            down_bias_sum += sums

    cots[last] = ring.gather_end(cots[last])
    for r in range(last):
        branch[r] = ring.scatter_end(branch[r])[0]
    if row_count == 1:
        cot_full[0], sums = beside(me, cots[0])
        down_bias_sum += sums

    def back(r, more=()):
        return feed_back(
            me, n, cot_full[r], slope[r], normed2[r], gain2, bias2, up_weight, down_weight, more
        )

    def take(r, got):
        nonlocal up_bias_sum
        up_grad[r], sums, up_sum, parts, joined = got
        up_bias_sum += up_sum
        parts2[r] = ring.scatter_start(parts, sums)
        return joined

    joined = take(0, back(0, cots[last] if row_count > 1 else ()))
    if row_count > 1:
        cot_full[last], sums = joined
        down_bias_sum += sums
    branch[last] = ring.scatter_end(branch[last])[0]
    if spread:
        down = Spread(activated, cot_full, 1, (1, 2, 4))
        down.first()
    parts2[0] = ring.scatter_end(parts2[0])
    for r in rows[1:]:
        take(r, back(r))

    def hidden_step(r):
        nonlocal gain2_sum, bias2_sum
        parts, sums = parts2[r]
        hidden_grad[r], low_grad, gain_part, bias_part = hidden_back(
            parts, cotangent, r, hidden[r], stat2[r], sums, own2, full
        )
        gain2_sum += gain_part
        bias2_sum += bias_part
        grads[r] = ring.gather_start(low_grad)

    hidden_step(0)
    if spread:
        up = [
            Spread(normed2, up_grad, 0, (1, 2, 4), (0, 2)),
            Spread(normed2, up_grad, 0, (2, 4, 1), (1, 2)),
        ]
        up[1].first()
    for r in rows[1:]:
        parts2[r] = ring.scatter_end(parts2[r])
    if spread:
        up[0].first()
        down.keep()
    grads[0] = ring.gather_end(grads[0])

    for r in rows:
        grad_full[r], attended_grad = attended_back(me, grads[r], out_weight)
        qkv_grad[r] = attend_back(starts[r], tables, qkv[r], attended_grad, logs[r])
        if r < last:
            hidden_step(r + 1)
        sums, parts = project_back(me, n, qkv_grad[r], normed1[r], gain1, bias1, qkv_weight)
        parts1[r] = ring.scatter_start(parts, sums)
        if spread and r == 0:
            up[1].keep_added()
            advance(down)
        if r < last:
            grads[r + 1] = ring.gather_end(grads[r + 1])
            parts1[r] = ring.scatter_end(parts1[r])

    if spread:
        qkv_sum = [
            Spread(normed1, qkv_grad, 0, (1, 2, 4), (0, 2)),
            Spread(normed1, qkv_grad, 0, (2, 4, 1), (1, 2)),
        ]
        out_sum = Spread(attended, grad_full, 1, (2, 4, 1))
        qkv_sum[0].first()
    parts1[last] = ring.scatter_end(parts1[last])
    if spread:
        qkv_sum[1].first()
        out_sum.first()
        up[0].keep_added()
        advance(down, up[1])
        out_sum.keep()
    made = output(branch, hidden, down_bias8)

    grad_history, depth_sum, gain1_sum, bias1_sum = None, 0.0, 0.0, 0.0
    for r in rows:
        parts, sums = parts1[r]
        grad_history, depth_part, gain_part, bias_part = average_back(
            depth_weights,
            parts,
            wide[r],
            stat1[r],
            sums,
            (own1, full),
            hidden_grad[r],
            history,
            r,
            grad_history,
        )
        depth_sum += depth_part
        gain1_sum += gain_part
        bias1_sum += bias_part
        if r == 0 and spread:
            qkv_sum[0].keep_added()
            qkv_sum[1].keep_added()
            advance(up[0], out_sum)

    if spread:
        advance(qkv_sum[0], qkv_sum[1], out_sum)
        down_total, up_total, out_total, qkv_total = finish([down], up, [out_sum], qkv_sum)
    else:
        down_total, up_total, out_total, qkv_total = (
            lax.psum_scatter(
                weight_grad(*pair), "dp", scatter_dimension=dim, tiled=True
            ).astype(F32)
            for pair, dim in (
                ((activated, cot_full), 1),
                ((normed2, up_grad), 0),
                ((attended, grad_full), 1),
                ((normed1, qkv_grad), 0),
            )
        )

    sums = [up_bias_sum, down_bias_sum, gain2_sum, bias2_sum, gain1_sum, bias1_sum]
    depth_part = ring.total(jnp.sum(depth_sum, (1, 2)))
    sums = dp_total([jnp.sum(v, 0) for v in sums] + [depth_part])
    return (
        made,
        grad_history,
        sums[6],
        sums[4],
        sums[5],
        qkv_total,
        out_total,
        sums[2],
        sums[3],
        up_total,
        sums[0],
        down_total,
        sums[1],
    )


def solution(mesh):
    placed = (
        P(None, "dp", "mp"),
        P(),
        P("dp", None),
        P("mp"),
        P("mp"),
        P(None, "mp"),
        P("mp", None),
        P("mp"),
        P("mp"),
        P(None, "mp"),
        P("mp"),
        P("mp", None),
        P("mp"),
        P("dp", "mp"),
    )
    return jax.shard_map(
        local,
        mesh=mesh,
        in_specs=placed,
        out_specs=(
            P("dp", "mp"),
            P(None, "dp", "mp"),
            P(),
            P("mp"),
            P("mp"),
            P("dp", "mp"),
            P("mp", "dp"),
            P("mp"),
            P("mp"),
            P("dp", "mp"),
            P("mp"),
            P("mp", "dp"),
            P("mp"),
        ),
        check_vma=False,
    )
```

time: 970 us -> 821 us (0.85)
  Pallas kernels: 558 us -> 482 us
  waiting for transfers between devices: 294 us -> 223 us
    ppermute x21, waiting for transfers between devices: 168 us -> 44.2 us  [over_chip(): return lax.ppermute(value, 'mp', self.chip)]
    pallas_call x63 -> x57, Pallas kernels: 558 us -> 482 us  [call(): pl.pallas_call(without_extra, grid_spec=pltpu.PrefetchScalarGridSpec(num_...]
    ppermute x6 -> x3, waiting for transfers between devices: 55 us -> 94.8 us  [dp_total(): lax.ppermute(packed, 'dp', [(i, i ^ bit) for i in range(groups)])]
    all_gather x1, waiting for transfers between devices: 2.97 us -> 21.1 us  [out_middle(): lax.all_gather(gate([piece])[0], 'dp', axis=0, tiled=True)]
    ppermute x18, waiting for transfers between devices: 64.1 us -> 52.1 us  [send(): lax.ppermute(value, 'dp', [(i, i ^ bit) for i in range(self.groups)])]
    unnamed x121 -> x152, local copies, waits for them, and re-layouts: 17.9 us -> 23.3 us
  transfers between devices with their start and end apart: 83 -> 80, of which waited for: 20 -> 21; matrix products, arithmetic and copies ran while one was open for 2% -> 2% of each run, Pallas kernels for 53% -> 58%
where the time goes in v3:
time: 821 us; the launch traced here: 817 us
  Pallas kernels  482 us (59%)
  waiting for transfers between devices  223 us (27%)
  starting transfers between devices  59.8 us (7%)
  local copies, waits for them, and re-layouts  33.4 us (4%)
  between operations  15.1 us (2%)
    pallas_call x57, Pallas kernels, call(): pl.pallas_call(without_extra, grid_spec=pltpu.PrefetchScalarGridSpec(num_...  482 us
    ppermute x3, waiting for transfers between devices, dp_total(): lax.ppermute(packed, 'dp', [(i, i ^ bit) for i in range(groups)])  94.8 us
    ppermute x18, waiting for transfers between devices, send(): lax.ppermute(value, 'dp', [(i, i ^ bit) for i in range(self.groups)])  52.1 us
    ppermute x21, waiting for transfers between devices, over_chip(): return lax.ppermute(value, 'mp', self.chip)  44.2 us
    ppermute x21, starting transfers between devices, over_chip(): return lax.ppermute(value, 'mp', self.chip)  24.4 us
    unnamed x152, local copies, waits for them, and re-layouts  23.3 us
    ppermute x18, starting transfers between devices, send(): lax.ppermute(value, 'dp', [(i, i ^ bit) for i in range(self.groups)])  22.7 us
    all_gather x1, waiting for transfers between devices, out_middle(): lax.all_gather(gate([piece])[0], 'dp', axis=0, tiled=True)  21.1 us
  transfers between devices with their start and end apart: 80, of which 21 were waited for; matrix products, arithmetic and copies ran while one was open for 2% of the time, Pallas kernels for 58%

profile of v3, /device:TPU:0, one launch (start us, length us, event | category | flops | bytes accessed | tf_op | source)
XLA Modules:
  0.0 816.8 jit_solution(6996238503693288808)
XLA Ops:
  11.2 7.8 average.2
  19.0 7.8 average.3
  29.9 24.1 %collective-permute-done.5 = f32[32,512]{1,0:T(8,128)S(1)} collective-permute-done((f32[32,512]{1,0:T(8,128)S(1)}, f32[32,512]{1,0:T(8,128)S(1)}, u32[]{:S(2)}, u32[]{:S(2)}) %collective-permute-start.5) | collective-permute-done | bytes 65568 | tf_op jit(solution)/shard_map/ppermute | solution.py:977
  56.3 21.1 %all-gather.2.cloned.1.call-done.refs_11_ = bf16[512,2048]{1,0:T(8,128)(2,1)} async-done(((bf16[64,2048]{1,0:T(8,128)(2,1)}), bf16[512,2048]{1,0:T(8,128)(2,1)}) %all-gather.2.cloned.1.call-update) | async-done | bytes 2097168 | tf_op jit(solution)/shard_map/all_gather | solution.py:1028
  80.3 17.1 %project.2 = (bf16[1024,1536]{1,0:T(8,128)(2,1)}, bf16[1024,2048]{1,0:T(8,128)(2,1)}, f32[1024,128]{1,0:T(8,128)}) custom-call(s32[1]{0:T(128)} %bitcast.refs_0_, bf16[1024,512]{1,0:T(8,128)(2,1)} %get-tuple-element.159.refs_1_.refs_5_, bf16[1024,512]{1,0:T(8,128)(2,1)} %copy-done.8, bf16[1024,512]{1,0:T(8,128)(2,1)} %get-tuple-element.160.refs_3_.refs_7_, ...), custom_call_target="tpu_custom_call" | custom-call | flops 1 | bytes 1 | tf_op jit(solution)/shard_map/project/pallas_call | solution.py:50
  98.0 9.7 %attend.2 = (bf16[1024,512]{1,0:T(8,128)(2,1)}, f32[4,8,1024]{2,1,0:T(8,128)}) custom-call(s32[8,1024]{1,0:T(8,128)} %broadcast_in_dim.20.refs_0_, bf16[1024,1536]{1,0:T(8,128)(2,1)} %get-tuple-element.161.refs_1_.refs_3_, f32[1024,128]{1,0:T(8,128)} %get-tuple-element.162.refs_2_.refs_6_), custom_call_target="tpu_custom_call" | custom-call | flops 1 | bytes 1 | tf_op jit(solution)/shard_map/attend/pallas_call | solution.py:50
  114.4 17.4 %project.3 = (bf16[1024,1536]{1,0:T(8,128)(2,1)}, bf16[1024,2048]{1,0:T(8,128)(2,1)}, f32[1024,128]{1,0:T(8,128)}) custom-call(s32[1]{0:T(128)} %bitcast.refs_0_, bf16[1024,512]{1,0:T(8,128)(2,1)} %get-tuple-element.165.refs_1_.refs_5_, bf16[1024,512]{1,0:T(8,128)(2,1)} %collective-permute-done.9.refs_2_.refs_6_, ...), custom_call_target="tpu_custom_call" | custom-call | flops 1 | bytes 1 | tf_op jit(solution)/shard_map/project/pallas_call | solution.py:50
  135.7 9.7 %attend.3 = (bf16[1024,512]{1,0:T(8,128)(2,1)}, f32[4,8,1024]{2,1,0:T(8,128)}) custom-call(s32[8,1024]{1,0:T(8,128)} %broadcast_in_dim.24.refs_0_, bf16[1024,1536]{1,0:T(8,128)(2,1)} %get-tuple-element.172.refs_1_.refs_3_, bf16[512,2048]{1,0:T(8,128)(2,1)} %get-tuple-element.170.refs_2_.refs_10_), custom_call_target="tpu_custom_call" | custom-call | flops 1 | bytes 1 | tf_op jit(solution)/shard_map/attend/pallas_call | solution.py:50
  148.1 38.5 %feed.2 = (f32[1024,512]{1,0:T(8,128)}, bf16[1024,2048]{1,0:T(8,128)(2,1)}, f32[1024,128]{1,0:T(8,128)}, bf16[1024,2048]{1,0:T(8,128)(2,1)}, bf16[1024,2048]{1,0...) custom-call(s32[1]{0:T(128)} %bitcast.refs_0_, ...), custom_call_target="tpu_custom_call" | custom-call | flops 1 | bytes 1 | tf_op jit(solution)/shard_map/feed/pallas_call | solution.py:50
  197.1 4.4 collective-permute-done.23.refs_22_
  203.4 40.0 %feed.3 = (f32[1024,512]{1,0:T(8,128)}, bf16[1024,2048]{1,0:T(8,128)(2,1)}, f32[1024,128]{1,0:T(8,128)}, bf16[1024,2048]{1,0:T(8,128)(2,1)}, bf16[1024,2048]{1,0...) custom-call(s32[1]{0:T(128)} %bitcast.refs_0_, ...), custom_call_target="tpu_custom_call" | custom-call | flops 1 | bytes 1 | tf_op jit(solution)/shard_map/feed/pallas_call | solution.py:50
  251.2 28.9 %feed_back.2 = (bf16[1024,2048]{1,0:T(8,128)(2,1)}, f32[8,1024]{1,0:T(8,128)}, f32[8,2048]{1,0:T(8,128)}, bf16[1024,512]{1,0:T(8,128)(2,1)}, bf16[1024,512]{1,0:...) custom-call(s32[1]{0:T(128)} %bitcast.refs_0_, ...), custom_call_target="tpu_custom_call" | custom-call | flops 1 | bytes 1 | tf_op jit(solution)/shard_map/feed_back/pallas_call | solution.py:50
  285.2 13.5 %weight_blocks.12.refs_6_ = bf16[4,2048,256]{2,1,0:T(8,128)(2,1)} custom-call(s32[1]{0:T(128)} %bitcast.8.refs_0_, bf16[1024,2048]{1,0:T(8,128)(2,1)} %get-tuple-element.206.refs_1_, bf16[1024,2048]{1,0:T(8,128)(2,1)} %get-tuple-element.207.refs_2_, bf16[1024,2048]{1,0:T(8,128)(2,1)} %get-tuple-element.194.refs_1_.refs_3_.refs_5_.refs_7_.refs_9_, ...), custom_call_target="tpu_custom_call" | custom-call | flops 1 | bytes 1 | tf_op jit(solution)/shard_map/weight_blocks/pallas_call | solution.py:50
  306.1 27.9 %feed_back.3 = (bf16[1024,2048]{1,0:T(8,128)(2,1)}, f32[8,1024]{1,0:T(8,128)}, f32[8,2048]{1,0:T(8,128)}, bf16[1024,512]{1,0:T(8,128)(2,1)}, bf16[1024,512]{1,0:...) custom-call(s32[1]{0:T(128)} %bitcast.refs_0_, ...), custom_call_target="tpu_custom_call" | custom-call | flops 1 | bytes 1 | tf_op jit(solution)/shard_map/feed_back/pallas_call | solution.py:50
  335.5 5.8 hidden_back.2
  342.8 9.9 %weight_blocks.13.refs_6_ = bf16[4,256,1024]{2,1,0:T(8,128)(2,1)} custom-call(s32[1]{0:T(128)} %bitcast.8.refs_0_, bf16[1024,2048]{1,0:T(8,128)(2,1)} %get-tuple-element.196.refs_3_.refs_1_.refs_5_.refs_7_, bf16[1024,2048]{1,0:T(8,128)(2,1)} %get-tuple-element.213.refs_3_.refs_2_.refs_4_.refs_6_.refs_8_, ...), custom_call_target="tpu_custom_call" | custom-call | flops 1 | bytes 1 | tf_op jit(solution)/shard_map/weight_blocks/pallas_call | solution.py:50
  357.5 10.3 %weight_blocks.14.refs_11_ = bf16[4,256,1024]{2,1,0:T(8,128)(2,1)} custom-call(s32[1]{0:T(128)} %bitcast.8.refs_0_, bf16[1024,2048]{1,0:T(8,128)(2,1)} %get-tuple-element.196.refs_3_.refs_1_.refs_5_.refs_7_, bf16[1024,2048]{1,0:T(8,128)(2,1)} %get-tuple-element.213.refs_3_.refs_2_.refs_4_.refs_6_.refs_8_, ...), custom_call_target="tpu_custom_call" | custom-call | flops 1 | bytes 1 | tf_op jit(solution)/shard_map/weight_blocks/pallas_call | solution.py:50
  367.8 13.5 %weight_blocks.15.refs_2_.refs_0_ = bf16[4,2048,256]{2,1,0:T(8,128)(2,1)} custom-call(s32[1]{0:T(128)} %bitcast.8.refs_0_, bf16[1024,2048]{1,0:T(8,128)(2,1)} %get-tuple-element.206.refs_1_, bf16[1024,2048]{1,0:T(8,128)(2,1)} %get-tuple-element.207.refs_2_, bf16[1024,2048]{1,0:T(8,128)(2,1)} %get-tuple-element.194.refs_1_.refs_3_.refs_5_.refs_7_.refs_9_, ...), custom_call_target="tpu_custom_call" | custom-call | flops 1 | bytes 1 | tf_op jit(solution)/shard_map/weight_blocks/pallas_call | solution.py:50
  386.9 6.8 attended_back.2
  393.7 12.4 %attend_back.2.refs_8_.refs_1_.refs_9_ = bf16[1024,1536]{1,0:T(8,128)(2,1)} custom-call(s32[8,1024]{1,0:T(8,128)} %broadcast_in_dim.20.refs_0_, f32[1024,128]{1,0:T(8,128)} %constant.22.clone.refs_7_.refs_1_, f32[1024,128]{1,0:T(8,128)} %constant.23.clone.refs_8_.refs_2_, bf16[1024,1536]{1,0:T(8,128)(2,1)} %get-tuple-element.161.refs_1_.refs_3_, ...), custom_call_target="tpu_custom_call" | custom-call | flops 1 | bytes 1 | tf_op jit(solution)/shard_map/attend_back/pallas_call | solution.py:50
  406.1 4.8 collective-permute-done.42.refs_3_
  411.8 5.7 hidden_back.3
  418.2 13.0 %project_back.2 = (f32[8,1024]{1,0:T(8,128)}, bf16[1024,512]{1,0:T(8,128)(2,1)}, bf16[1024,512]{1,0:T(8,128)(2,1)}, bf16[1024,512]{1,0:T(8,128)(2,1)}, bf16[1024,512]{1,0:T(8,128)(2,1)}) custom-call(s32[1]{0:T(128)} %bitcast.refs_0_, bf16[1024,1536]{1,0:T(8,128)(2,1)} %attend_back.2.refs_8_.refs_1_.refs_9_, ...), custom_call_target="tpu_custom_call" | custom-call | flops 1 | bytes 1 | tf_op jit(solution)/shard_map/project_back/pallas_call | solution.py:50
  431.7 10.5 %weight_blocks.16 = (bf16[2,256,1024]{2,1,0:T(8,128)(2,1)}, bf16[2,256,1024]{2,1,0:T(8,128)(2,1)}) custom-call(s32[1]{0:T(128)} %bitcast.8.refs_0_, bf16[1024,2048]{1,0:T(8,128)(2,1)} %get-tuple-element.196.refs_3_.refs_1_.refs_5_.refs_7_, bf16[1024,2048]{1,0:T(8,128)(2,1)} %get-tuple-element.213.refs_3_.refs_2_.refs_4_.refs_6_.refs_8_, ...), custom_call_target="tpu_custom_call" | custom-call | flops 1 | bytes 1 | tf_op jit(solution)/shard_map/weight_blocks/pallas_call | solution.py:50
  442.2 6.0 fold.4
  460.8 6.8 attended_back.3
  467.6 12.4 %attend_back.3.refs_1_.refs_10_ = bf16[1024,1536]{1,0:T(8,128)(2,1)} custom-call(s32[8,1024]{1,0:T(8,128)} %broadcast_in_dim.24.refs_0_, f32[1024,128]{1,0:T(8,128)} %constant.22.clone.refs_7_.refs_1_, f32[1024,128]{1,0:T(8,128)} %constant.23.clone.refs_8_.refs_2_, bf16[1024,1536]{1,0:T(8,128)(2,1)} %get-tuple-element.172.refs_1_.refs_3_, ...), custom_call_target="tpu_custom_call" | custom-call | flops 1 | bytes 1 | tf_op jit(solution)/shard_map/attend_back/pallas_call | solution.py:50
  480.0 12.9 %project_back.3 = (f32[8,1024]{1,0:T(8,128)}, bf16[1024,512]{1,0:T(8,128)(2,1)}, bf16[1024,512]{1,0:T(8,128)(2,1)}, bf16[1024,512]{1,0:T(8,128)(2,1)}, bf16[1024,512]{1,0:T(8,128)(2,1)}) custom-call(s32[1]{0:T(128)} %bitcast.refs_0_, bf16[1024,1536]{1,0:T(8,128)(2,1)} %attend_back.3.refs_1_.refs_10_, ...), custom_call_target="tpu_custom_call" | custom-call | flops 1 | bytes 1 | tf_op jit(solution)/shard_map/project_back/pallas_call | solution.py:50
  493.5 7.1 collective-permute-done.29.refs_5_
  504.4 9.8 %weight_blocks.17.refs_6_ = bf16[4,256,768]{2,1,0:T(8,128)(2,1)} custom-call(s32[1]{0:T(128)} %bitcast.8.refs_0_, bf16[1024,2048]{1,0:T(8,128)(2,1)} %get-tuple-element.232.refs_2_.refs_1_.refs_3_.refs_5_.refs_7_, bf16[1024,2048]{1,0:T(8,128)(2,1)} %get-tuple-element.247.refs_2_.refs_4_.refs_6_.refs_8_, ...), custom_call_target="tpu_custom_call" | custom-call | flops 1 | bytes 1 | tf_op jit(solution)/shard_map/weight_blocks/pallas_call | solution.py:50
  519.1 9.8 %weight_blocks.18.refs_11_ = bf16[4,256,768]{2,1,0:T(8,128)(2,1)} custom-call(s32[1]{0:T(128)} %bitcast.8.refs_0_, bf16[1024,2048]{1,0:T(8,128)(2,1)} %get-tuple-element.232.refs_2_.refs_1_.refs_3_.refs_5_.refs_7_, bf16[1024,2048]{1,0:T(8,128)(2,1)} %get-tuple-element.247.refs_2_.refs_4_.refs_6_.refs_8_, ...), custom_call_target="tpu_custom_call" | custom-call | flops 1 | bytes 1 | tf_op jit(solution)/shard_map/weight_blocks/pallas_call | solution.py:50
  530.7 20.3 %collective-permute-done.52.refs_3_ = bf16[2,256,1024]{2,1,0:T(8,128)(2,1)} collective-permute-done((bf16[2,256,1024]{2,1,0:T(8,128)(2,1)}, bf16[2,256,1024]{2,1,0:T(8,128)(2,1)}, u32[]{:S(2)}, u32[]{:S(2)}) %collective-permute-start.52) | collective-permute-done | bytes 1048608 | tf_op jit(solution)/shard_map/ppermute | solution.py:847
  552.5 6.2 weight_blocks.19.refs_12_
  558.8 10.4 %weight_blocks.20 = (bf16[2,256,1024]{2,1,0:T(8,128)(2,1)}, bf16[2,256,1024]{2,1,0:T(8,128)(2,1)}) custom-call(s32[1]{0:T(128)} %bitcast.8.refs_0_, bf16[1024,2048]{1,0:T(8,128)(2,1)} %get-tuple-element.196.refs_3_.refs_1_.refs_5_.refs_7_, bf16[1024,2048]{1,0:T(8,128)(2,1)} %get-tuple-element.213.refs_3_.refs_2_.refs_4_.refs_6_.refs_8_, ...), custom_call_target="tpu_custom_call" | custom-call | flops 1 | bytes 1 | tf_op jit(solution)/shard_map/weight_blocks/pallas_call | solution.py:50
  573.6 5.3 fold.5
  578.9 6.2 weight_blocks.21.refs_7_.refs_2_
  585.7 6.3 output.1.refs_10_
  592.6 14.5 %average_back.2 = (bf16[13,2048,512]{2,1,0:T(8,128)(2,1)}, f32[13,8,128]{2,1,0:T(8,128)}, f32[8,512]{1,0:T(8,128)}, f32[8,512]{1,0:T(8,128)}) custom-call(f32[13]{0:T(128)} %refs_0_.7, bf16[1024,512]{1,0:T(8,128)(2,1)} %get-tuple-element.260.refs_1_, bf16[1024,512]{1,0:T(8,128)(2,1)} %collective-permute-done.59.refs_2_, ...), custom_call_target="tpu_custom_call" | custom-call | flops 1 | bytes 1 | tf_op jit(solution)/shard_map/average_back/pallas_call | solution.py:50
  607.1 10.0 %weight_blocks.22 = (bf16[2,256,768]{2,1,0:T(8,128)(2,1)}, bf16[2,256,768]{2,1,0:T(8,128)(2,1)}) custom-call(s32[1]{0:T(128)} %bitcast.8.refs_0_, bf16[1024,2048]{1,0:T(8,128)(2,1)} %get-tuple-element.232.refs_2_.refs_1_.refs_3_.refs_5_.refs_7_, bf16[1024,2048]{1,0:T(8,128)(2,1)} %get-tuple-element.247.refs_2_.refs_4_.refs_6_.refs_8_, ...), custom_call_target="tpu_custom_call" | custom-call | flops 1 | bytes 1 | tf_op jit(solution)/shard_map/weight_blocks/pallas_call | solution.py:50
  617.3 10.3 %weight_blocks.23 = (bf16[2,256,768]{2,1,0:T(8,128)(2,1)}, bf16[2,256,768]{2,1,0:T(8,128)(2,1)}) custom-call(s32[1]{0:T(128)} %bitcast.8.refs_0_, bf16[1024,2048]{1,0:T(8,128)(2,1)} %get-tuple-element.232.refs_2_.refs_1_.refs_3_.refs_5_.refs_7_, bf16[1024,2048]{1,0:T(8,128)(2,1)} %get-tuple-element.247.refs_2_.refs_4_.refs_6_.refs_8_, ...), custom_call_target="tpu_custom_call" | custom-call | flops 1 | bytes 1 | tf_op jit(solution)/shard_map/weight_blocks/pallas_call | solution.py:50
  629.7 4.1 fold.6
  634.8 14.8 %average_back.3 = (bf16[13,2048,512]{2,1,0:T(8,128)(2,1)}, f32[13,8,128]{2,1,0:T(8,128)}, f32[8,512]{1,0:T(8,128)}, f32[8,512]{1,0:T(8,128)}) custom-call(f32[13]{0:T(128)} %refs_0_.7, bf16[1024,512]{1,0:T(8,128)(2,1)} %get-tuple-element.257.refs_1_, bf16[1024,512]{1,0:T(8,128)(2,1)} %copy-done.17, ...), custom_call_target="tpu_custom_call", output_to_operand_aliasing={{0}: (10, {})} | custom-call | flops 1 | bytes 1 | tf_op jit(solution)/shard_map/average_back/pallas_call | solution.py:50
  662.4 36.0 %collective-permute-done.68 = f32[40,128]{1,0:T(8,128)S(1)} collective-permute-done((f32[40,128]{1,0:T(8,128)S(1)}, f32[40,128]{1,0:T(8,128)S(1)}, u32[]{:S(2)}, u32[]{:S(2)}) %collective-permute-start.68) | collective-permute-done | bytes 20512 | tf_op jit(solution)/shard_map/ppermute | solution.py:1049
  701.9 58.8 %collective-permute-done.69 = f32[40,128]{1,0:T(8,128)S(1)} collective-permute-done((f32[40,128]{1,0:T(8,128)S(1)}, f32[40,128]{1,0:T(8,128)S(1)}, u32[]{:S(2)}, u32[]{:S(2)}) %collective-permute-start.69) | collective-permute-done | bytes 20512 | tf_op jit(solution)/shard_map/ppermute | solution.py:1049
  762.4 4.3 fold.7
  773.4 21.3 %collective-permute-done.71.refs_3_ = bf16[1,256,1024]{2,1,0:T(8,128)(2,1)S(1)} collective-permute-done((bf16[1,256,1024]{2,1,0:T(8,128)(2,1)}, bf16[1,256,1024]{2,1,0:T(8,128)(2,1)S(1)}, u32[]{:S(2)}, u32[]{:S(2)}) %collective-permute-start.71) | collective-permute-done | bytes 524320 | tf_op jit(solution)/shard_map/ppermute | solution.py:847
  794.7 8.3 %collective-permute-done.77.refs_9_ = bf16[1,256,768]{2,1,0:T(8,128)(2,1)S(1)} collective-permute-done((bf16[1,256,768]{2,1,0:T(8,128)(2,1)}, bf16[1,256,768]{2,1,0:T(8,128)(2,1)S(1)}, u32[]{:S(2)}, u32[]{:S(2)}) %collective-permute-start.77) | collective-permute-done | bytes 393248 | tf_op jit(solution)/shard_map/ppermute | solution.py:847
  803.9 5.8 finish.1
  (351 shorter events, 133.4 us)
Async XLA Ops:
  7.2 70.2 %all-gather.2.cloned.1.call-start = ((), (), s32[]{:S(2)}) async-start(), calls=%async_computation | async-start | bytes 2359296 | tf_op jit(solution)/shard_map/all_gather | solution.py:1028
  27.6 26.8 %collective-permute-start = (bf16[1024,512]{1,0:T(8,128)(2,1)}, bf16[1024,512]{1,0:T(8,128)(2,1)S(1)}, u32[]{:S(2)}, u32[]{:S(2)}) collective-permute-start(bf16[1024,512]{1,0:T(8,128)(2,1)} %get-tuple-element.155.refs_0_), channel_id=1, source_target_pairs={{0,2},{1,3},{2,0},{3,1},{4,6},{5,7},{6,4},{7,5},{8,10},{9,11},{10,... | collective-permute-start | bytes 3145736 | tf_op jit(solution)/shard_map/ppermute | solution.py:977
  27.8 26.1 %collective-permute-start.5 = (f32[32,512]{1,0:T(8,128)S(1)}, f32[32,512]{1,0:T(8,128)S(1)}, u32[]{:S(2)}, u32[]{:S(2)}) collective-permute-start(f32[32,512]{1,0:T(8,128)S(1)} %broadcast_bitcast_fusion), channel_id=1, source_target_pairs={{0,2},{1,3},{2,0},{3,1},{4,6},{5,7},{6,4},{7,5},{8,10},{9,11},{10,... | collective-permute-start | bytes 196616 | tf_op jit(solution)/shard_map/ppermute | solution.py:977
  29.9 25.9 %collective-permute-start.4 = (f32[32,512]{1,0:T(8,128)S(1)}, f32[32,512]{1,0:T(8,128)S(1)}, u32[]{:S(2)}, u32[]{:S(2)}) collective-permute-start(f32[32,512]{1,0:T(8,128)S(1)} %broadcast_bitcast_fusion), channel_id=1, source_target_pairs={{0,1},{1,0},{2,3},{3,2},{4,5},{5,4},{6,7},{7,6},{8,9},{9,8},{10,11... | collective-permute-start | bytes 196616 | tf_op jit(solution)/shard_map/ppermute | solution.py:974
  54.0 81.1 %collective-permute-start.13 = (bf16[512,2048]{1,0:T(8,128)(2,1)S(1)}, bf16[512,2048]{1,0:T(8,128)(2,1)}, u32[]{:S(2)}, u32[]{:S(2)}) collective-permute-start(bf16[512,2048]{1,0:T(8,128)(2,1)S(1)} %copy-done.1), channel_id=1, source_target_pairs={{0,1},{1,0},{2,3},{3,2},{4,5},{5,4},{6,7},{7,6},{8,9},{9,8},{10,11... | collective-permute-start | bytes 6291464 | tf_op jit(solution)/shard_map/ppermute | solution.py:974
  55.4 52.3 %collective-permute-start.8 = (bf16[1024,512]{1,0:T(8,128)(2,1)}, bf16[1024,512]{1,0:T(8,128)(2,1)}, u32[]{:S(2)}, u32[]{:S(2)}) collective-permute-start(bf16[1024,512]{1,0:T(8,128)(2,1)} %gate.14.refs_2_.refs_0_), channel_id=1, source_target_pairs={{0,2},{1,3},{2,0},{3,1},{4,6},{5,7},{6,4},{7,5},{8,10},{9,11},{10,... | collective-permute-start | bytes 3145736 | tf_op jit(solution)/shard_map/ppermute | solution.py:977
  55.8 23.6 %collective-permute-start.2 = (bf16[1024,512]{1,0:T(8,128)(2,1)}, bf16[1024,512]{1,0:T(8,128)(2,1)S(1)}, u32[]{:S(2)}, u32[]{:S(2)}) collective-permute-start(bf16[1024,512]{1,0:T(8,128)(2,1)} %get-tuple-element.159.refs_1_.refs_5_), channel_id=1, source_target_pairs={{0,1},{1,0},{2,3},{3,2},{4,5},{5,4},{6,7},{7,6},{8,9},{9,8},{10,11... | collective-permute-start | bytes 3145736 | tf_op jit(solution)/shard_map/ppermute | solution.py:974
  77.4 57.7 %collective-permute-start.14 = (bf16[512,2048]{1,0:T(8,128)(2,1)}, bf16[512,2048]{1,0:T(8,128)(2,1)}, u32[]{:S(2)}, u32[]{:S(2)}) collective-permute-start(bf16[512,2048]{1,0:T(8,128)(2,1)} %all-gather.2.cloned.1.call-done.refs_11_), channel_id=1, source_target_pairs={{0,1},{1,0},{2,3},{3,2},{4,5},{5,4},{6,7},{7,6},{8,9},{9,8},{10,11... | collective-permute-start | bytes 6291464 | tf_op jit(solution)/shard_map/ppermute | solution.py:974
  108.9 25.6 %collective-permute-start.7 = (bf16[1024,512]{1,0:T(8,128)(2,1)S(1)}, bf16[1024,512]{1,0:T(8,128)(2,1)}, u32[]{:S(2)}, u32[]{:S(2)}) collective-permute-start(bf16[1024,512]{1,0:T(8,128)(2,1)S(1)} %copy-done.4), channel_id=1, source_target_pairs={{0,2},{1,3},{2,0},{3,1},{4,6},{5,7},{6,4},{7,5},{8,10},{9,11},{10,... | collective-permute-start | bytes 3145736 | tf_op jit(solution)/shard_map/ppermute | solution.py:977
  145.4 43.4 %collective-permute-start.18 = (bf16[1024,512]{1,0:T(8,128)(2,1)}, bf16[1024,512]{1,0:T(8,128)(2,1)S(1)}, u32[]{:S(2)}, u32[]{:S(2)}) collective-permute-start(bf16[1024,512]{1,0:T(8,128)(2,1)} %get-tuple-element.180.refs_2_), channel_id=1, source_target_pairs={{0,2},{1,3},{2,0},{3,1},{4,6},{5,7},{6,4},{7,5},{8,10},{9,11},{10,... | collective-permute-start | bytes 3145736 | tf_op jit(solution)/shard_map/ppermute | solution.py:977
  146.9 46.3 %collective-permute-start.21 = (bf16[1024,512]{1,0:T(8,128)(2,1)}, bf16[1024,512]{1,0:T(8,128)(2,1)S(1)}, u32[]{:S(2)}, u32[]{:S(2)}) collective-permute-start(bf16[1024,512]{1,0:T(8,128)(2,1)} %gate.19.refs_19_.refs_0_), channel_id=1, source_target_pairs={{0,2},{1,3},{2,0},{3,1},{4,6},{5,7},{6,4},{7,5},{8,10},{9,11},{10,... | collective-permute-start | bytes 3145736 | tf_op jit(solution)/shard_map/ppermute | solution.py:977
  195.2 48.3 %collective-permute-start.17 = (bf16[1024,512]{1,0:T(8,128)(2,1)S(1)}, bf16[1024,512]{1,0:T(8,128)(2,1)S(1)}, u32[]{:S(2)}, u32[]{:S(2)}) collective-permute-start(bf16[1024,512]{1,0:T(8,128)(2,1)S(1)} %copy-done), channel_id=1, source_target_pairs={{0,2},{1,3},{2,0},{3,1},{4,6},{5,7},{6,4},{7,5},{8,10},{9,11},{10,... | collective-permute-start | bytes 3145736 | tf_op jit(solution)/shard_map/ppermute | solution.py:977
  197.0 48.0 %collective-permute-start.15 = (bf16[1024,512]{1,0:T(8,128)(2,1)}, bf16[1024,512]{1,0:T(8,128)(2,1)}, u32[]{:S(2)}, u32[]{:S(2)}) collective-permute-start(bf16[1024,512]{1,0:T(8,128)(2,1)} %get-tuple-element.177), channel_id=1, source_target_pairs={{0,1},{1,0},{2,3},{3,2},{4,5},{5,4},{6,7},{7,6},{8,9},{9,8},{10,11... | collective-permute-start | bytes 3145736 | tf_op jit(solution)/shard_map/ppermute | solution.py:974
  201.5 43.9 %collective-permute-start.16 = (bf16[1024,512]{1,0:T(8,128)(2,1)}, bf16[1024,512]{1,0:T(8,128)(2,1)}, u32[]{:S(2)}, u32[]{:S(2)}) collective-permute-start(bf16[1024,512]{1,0:T(8,128)(2,1)} %get-tuple-element.178), channel_id=1, source_target_pairs={{0,1},{1,0},{2,3},{3,2},{4,5},{5,4},{6,7},{7,6},{8,9},{9,8},{10,11... | collective-permute-start | bytes 3145736 | tf_op jit(solution)/shard_map/ppermute | solution.py:974
  244.9 36.0 %collective-permute-start.25 = (bf16[1024,512]{1,0:T(8,128)(2,1)}, bf16[1024,512]{1,0:T(8,128)(2,1)S(1)}, u32[]{:S(2)}, u32[]{:S(2)}) collective-permute-start(bf16[1024,512]{1,0:T(8,128)(2,1)} %get-tuple-element.192), channel_id=1, source_target_pairs={{0,1},{1,0},{2,3},{3,2},{4,5},{5,4},{6,7},{7,6},{8,9},{9,8},{10,11... | collective-permute-start | bytes 3145736 | tf_op jit(solution)/shard_map/ppermute | solution.py:974
  245.0 35.9 %collective-permute-start.26 = (bf16[1024,512]{1,0:T(8,128)(2,1)}, bf16[1024,512]{1,0:T(8,128)(2,1)}, u32[]{:S(2)}, u32[]{:S(2)}) collective-permute-start(bf16[1024,512]{1,0:T(8,128)(2,1)} %get-tuple-element.193), channel_id=1, source_target_pairs={{0,1},{1,0},{2,3},{3,2},{4,5},{5,4},{6,7},{7,6},{8,9},{9,8},{10,11... | collective-permute-start | bytes 3145736 | tf_op jit(solution)/shard_map/ppermute | solution.py:974
  303.5 31.0 %collective-permute-start.33 = (bf16[1024,512]{1,0:T(8,128)(2,1)}, bf16[1024,512]{1,0:T(8,128)(2,1)S(1)}, u32[]{:S(2)}, u32[]{:S(2)}) collective-permute-start(bf16[1024,512]{1,0:T(8,128)(2,1)} %get-tuple-element.210), channel_id=1, source_target_pairs={{0,2},{1,3},{2,0},{3,1},{4,6},{5,7},{6,4},{7,5},{8,10},{9,11},{10,... | collective-permute-start | bytes 3145736 | tf_op jit(solution)/shard_map/ppermute | solution.py:977
  304.9 137.2 %collective-permute-start.44 = (bf16[4,2048,256]{2,1,0:T(8,128)(2,1)}, bf16[4,2048,256]{2,1,0:T(8,128)(2,1)}, u32[]{:S(2)}, u32[]{:S(2)}) collective-permute-start(bf16[4,2048,256]{2,1,0:T(8,128)(2,1)} %weight_blocks.12.refs_6_), channel_id=1, source_target_pairs={{0,4},{4,0},{8,12},{12,8},{16,20},{20,16},{24,28},{28,24},{1,5},{5... | collective-permute-start | bytes 12582920 | tf_op jit(solution)/shard_map/ppermute | solution.py:847
  305.5 29.0 %collective-permute-start.34 = (f32[8,1024]{1,0:T(8,128)}, f32[8,1024]{1,0:T(8,128)S(1)}, u32[]{:S(2)}, u32[]{:S(2)}) collective-permute-start(f32[8,1024]{1,0:T(8,128)} %get-tuple-element.211.refs_8_.refs_2_), channel_id=1, source_target_pairs={{0,2},{1,3},{2,0},{3,1},{4,6},{5,7},{6,4},{7,5},{8,10},{9,11},{10,... | collective-permute-start | bytes 98312 | tf_op jit(solution)/shard_map/ppermute | solution.py:977
  341.3 40.0 %collective-permute-start.35 = (bf16[1024,512]{1,0:T(8,128)(2,1)}, bf16[1024,512]{1,0:T(8,128)(2,1)S(1)}, u32[]{:S(2)}, u32[]{:S(2)}) collective-permute-start(bf16[1024,512]{1,0:T(8,128)(2,1)} %get-tuple-element.215.refs_0_), channel_id=1, source_target_pairs={{0,2},{1,3},{2,0},{3,1},{4,6},{5,7},{6,4},{7,5},{8,10},{9,11},{10,... | collective-permute-start | bytes 3145736 | tf_op jit(solution)/shard_map/ppermute | solution.py:977
  383.3 48.4 %collective-permute-start.45 = (bf16[4,256,1024]{2,1,0:T(8,128)(2,1)S(1)}, bf16[4,256,1024]{2,1,0:T(8,128)(2,1)}, u32[]{:S(2)}, u32[]{:S(2)}) collective-permute-start(bf16[4,256,1024]{2,1,0:T(8,128)(2,1)S(1)} %copy-done.7), channel_id=1, source_target_pairs={{0,8},{4,12},{8,0},{12,4},{16,24},{20,28},{24,16},{28,20},{1,9},{5... | collective-permute-start | bytes 6291464 | tf_op jit(solution)/shard_map/ppermute | solution.py:847
  384.7 26.2 %collective-permute-start.41 = (bf16[1024,512]{1,0:T(8,128)(2,1)}, bf16[1024,512]{1,0:T(8,128)(2,1)S(1)}, u32[]{:S(2)}, u32[]{:S(2)}) collective-permute-start(bf16[1024,512]{1,0:T(8,128)(2,1)} %get-tuple-element.228), channel_id=1, source_target_pairs={{0,2},{1,3},{2,0},{3,1},{4,6},{5,7},{6,4},{7,5},{8,10},{9,11},{10,... | collective-permute-start | bytes 3145736 | tf_op jit(solution)/shard_map/ppermute | solution.py:977
  385.4 25.5 %collective-permute-start.42 = (f32[8,1024]{1,0:T(8,128)S(1)}, f32[8,1024]{1,0:T(8,128)S(1)}, u32[]{:S(2)}, u32[]{:S(2)}) collective-permute-start(f32[8,1024]{1,0:T(8,128)S(1)} %copy-done.42), channel_id=1, source_target_pairs={{0,2},{1,3},{2,0},{3,1},{4,6},{5,7},{6,4},{7,5},{8,10},{9,11},{10,... | collective-permute-start | bytes 98312 | tf_op jit(solution)/shard_map/ppermute | solution.py:977
  417.5 30.7 %collective-permute-start.43 = (bf16[1024,512]{1,0:T(8,128)(2,1)}, bf16[1024,512]{1,0:T(8,128)(2,1)S(1)}, u32[]{:S(2)}, u32[]{:S(2)}) collective-permute-start(bf16[1024,512]{1,0:T(8,128)(2,1)} %get-tuple-element.231.refs_0_), channel_id=1, source_target_pairs={{0,2},{1,3},{2,0},{3,1},{4,6},{5,7},{6,4},{7,5},{8,10},{9,11},{10,... | collective-permute-start | bytes 3145736 | tf_op jit(solution)/shard_map/ppermute | solution.py:977
  431.2 24.4 %collective-permute-start.50 = (bf16[1024,512]{1,0:T(8,128)(2,1)}, bf16[1024,512]{1,0:T(8,128)(2,1)}, u32[]{:S(2)}, u32[]{:S(2)}) collective-permute-start(bf16[1024,512]{1,0:T(8,128)(2,1)} %get-tuple-element.242), channel_id=1, source_target_pairs={{0,1},{1,0},{2,3},{3,2},{4,5},{5,4},{6,7},{7,6},{8,9},{9,8},{10,11... | collective-permute-start | bytes 3145736 | tf_op jit(solution)/shard_map/ppermute | solution.py:974
  452.6 40.4 %collective-permute-start.24 = (bf16[1024,512]{1,0:T(8,128)(2,1)}, bf16[1024,512]{1,0:T(8,128)(2,1)}, u32[]{:S(2)}, u32[]{:S(2)}) collective-permute-start(bf16[1024,512]{1,0:T(8,128)(2,1)} %get-tuple-element.188.refs_12_), channel_id=1, source_target_pairs={{0,2},{1,3},{2,0},{3,1},{4,6},{5,7},{6,4},{7,5},{8,10},{9,11},{10,... | collective-permute-start | bytes 3145736 | tf_op jit(solution)/shard_map/ppermute | solution.py:977
  454.1 74.9 %collective-permute-start.53 = (bf16[4,256,1024]{2,1,0:T(8,128)(2,1)S(1)}, bf16[4,256,1024]{2,1,0:T(8,128)(2,1)}, u32[]{:S(2)}, u32[]{:S(2)}) collective-permute-start(bf16[4,256,1024]{2,1,0:T(8,128)(2,1)S(1)} %copy-done.6), channel_id=1, source_target_pairs={{0,4},{4,0},{8,12},{12,8},{16,20},{20,16},{24,28},{28,24},{1,5},{5... | collective-permute-start | bytes 6291464 | tf_op jit(solution)/shard_map/ppermute | solution.py:847
  455.6 45.0 %collective-permute-start.29 = (bf16[1024,512]{1,0:T(8,128)(2,1)}, bf16[1024,512]{1,0:T(8,128)(2,1)}, u32[]{:S(2)}, u32[]{:S(2)}) collective-permute-start(bf16[1024,512]{1,0:T(8,128)(2,1)} %get-tuple-element.200.refs_11_), channel_id=1, source_target_pairs={{0,2},{1,3},{2,0},{3,1},{4,6},{5,7},{6,4},{7,5},{8,10},{9,11},{10,... | collective-permute-start | bytes 3145736 | tf_op jit(solution)/shard_map/ppermute | solution.py:977
  459.6 109.7 %collective-permute-start.51 = (bf16[2,2048,256]{2,1,0:T(8,128)(2,1)}, bf16[2,2048,256]{2,1,0:T(8,128)(2,1)}, u32[]{:S(2)}, u32[]{:S(2)}) collective-permute-start(bf16[2,2048,256]{2,1,0:T(8,128)(2,1)} %get-tuple-element.245), channel_id=1, source_target_pairs={{0,8},{4,12},{8,0},{12,4},{16,24},{20,28},{24,16},{28,20},{1,9},{5... | collective-permute-start | bytes 6291464 | tf_op jit(solution)/shard_map/ppermute | solution.py:847
  502.0 49.0 %collective-permute-start.52 = (bf16[2,256,1024]{2,1,0:T(8,128)(2,1)}, bf16[2,256,1024]{2,1,0:T(8,128)(2,1)}, u32[]{:S(2)}, u32[]{:S(2)}) collective-permute-start(bf16[2,256,1024]{2,1,0:T(8,128)(2,1)} %get-tuple-element.246), channel_id=1, source_target_pairs={{0,16},{4,20},{8,24},{12,28},{16,0},{20,4},{24,8},{28,12},{1,17},{... | collective-permute-start | bytes 3145736 | tf_op jit(solution)/shard_map/ppermute | solution.py:847
  503.6 67.7 %collective-permute-start.59 = (bf16[1024,512]{1,0:T(8,128)(2,1)}, bf16[1024,512]{1,0:T(8,128)(2,1)}, u32[]{:S(2)}, u32[]{:S(2)}) collective-permute-start(bf16[1024,512]{1,0:T(8,128)(2,1)} %get-tuple-element.261), channel_id=1, source_target_pairs={{0,2},{1,3},{2,0},{3,1},{4,6},{5,7},{6,4},{7,5},{8,10},{9,11},{10,... | collective-permute-start | bytes 3145736 | tf_op jit(solution)/shard_map/ppermute | solution.py:977
  514.2 57.8 %collective-permute-start.64 = (bf16[4,256,768]{2,1,0:T(8,128)(2,1)}, bf16[4,256,768]{2,1,0:T(8,128)(2,1)S(1)}, u32[]{:S(2)}, u32[]{:S(2)}) collective-permute-start(bf16[4,256,768]{2,1,0:T(8,128)(2,1)} %weight_blocks.17.refs_6_), channel_id=1, source_target_pairs={{0,4},{4,0},{8,12},{12,8},{16,20},{20,16},{24,28},{28,24},{1,5},{5... | collective-permute-start | bytes 4718600 | tf_op jit(solution)/shard_map/ppermute | solution.py:847
  529.0 88.2 %collective-permute-start.63 = (bf16[4,256,768]{2,1,0:T(8,128)(2,1)}, bf16[4,256,768]{2,1,0:T(8,128)(2,1)}, u32[]{:S(2)}, u32[]{:S(2)}) collective-permute-start(bf16[4,256,768]{2,1,0:T(8,128)(2,1)} %weight_blocks.18.refs_11_), channel_id=1, source_target_pairs={{0,8},{4,12},{8,0},{12,4},{16,24},{20,28},{24,16},{28,20},{1,9},{5... | collective-permute-start | bytes 4718600 | tf_op jit(solution)/shard_map/ppermute | solution.py:847
  569.2 58.4 %collective-permute-start.61 = (bf16[2,256,1024]{2,1,0:T(8,128)(2,1)}, bf16[2,256,1024]{2,1,0:T(8,128)(2,1)}, u32[]{:S(2)}, u32[]{:S(2)}) collective-permute-start(bf16[2,256,1024]{2,1,0:T(8,128)(2,1)} %get-tuple-element.264), channel_id=1, source_target_pairs={{0,8},{4,12},{8,0},{12,4},{16,24},{20,28},{24,16},{28,20},{1,9},{5... | collective-permute-start | bytes 3145736 | tf_op jit(solution)/shard_map/ppermute | solution.py:847
  569.3 60.4 %collective-permute-start.62 = (bf16[4,512,256]{2,1,0:T(8,128)(2,1)S(1)}, bf16[4,512,256]{2,1,0:T(8,128)(2,1)}, u32[]{:S(2)}, u32[]{:S(2)}) collective-permute-start(bf16[4,512,256]{2,1,0:T(8,128)(2,1)S(1)} %copy-done.9), channel_id=1, source_target_pairs={{0,8},{4,12},{8,0},{12,4},{16,24},{20,28},{24,16},{28,20},{1,9},{5... | collective-permute-start | bytes 3145736 | tf_op jit(solution)/shard_map/ppermute | solution.py:847
  571.3 62.5 %collective-permute-start.57 = (bf16[1024,512]{1,0:T(8,128)(2,1)}, bf16[1024,512]{1,0:T(8,128)(2,1)S(1)}, u32[]{:S(2)}, u32[]{:S(2)}) collective-permute-start(bf16[1024,512]{1,0:T(8,128)(2,1)} %get-tuple-element.258), channel_id=1, source_target_pairs={{0,2},{1,3},{2,0},{3,1},{4,6},{5,7},{6,4},{7,5},{8,10},{9,11},{10,... | collective-permute-start | bytes 3145736 | tf_op jit(solution)/shard_map/ppermute | solution.py:977
  572.1 61.7 %collective-permute-start.58 = (f32[8,1024]{1,0:T(8,128)S(1)}, f32[8,1024]{1,0:T(8,128)S(1)}, u32[]{:S(2)}, u32[]{:S(2)}) collective-permute-start(f32[8,1024]{1,0:T(8,128)S(1)} %copy-done.41), channel_id=1, source_target_pairs={{0,2},{1,3},{2,0},{3,1},{4,6},{5,7},{6,4},{7,5},{8,10},{9,11},{10,... | collective-permute-start | bytes 98312 | tf_op jit(solution)/shard_map/ppermute | solution.py:977
  617.2 81.8 %collective-permute-start.73 = (bf16[2,256,768]{2,1,0:T(8,128)(2,1)}, bf16[2,256,768]{2,1,0:T(8,128)(2,1)S(1)}, u32[]{:S(2)}, u32[]{:S(2)}) collective-permute-start(bf16[2,256,768]{2,1,0:T(8,128)(2,1)} %get-tuple-element.283), channel_id=1, source_target_pairs={{0,8},{4,12},{8,0},{12,4},{16,24},{20,28},{24,16},{28,20},{1,9},{5... | collective-permute-start | bytes 2359304 | tf_op jit(solution)/shard_map/ppermute | solution.py:847
  656.9 103.8 %collective-permute-start.74 = (bf16[2,256,768]{2,1,0:T(8,128)(2,1)}, bf16[2,256,768]{2,1,0:T(8,128)(2,1)S(1)}, u32[]{:S(2)}, u32[]{:S(2)}) collective-permute-start(bf16[2,256,768]{2,1,0:T(8,128)(2,1)} %get-tuple-element.284), channel_id=1, source_target_pairs={{0,16},{4,20},{8,24},{12,28},{16,0},{20,4},{24,8},{28,12},{1,17},{... | collective-permute-start | bytes 2359304 | tf_op jit(solution)/shard_map/ppermute | solution.py:847
  657.2 116.2 %collective-permute-start.70 = (bf16[1,2048,256]{2,1,0:T(8,128)(2,1)}, bf16[1,2048,256]{2,1,0:T(8,128)(2,1)S(1)}, u32[]{:S(2)}, u32[]{:S(2)}) collective-permute-start(bf16[1,2048,256]{2,1,0:T(8,128)(2,1)} %get-tuple-element.280), channel_id=1, source_target_pairs={{0,16},{4,20},{8,24},{12,28},{16,0},{20,4},{24,8},{28,12},{1,17},{... | collective-permute-start | bytes 3145736 | tf_op jit(solution)/shard_map/ppermute | solution.py:847
  659.9 38.5 %collective-permute-start.68 = (f32[40,128]{1,0:T(8,128)S(1)}, f32[40,128]{1,0:T(8,128)S(1)}, u32[]{:S(2)}, u32[]{:S(2)}) collective-permute-start(f32[40,128]{1,0:T(8,128)S(1)} %fusion), channel_id=1, source_target_pairs={{0,8},{4,12},{8,0},{12,4},{16,24},{20,28},{24,16},{28,20},{1,9},{5... | collective-permute-start | bytes 61448 | tf_op jit(solution)/shard_map/ppermute | solution.py:1049
  659.9 100.8 %collective-permute-start.75 = (bf16[2,512,256]{2,1,0:T(8,128)(2,1)}, bf16[2,512,256]{2,1,0:T(8,128)(2,1)S(1)}, u32[]{:S(2)}, u32[]{:S(2)}) collective-permute-start(bf16[2,512,256]{2,1,0:T(8,128)(2,1)} %get-tuple-element.286), channel_id=1, source_target_pairs={{0,16},{4,20},{8,24},{12,28},{16,0},{20,4},{24,8},{28,12},{1,17},{... | collective-permute-start | bytes 1572872 | tf_op jit(solution)/shard_map/ppermute | solution.py:847
  698.4 71.8 %collective-permute-start.72 = (bf16[1,256,1024]{2,1,0:T(8,128)(2,1)}, bf16[1,256,1024]{2,1,0:T(8,128)(2,1)S(1)}, u32[]{:S(2)}, u32[]{:S(2)}) collective-permute-start(bf16[1,256,1024]{2,1,0:T(8,128)(2,1)} %get-tuple-element.282), channel_id=1, source_target_pairs={{0,4},{4,0},{8,12},{12,8},{16,20},{20,16},{24,28},{28,24},{1,5},{5... | collective-permute-start | bytes 1572872 | tf_op jit(solution)/shard_map/ppermute | solution.py:847
  698.9 61.7 %collective-permute-start.69 = (f32[40,128]{1,0:T(8,128)S(1)}, f32[40,128]{1,0:T(8,128)S(1)}, u32[]{:S(2)}, u32[]{:S(2)}) collective-permute-start(f32[40,128]{1,0:T(8,128)S(1)} %fusion.4), channel_id=1, source_target_pairs={{0,16},{4,20},{8,24},{12,28},{16,0},{20,4},{24,8},{28,12},{1,17},{... | collective-permute-start | bytes 61448 | tf_op jit(solution)/shard_map/ppermute | solution.py:1049
  760.7 34.0 %collective-permute-start.71 = (bf16[1,256,1024]{2,1,0:T(8,128)(2,1)}, bf16[1,256,1024]{2,1,0:T(8,128)(2,1)S(1)}, u32[]{:S(2)}, u32[]{:S(2)}) collective-permute-start(bf16[1,256,1024]{2,1,0:T(8,128)(2,1)} %get-tuple-element.281), channel_id=1, source_target_pairs={{0,16},{4,20},{8,24},{12,28},{16,0},{20,4},{24,8},{28,12},{1,17},{... | collective-permute-start | bytes 1572872 | tf_op jit(solution)/shard_map/ppermute | solution.py:847
  766.7 36.4 %collective-permute-start.77 = (bf16[1,256,768]{2,1,0:T(8,128)(2,1)}, bf16[1,256,768]{2,1,0:T(8,128)(2,1)S(1)}, u32[]{:S(2)}, u32[]{:S(2)}) collective-permute-start(bf16[1,256,768]{2,1,0:T(8,128)(2,1)} %get-tuple-element.290), channel_id=1, source_target_pairs={{0,16},{4,20},{8,24},{12,28},{16,0},{20,4},{24,8},{28,12},{1,17},{... | collective-permute-start | bytes 1179656 | tf_op jit(solution)/shard_map/ppermute | solution.py:847
  769.6 33.4 %collective-permute-start.78 = (bf16[1,256,768]{2,1,0:T(8,128)(2,1)}, bf16[1,256,768]{2,1,0:T(8,128)(2,1)S(1)}, u32[]{:S(2)}, u32[]{:S(2)}) collective-permute-start(bf16[1,256,768]{2,1,0:T(8,128)(2,1)} %get-tuple-element.292), channel_id=1, source_target_pairs={{0,4},{4,0},{8,12},{12,8},{16,20},{20,16},{24,28},{28,24},{1,5},{5... | collective-permute-start | bytes 1179656 | tf_op jit(solution)/shard_map/ppermute | solution.py:847
  770.2 24.5 %collective-permute-start.76 = (bf16[1,512,256]{2,1,0:T(8,128)(2,1)}, bf16[1,512,256]{2,1,0:T(8,128)(2,1)S(1)}, u32[]{:S(2)}, u32[]{:S(2)}) collective-permute-start(bf16[1,512,256]{2,1,0:T(8,128)(2,1)} %get-tuple-element.288), channel_id=1, source_target_pairs={{0,4},{4,0},{8,12},{12,8},{16,20},{20,16},{24,28},{28,24},{1,5},{5... | collective-permute-start | bytes 786440 | tf_op jit(solution)/shard_map/ppermute | solution.py:847
  (104 other events, 850.9 us)
Sparse Core Ops, SparseCore 0:
  27.8 49.5 all-gather.1

commit v4 on v3

--- a/solution.py
+++ b/solution.py
@@ -34,10 +34,16 @@
 
 class Order:
     last = None
+    names = 0
+
+    @staticmethod
+    def name(remote):
+        Order.names += remote
+        return Order.names - 1 if remote else None
 
 
 def call(
-    name, body, grid, args, in_specs, outs, out_specs, scratch=(), prefetch=0, after=(), aliases=None
+    name, body, grid, args, in_specs, outs, out_specs, scratch=(), prefetch=0, after=(), aliases=None, remote=False
 ):
     count = len(args)
     extra = [*after]
@@ -58,8 +64,10 @@
         ),
         out_shape=outs,
         input_output_aliases=aliases or {},
-        compiler_params=pltpu.CompilerParams(vmem_limit_bytes=60 * MIB),
-        cost_estimate=pl.CostEstimate(flops=1, bytes_accessed=1, transcendentals=0),
+        compiler_params=pltpu.CompilerParams(
+            vmem_limit_bytes=60 * MIB, collective_id=Order.name(remote), has_side_effects=remote
+        ),
+        cost_estimate=pl.CostEstimate(flops=10**12, bytes_accessed=10**8, transcendentals=0),
         name=name,
     )(*args, *extra)
     fresh = [v for i, v in enumerate(got) if i not in (aliases or {}).values()]
@@ -69,6 +77,10 @@
 
 def shape(dims, dtype):
     return jax.ShapeDtypeStruct(dims, dtype)
+
+
+def sent(dims, dtype):
+    return pltpu.HBM(dims, dtype)
 
 
 SMEM = pl.BlockSpec(memory_space=pltpu.SMEM)
@@ -102,14 +114,181 @@
     return pl.BlockSpec(block, lambda i: (0,) * len(block))
 
 
+def flip(me, j):
+    there, bit = me, 1
+    while bit <= j:
+        if j & bit:
+            there = there + bit * (1 - 2 * ((me // bit) % 2))
+        bit *= 2
+    return there
+
+
 def place_of(me, j, width):
-    return pl.ds(pl.multiple_of((me ^ j) * width, width), width)
-
-
-def with_weights(copies, work):
+    return pl.ds(pl.multiple_of(flip(me, j) * width, width), width)
+
+
+def greet():
+    barrier = pltpu.get_barrier_semaphore()
+    sibling = flip(lax.axis_index("mp"), 1)
+    pl.semaphore_signal(
+        barrier, inc=1, device_id={"mp": sibling}, device_id_type=pl.DeviceIdType.MESH
+    )
+    pl.semaphore_wait(barrier, 1)
+
+
+def to_sibling(source, target, sems, at):
+    return pltpu.make_async_remote_copy(
+        src_ref=source,
+        dst_ref=target,
+        send_sem=sems.at[0, at],
+        recv_sem=sems.at[1, at],
+        device_id={"mp": flip(lax.axis_index("mp"), 1)},
+        device_id_type=pl.DeviceIdType.MESH,
+    )
+
+
+class Gathered:
+    def __init__(self, refs, pairs, steps):
+        self.pairs, self.steps = pairs, steps
+        self.blocks, self.whole = refs[:2] if pairs else refs, refs[2:4] if pairs else ()
+
+    @staticmethod
+    def specs(blocks, pairs, tile):
+        width = blocks[0].shape[1]
+        return [rows_of((tile, width))] * len(blocks) + ([ANY] * 2 if pairs else [])
+
+    @staticmethod
+    def scratch(blocks, pairs, steps):
+        if not pairs:
+            return []
+        return [pltpu.VMEM((2, *blocks[0].shape), BF16), pltpu.SemaphoreType.DMA((2, 2 * steps))]
+
+    def attach(self, refs):
+        if self.pairs:
+            self.came, self.sems = refs
+        return self
+
+    def copies(self, step):
+        tile = self.blocks[0].shape[0]
+        rows = pl.ds(pl.multiple_of(step * tile, tile), tile)
+        return [
+            to_sibling(self.whole[k].at[rows, :], self.came.at[k, rows, :], self.sems, 2 * step + k)
+            for k in range(2)
+        ]
+
+    def start(self):
+        if self.pairs:
+            for step in range(self.steps):
+                for one in self.copies(step):
+                    one.start()
+
+    def refs(self):
+        if not self.pairs:
+            return self.blocks
+        step = pl.program_id(0)
+        tile = self.blocks[0].shape[0]
+        for one in self.copies(step):
+            one.wait()
+        rows = pl.ds(pl.multiple_of(step * tile, tile), tile)
+        return [self.blocks[0], self.came.at[0, rows, :], self.blocks[1], self.came.at[1, rows, :]]
+
+
+class Scattered:
+    def __init__(self, pairs, n, steps, with_sums):
+        self.pairs, self.n, self.steps, self.with_sums = pairs, n, steps, with_sums
+
+    def outs(self, length, width):
+        tile = length // self.steps
+        if self.pairs:
+            outs = [shape((length, width), BF16), sent((length, width), BF16)]
+            specs = [fixed((length, width))] * 2
+            if self.with_sums:
+                outs, specs = outs + [sent((8, length), F32)], specs + [fixed((8, length))]
+            return outs, specs
+        outs, specs = [shape((length, width), BF16)] * self.n, [rows_of((tile, width))] * self.n
+        if self.with_sums:
+            outs, specs = outs + [shape((8, length), F32)], specs + [cols_of((8, tile))]
+        return outs, specs
+
+    def count(self):
+        return (2 if self.pairs else self.n) + self.with_sums
+
+    def scratch(self, length, width):
+        if not self.pairs:
+            return []
+        tile = length // self.steps
+        block = pltpu.VMEM((self.steps, 2, tile, width), BF16)
+        made = [block, block, pltpu.VMEM((2, 2, tile, width), F32)]
+        if self.with_sums:
+            made += [pltpu.VMEM((self.steps, 8, tile), F32)] * 3
+        return made + [pltpu.SemaphoreType.DMA((2, 3 * self.steps))]
+
+    def attach(self, outs, scratch):
+        self.out = outs
+        if self.pairs:
+            self.send, self.came, self.kept = scratch[:3]
+            self.sums = scratch[3:-1]
+            self.sems = scratch[-1]
+        return self
+
+    def copies(self, step):
+        made = [
+            to_sibling(self.send.at[step, k], self.came.at[step, k], self.sems, 3 * step + k)
+            for k in range(2)
+        ]
+        if self.with_sums:
+            made.append(to_sibling(self.sums[0].at[step], self.sums[1].at[step], self.sems, 3 * step + 2))
+        return made
+
+    def put(self, j, value):
+        step = pl.program_id(0)
+        if not self.pairs:
+            self.out[j][...] = value.astype(BF16)
+        elif j % 2:
+            self.send[step, j // 2] = value.astype(BF16)
+        else:
+            self.kept[step % 2, j // 2] = value
+
+    def take(self, step):
+        tile = self.kept.shape[2]
+        for one in self.copies(step):
+            one.wait()
+        rows = pl.ds(pl.multiple_of(step * tile, tile), tile)
+        for k in range(2):
+            total = self.kept[step % 2, k] + self.came[step, k].astype(F32)
+            self.out[k][rows, :] = total.astype(BF16)
+        if self.with_sums:
+            self.out[2][:, rows] = self.sums[2][step] + self.sums[1][step]
+
+    def finish(self, sums=None):
+        if not self.pairs:
+            if sums is not None:
+                self.out[-1][...] = sums
+            return
+        step = pl.program_id(0)
+        if sums is not None:
+            self.sums[0][step] = sums
+            self.sums[2][step] = sums
+        for one in self.copies(step):
+            one.start()
+
+        @pl.when(step > 0)
+        def _():
+            self.take(step - 1)
+
+        @pl.when(step == self.steps - 1)
+        def _():
+            self.take(step)
+
+
+def with_weights(copies, work, remote=False, gathered=()):
     @pl.when(pl.program_id(0) == 0)
     def _():
         for one in copies:
+            one.start()
+        if remote:
+            greet()
+        for one in gathered:
             one.start()
 
         def wait(some):
@@ -182,37 +361,45 @@
         (steps,),
         (weights, history),
         [SMEM, pl.BlockSpec((count, tile, width), lambda i: (0, row * steps + i, 0))],
-        [shape((length, width), F32), shape((length, width), BF16)],
+        [shape((length, width), F32), sent((length, width), BF16)],
         [rows_of((tile, width))] * 2,
     )
 
 
-def project_body(n, me, *refs):
-    xs = refs[:n]
-    gain, bias, cosine, sine, weight, qkv, normed, stat, held, joined, sems = refs[n:]
-    width = xs[0].shape[1]
+def project_body(n, pairs, steps, *refs):
+    count = 4 if pairs else n
+    x = Gathered(refs[:count], pairs, steps)
+    gain, bias, cosine, sine, weight, qkv, normed, stat = refs[count : count + 8]
+    refs = refs[count + 8 :]
+    shared = refs[:2] if pairs else ()
+    held, joined, sems, *more = refs[len(shared) :]
+    x.attach(more)
+    me = lax.axis_index("mp")
+    tile, width = x.blocks[0].shape
     full = n * width
     heads = held.shape[1] // (3 * HEAD)
-    tile = xs[0].shape[0]
     sub = min(256, tile)
-    copies = row_blocks(me[0], n, width, weight, held, sems, 0)
+    copies = row_blocks(me, n, width, weight, held, sems, 0)
 
     def work(wait):
+        xs = x.refs()
+        for out, k in zip(shared, (1, 3)):
+            out[...] = xs[k][...]
         for t in range(tile // sub):
             rows = slice(t * sub, (t + 1) * sub)
             total = square = 0.0
-            for x in xs:
-                value = x[rows, :].astype(F32)
+            for one in xs:
+                value = one[rows, :].astype(F32)
                 total += jnp.sum(value, 1, keepdims=True)
                 square += jnp.sum(value * value, 1, keepdims=True)
             mean = total / full
             inv = lax.rsqrt(square / full - mean * mean + EPSILON)
             stat[rows, :] = stat_columns(mean, inv)
-            for j, x in enumerate(xs):
+            for j, one in enumerate(xs):
                 part = slice(j * width, (j + 1) * width)
-                value = (x[rows, :].astype(F32) - mean) * inv * gain[0:1, part] + bias[0:1, part]
+                value = (one[rows, :].astype(F32) - mean) * inv * gain[0:1, part] + bias[0:1, part]
                 joined[rows, part] = value.astype(BF16)
-                normed[rows, place_of(me[0], j, width)] = value.astype(BF16)
+                normed[rows, place_of(me, j, width)] = value.astype(BF16)
             if t == 0:
                 wait(copies)
             for h in range(heads):
@@ -224,31 +411,36 @@
                     qkv[rows, base + s * HEAD : base + (s + 1) * HEAD] = turned.astype(BF16)
                 qkv[rows, base + 2 * HEAD : base + 3 * HEAD] = out[:, 2 * HEAD :].astype(BF16)
 
-    with_weights(copies, work)
-
-
-def project(me, xs, gain, bias, tables, weight):
-    n, (length, width) = len(xs), xs[0].shape
+    with_weights(copies, work, pairs, [x])
+
+
+def project(n, pairs, xs, gain, bias, tables, weight):
+    length, width = xs[0].shape
     full, out = weight.shape
     tile = min(512, length)
-    return call(
+    steps = length // tile
+    got = call(
         "project",
-        lambda *refs: project_body(n, *refs),
-        (length // tile,),
-        (me, *xs, gain, bias, *tables, weight),
-        [SMEM]
-        + [rows_of((tile, width))] * n
+        lambda *refs: project_body(n, pairs, steps, *refs),
+        (steps,),
+        (*xs, *(xs if pairs else ()), gain, bias, *tables, weight),
+        Gathered.specs(xs, pairs, tile)
         + [fixed((8, full))] * 2
         + [rows_of((tile, HEAD))] * 2
         + [ANY],
-        [shape((length, out), BF16), shape((length, full), BF16), shape((length, 128), F32)],
-        [rows_of((tile, out)), rows_of((tile, full)), rows_of((tile, 128))],
+        [shape((length, out), BF16), shape((length, full), BF16), shape((length, 128), F32)]
+        + [shape((length, width), BF16)] * (2 * pairs),
+        [rows_of((tile, out)), rows_of((tile, full)), rows_of((tile, 128))]
+        + [rows_of((tile, width))] * (2 * pairs),
         scratch=[
             pltpu.VMEM((full, out), BF16),
             pltpu.VMEM((tile, full), BF16),
             pltpu.SemaphoreType.DMA((n,)),
-        ],
-    )
+        ]
+        + Gathered.scratch(xs, pairs, steps),
+        remote=pairs,
+    )
+    return *got[:3], [xs[0], got[3], xs[1], got[4]] if pairs else xs
 
 
 def windows(length):
@@ -289,7 +481,7 @@
         (heads,),
         (start, qkv),
         [fixed((8, length)), cols_of((length, 3 * HEAD))],
-        [shape((length, heads * HEAD), BF16), shape((heads, 8, length), F32)],
+        [sent((length, heads * HEAD), BF16), shape((heads, 8, length), F32)],
         [cols_of((length, HEAD)), pl.BlockSpec((1, 8, length), lambda i: (i, 0, 0))],
     )
 
@@ -343,19 +535,31 @@
     )[0]
 
 
-def feed_body(n, beside, me, *refs):
-    attended, xs, outs_w = refs[:n], refs[n : 2 * n], refs[2 * n : 3 * n]
-    own, gain, bias, up_bias, up_weight, down_weight = refs[3 * n : 3 * n + 6]
-    extra = refs[3 * n + 6 : 3 * n + 6 + beside]
-    refs = refs[3 * n + 6 + beside :]
+def feed_body(n, pairs, beside, steps, *refs):
+    count = 4 if pairs else n
+    attended = Gathered(refs[:count], pairs, steps)
+    refs = refs[count:]
+    xs, outs_w = refs[: n - 1], refs[n - 1 : 2 * n - 1]
+    own, gain, bias, up_bias, up_weight, down_weight = refs[2 * n - 1 : 2 * n + 5]
+    refs = refs[2 * n + 5 :]
+    extra = None
+    if beside:
+        extra, refs = Gathered(refs[:count], pairs, steps), refs[count:]
     hidden, normed, stat, activated, slope = refs[:5]
-    parts = refs[5 : n + 5]
-    refs = refs[n + 5 :]
+    refs = refs[5:]
+    parts = Scattered(pairs, n, steps, False)
+    part_outs, refs = refs[: parts.count()], refs[parts.count() :]
     if beside:
-        put_beside(me, extra, *refs[:2])
-        refs = refs[2:]
-    out_held, up_held, down_held, joined, whole, sems = refs
-    width = xs[0].shape[1]
+        joined_outs, refs = refs[:2], refs[2:]
+    out_held, up_held, down_held, joined, whole, sems, *refs = refs
+    if pairs:
+        attended.attach(refs[:2])
+        if beside:
+            extra.attach(refs[2:4])
+        refs = refs[2 + 2 * beside :]
+    parts.attach(part_outs, refs)
+    me = lax.axis_index("mp")
+    width = own.shape[1]
     full = n * width
     inner = up_held.shape[1]
     out_copies = []
@@ -363,22 +567,24 @@
         for k in range(n):
             out_copies.append(
                 pltpu.make_async_copy(
-                    outs_w[k].at[:, place_of(me[0], j, width)],
+                    outs_w[k].at[:, place_of(me, j, width)],
                     out_held.at[pl.ds(k * width, width), pl.ds(j * width, width)],
                     sems.at[j * n + k],
                 )
             )
-    up_copies = row_blocks(me[0], n, width, up_weight, up_held, sems, n * n)
-    down_copies = col_blocks(me[0], n, width, down_weight, down_held, sems, n * n + n)
+    up_copies = row_blocks(me, n, width, up_weight, up_held, sems, n * n)
+    down_copies = col_blocks(me, n, width, down_weight, down_held, sems, n * n + n)
 
     def work(wait):
-        for j in range(n):
-            joined[:, j * width : (j + 1) * width] = attended[j][...]
+        for j, one in enumerate(attended.refs()):
+            joined[:, j * width : (j + 1) * width] = one[...]
+        if beside:
+            put_beside(me, extra.refs(), *joined_outs)
         total = square = 0.0
         for j in range(n):
             wait(out_copies[j * n : (j + 1) * n])
             part = slice(j * width, (j + 1) * width)
-            base = own[...] if j == 0 else xs[j][...].astype(F32)
+            base = own[...] if j == 0 else xs[j - 1][...].astype(F32)
             value = base + dot_nn(joined[...], out_held[:, part])
             whole[:, part] = value
             if j == 0:
@@ -392,7 +598,7 @@
             part = slice(j * width, (j + 1) * width)
             value = ((whole[:, part] - mean) * inv * gain[0:1, part] + bias[0:1, part]).astype(BF16)
             joined[:, part] = value
-            normed[:, place_of(me[0], j, width)] = value
+            normed[:, place_of(me, j, width)] = value
         wait(up_copies)
         step = divisor(inner, 512)
         for c in range(inner // step):
@@ -403,37 +609,57 @@
             slope[:, part] = (half + up * INV_ROOT_TWO_PI * jnp.exp(-0.5 * up * up)).astype(BF16)
         wait(down_copies)
         for j in range(n):
-            parts[j][...] = dot_nn(
-                activated[...], down_held[:, j * width : (j + 1) * width]
-            ).astype(BF16)
-
-    with_weights(out_copies + up_copies + down_copies, work)
+            parts.put(j, dot_nn(activated[...], down_held[:, j * width : (j + 1) * width]))
+
+    with_weights(
+        out_copies + up_copies + down_copies, work, pairs, [attended] + ([extra] if beside else [])
+    )
+    parts.finish()
 
 
 def put_beside(me, blocks, whole, sums):
     width = blocks[0].shape[1]
     for j, block in enumerate(blocks):
-        whole[:, place_of(me[0], j, width)] = block[...]
+        whole[:, place_of(me, j, width)] = block[...]
     accumulate(sums, fold_rows(blocks[0][...].astype(F32)))
 
 
-def feed(me, attended, xs, outs_w, own, gain, bias, up_bias, up_weight, down_weight, beside=()):
-    n, (length, width) = len(xs), own.shape
+def feed(
+    n, pairs, attended, xs, outs_w, own, gain, bias, up_bias, up_weight, down_weight, beside=()
+):
+    length, width = own.shape
     full, inner = up_weight.shape
     tile = min(256, length)
+    steps = length // tile
+    parts = Scattered(pairs, n, steps, False)
+    part_outs, part_specs = parts.outs(length, width)
+    twice = tuple(attended) if pairs else ()
+    extra = (*beside, *(beside if pairs else ()))
     got = call(
         "feed",
-        lambda *refs: feed_body(n, len(beside), *refs),
-        (length // tile,),
-        (me, *attended, *xs, *outs_w, own, gain, bias, up_bias, up_weight, down_weight, *beside),
-        [SMEM]
-        + [rows_of((tile, width))] * (2 * n)
+        lambda *refs: feed_body(n, pairs, bool(beside), steps, *refs),
+        (steps,),
+        (
+            *attended,
+            *twice,
+            *xs[1:],
+            *outs_w,
+            own,
+            gain,
+            bias,
+            up_bias,
+            up_weight,
+            down_weight,
+            *extra,
+        ),
+        Gathered.specs(attended, pairs, tile)
+        + [rows_of((tile, width))] * (n - 1)
         + [ANY] * n
         + [rows_of((tile, width))]
         + [fixed((8, full))] * 2
         + [fixed((8, inner))]
         + [ANY] * 2
-        + [rows_of((tile, width))] * len(beside),
+        + (Gathered.specs(beside, pairs, tile) if beside else []),
         [
             shape((length, width), F32),
             shape((length, full), BF16),
@@ -441,7 +667,7 @@
             shape((length, inner), BF16),
             shape((length, inner), BF16),
         ]
-        + [shape((length, width), BF16)] * n
+        + part_outs
         + ([shape((length, full), BF16), shape((8, width), F32)] if beside else []),
         [
             rows_of((tile, width)),
@@ -450,7 +676,7 @@
             rows_of((tile, inner)),
             rows_of((tile, inner)),
         ]
-        + [rows_of((tile, width))] * n
+        + part_specs
         + ([rows_of((tile, full)), fixed((8, width))] if beside else []),
         scratch=[
             pltpu.VMEM((full, full), BF16),
@@ -459,47 +685,60 @@
             pltpu.VMEM((tile, full), BF16),
             pltpu.VMEM((tile, full), F32),
             pltpu.SemaphoreType.DMA((n * n + 2 * n,)),
-        ],
-    )
-    return (*got[:5], got[5 : n + 5], got[n + 5 :])
+        ]
+        + Gathered.scratch(attended, pairs, steps)
+        + (Gathered.scratch(beside, pairs, steps) if beside else [])
+        + parts.scratch(length, width),
+        remote=pairs,
+    )
+    return (*got[:5], got[5 : 5 + parts.count()], got[5 + parts.count() :])
 
 
 def row_stats(total, weighted):
     return stat_columns(total, weighted).T[0:8, :]
 
 
-def beside(me, blocks):
-    n, (length, width) = len(blocks), blocks[0].shape
-    tile = min(256, length)
-    return call(
-        "beside",
-        lambda me, *refs: put_beside(me, refs[:n], *refs[n:]),
-        (length // tile,),
-        (me, *blocks),
-        [SMEM] + [rows_of((tile, width))] * n,
-        [shape((length, n * width), BF16), shape((8, width), F32)],
-        [rows_of((tile, n * width)), fixed((8, width))],
-    )
-
-
-def feed_back_body(n, beside, joined_in, me, *refs):
-    cots, refs = refs[:joined_in], refs[joined_in:]
-    slope, normed, gain, bias, up_weight, down_weight = refs[:6]
-    extra, refs = refs[6 : 6 + beside], refs[6 + beside :]
-    up_grad, sums, up_bias_sum = refs[:3]
-    parts, refs = refs[3 : n + 3], refs[n + 3 :]
+def norm_sums(parts, n, product, normed, gain, bias, me):
+    width = gain.shape[1] // n
+    total = weighted = 0.0
+    for j in range(n):
+        part = slice(j * width, (j + 1) * width)
+        value = product(j)
+        parts.put(j, value)
+        total += jnp.sum(value * gain[0:1, part], 1, keepdims=True)
+        there = normed[:, place_of(me, j, width)].astype(F32)
+        weighted += jnp.sum(value * (there - bias[0:1, part]), 1, keepdims=True)
+    return row_stats(total, weighted)
+
+
+def feed_back_body(n, pairs, beside, steps, *refs):
+    cot, slope, normed, gain, bias, up_weight, down_weight = refs[:7]
+    refs = refs[7:]
+    count = 4 if pairs else n
+    extra = None
     if beside:
-        put_beside(me, extra, *refs[:2])
+        extra, refs = Gathered(refs[:count], pairs, steps), refs[count:]
+    up_grad, up_bias_sum = refs[:2]
+    refs = refs[2:]
+    parts = Scattered(pairs, n, steps, True)
+    part_outs, refs = refs[: parts.count()], refs[parts.count() :]
+    if beside:
+        joined_outs, refs = refs[:2], refs[2:]
+    up_held, down_held, row_sums, sems, *refs = refs
+    if pairs and beside:
+        extra.attach(refs[:2])
         refs = refs[2:]
-    up_held, down_held, sems = refs
-    width = parts[0].shape[1]
+    parts.attach(part_outs, refs)
+    me = lax.axis_index("mp")
     inner = up_held.shape[1]
+    width = gain.shape[1] // n
     step = divisor(inner, 512)
     down_copies = [pltpu.make_async_copy(down_weight, down_held, sems.at[n])]
-    up_copies = row_blocks(me[0], n, width, up_weight, up_held, sems, 0)
-    cot = cots[0]
+    up_copies = row_blocks(me, n, width, up_weight, up_held, sems, 0)
 
     def work(wait):
+        if beside:
+            put_beside(me, extra.refs(), *joined_outs)
         wait(down_copies)
         bias_parts = []
         for c in range(inner // step):
@@ -509,48 +748,65 @@
             up_grad[:, part] = low
             bias_parts.append(fold_rows(low.astype(F32)))
         accumulate(up_bias_sum, jnp.concatenate(bias_parts, 1))
-        total = weighted = 0.0
         wait(up_copies)
-        for j in range(n):
-            part = slice(j * width, (j + 1) * width)
-            value = dot_nt(up_grad[...], up_held[part, :])
-            parts[j][...] = value.astype(BF16)
-            total += jnp.sum(value * gain[0:1, part], 1, keepdims=True)
-            there = normed[:, place_of(me[0], j, width)].astype(F32)
-            weighted += jnp.sum(value * (there - bias[0:1, part]), 1, keepdims=True)
-        sums[...] = row_stats(total, weighted)
-
-    with_weights(down_copies + up_copies, work)
-
-
-def feed_back(me, n, cot, slope, normed, gain, bias, up_weight, down_weight, beside=()):
+        row_sums[...] = norm_sums(
+            parts,
+            n,
+            lambda j: dot_nt(up_grad[...], up_held[j * width : (j + 1) * width, :]),
+            normed,
+            gain,
+            bias,
+            me,
+        )
+
+    with_weights(down_copies + up_copies, work, pairs, [extra] if beside else [])
+    parts.finish(row_sums[...])
+
+
+def feed_back(n, pairs, cot, slope, normed, gain, bias, up_weight, down_weight, beside=()):
     length, full = cot.shape
     width = full // n
     inner = up_weight.shape[1]
     tile = min(256, length)
+    steps = length // tile
+    parts = Scattered(pairs, n, steps, True)
+    part_outs, part_specs = parts.outs(length, width)
     got = call(
         "feed_back",
-        lambda *refs: feed_back_body(n, len(beside), 1, *refs),
-        (length // tile,),
-        (me, cot, slope, normed, gain, bias, up_weight, down_weight, *beside),
-        [SMEM]
-        + [rows_of((tile, full)), rows_of((tile, inner)), rows_of((tile, full))]
+        lambda *refs: feed_back_body(n, pairs, bool(beside), steps, *refs),
+        (steps,),
+        (
+            cot,
+            slope,
+            normed,
+            gain,
+            bias,
+            up_weight,
+            down_weight,
+            *beside,
+            *(beside if pairs else ()),
+        ),
+        [rows_of((tile, full)), rows_of((tile, inner)), rows_of((tile, full))]
         + [fixed((8, full))] * 2
         + [ANY] * 2
-        + [rows_of((tile, width))] * len(beside),
-        [shape((length, inner), BF16), shape((8, length), F32), shape((8, inner), F32)]
-        + [shape((length, width), BF16)] * n
+        + (Gathered.specs(beside, pairs, tile) if beside else []),
+        [shape((length, inner), BF16), shape((8, inner), F32)]
+        + part_outs
         + ([shape((length, full), BF16), shape((8, width), F32)] if beside else []),
-        [rows_of((tile, inner)), cols_of((8, tile)), fixed((8, inner))]
-        + [rows_of((tile, width))] * n
+        [rows_of((tile, inner)), fixed((8, inner))]
+        + part_specs
         + ([rows_of((tile, full)), fixed((8, width))] if beside else []),
         scratch=[
             pltpu.VMEM((full, inner), BF16),
             pltpu.VMEM((inner, full), BF16),
+            pltpu.VMEM((8, tile), F32),
             pltpu.SemaphoreType.DMA((n + 1,)),
-        ],
-    )
-    return (*got[:3], got[3 : n + 3], got[n + 3 :])
+        ]
+        + (Gathered.scratch(beside, pairs, steps) if beside else [])
+        + parts.scratch(length, width),
+        remote=pairs,
+    )
+    return (*got[:2], got[2 : 2 + parts.count()], got[2 + parts.count() :])
 
 
 def norm_back(refs, n_parts, source, stat, sums, gain, full):
@@ -594,72 +850,89 @@
             rows_of((tile, 128)),
             fixed((8, width)),
         ],
-        [shape((length, width), F32), shape((length, width), BF16)] + [shape((8, width), F32)] * 2,
+        [shape((length, width), F32), sent((length, width), BF16)] + [shape((8, width), F32)] * 2,
         [rows_of((tile, width))] * 2 + [fixed((8, width))] * 2,
     )
 
 
-def attended_back_body(n, me, *refs):
-    grads = refs[:n]
-    weight, joined, out = refs[n:]
-    width = grads[0].shape[1]
-    for j in range(n):
-        joined[:, place_of(me[0], j, width)] = grads[j][...]
-    out[...] = dot_nt(joined[...], weight[...]).astype(BF16)
-
-
-def attended_back(me, grads, weight):
-    n, (length, width) = len(grads), grads[0].shape
+def attended_back_body(n, pairs, steps, *refs):
+    count = 4 if pairs else n
+    grads = Gathered(refs[:count], pairs, steps)
+    weight, joined, out, *more = refs[count:]
+    grads.attach(more)
+    me = lax.axis_index("mp")
+    width = grads.blocks[0].shape[1]
+
+    def work(wait):
+        for j, one in enumerate(grads.refs()):
+            joined[:, place_of(me, j, width)] = one[...]
+        out[...] = dot_nt(joined[...], weight[...]).astype(BF16)
+
+    with_weights([], work, pairs, [grads])
+
+
+def attended_back(n, pairs, grads, weight):
+    length, width = grads[0].shape
     rows, full = weight.shape
     tile = min(256, length)
+    steps = length // tile
     return call(
         "attended_back",
-        lambda *refs: attended_back_body(n, *refs),
-        (length // tile,),
-        (me, *grads, weight),
-        [SMEM] + [rows_of((tile, width))] * n + [fixed((rows, full))],
+        lambda *refs: attended_back_body(n, pairs, steps, *refs),
+        (steps,),
+        (*grads, *(grads if pairs else ()), weight),
+        Gathered.specs(grads, pairs, tile) + [fixed((rows, full))],
         [shape((length, full), BF16), shape((length, rows), BF16)],
         [rows_of((tile, full)), rows_of((tile, rows))],
-    )
-
-
-def project_back_body(n, me, grad, normed, gain, bias, weight, sums, *refs):
-    parts = refs[:n]
-    held, sems = refs[n:]
-    width = parts[0].shape[1]
-    copies = row_blocks(me[0], n, width, weight, held, sems, 0)
+        scratch=Gathered.scratch(grads, pairs, steps),
+        remote=pairs,
+    )
+
+
+def project_back_body(n, pairs, steps, grad, normed, gain, bias, weight, *refs):
+    parts = Scattered(pairs, n, steps, True)
+    part_outs, refs = refs[: parts.count()], refs[parts.count() :]
+    held, row_sums, sems, *refs = refs
+    parts.attach(part_outs, refs)
+    me = lax.axis_index("mp")
+    width = gain.shape[1] // n
+    copies = row_blocks(me, n, width, weight, held, sems, 0)
 
     def work(wait):
-        total = weighted = 0.0
-        for j in range(n):
+        def product(j):
             wait(copies[j : j + 1])
-            part = slice(j * width, (j + 1) * width)
-            value = dot_nt(grad[...], held[part, :])
-            parts[j][...] = value.astype(BF16)
-            total += jnp.sum(value * gain[0:1, part], 1, keepdims=True)
-            there = normed[:, place_of(me[0], j, width)].astype(F32)
-            weighted += jnp.sum(value * (there - bias[0:1, part]), 1, keepdims=True)
-        sums[...] = row_stats(total, weighted)
-
-    with_weights(copies, work)
-
-
-def project_back(me, n, grad, normed, gain, bias, weight):
+            return dot_nt(grad[...], held[j * width : (j + 1) * width, :])
+
+        row_sums[...] = norm_sums(parts, n, product, normed, gain, bias, me)
+
+    with_weights(copies, work, pairs)
+    parts.finish(row_sums[...])
+
+
+def project_back(n, pairs, grad, normed, gain, bias, weight):
     length, out = grad.shape
     full = weight.shape[0]
     width = full // n
     tile = min(256, length)
-    got = call(
+    steps = length // tile
+    parts = Scattered(pairs, n, steps, True)
+    part_outs, part_specs = parts.outs(length, width)
+    return call(
         "project_back",
-        lambda *refs: project_back_body(n, *refs),
-        (length // tile,),
-        (me, grad, normed, gain, bias, weight),
-        [SMEM, rows_of((tile, out)), rows_of((tile, full))] + [fixed((8, full))] * 2 + [ANY],
-        [shape((8, length), F32)] + [shape((length, width), BF16)] * n,
-        [cols_of((8, tile))] + [rows_of((tile, width))] * n,
-        scratch=[pltpu.VMEM((full, out), BF16), pltpu.SemaphoreType.DMA((n,))],
-    )
-    return got[0], got[1:]
+        lambda *refs: project_back_body(n, pairs, steps, *refs),
+        (steps,),
+        (grad, normed, gain, bias, weight),
+        [rows_of((tile, out)), rows_of((tile, full))] + [fixed((8, full))] * 2 + [ANY],
+        part_outs,
+        part_specs,
+        scratch=[
+            pltpu.VMEM((full, out), BF16),
+            pltpu.VMEM((8, tile), F32),
+            pltpu.SemaphoreType.DMA((n,)),
+        ]
+        + parts.scratch(length, width),
+        remote=pairs,
+    )
 
 
 def average_back_body(k, m, full, count, *refs):
@@ -809,11 +1082,11 @@
         def blocked(number):
             if self.dim == 0:
                 return (
-                    shape((number, size, extent), BF16),
+                    sent((number, size, extent), BF16),
                     pl.BlockSpec((number, size, tile), lambda i, group: (0, 0, i)),
                 )
             return (
-                shape((number, extent, size), BF16),
+                sent((number, extent, size), BF16),
                 pl.BlockSpec((number, tile, size), lambda i, group: (0, i, 0)),
             )
 
@@ -873,7 +1146,7 @@
         count, high, wide = one.held.shape
         args += [one.held, one.coming]
         specs += [pl.BlockSpec((count, high // steps, wide), lambda i: (0, i, 0))] * 2
-        outs += [shape((count // 2, high, wide), BF16)] * 2
+        outs += [sent((count // 2, high, wide), BF16)] * 2
         out_specs += [pl.BlockSpec((count // 2, high // steps, wide), lambda i: (0, i, 0))] * 2
     got = call("fold", lambda *refs: fold_body(len(spreads), *refs), (steps,), args, specs, outs, out_specs)
     for i, one in enumerate(spreads):
@@ -906,26 +1179,6 @@
         out_specs.append(rows_of((high // steps, first)))
         places.append(place)
     return call("finish", lambda *refs: finish_body(places, *refs), (steps,), args, specs, outs, out_specs)
-
-
-def add_body(*refs):
-    count = len(refs) // 3
-    for left, right, out in zip(refs[:count], refs[count : 2 * count], refs[2 * count :]):
-        out[...] = (left[...].astype(F32) + right[...].astype(F32)).astype(out.dtype)
-
-
-def add(lefts, rights):
-    steps = 2
-
-    def spec(v):
-        if v.dtype == BF16:
-            return rows_of((v.shape[0] // steps, v.shape[1]))
-        return cols_of((v.shape[0], v.shape[1] // steps))
-
-    specs = [spec(v) for v in lefts]
-    return call(
-        "add", add_body, (steps,), (*lefts, *rights), specs * 2, [shape(v.shape, v.dtype) for v in lefts], specs
-    )
 
 
 def output_body(rows, steps, *refs):
@@ -979,36 +1232,25 @@
     def gather_start(self, block):
         if self.pairs:
             return [block, self.over_chip(block)]
+        return self.gather(block)
+
+    def gather(self, block):
+        if self.pairs:
+            across = self.over_chip(block)
+            return [block, self.over_core(block), across, self.over_core(across)]
         every = lax.all_gather(block, "mp")
         return [
             lax.dynamic_index_in_dim(every, self.me ^ j, 0, keepdims=False) for j in range(self.n)
         ]
 
-    def gather_end(self, blocks, held=True):
+    def scatter(self, parts, sums=False):
+        parts, extra = (parts[:-1], parts[-1:]) if sums else (parts, [])
         if self.pairs:
-            block, across = gate(blocks) if held else blocks
-            return [block, self.over_core(block), across, self.over_core(across)]
-        return blocks
-
-    def gather(self, block):
-        return self.gather_end(self.gather_start(block), False)
-
-    def scatter_start(self, parts, sums=None):
-        extra = [] if sums is None else [sums]
-        if self.pairs:
-            sent = [parts[3], *extra, parts[1]]
-            return [parts[2], *extra, parts[0]], [self.over_core(v) for v in sent]
+            return [parts[0], self.over_chip(parts[1])], [*extra, *map(self.over_chip, extra)]
         stacked = jnp.stack([part.astype(F32) for part in parts])
         ordered = jnp.take(stacked, self.me ^ jnp.arange(self.n), axis=0)
         total = lax.psum_scatter(ordered, "mp", scatter_dimension=0, tiled=False)
         return [total], [lax.psum(v, "mp") for v in extra]
-
-    def scatter_end(self, state):
-        if not self.pairs:
-            return state
-        got = add(*state)
-        sums = list(got[1:-1])
-        return [got[-1], self.over_chip(got[0])], sums + [self.over_chip(v) for v in sums]
 
     def total(self, value):
         if self.pairs:
@@ -1025,18 +1267,13 @@
         return None
 
     def out_middle(self, piece):
-        return None if piece is None else lax.all_gather(gate([piece])[0], "dp", axis=0, tiled=True)
+        return None if piece is None else lax.all_gather(piece, "dp", axis=0, tiled=True)
 
     def out_end(self, weight, across):
         if across is None:
-            return lambda: self.gather(weight)
-        sent = [self.over_core(weight), self.over_core(across)]
-
-        def end():
-            sibling, far = gate(sent)
-            return [weight, sibling, across, far]
-
-        return end
+            return self.gather(weight)
+        across = gate([across])[0]
+        return [weight, self.over_core(weight), across, self.over_core(across)]
 
 
 def dp_total(vectors):
@@ -1082,7 +1319,7 @@
 ):
     ring = Ring()
     n = ring.n
-    me = ring.me[None]
+    pairs = ring.pairs
     width = history.shape[2]
     full = n * width
     row_count, length = segment_ids.shape
@@ -1091,10 +1328,6 @@
     earlier = (segment_ids[:, None, :] < segment_ids[:, :, None]).astype(jnp.int32)
     starts = jnp.broadcast_to(jnp.sum(earlier, -1)[:, None, :], (row_count, 8, length))
 
-    vectors = jnp.stack([first_gain, first_bias, second_gain, second_bias])
-    vectors = jnp.concatenate(ring.gather(jnp.repeat(vectors, 8, 0)), 1)
-    gain1, bias1, gain2, bias2 = (vectors[8 * i : 8 * i + 8] for i in range(4))
-    own1, own2 = gain1[:, :width], gain2[:, :width]
     up_bias8 = jnp.broadcast_to(up_bias[None], (8, up_bias.shape[0]))
 
     down_bias8 = jnp.broadcast_to(down_bias[None], (8, width))
@@ -1102,49 +1335,51 @@
     spread = full % (128 * groups) == 0 and groups >= 4
     last = row_count - 1
 
-    Order.last = None
+    Order.last, Order.names = None, 0
+    vectors = jnp.stack([first_gain, first_bias, second_gain, second_bias])
+    vectors = ring.gather_start(jnp.repeat(vectors, 8, 0))
     piece = ring.out_start(out_weight)
     cot_rows = [lax.slice_in_dim(cotangent, r * length, (r + 1) * length) for r in rows]
     none = [None] * row_count
-    wide, xs, qkv, normed1, stat1 = list(none), list(none), list(none), list(none), list(none)
-    attended, logs, heads, cots, cot_full = list(none), list(none), list(none), list(none), list(none)
+    wide, low, xs, qkv, normed1, stat1 = (list(none) for _ in range(6))
+    attended, logs, heads, cots, cot_full = (list(none) for _ in range(5))
     hidden, normed2, stat2, activated, slope = (list(none) for _ in range(5))
-    branch, up_grad, parts2, parts1 = list(none), list(none), list(none), list(none)
-    hidden_grad, grads, grad_full, qkv_grad = list(none), list(none), list(none), list(none)
+    branch, up_grad, parts2, parts1 = (list(none) for _ in range(4))
+    hidden_grad, grads, grad_full, qkv_grad = (list(none) for _ in range(4))
     up_bias_sum = down_bias_sum = gain2_sum = bias2_sum = 0.0
 
-    low = list(none)
     for r in rows:
         wide[r], low[r] = average(depth_weights, history, r, length)
         if r == 0:
             xs[0] = ring.gather_start(low[0])
-    across = ring.out_middle(piece)
+            if pairs:
+                vectors[1], piece = gate([vectors[1], piece])
+                vectors = [
+                    vectors[0],
+                    ring.over_core(vectors[0]),
+                    vectors[1],
+                    ring.over_core(vectors[1]),
+                ]
+            across = ring.out_middle(piece)
+    vectors = jnp.concatenate(vectors, 1)
+    gain1, bias1, gain2, bias2 = (vectors[8 * i : 8 * i + 8] for i in range(4))
+    own1, own2 = gain1[:, :width], gain2[:, :width]
+    for r in rows[1:]:
+        xs[r] = ring.gather_start(gate([low[r]], xs[r - 1][1:2])[0])
     for r in rows:
-        if r > 0:
-            xs[r] = ring.gather_start(gate([low[r]], xs[r - 1][1:2])[0])
-        if r == min(1, last):
-            xs[0] = ring.gather_end(xs[0])
-    out_w = ring.out_end(out_weight, across)
-    for r in rows:
-        if r > 0:
-            xs[r] = ring.gather_end(xs[r])
-        got = project(me, xs[r], gain1, bias1, tables, qkv_weight)
-        qkv[r], normed1[r], stat1[r] = got
-        if r > 0:
-            heads[r - 1] = ring.gather_end(heads[r - 1])
-        if r == last:
-            out_w = out_w()
+        qkv[r], normed1[r], stat1[r], xs[r] = project(
+            n, pairs, xs[r], gain1, bias1, tables, qkv_weight
+        )
         attended[r], logs[r] = attend(starts[r], qkv[r])
         heads[r] = ring.gather_start(attended[r])
+        if r == 0:
+            out_w = ring.out_end(out_weight, across)
 
     for r in rows:
         cots[r] = ring.gather_start(gate([cot_rows[r]])[0])
-        if r == last:
-            heads[r] = ring.gather_end(heads[r])
-        if r > 0:
-            cots[r - 1] = ring.gather_end(cots[r - 1])
         got = feed(
-            me,
+            n,
+            pairs,
             heads[r],
             xs[r],
             out_w,
@@ -1157,39 +1392,30 @@
             cots[r - 1] if r > 0 else (),
         )
         hidden[r], normed2[r], stat2[r], activated[r], slope[r], parts, joined = got
-        branch[r] = ring.scatter_start(parts)
+        branch[r] = ring.scatter(parts)[0]
         if r > 0:
             cot_full[r - 1], sums = joined
             down_bias_sum += sums
 
-    cots[last] = ring.gather_end(cots[last])
-    for r in range(last):
-        branch[r] = ring.scatter_end(branch[r])[0]
-    if row_count == 1:
-        cot_full[0], sums = beside(me, cots[0])
-        down_bias_sum += sums
-
     def back(r, more=()):
         return feed_back(
-            me, n, cot_full[r], slope[r], normed2[r], gain2, bias2, up_weight, down_weight, more
+            n, pairs, cot_full[r], slope[r], normed2[r], gain2, bias2, up_weight, down_weight, more
         )
 
     def take(r, got):
         nonlocal up_bias_sum
-        up_grad[r], sums, up_sum, parts, joined = got
+        up_grad[r], up_sum, parts, joined = got
         up_bias_sum += up_sum
-        parts2[r] = ring.scatter_start(parts, sums)
+        parts2[r] = ring.scatter(parts, True)
         return joined
 
-    joined = take(0, back(0, cots[last] if row_count > 1 else ()))
-    if row_count > 1:
-        cot_full[last], sums = joined
-        down_bias_sum += sums
-    branch[last] = ring.scatter_end(branch[last])[0]
+    cot_full[last], sums = take(0, back(0, cots[last]))
+    down_bias_sum += sums
     if spread:
         down = Spread(activated, cot_full, 1, (1, 2, 4))
         down.first()
-    parts2[0] = ring.scatter_end(parts2[0])
+    if pairs:
+        branch[0][1] = gate(branch[0][1:])[0]
     for r in rows[1:]:
         take(r, back(r))
 
@@ -1210,26 +1436,21 @@
             Spread(normed2, up_grad, 0, (2, 4, 1), (1, 2)),
         ]
         up[1].first()
-    for r in rows[1:]:
-        parts2[r] = ring.scatter_end(parts2[r])
-    if spread:
+        if pairs:
+            branch[last][1] = gate(branch[last][1:])[0]
         up[0].first()
         down.keep()
-    grads[0] = ring.gather_end(grads[0])
 
     for r in rows:
-        grad_full[r], attended_grad = attended_back(me, grads[r], out_weight)
-        qkv_grad[r] = attend_back(starts[r], tables, qkv[r], attended_grad, logs[r])
+        grad_full[r], attended_grad = attended_back(n, pairs, grads[r], out_weight)
         if r < last:
             hidden_step(r + 1)
-        sums, parts = project_back(me, n, qkv_grad[r], normed1[r], gain1, bias1, qkv_weight)
-        parts1[r] = ring.scatter_start(parts, sums)
+        qkv_grad[r] = attend_back(starts[r], tables, qkv[r], attended_grad, logs[r])
+        parts = project_back(n, pairs, qkv_grad[r], normed1[r], gain1, bias1, qkv_weight)
+        parts1[r] = ring.scatter(parts, True)
         if spread and r == 0:
             up[1].keep_added()
             advance(down)
-        if r < last:
-            grads[r + 1] = ring.gather_end(grads[r + 1])
-            parts1[r] = ring.scatter_end(parts1[r])
 
     if spread:
         qkv_sum = [
@@ -1238,8 +1459,6 @@
         ]
         out_sum = Spread(attended, grad_full, 1, (2, 4, 1))
         qkv_sum[0].first()
-    parts1[last] = ring.scatter_end(parts1[last])
-    if spread:
         qkv_sum[1].first()
         out_sum.first()
         up[0].keep_added()

time: 821 us -> 769 us (0.937)
  waiting for transfers between devices: 223 us -> 185 us
  local copies, waits for them, and re-layouts: 33.4 us -> 19.2 us
  starting transfers between devices: 59.8 us -> 49.5 us
    ppermute x18, waiting for transfers between devices: 52.1 us -> 115 us  [send(): lax.ppermute(value, 'dp', [(i, i ^ bit) for i in range(self.groups)])]
    ppermute x3, waiting for transfers between devices: 94.8 us -> 37.8 us  [dp_total(): lax.ppermute(packed, 'dp', [(i, i ^ bit) for i in range(groups)])]
    ppermute x21, waiting for transfers between devices: 44.2 us -> 25.5 us  [over_chip(): return lax.ppermute(value, 'mp', self.chip)]
    unnamed x152 -> x50, local copies, waits for them, and re-layouts: 23.3 us -> 8.05 us
    all_gather x1, waiting for transfers between devices: 21.1 us -> 6.59 us  [out_middle(): lax.all_gather(piece, 'dp', axis=0, tiled=True)]
    ppermute x37 -> x5, waiting for transfers between devices: 10.8 us -> 0.01 us  [over_core(): return lax.ppermute(value, 'mp', self.core)]
    pallas_call x57 -> x45, Pallas kernels: 482 us -> 487 us  [call(): pl.pallas_call(without_extra, grid_spec=pltpu.PrefetchScalarGridSpec(num_...]
  transfers between devices with their start and end apart: 80 -> 48, of which waited for: 21 -> 14; matrix products, arithmetic and copies ran while one was open for 2% -> 3% of each run, Pallas kernels for 58% -> 63%
where the time goes in v4:
time: 769 us; the launch traced here: 765 us
  Pallas kernels  487 us (63%)
  waiting for transfers between devices  185 us (24%)
  starting transfers between devices  49.5 us (6%)
  local copies, waits for them, and re-layouts  19.2 us (2%)
  between operations  14.6 us (2%)
  other arithmetic  8.86 us (1%)
    pallas_call x45, Pallas kernels, call(): pl.pallas_call(without_extra, grid_spec=pltpu.PrefetchScalarGridSpec(num_...  487 us
    ppermute x18, waiting for transfers between devices, send(): lax.ppermute(value, 'dp', [(i, i ^ bit) for i in range(self.groups)])  115 us
    ppermute x3, waiting for transfers between devices, dp_total(): lax.ppermute(packed, 'dp', [(i, i ^ bit) for i in range(groups)])  37.8 us
    ppermute x21, waiting for transfers between devices, over_chip(): return lax.ppermute(value, 'mp', self.chip)  25.5 us
    ppermute x21, starting transfers between devices, over_chip(): return lax.ppermute(value, 'mp', self.chip)  23.8 us
    ppermute x18, starting transfers between devices, send(): lax.ppermute(value, 'dp', [(i, i ^ bit) for i in range(self.groups)])  22.8 us
  transfers between devices with their start and end apart: 48, of which 14 were waited for; matrix products, arithmetic and copies ran while one was open for 3% of the time, Pallas kernels for 63%

profile of v4, /device:TPU:0, one launch (start us, length us, event | category | flops | bytes accessed | tf_op | source)
XLA Modules:
  0.0 764.9 jit_solution(16839047295647014360)
XLA Ops:
  13.7 8.0 %average.2 = (f32[1024,512]{1,0:T(8,128)}, bf16[1024,512]{1,0:T(8,128)(2,1)}) custom-call(f32[13]{0:T(128)} %refs_0_.7, bf16[13,2048,512]{2,1,0:T(8,128)(2,1)} %refs_9_.3), custom_call_target="tpu_custom_call" | custom-call | flops 999999995904 | bytes 100000000 | tf_op jit(solution)/shard_map/average/pallas_call | solution.py:56
  27.0 7.8 %average.3 = (f32[1024,512]{1,0:T(8,128)}, bf16[1024,512]{1,0:T(8,128)(2,1)}) custom-call(f32[13]{0:T(128)} %refs_0_.7, bf16[13,2048,512]{2,1,0:T(8,128)(2,1)} %refs_9_.3, f32[32,512]{1,0:T(8,128)} %get-tuple-element.117.refs_2_), custom_call_target="tpu_custom_call" | custom-call | flops 999999995904 | bytes 100000000 | tf_op jit(solution)/shard_map/average/pallas_call | solution.py:56
  36.6 10.5 %collective-permute-done.refs_1_.refs_3_.refs_5_ = bf16[1024,512]{1,0:T(8,128)(2,1)} collective-permute-done((bf16[1024,512]{1,0:T(8,128)(2,1)}, bf16[1024,512]{1,0:T(8,128)(2,1)}, u32[]{:S(2)}, u32[]{:S(2)}) %collective-permute-start) | collective-permute-done | bytes 1048608 | tf_op jit(solution)/shard_map/ppermute | solution.py:1230
  48.8 18.2 %project.2 = (bf16[1024,1536]{1,0:T(8,128)(2,1)}, bf16[1024,2048]{1,0:T(8,128)(2,1)}, f32[1024,128]{1,0:T(8,128)}, bf16[1024,512]{1,0:T(8,128)(2,1)}, bf16[1024,512]{1,0:T(8,128)(2,1)}) custom-call(bf16[1024,512]{1,0:T(8,128)(2,1)} %get-tuple-element.115.refs_0_.refs_2_, bf16[1024,512]{1,0:T(8,128)(2,1)} %collective-permute-done.refs_1_.refs_3_.refs_5_, ...), custom_call_target="tpu_custom_call" | custom-call | flops 999999995904 | bytes 100000000 | tf_op jit(solution)/shard_map/project/pallas_call | solution.py:56
  67.7 10.3 %attend.2 = (bf16[1024,512]{1,0:T(8,128)(2,1)}, f32[4,8,1024]{2,1,0:T(8,128)}) custom-call(s32[8,1024]{1,0:T(8,128)} %broadcast_in_dim.17.refs_0_, bf16[1024,1536]{1,0:T(8,128)(2,1)} %get-tuple-element.120.refs_1_.refs_3_, f32[1024,128]{1,0:T(8,128)} %get-tuple-element.121.refs_2_.refs_6_), custom_call_target="tpu_custom_call" | custom-call | flops 999999995904 | bytes 100000000 | tf_op jit(solution)/shard_map/attend/pallas_call | solution.py:56
  78.2 6.6 all-gather.2.cloned.1.call-done.refs_0_
  84.8 19.3 %project.3 = (bf16[1024,1536]{1,0:T(8,128)(2,1)}, bf16[1024,2048]{1,0:T(8,128)(2,1)}, f32[1024,128]{1,0:T(8,128)}, bf16[1024,512]{1,0:T(8,128)(2,1)}, bf16[1024,512]{1,0:T(8,128)(2,1)}) custom-call(bf16[1024,512]{1,0:T(8,128)(2,1)} %gate.8.refs_9_.refs_0_.refs_2_, bf16[1024,512]{1,0:T(8,128)(2,1)} %collective-permute-done.8.refs_1_.refs_3_.refs_5_, ...), custom_call_target="tpu_custom_call" | custom-call | flops 999999995904 | bytes 100000000 | tf_op jit(solution)/shard_map/project/pallas_call | solution.py:56
  104.8 9.7 %attend.3 = (bf16[1024,512]{1,0:T(8,128)(2,1)}, f32[4,8,1024]{2,1,0:T(8,128)}) custom-call(s32[8,1024]{1,0:T(8,128)} %broadcast_in_dim.21.refs_0_, bf16[1024,1536]{1,0:T(8,128)(2,1)} %get-tuple-element.127.refs_1_.refs_3_, f32[1024,128]{1,0:T(8,128)} %get-tuple-element.128.refs_2_.refs_6_), custom_call_target="tpu_custom_call" | custom-call | flops 999999995904 | bytes 100000000 | tf_op jit(solution)/shard_map/attend/pallas_call | solution.py:56
  117.1 40.7 %feed.2 = (f32[1024,512]{1,0:T(8,128)}, bf16[1024,2048]{1,0:T(8,128)(2,1)}, f32[1024,128]{1,0:T(8,128)}, bf16[1024,2048]{1,0:T(8,128)(2,1)}, bf16[1024,2048]{1,0...) custom-call(bf16[1024,512]{1,0:T(8,128)(2,1)} %get-tuple-element.122.refs_0_.refs_2_.refs_1_, ...), custom_call_target="tpu_custom_call" | custom-call | flops 999999995904 | bytes 100000000 | tf_op jit(solution)/shard_map/feed/pallas_call | solution.py:56
  163.3 45.5 %feed.3 = (f32[1024,512]{1,0:T(8,128)}, bf16[1024,2048]{1,0:T(8,128)(2,1)}, f32[1024,128]{1,0:T(8,128)}, bf16[1024,2048]{1,0:T(8,128)(2,1)}, bf16[1024,2048]{1,0...) custom-call(bf16[1024,512]{1,0:T(8,128)(2,1)} %get-tuple-element.134, ...), custom_call_target="tpu_custom_call" | custom-call | flops 999999995904 | bytes 100000000 | tf_op jit(solution)/shard_map/feed/pallas_call | solution.py:56
  210.3 31.3 %feed_back.2 = (bf16[1024,2048]{1,0:T(8,128)(2,1)}, f32[8,2048]{1,0:T(8,128)}, bf16[1024,512]{1,0:T(8,128)(2,1)}, bf16[1024,512]{1,0:T(8,128)(2,1)}, f32[8,1024]...) custom-call(bf16[1024,2048]{1,0:T(8,128)(2,1)} %get-tuple-element.139.refs_0_.refs_3_.refs_5_.refs_7_.refs_9_, ...), custom_call_target="tpu_custom_call" | custom-call | flops 999999995904 | bytes 100000000 | tf_op jit(solution)/shard_map/feed_back/pallas_call | solution.py:56
  243.7 13.5 %weight_blocks.12.refs_1_ = bf16[4,2048,256]{2,1,0:T(8,128)(2,1)} custom-call(s32[1]{0:T(128)} %bitcast.7.refs_0_, bf16[1024,2048]{1,0:T(8,128)(2,1)} %get-tuple-element.133.refs_1_, bf16[1024,2048]{1,0:T(8,128)(2,1)} %get-tuple-element.138.refs_2_, bf16[1024,2048]{1,0:T(8,128)(2,1)} %get-tuple-element.139.refs_0_.refs_3_.refs_5_.refs_7_.refs_9_, ...), custom_call_target="tpu_custom_call" | custom-call | flops 999999995904 | bytes 100000000 | tf_op jit(solution)/shard_map/weight_blocks/pallas_call | solution.py:56
  257.8 30.5 %feed_back.3 = (bf16[1024,2048]{1,0:T(8,128)(2,1)}, f32[8,2048]{1,0:T(8,128)}, bf16[1024,512]{1,0:T(8,128)(2,1)}, bf16[1024,512]{1,0:T(8,128)(2,1)}, f32[8,1024]{1,0:T(8,128)}) custom-call(bf16[1024,2048]{1,0:T(8,128)(2,1)} %get-tuple-element.143.refs_4_.refs_6_.refs_8_.refs_10_.refs_0_, bf16[1024,2048]{1,0:T(8,128)(2,1)} %get-tuple-element.150.refs_1_, ...), custom_call_target="tpu_custom_call" | custom-call | flops 999999995904 | bytes 100000000 | tf_op jit(solution)/shard_map/feed_back/pallas_call | solution.py:56
  293.8 5.7 hidden_back.2
  299.5 9.8 %weight_blocks.13.refs_1_ = bf16[4,256,1024]{2,1,0:T(8,128)(2,1)} custom-call(s32[1]{0:T(128)} %bitcast.7.refs_0_, bf16[1024,2048]{1,0:T(8,128)(2,1)} %get-tuple-element.141.refs_2_.refs_1_.refs_3_.refs_5_.refs_7_, bf16[1024,2048]{1,0:T(8,128)(2,1)} %get-tuple-element.148.refs_2_.refs_4_.refs_6_.refs_8_, ...), custom_call_target="tpu_custom_call" | custom-call | flops 999999995904 | bytes 100000000 | tf_op jit(solution)/shard_map/weight_blocks/pallas_call | solution.py:56
  310.9 10.3 %weight_blocks.14.refs_11_ = bf16[4,256,1024]{2,1,0:T(8,128)(2,1)} custom-call(s32[1]{0:T(128)} %bitcast.7.refs_0_, bf16[1024,2048]{1,0:T(8,128)(2,1)} %get-tuple-element.141.refs_2_.refs_1_.refs_3_.refs_5_.refs_7_, bf16[1024,2048]{1,0:T(8,128)(2,1)} %get-tuple-element.148.refs_2_.refs_4_.refs_6_.refs_8_, ...), custom_call_target="tpu_custom_call" | custom-call | flops 999999995904 | bytes 100000000 | tf_op jit(solution)/shard_map/weight_blocks/pallas_call | solution.py:56
  321.6 13.5 %weight_blocks.15.refs_5_.refs_0_ = bf16[4,2048,256]{2,1,0:T(8,128)(2,1)} custom-call(s32[1]{0:T(128)} %bitcast.7.refs_0_, bf16[1024,2048]{1,0:T(8,128)(2,1)} %get-tuple-element.133.refs_1_, bf16[1024,2048]{1,0:T(8,128)(2,1)} %get-tuple-element.138.refs_2_, bf16[1024,2048]{1,0:T(8,128)(2,1)} %get-tuple-element.139.refs_0_.refs_3_.refs_5_.refs_7_.refs_9_, ...), custom_call_target="tpu_custom_call" | custom-call | flops 999999995904 | bytes 100000000 | tf_op jit(solution)/shard_map/weight_blocks/pallas_call | solution.py:56
  335.1 10.9 %collective-permute-done.16.refs_1_.refs_3_ = bf16[1024,512]{1,0:T(8,128)(2,1)} collective-permute-done((bf16[1024,512]{1,0:T(8,128)(2,1)}, bf16[1024,512]{1,0:T(8,128)(2,1)}, u32[]{:S(2)}, u32[]{:S(2)}) %collective-permute-start.16) | collective-permute-done | bytes 1048608 | tf_op jit(solution)/shard_map/ppermute | solution.py:1230
  347.5 9.0 %attended_back.2 = (bf16[1024,2048]{1,0:T(8,128)(2,1)}, bf16[1024,512]{1,0:T(8,128)(2,1)}) custom-call(bf16[1024,512]{1,0:T(8,128)(2,1)} %get-tuple-element.157.refs_0_.refs_2_, bf16[1024,512]{1,0:T(8,128)(2,1)} %collective-permute-done.16.refs_1_.refs_3_, bf16[1024,512]{1,0:T(8,128)(2,1)} %get-tuple-element.157.refs_0_.refs_2_, ...), custom_call_target="tpu_custom_call" | custom-call | flops 999999995904 | bytes 100000000 | tf_op jit(solution)/shard_map/attended_back/pallas_call | solution.py:56
  356.5 5.6 hidden_back.3
  362.2 12.4 %attend_back.2.refs_0_.refs_9_ = bf16[1024,1536]{1,0:T(8,128)(2,1)} custom-call(s32[8,1024]{1,0:T(8,128)} %broadcast_in_dim.17.refs_0_, f32[1024,128]{1,0:T(8,128)} %constant.19.clone.refs_6_.refs_1_, f32[1024,128]{1,0:T(8,128)} %constant.20.clone.refs_7_.refs_2_, bf16[1024,1536]{1,0:T(8,128)(2,1)} %get-tuple-element.120.refs_1_.refs_3_, ...), custom_call_target="tpu_custom_call" | custom-call | flops 999999995904 | bytes 100000000 | tf_op jit(solution)/shard_map/attend_back/pallas_call | solution.py:56
  375.2 15.6 %project_back.2 = (bf16[1024,512]{1,0:T(8,128)(2,1)}, bf16[1024,512]{1,0:T(8,128)(2,1)}, f32[8,1024]{1,0:T(8,128)}) custom-call(bf16[1024,1536]{1,0:T(8,128)(2,1)} %attend_back.2.refs_0_.refs_9_, bf16[1024,2048]{1,0:T(8,128)(2,1)} %get-tuple-element.165.refs_1_.refs_3_.refs_5_.refs_7_, f32[8,2048]{1,0:T(8,128)} %get-tuple-element.222.refs_4_.refs_2_, ...), custom_call_target="tpu_custom_call" | custom-call | flops 999999995904 | bytes 100000000 | tf_op jit(solution)/shard_map/project_back/pallas_call | solution.py:56
  395.6 10.3 %weight_blocks.16 = (bf16[2,256,1024]{2,1,0:T(8,128)(2,1)}, bf16[2,256,1024]{2,1,0:T(8,128)(2,1)}) custom-call(s32[1]{0:T(128)} %bitcast.7.refs_0_, bf16[1024,2048]{1,0:T(8,128)(2,1)} %get-tuple-element.141.refs_2_.refs_1_.refs_3_.refs_5_.refs_7_, bf16[1024,2048]{1,0:T(8,128)(2,1)} %get-tuple-element.148.refs_2_.refs_4_.refs_6_.refs_8_, ...), custom_call_target="tpu_custom_call" | custom-call | flops 999999995904 | bytes 100000000 | tf_op jit(solution)/shard_map/weight_blocks/pallas_call | solution.py:56
  406.8 6.0 fold.4
  412.8 9.1 %attended_back.3 = (bf16[1024,2048]{1,0:T(8,128)(2,1)}, bf16[1024,512]{1,0:T(8,128)(2,1)}) custom-call(bf16[1024,512]{1,0:T(8,128)(2,1)} %get-tuple-element.163.refs_0_.refs_2_, bf16[1024,512]{1,0:T(8,128)(2,1)} %collective-permute-done.19.refs_1_.refs_3_, bf16[1024,512]{1,0:T(8,128)(2,1)} %get-tuple-element.163.refs_0_.refs_2_, ...), custom_call_target="tpu_custom_call" | custom-call | flops 999999995904 | bytes 100000000 | tf_op jit(solution)/shard_map/attended_back/pallas_call | solution.py:56
  421.9 12.4 %attend_back.3.refs_0_.refs_10_ = bf16[1024,1536]{1,0:T(8,128)(2,1)} custom-call(s32[8,1024]{1,0:T(8,128)} %broadcast_in_dim.21.refs_0_, f32[1024,128]{1,0:T(8,128)} %constant.19.clone.refs_6_.refs_1_, f32[1024,128]{1,0:T(8,128)} %constant.20.clone.refs_7_.refs_2_, bf16[1024,1536]{1,0:T(8,128)(2,1)} %get-tuple-element.127.refs_1_.refs_3_, ...), custom_call_target="tpu_custom_call" | custom-call | flops 999999995904 | bytes 100000000 | tf_op jit(solution)/shard_map/attend_back/pallas_call | solution.py:56
  434.4 15.4 %project_back.3 = (bf16[1024,512]{1,0:T(8,128)(2,1)}, bf16[1024,512]{1,0:T(8,128)(2,1)}, f32[8,1024]{1,0:T(8,128)}) custom-call(bf16[1024,1536]{1,0:T(8,128)(2,1)} %attend_back.3.refs_0_.refs_10_, bf16[1024,2048]{1,0:T(8,128)(2,1)} %get-tuple-element.172.refs_1_.refs_2_.refs_4_.refs_6_.refs_8_, f32[8,2048]{1,0:T(8,128)} %get-tuple-element.222.refs_4_.refs_2_, ...), custom_call_target="tpu_custom_call" | custom-call | flops 999999995904 | bytes 100000000 | tf_op jit(solution)/shard_map/project_back/pallas_call | solution.py:56
  449.8 9.8 %weight_blocks.17.refs_11_ = bf16[4,256,768]{2,1,0:T(8,128)(2,1)} custom-call(s32[1]{0:T(128)} %bitcast.7.refs_0_, bf16[1024,2048]{1,0:T(8,128)(2,1)} %get-tuple-element.165.refs_1_.refs_3_.refs_5_.refs_7_, bf16[1024,2048]{1,0:T(8,128)(2,1)} %get-tuple-element.172.refs_1_.refs_2_.refs_4_.refs_6_.refs_8_, ...), custom_call_target="tpu_custom_call" | custom-call | flops 999999995904 | bytes 100000000 | tf_op jit(solution)/shard_map/weight_blocks/pallas_call | solution.py:56
  459.6 9.8 %weight_blocks.18.refs_11_ = bf16[4,256,768]{2,1,0:T(8,128)(2,1)} custom-call(s32[1]{0:T(128)} %bitcast.7.refs_0_, bf16[1024,2048]{1,0:T(8,128)(2,1)} %get-tuple-element.165.refs_1_.refs_3_.refs_5_.refs_7_, bf16[1024,2048]{1,0:T(8,128)(2,1)} %get-tuple-element.172.refs_1_.refs_2_.refs_4_.refs_6_.refs_8_, ...), custom_call_target="tpu_custom_call" | custom-call | flops 999999995904 | bytes 100000000 | tf_op jit(solution)/shard_map/weight_blocks/pallas_call | solution.py:56
  469.9 6.2 weight_blocks.19.refs_12_
  477.5 10.3 %weight_blocks.20 = (bf16[2,256,1024]{2,1,0:T(8,128)(2,1)}, bf16[2,256,1024]{2,1,0:T(8,128)(2,1)}) custom-call(s32[1]{0:T(128)} %bitcast.7.refs_0_, bf16[1024,2048]{1,0:T(8,128)(2,1)} %get-tuple-element.141.refs_2_.refs_1_.refs_3_.refs_5_.refs_7_, bf16[1024,2048]{1,0:T(8,128)(2,1)} %get-tuple-element.148.refs_2_.refs_4_.refs_6_.refs_8_, ...), custom_call_target="tpu_custom_call" | custom-call | flops 999999995904 | bytes 100000000 | tf_op jit(solution)/shard_map/weight_blocks/pallas_call | solution.py:56
  488.5 36.4 %collective-permute-done.22.refs_1_ = bf16[2,2048,256]{2,1,0:T(8,128)(2,1)} collective-permute-done((bf16[2,2048,256]{2,1,0:T(8,128)(2,1)}, bf16[2,2048,256]{2,1,0:T(8,128)(2,1)}, u32[]{:S(2)}, u32[]{:S(2)}) %collective-permute-start.22) | collective-permute-done | bytes 2097184 | tf_op jit(solution)/shard_map/ppermute | solution.py:1120
  526.3 5.3 fold.5
  531.5 6.2 weight_blocks.21.refs_7_.refs_2_
  538.3 6.3 output.1.refs_10_
  547.5 14.5 %average_back.2 = (bf16[13,2048,512]{2,1,0:T(8,128)(2,1)}, f32[13,8,128]{2,1,0:T(8,128)}, f32[8,512]{1,0:T(8,128)}, f32[8,512]{1,0:T(8,128)}) custom-call(f32[13]{0:T(128)} %refs_0_.7, bf16[1024,512]{1,0:T(8,128)(2,1)} %get-tuple-element.180.refs_1_, bf16[1024,512]{1,0:T(8,128)(2,1)} %collective-permute-done.27.refs_2_, ...), custom_call_target="tpu_custom_call" | custom-call | flops 999999995904 | bytes 100000000 | tf_op jit(solution)/shard_map/average_back/pallas_call | solution.py:56
  562.7 9.9 %weight_blocks.22 = (bf16[2,256,768]{2,1,0:T(8,128)(2,1)}, bf16[2,256,768]{2,1,0:T(8,128)(2,1)}) custom-call(s32[1]{0:T(128)} %bitcast.7.refs_0_, bf16[1024,2048]{1,0:T(8,128)(2,1)} %get-tuple-element.165.refs_1_.refs_3_.refs_5_.refs_7_, bf16[1024,2048]{1,0:T(8,128)(2,1)} %get-tuple-element.172.refs_1_.refs_2_.refs_4_.refs_6_.refs_8_, ...), custom_call_target="tpu_custom_call" | custom-call | flops 999999995904 | bytes 100000000 | tf_op jit(solution)/shard_map/weight_blocks/pallas_call | solution.py:56
  572.6 10.0 %weight_blocks.23 = (bf16[2,256,768]{2,1,0:T(8,128)(2,1)}, bf16[2,256,768]{2,1,0:T(8,128)(2,1)}) custom-call(s32[1]{0:T(128)} %bitcast.7.refs_0_, bf16[1024,2048]{1,0:T(8,128)(2,1)} %get-tuple-element.165.refs_1_.refs_3_.refs_5_.refs_7_, bf16[1024,2048]{1,0:T(8,128)(2,1)} %get-tuple-element.172.refs_1_.refs_2_.refs_4_.refs_6_.refs_8_, ...), custom_call_target="tpu_custom_call" | custom-call | flops 999999995904 | bytes 100000000 | tf_op jit(solution)/shard_map/weight_blocks/pallas_call | solution.py:56
  582.6 20.0 %collective-permute-done.29.refs_1_ = bf16[2,256,1024]{2,1,0:T(8,128)(2,1)} collective-permute-done((bf16[2,256,1024]{2,1,0:T(8,128)(2,1)}, bf16[2,256,1024]{2,1,0:T(8,128)(2,1)}, u32[]{:S(2)}, u32[]{:S(2)}) %collective-permute-start.29) | collective-permute-done | bytes 1048608 | tf_op jit(solution)/shard_map/ppermute | solution.py:1120
  602.7 4.2 fold.6
  611.2 14.9 %average_back.3 = (bf16[13,2048,512]{2,1,0:T(8,128)(2,1)}, f32[13,8,128]{2,1,0:T(8,128)}, f32[8,512]{1,0:T(8,128)}, f32[8,512]{1,0:T(8,128)}) custom-call(f32[13]{0:T(128)} %refs_0_.7, bf16[1024,512]{1,0:T(8,128)(2,1)} %get-tuple-element.177.refs_1_, bf16[1024,512]{1,0:T(8,128)(2,1)} %collective-permute-done.25.refs_2_, ...), custom_call_target="tpu_custom_call", output_to_operand_aliasing={{0}: (10, {})} | custom-call | flops 999999995904 | bytes 100000000 | tf_op jit(solution)/shard_map/average_back/pallas_call | solution.py:56
  639.9 18.9 %collective-permute-done.36 = f32[40,128]{1,0:T(8,128)S(1)} collective-permute-done((f32[40,128]{1,0:T(8,128)S(1)}, f32[40,128]{1,0:T(8,128)S(1)}, u32[]{:S(2)}, u32[]{:S(2)}) %collective-permute-start.36) | collective-permute-done | bytes 20512 | tf_op jit(solution)/shard_map/ppermute | solution.py:1286
  662.4 16.6 %collective-permute-done.37 = f32[40,128]{1,0:T(8,128)S(1)} collective-permute-done((f32[40,128]{1,0:T(8,128)S(1)}, f32[40,128]{1,0:T(8,128)S(1)}, u32[]{:S(2)}, u32[]{:S(2)}) %collective-permute-start.37) | collective-permute-done | bytes 20512 | tf_op jit(solution)/shard_map/ppermute | solution.py:1286
  681.2 4.2 fold.7
  688.9 32.4 %collective-permute-done.39.refs_3_ = bf16[1,256,1024]{2,1,0:T(8,128)(2,1)} collective-permute-done((bf16[1,256,1024]{2,1,0:T(8,128)(2,1)}, bf16[1,256,1024]{2,1,0:T(8,128)(2,1)}, u32[]{:S(2)}, u32[]{:S(2)}) %collective-permute-start.39) | collective-permute-done | bytes 524320 | tf_op jit(solution)/shard_map/ppermute | solution.py:1120
  727.9 15.8 %collective-permute-done.38.refs_1_ = bf16[1,2048,256]{2,1,0:T(8,128)(2,1)} collective-permute-done((bf16[1,2048,256]{2,1,0:T(8,128)(2,1)}, bf16[1,2048,256]{2,1,0:T(8,128)(2,1)}, u32[]{:S(2)}, u32[]{:S(2)}) %collective-permute-start.38) | collective-permute-done | bytes 1048608 | tf_op jit(solution)/shard_map/ppermute | solution.py:1120
  743.8 7.4 collective-permute-done.45.refs_9_
  752.1 5.8 finish.1
  (173 shorter events, 87.3 us)
Async XLA Ops:
  7.2 77.6 %all-gather.2.cloned.1.call-start = ((), (), s32[]{:S(2)}) async-start(), calls=%async_computation | async-start | bytes 2359296 | tf_op jit(solution)/shard_map/all_gather | solution.py:1270
  8.6 18.3 %collective-permute-start.2 = (f32[32,512]{1,0:T(8,128)}, f32[32,512]{1,0:T(8,128)}, u32[]{:S(2)}, u32[]{:S(2)}) collective-permute-start(f32[32,512]{1,0:T(8,128)} %broadcast_bitcast_fusion), channel_id=1, source_target_pairs={{0,2},{1,3},{2,0},{3,1},{4,6},{5,7},{6,4},{7,5},{8,10},{9,11},{10,... | collective-permute-start | bytes 196616 | tf_op jit(solution)/shard_map/ppermute | solution.py:1230
  11.6 23.3 %collective-permute-start.1 = (f32[32,512]{1,0:T(8,128)}, f32[32,512]{1,0:T(8,128)}, u32[]{:S(2)}, u32[]{:S(2)}) collective-permute-start(f32[32,512]{1,0:T(8,128)} %broadcast_bitcast_fusion), channel_id=1, source_target_pairs={{0,1},{1,0},{2,3},{3,2},{4,5},{5,4},{6,7},{7,6},{8,9},{9,8},{10,11... | collective-permute-start | bytes 196616 | tf_op jit(solution)/shard_map/ppermute | solution.py:1227
  11.6 104.9 %collective-permute-start.6 = (bf16[512,2048]{1,0:T(8,128)(2,1)}, bf16[512,2048]{1,0:T(8,128)(2,1)}, u32[]{:S(2)}, u32[]{:S(2)}) collective-permute-start(bf16[512,2048]{1,0:T(8,128)(2,1)} %refs_4_.10), channel_id=1, source_target_pairs={{0,1},{1,0},{2,3},{3,2},{4,5},{5,4},{6,7},{7,6},{8,9},{9,8},{10,11... | collective-permute-start | bytes 6291464 | tf_op jit(solution)/shard_map/ppermute | solution.py:1227
  13.7 13.2 %collective-permute-start.3 = (bf16[64,2048]{1,0:T(8,128)(2,1)}, bf16[64,2048]{1,0:T(8,128)(2,1)}, u32[]{:S(2)}, u32[]{:S(2)}) collective-permute-start(bf16[64,2048]{1,0:T(8,128)(2,1)} %constant_dynamic-slice_fusion), channel_id=1, source_target_pairs={{0,2},{1,3},{2,0},{3,1},{4,6},{5,7},{6,4},{7,5},{8,10},{9,11},{10,... | collective-permute-start | bytes 786440 | tf_op jit(solution)/shard_map/ppermute | solution.py:1230
  21.7 25.4 %collective-permute-start = (bf16[1024,512]{1,0:T(8,128)(2,1)}, bf16[1024,512]{1,0:T(8,128)(2,1)}, u32[]{:S(2)}, u32[]{:S(2)}) collective-permute-start(bf16[1024,512]{1,0:T(8,128)(2,1)} %get-tuple-element.115.refs_0_.refs_2_), channel_id=1, source_target_pairs={{0,2},{1,3},{2,0},{3,1},{4,6},{5,7},{6,4},{7,5},{8,10},{9,11},{10,... | collective-permute-start | bytes 3145736 | tf_op jit(solution)/shard_map/ppermute | solution.py:1230
  26.9 8.0 %collective-permute-start.4 = (f32[32,512]{1,0:T(8,128)}, f32[32,512]{1,0:T(8,128)}, u32[]{:S(2)}, u32[]{:S(2)}) collective-permute-start(f32[32,512]{1,0:T(8,128)} %get-tuple-element.117.refs_2_), channel_id=1, source_target_pairs={{0,1},{1,0},{2,3},{3,2},{4,5},{5,4},{6,7},{7,6},{8,9},{9,8},{10,11... | collective-permute-start | bytes 196616 | tf_op jit(solution)/shard_map/ppermute | solution.py:1227
  47.1 37.7 %collective-permute-start.8 = (bf16[1024,512]{1,0:T(8,128)(2,1)}, bf16[1024,512]{1,0:T(8,128)(2,1)}, u32[]{:S(2)}, u32[]{:S(2)}) collective-permute-start(bf16[1024,512]{1,0:T(8,128)(2,1)} %gate.8.refs_9_.refs_0_.refs_2_), channel_id=1, source_target_pairs={{0,2},{1,3},{2,0},{3,1},{4,6},{5,7},{6,4},{7,5},{8,10},{9,11},{10,... | collective-permute-start | bytes 3145736 | tf_op jit(solution)/shard_map/ppermute | solution.py:1230
  77.9 38.6 %collective-permute-start.5 = (bf16[1024,512]{1,0:T(8,128)(2,1)}, bf16[1024,512]{1,0:T(8,128)(2,1)}, u32[]{:S(2)}, u32[]{:S(2)}) collective-permute-start(bf16[1024,512]{1,0:T(8,128)(2,1)} %get-tuple-element.122.refs_0_.refs_2_.refs_1_), channel_id=1, source_target_pairs={{0,2},{1,3},{2,0},{3,1},{4,6},{5,7},{6,4},{7,5},{8,10},{9,11},{10,... | collective-permute-start | bytes 3145736 | tf_op jit(solution)/shard_map/ppermute | solution.py:1230
  84.8 31.7 %collective-permute-start.7 = (bf16[512,2048]{1,0:T(8,128)(2,1)}, bf16[512,2048]{1,0:T(8,128)(2,1)}, u32[]{:S(2)}, u32[]{:S(2)}) collective-permute-start(bf16[512,2048]{1,0:T(8,128)(2,1)} %gate.9.refs_9_), channel_id=1, source_target_pairs={{0,1},{1,0},{2,3},{3,2},{4,5},{5,4},{6,7},{7,6},{8,9},{9,8},{10,11... | collective-permute-start | bytes 6291464 | tf_op jit(solution)/shard_map/ppermute | solution.py:1227
  114.5 45.5 %collective-permute-start.11 = (bf16[1024,512]{1,0:T(8,128)(2,1)}, bf16[1024,512]{1,0:T(8,128)(2,1)}, u32[]{:S(2)}, u32[]{:S(2)}) collective-permute-start(bf16[1024,512]{1,0:T(8,128)(2,1)} %gate.10.refs_17_.refs_19_), channel_id=1, source_target_pairs={{0,2},{1,3},{2,0},{3,1},{4,6},{5,7},{6,4},{7,5},{8,10},{9,11},{10,... | collective-permute-start | bytes 3145736 | tf_op jit(solution)/shard_map/ppermute | solution.py:1230
  115.9 47.4 %collective-permute-start.10 = (bf16[1024,512]{1,0:T(8,128)(2,1)}, bf16[1024,512]{1,0:T(8,128)(2,1)}, u32[]{:S(2)}, u32[]{:S(2)}) collective-permute-start(bf16[1024,512]{1,0:T(8,128)(2,1)} %get-tuple-element.134.refs_0_.refs_2_), channel_id=1, source_target_pairs={{0,2},{1,3},{2,0},{3,1},{4,6},{5,7},{6,4},{7,5},{8,10},{9,11},{10,... | collective-permute-start | bytes 3145736 | tf_op jit(solution)/shard_map/ppermute | solution.py:1230
  157.9 52.4 %collective-permute-start.12 = (bf16[1024,512]{1,0:T(8,128)(2,1)}, bf16[1024,512]{1,0:T(8,128)(2,1)}, u32[]{:S(2)}, u32[]{:S(2)}) collective-permute-start(bf16[1024,512]{1,0:T(8,128)(2,1)} %gate.11.refs_21_.refs_7_.refs_9_), channel_id=1, source_target_pairs={{0,2},{1,3},{2,0},{3,1},{4,6},{5,7},{6,4},{7,5},{8,10},{9,11},{10,... | collective-permute-start | bytes 3145736 | tf_op jit(solution)/shard_map/ppermute | solution.py:1230
  159.3 98.4 %collective-permute-start.9 = (bf16[1024,512]{1,0:T(8,128)(2,1)}, bf16[1024,512]{1,0:T(8,128)(2,1)}, u32[]{:S(2)}, u32[]{:S(2)}) collective-permute-start(bf16[1024,512]{1,0:T(8,128)(2,1)} %get-tuple-element.132), channel_id=1, source_target_pairs={{0,2},{1,3},{2,0},{3,1},{4,6},{5,7},{6,4},{7,5},{8,10},{9,11},{10,... | collective-permute-start | bytes 3145736 | tf_op jit(solution)/shard_map/ppermute | solution.py:1230
  208.8 102.1 %collective-permute-start.13 = (bf16[1024,512]{1,0:T(8,128)(2,1)}, bf16[1024,512]{1,0:T(8,128)(2,1)}, u32[]{:S(2)}, u32[]{:S(2)}) collective-permute-start(bf16[1024,512]{1,0:T(8,128)(2,1)} %get-tuple-element.147), channel_id=1, source_target_pairs={{0,2},{1,3},{2,0},{3,1},{4,6},{5,7},{6,4},{7,5},{8,10},{9,11},{10,... | collective-permute-start | bytes 3145736 | tf_op jit(solution)/shard_map/ppermute | solution.py:1230
  241.6 51.6 %collective-permute-start.14 = (bf16[1024,512]{1,0:T(8,128)(2,1)}, bf16[1024,512]{1,0:T(8,128)(2,1)}, u32[]{:S(2)}, u32[]{:S(2)}) collective-permute-start(bf16[1024,512]{1,0:T(8,128)(2,1)} %get-tuple-element.153), channel_id=1, source_target_pairs={{0,2},{1,3},{2,0},{3,1},{4,6},{5,7},{6,4},{7,5},{8,10},{9,11},{10,... | collective-permute-start | bytes 3145736 | tf_op jit(solution)/shard_map/ppermute | solution.py:1230
  242.3 49.4 %collective-permute-start.15 = (f32[8,1024]{1,0:T(8,128)}, f32[8,1024]{1,0:T(8,128)}, u32[]{:S(2)}, u32[]{:S(2)}) collective-permute-start(f32[8,1024]{1,0:T(8,128)} %get-tuple-element.154.refs_2_), channel_id=1, source_target_pairs={{0,2},{1,3},{2,0},{3,1},{4,6},{5,7},{6,4},{7,5},{8,10},{9,11},{10,... | collective-permute-start | bytes 98312 | tf_op jit(solution)/shard_map/ppermute | solution.py:1230
  257.2 148.7 %collective-permute-start.20 = (bf16[4,2048,256]{2,1,0:T(8,128)(2,1)}, bf16[4,2048,256]{2,1,0:T(8,128)(2,1)}, u32[]{:S(2)}, u32[]{:S(2)}) collective-permute-start(bf16[4,2048,256]{2,1,0:T(8,128)(2,1)} %weight_blocks.12.refs_1_), channel_id=1, source_target_pairs={{0,4},{4,0},{8,12},{12,8},{16,20},{20,16},{24,28},{28,24},{1,5},{5... | collective-permute-start | bytes 12582920 | tf_op jit(solution)/shard_map/ppermute | solution.py:1120
  288.3 68.2 %collective-permute-start.17 = (bf16[1024,512]{1,0:T(8,128)(2,1)}, bf16[1024,512]{1,0:T(8,128)(2,1)}, u32[]{:S(2)}, u32[]{:S(2)}) collective-permute-start(bf16[1024,512]{1,0:T(8,128)(2,1)} %get-tuple-element.160), channel_id=1, source_target_pairs={{0,2},{1,3},{2,0},{3,1},{4,6},{5,7},{6,4},{7,5},{8,10},{9,11},{10,... | collective-permute-start | bytes 3145736 | tf_op jit(solution)/shard_map/ppermute | solution.py:1230
  291.7 64.8 %collective-permute-start.18 = (f32[8,1024]{1,0:T(8,128)}, f32[8,1024]{1,0:T(8,128)}, u32[]{:S(2)}, u32[]{:S(2)}) collective-permute-start(f32[8,1024]{1,0:T(8,128)} %get-tuple-element.155.refs_8_.refs_2_), channel_id=1, source_target_pairs={{0,2},{1,3},{2,0},{3,1},{4,6},{5,7},{6,4},{7,5},{8,10},{9,11},{10,... | collective-permute-start | bytes 98312 | tf_op jit(solution)/shard_map/ppermute | solution.py:1230
  309.4 85.6 %collective-permute-start.21 = (bf16[4,256,1024]{2,1,0:T(8,128)(2,1)}, bf16[4,256,1024]{2,1,0:T(8,128)(2,1)}, u32[]{:S(2)}, u32[]{:S(2)}) collective-permute-start(bf16[4,256,1024]{2,1,0:T(8,128)(2,1)} %weight_blocks.13.refs_1_), channel_id=1, source_target_pairs={{0,8},{4,12},{8,0},{12,4},{16,24},{20,28},{24,16},{28,20},{1,9},{5... | collective-permute-start | bytes 6291464 | tf_op jit(solution)/shard_map/ppermute | solution.py:1120
  321.1 24.9 %collective-permute-start.16 = (bf16[1024,512]{1,0:T(8,128)(2,1)}, bf16[1024,512]{1,0:T(8,128)(2,1)}, u32[]{:S(2)}, u32[]{:S(2)}) collective-permute-start(bf16[1024,512]{1,0:T(8,128)(2,1)} %get-tuple-element.157.refs_0_.refs_2_), channel_id=1, source_target_pairs={{0,2},{1,3},{2,0},{3,1},{4,6},{5,7},{6,4},{7,5},{8,10},{9,11},{10,... | collective-permute-start | bytes 3145736 | tf_op jit(solution)/shard_map/ppermute | solution.py:1230
  346.0 130.1 %collective-permute-start.24 = (bf16[4,256,1024]{2,1,0:T(8,128)(2,1)}, bf16[4,256,1024]{2,1,0:T(8,128)(2,1)}, u32[]{:S(2)}, u32[]{:S(2)}) collective-permute-start(bf16[4,256,1024]{2,1,0:T(8,128)(2,1)} %weight_blocks.14.refs_11_), channel_id=1, source_target_pairs={{0,4},{4,0},{8,12},{12,8},{16,20},{20,16},{24,28},{28,24},{1,5},{5... | collective-permute-start | bytes 6291464 | tf_op jit(solution)/shard_map/ppermute | solution.py:1120
  374.6 38.3 %collective-permute-start.19 = (bf16[1024,512]{1,0:T(8,128)(2,1)}, bf16[1024,512]{1,0:T(8,128)(2,1)}, u32[]{:S(2)}, u32[]{:S(2)}) collective-permute-start(bf16[1024,512]{1,0:T(8,128)(2,1)} %get-tuple-element.163.refs_0_.refs_2_), channel_id=1, source_target_pairs={{0,2},{1,3},{2,0},{3,1},{4,6},{5,7},{6,4},{7,5},{8,10},{9,11},{10,... | collective-permute-start | bytes 3145736 | tf_op jit(solution)/shard_map/ppermute | solution.py:1230
  390.8 155.4 %collective-permute-start.27 = (bf16[1024,512]{1,0:T(8,128)(2,1)}, bf16[1024,512]{1,0:T(8,128)(2,1)}, u32[]{:S(2)}, u32[]{:S(2)}) collective-permute-start(bf16[1024,512]{1,0:T(8,128)(2,1)} %get-tuple-element.181), channel_id=1, source_target_pairs={{0,2},{1,3},{2,0},{3,1},{4,6},{5,7},{6,4},{7,5},{8,10},{9,11},{10,... | collective-permute-start | bytes 3145736 | tf_op jit(solution)/shard_map/ppermute | solution.py:1230
  395.0 149.7 %collective-permute-start.28 = (f32[8,1024]{1,0:T(8,128)}, f32[8,1024]{1,0:T(8,128)}, u32[]{:S(2)}, u32[]{:S(2)}) collective-permute-start(f32[8,1024]{1,0:T(8,128)} %get-tuple-element.166.refs_12_.refs_3_), channel_id=1, source_target_pairs={{0,2},{1,3},{2,0},{3,1},{4,6},{5,7},{6,4},{7,5},{8,10},{9,11},{10,... | collective-permute-start | bytes 98312 | tf_op jit(solution)/shard_map/ppermute | solution.py:1230
  405.9 81.9 %collective-permute-start.23 = (bf16[2,256,1024]{2,1,0:T(8,128)(2,1)}, bf16[2,256,1024]{2,1,0:T(8,128)(2,1)}, u32[]{:S(2)}, u32[]{:S(2)}) collective-permute-start(bf16[2,256,1024]{2,1,0:T(8,128)(2,1)} %get-tuple-element.171), channel_id=1, source_target_pairs={{0,16},{4,20},{8,24},{12,28},{16,0},{20,4},{24,8},{28,12},{1,17},{... | collective-permute-start | bytes 3145736 | tf_op jit(solution)/shard_map/ppermute | solution.py:1120
  469.4 92.6 %collective-permute-start.32 = (bf16[4,256,768]{2,1,0:T(8,128)(2,1)}, bf16[4,256,768]{2,1,0:T(8,128)(2,1)}, u32[]{:S(2)}, u32[]{:S(2)}) collective-permute-start(bf16[4,256,768]{2,1,0:T(8,128)(2,1)} %weight_blocks.17.refs_11_), channel_id=1, source_target_pairs={{0,4},{4,0},{8,12},{12,8},{16,20},{20,16},{24,28},{28,24},{1,5},{5... | collective-permute-start | bytes 4718600 | tf_op jit(solution)/shard_map/ppermute | solution.py:1120
  476.1 48.8 %collective-permute-start.22 = (bf16[2,2048,256]{2,1,0:T(8,128)(2,1)}, bf16[2,2048,256]{2,1,0:T(8,128)(2,1)}, u32[]{:S(2)}, u32[]{:S(2)}) collective-permute-start(bf16[2,2048,256]{2,1,0:T(8,128)(2,1)} %get-tuple-element.170), channel_id=1, source_target_pairs={{0,8},{4,12},{8,0},{12,4},{16,24},{20,28},{24,16},{28,20},{1,9},{5... | collective-permute-start | bytes 6291464 | tf_op jit(solution)/shard_map/ppermute | solution.py:1120
  487.7 84.9 %collective-permute-start.31 = (bf16[4,256,768]{2,1,0:T(8,128)(2,1)}, bf16[4,256,768]{2,1,0:T(8,128)(2,1)}, u32[]{:S(2)}, u32[]{:S(2)}) collective-permute-start(bf16[4,256,768]{2,1,0:T(8,128)(2,1)} %weight_blocks.18.refs_11_), channel_id=1, source_target_pairs={{0,8},{4,12},{8,0},{12,4},{16,24},{20,28},{24,16},{28,20},{1,9},{5... | collective-permute-start | bytes 4718600 | tf_op jit(solution)/shard_map/ppermute | solution.py:1120
  524.9 77.8 %collective-permute-start.30 = (bf16[4,512,256]{2,1,0:T(8,128)(2,1)}, bf16[4,512,256]{2,1,0:T(8,128)(2,1)}, u32[]{:S(2)}, u32[]{:S(2)}) collective-permute-start(bf16[4,512,256]{2,1,0:T(8,128)(2,1)} %weight_blocks.19.refs_12_), channel_id=1, source_target_pairs={{0,8},{4,12},{8,0},{12,4},{16,24},{20,28},{24,16},{28,20},{1,9},{5... | collective-permute-start | bytes 3145736 | tf_op jit(solution)/shard_map/ppermute | solution.py:1120
  544.7 66.4 %collective-permute-start.26 = (f32[8,1024]{1,0:T(8,128)}, f32[8,1024]{1,0:T(8,128)}, u32[]{:S(2)}, u32[]{:S(2)}) collective-permute-start(f32[8,1024]{1,0:T(8,128)} %get-tuple-element.174.refs_11_.refs_3_), channel_id=1, source_target_pairs={{0,2},{1,3},{2,0},{3,1},{4,6},{5,7},{6,4},{7,5},{8,10},{9,11},{10,... | collective-permute-start | bytes 98312 | tf_op jit(solution)/shard_map/ppermute | solution.py:1230
  546.3 56.4 %collective-permute-start.29 = (bf16[2,256,1024]{2,1,0:T(8,128)(2,1)}, bf16[2,256,1024]{2,1,0:T(8,128)(2,1)}, u32[]{:S(2)}, u32[]{:S(2)}) collective-permute-start(bf16[2,256,1024]{2,1,0:T(8,128)(2,1)} %get-tuple-element.184), channel_id=1, source_target_pairs={{0,8},{4,12},{8,0},{12,4},{16,24},{20,28},{24,16},{28,20},{1,9},{5... | collective-permute-start | bytes 3145736 | tf_op jit(solution)/shard_map/ppermute | solution.py:1120
  562.1 49.1 %collective-permute-start.25 = (bf16[1024,512]{1,0:T(8,128)(2,1)}, bf16[1024,512]{1,0:T(8,128)(2,1)}, u32[]{:S(2)}, u32[]{:S(2)}) collective-permute-start(bf16[1024,512]{1,0:T(8,128)(2,1)} %get-tuple-element.178), channel_id=1, source_target_pairs={{0,2},{1,3},{2,0},{3,1},{4,6},{5,7},{6,4},{7,5},{8,10},{9,11},{10,... | collective-permute-start | bytes 3145736 | tf_op jit(solution)/shard_map/ppermute | solution.py:1230
  606.8 72.8 %collective-permute-start.43 = (bf16[2,512,256]{2,1,0:T(8,128)(2,1)}, bf16[2,512,256]{2,1,0:T(8,128)(2,1)}, u32[]{:S(2)}, u32[]{:S(2)}) collective-permute-start(bf16[2,512,256]{2,1,0:T(8,128)(2,1)} %get-tuple-element.206), channel_id=1, source_target_pairs={{0,16},{4,20},{8,24},{12,28},{16,0},{20,4},{24,8},{28,12},{1,17},{... | collective-permute-start | bytes 1572872 | tf_op jit(solution)/shard_map/ppermute | solution.py:1120
  608.9 72.4 %collective-permute-start.42 = (bf16[2,256,768]{2,1,0:T(8,128)(2,1)}, bf16[2,256,768]{2,1,0:T(8,128)(2,1)}, u32[]{:S(2)}, u32[]{:S(2)}) collective-permute-start(bf16[2,256,768]{2,1,0:T(8,128)(2,1)} %get-tuple-element.204), channel_id=1, source_target_pairs={{0,16},{4,20},{8,24},{12,28},{16,0},{20,4},{24,8},{28,12},{1,17},{... | collective-permute-start | bytes 2359304 | tf_op jit(solution)/shard_map/ppermute | solution.py:1120
  609.8 71.4 %collective-permute-start.41 = (bf16[2,256,768]{2,1,0:T(8,128)(2,1)}, bf16[2,256,768]{2,1,0:T(8,128)(2,1)}, u32[]{:S(2)}, u32[]{:S(2)}) collective-permute-start(bf16[2,256,768]{2,1,0:T(8,128)(2,1)} %get-tuple-element.203), channel_id=1, source_target_pairs={{0,8},{4,12},{8,0},{12,4},{16,24},{20,28},{24,16},{28,20},{1,9},{5... | collective-permute-start | bytes 2359304 | tf_op jit(solution)/shard_map/ppermute | solution.py:1120
  627.0 2.1 collective-permute-start.33
  629.2 3.5 collective-permute-start.34
  634.7 3.8 collective-permute-start.35
  639.2 19.5 %collective-permute-start.36 = (f32[40,128]{1,0:T(8,128)S(1)}, f32[40,128]{1,0:T(8,128)S(1)}, u32[]{:S(2)}, u32[]{:S(2)}) collective-permute-start(f32[40,128]{1,0:T(8,128)S(1)} %fusion), channel_id=1, source_target_pairs={{0,8},{4,12},{8,0},{12,4},{16,24},{20,28},{24,16},{28,20},{1,9},{5... | collective-permute-start | bytes 61448 | tf_op jit(solution)/shard_map/ppermute | solution.py:1286
  659.5 19.6 %collective-permute-start.37 = (f32[40,128]{1,0:T(8,128)S(1)}, f32[40,128]{1,0:T(8,128)S(1)}, u32[]{:S(2)}, u32[]{:S(2)}) collective-permute-start(f32[40,128]{1,0:T(8,128)S(1)} %fusion.4), channel_id=1, source_target_pairs={{0,16},{4,20},{8,24},{12,28},{16,0},{20,4},{24,8},{28,12},{1,17},{... | collective-permute-start | bytes 61448 | tf_op jit(solution)/shard_map/ppermute | solution.py:1286
  659.5 61.8 %collective-permute-start.39 = (bf16[1,256,1024]{2,1,0:T(8,128)(2,1)}, bf16[1,256,1024]{2,1,0:T(8,128)(2,1)}, u32[]{:S(2)}, u32[]{:S(2)}) collective-permute-start(bf16[1,256,1024]{2,1,0:T(8,128)(2,1)} %get-tuple-element.201), channel_id=1, source_target_pairs={{0,16},{4,20},{8,24},{12,28},{16,0},{20,4},{24,8},{28,12},{1,17},{... | collective-permute-start | bytes 1572872 | tf_op jit(solution)/shard_map/ppermute | solution.py:1120
  679.1 64.7 %collective-permute-start.38 = (bf16[1,2048,256]{2,1,0:T(8,128)(2,1)}, bf16[1,2048,256]{2,1,0:T(8,128)(2,1)}, u32[]{:S(2)}, u32[]{:S(2)}) collective-permute-start(bf16[1,2048,256]{2,1,0:T(8,128)(2,1)} %get-tuple-element.200), channel_id=1, source_target_pairs={{0,16},{4,20},{8,24},{12,28},{16,0},{20,4},{24,8},{28,12},{1,17},{... | collective-permute-start | bytes 3145736 | tf_op jit(solution)/shard_map/ppermute | solution.py:1120
  679.7 44.9 %collective-permute-start.40 = (bf16[1,256,1024]{2,1,0:T(8,128)(2,1)}, bf16[1,256,1024]{2,1,0:T(8,128)(2,1)}, u32[]{:S(2)}, u32[]{:S(2)}) collective-permute-start(bf16[1,256,1024]{2,1,0:T(8,128)(2,1)} %get-tuple-element.202), channel_id=1, source_target_pairs={{0,4},{4,0},{8,12},{12,8},{16,20},{20,16},{24,28},{28,24},{1,5},{5... | collective-permute-start | bytes 1572872 | tf_op jit(solution)/shard_map/ppermute | solution.py:1120
  685.5 65.7 %collective-permute-start.45 = (bf16[1,256,768]{2,1,0:T(8,128)(2,1)}, bf16[1,256,768]{2,1,0:T(8,128)(2,1)S(1)}, u32[]{:S(2)}, u32[]{:S(2)}) collective-permute-start(bf16[1,256,768]{2,1,0:T(8,128)(2,1)} %get-tuple-element.210), channel_id=1, source_target_pairs={{0,16},{4,20},{8,24},{12,28},{16,0},{20,4},{24,8},{28,12},{1,17},{... | collective-permute-start | bytes 1179656 | tf_op jit(solution)/shard_map/ppermute | solution.py:1120
  688.4 62.7 %collective-permute-start.46 = (bf16[1,256,768]{2,1,0:T(8,128)(2,1)}, bf16[1,256,768]{2,1,0:T(8,128)(2,1)S(1)}, u32[]{:S(2)}, u32[]{:S(2)}) collective-permute-start(bf16[1,256,768]{2,1,0:T(8,128)(2,1)} %get-tuple-element.212), channel_id=1, source_target_pairs={{0,4},{4,0},{8,12},{12,8},{16,20},{20,16},{24,28},{28,24},{1,5},{5... | collective-permute-start | bytes 1179656 | tf_op jit(solution)/shard_map/ppermute | solution.py:1120
  721.3 6.6 collective-permute-start.44
  (22 other events, 384.1 us)
Sparse Core Ops, SparseCore 0:
  35.0 49.7 all-gather.1

commit v5 on v4

--- a/solution.py
+++ b/solution.py
@@ -35,6 +35,7 @@
 class Order:
     last = None
     names = 0
+    cost = 10**12
 
     @staticmethod
     def name(remote):
@@ -67,7 +68,7 @@
         compiler_params=pltpu.CompilerParams(
             vmem_limit_bytes=60 * MIB, collective_id=Order.name(remote), has_side_effects=remote
         ),
-        cost_estimate=pl.CostEstimate(flops=10**12, bytes_accessed=10**8, transcendentals=0),
+        cost_estimate=pl.CostEstimate(flops=Order.cost, bytes_accessed=Order.cost // 10**4, transcendentals=0),
         name=name,
     )(*args, *extra)
     fresh = [v for i, v in enumerate(got) if i not in (aliases or {}).values()]
@@ -344,11 +345,14 @@
 
 
 def average_body(weights, history, wide, low):
-    total = weights[0] * history[0].astype(F32)
-    for j in range(1, history.shape[0]):
-        total += weights[j] * history[j].astype(F32)
-    wide[...] = total
-    low[...] = total.astype(BF16)
+    chunk = min(32, wide.shape[0])
+    for t in range(wide.shape[0] // chunk):
+        rows = slice(t * chunk, (t + 1) * chunk)
+        total = weights[0] * history[0, rows, :].astype(F32)
+        for j in range(1, history.shape[0]):
+            total += weights[j] * history[j, rows, :].astype(F32)
+        wide[rows, :] = total
+        low[rows, :] = total.astype(BF16)
 
 
 def average(weights, history, row, length):
@@ -535,28 +539,21 @@
     )[0]
 
 
-def feed_body(n, pairs, beside, steps, *refs):
+def feed_body(n, pairs, steps, *refs):
     count = 4 if pairs else n
     attended = Gathered(refs[:count], pairs, steps)
     refs = refs[count:]
     xs, outs_w = refs[: n - 1], refs[n - 1 : 2 * n - 1]
     own, gain, bias, up_bias, up_weight, down_weight = refs[2 * n - 1 : 2 * n + 5]
     refs = refs[2 * n + 5 :]
-    extra = None
-    if beside:
-        extra, refs = Gathered(refs[:count], pairs, steps), refs[count:]
     hidden, normed, stat, activated, slope = refs[:5]
     refs = refs[5:]
     parts = Scattered(pairs, n, steps, False)
     part_outs, refs = refs[: parts.count()], refs[parts.count() :]
-    if beside:
-        joined_outs, refs = refs[:2], refs[2:]
     out_held, up_held, down_held, joined, whole, sems, *refs = refs
     if pairs:
         attended.attach(refs[:2])
-        if beside:
-            extra.attach(refs[2:4])
-        refs = refs[2 + 2 * beside :]
+        refs = refs[2:]
     parts.attach(part_outs, refs)
     me = lax.axis_index("mp")
     width = own.shape[1]
@@ -578,8 +575,6 @@
     def work(wait):
         for j, one in enumerate(attended.refs()):
             joined[:, j * width : (j + 1) * width] = one[...]
-        if beside:
-            put_beside(me, extra.refs(), *joined_outs)
         total = square = 0.0
         for j in range(n):
             wait(out_copies[j * n : (j + 1) * n])
@@ -611,22 +606,11 @@
         for j in range(n):
             parts.put(j, dot_nn(activated[...], down_held[:, j * width : (j + 1) * width]))
 
-    with_weights(
-        out_copies + up_copies + down_copies, work, pairs, [attended] + ([extra] if beside else [])
-    )
+    with_weights(out_copies + up_copies + down_copies, work, pairs, [attended])
     parts.finish()
 
 
-def put_beside(me, blocks, whole, sums):
-    width = blocks[0].shape[1]
-    for j, block in enumerate(blocks):
-        whole[:, place_of(me, j, width)] = block[...]
-    accumulate(sums, fold_rows(blocks[0][...].astype(F32)))
-
-
-def feed(
-    n, pairs, attended, xs, outs_w, own, gain, bias, up_bias, up_weight, down_weight, beside=()
-):
+def feed(n, pairs, attended, xs, outs_w, own, gain, bias, up_bias, up_weight, down_weight):
     length, width = own.shape
     full, inner = up_weight.shape
     tile = min(256, length)
@@ -634,10 +618,9 @@
     parts = Scattered(pairs, n, steps, False)
     part_outs, part_specs = parts.outs(length, width)
     twice = tuple(attended) if pairs else ()
-    extra = (*beside, *(beside if pairs else ()))
     got = call(
         "feed",
-        lambda *refs: feed_body(n, pairs, bool(beside), steps, *refs),
+        lambda *refs: feed_body(n, pairs, steps, *refs),
         (steps,),
         (
             *attended,
@@ -650,7 +633,6 @@
             up_bias,
             up_weight,
             down_weight,
-            *extra,
         ),
         Gathered.specs(attended, pairs, tile)
         + [rows_of((tile, width))] * (n - 1)
@@ -658,8 +640,7 @@
         + [rows_of((tile, width))]
         + [fixed((8, full))] * 2
         + [fixed((8, inner))]
-        + [ANY] * 2
-        + (Gathered.specs(beside, pairs, tile) if beside else []),
+        + [ANY] * 2,
         [
             shape((length, width), F32),
             shape((length, full), BF16),
@@ -667,8 +648,7 @@
             shape((length, inner), BF16),
             shape((length, inner), BF16),
         ]
-        + part_outs
-        + ([shape((length, full), BF16), shape((8, width), F32)] if beside else []),
+        + part_outs,
         [
             rows_of((tile, width)),
             rows_of((tile, full)),
@@ -676,8 +656,7 @@
             rows_of((tile, inner)),
             rows_of((tile, inner)),
         ]
-        + part_specs
-        + ([rows_of((tile, full)), fixed((8, width))] if beside else []),
+        + part_specs,
         scratch=[
             pltpu.VMEM((full, full), BF16),
             pltpu.VMEM((full, inner), BF16),
@@ -687,11 +666,10 @@
             pltpu.SemaphoreType.DMA((n * n + 2 * n,)),
         ]
         + Gathered.scratch(attended, pairs, steps)
-        + (Gathered.scratch(beside, pairs, steps) if beside else [])
         + parts.scratch(length, width),
         remote=pairs,
     )
-    return (*got[:5], got[5 : 5 + parts.count()], got[5 + parts.count() :])
+    return (*got[:5], got[5:])
 
 
 def row_stats(total, weighted):
@@ -711,39 +689,45 @@
     return row_stats(total, weighted)
 
 
-def feed_back_body(n, pairs, beside, steps, *refs):
-    cot, slope, normed, gain, bias, up_weight, down_weight = refs[:7]
-    refs = refs[7:]
-    count = 4 if pairs else n
-    extra = None
-    if beside:
-        extra, refs = Gathered(refs[:count], pairs, steps), refs[count:]
-    up_grad, up_bias_sum = refs[:2]
-    refs = refs[2:]
+def feed_back_body(n, pairs, steps, held_in, passed, *refs):
+    count = n if held_in or not pairs else 4
+    cots, refs = Gathered(refs[:count], pairs and not held_in, steps), refs[count:]
+    others = []
+    for _ in range(passed):
+        others.append(Gathered(refs[:4], pairs, steps))
+        refs = refs[4:]
+    slope, normed, gain, bias, up_weight, down_weight, up_grad, up_bias_sum, cot_sum = refs[:9]
+    refs = refs[9:]
     parts = Scattered(pairs, n, steps, True)
     part_outs, refs = refs[: parts.count()], refs[parts.count() :]
-    if beside:
-        joined_outs, refs = refs[:2], refs[2:]
-    up_held, down_held, row_sums, sems, *refs = refs
-    if pairs and beside:
-        extra.attach(refs[:2])
+    fetched = ([] if held_in or not pairs else [cots]) + others
+    shared, refs = refs[: 2 * len(fetched)], refs[2 * len(fetched) :]
+    up_held, down_held, joined, row_sums, sems, *refs = refs
+    for one in fetched:
+        one.attach(refs[:2])
         refs = refs[2:]
     parts.attach(part_outs, refs)
     me = lax.axis_index("mp")
     inner = up_held.shape[1]
     width = gain.shape[1] // n
     step = divisor(inner, 512)
-    down_copies = [pltpu.make_async_copy(down_weight, down_held, sems.at[n])]
+    down_copies = col_blocks(me, n, width, down_weight, down_held, sems, n)
     up_copies = row_blocks(me, n, width, up_weight, up_held, sems, 0)
 
     def work(wait):
-        if beside:
-            put_beside(me, extra.refs(), *joined_outs)
+        blocks = cots.refs()
+        for j, block in enumerate(blocks):
+            joined[:, j * width : (j + 1) * width] = block[...]
+        for i, one in enumerate(fetched):
+            there = blocks if one is cots else one.refs()
+            shared[2 * i][...] = there[1][...]
+            shared[2 * i + 1][...] = there[3][...]
+        accumulate(cot_sum, fold_rows(blocks[0][...].astype(F32)))
         wait(down_copies)
         bias_parts = []
         for c in range(inner // step):
             part = slice(c * step, (c + 1) * step)
-            value = dot_nt(cot[...], down_held[part, :]) * slope[:, part].astype(F32)
+            value = dot_nt(joined[...], down_held[part, :]) * slope[:, part].astype(F32)
             low = value.astype(BF16)
             up_grad[:, part] = low
             bias_parts.append(fold_rows(low.astype(F32)))
@@ -759,54 +743,57 @@
             me,
         )
 
-    with_weights(down_copies + up_copies, work, pairs, [extra] if beside else [])
+    with_weights(down_copies + up_copies, work, pairs, fetched)
     parts.finish(row_sums[...])
 
 
-def feed_back(n, pairs, cot, slope, normed, gain, bias, up_weight, down_weight, beside=()):
-    length, full = cot.shape
+def feed_back(n, pairs, cots, others, slope, normed, gain, bias, up_weight, down_weight):
+    length, full = normed.shape
     width = full // n
     inner = up_weight.shape[1]
     tile = min(256, length)
     steps = length // tile
+    held_in = pairs and len(cots) == n
+    others = others if pairs else []
+    fetch = ([] if held_in or not pairs else [cots]) + others
     parts = Scattered(pairs, n, steps, True)
     part_outs, part_specs = parts.outs(length, width)
+    args = [*cots, *(cots if pairs and not held_in else ())]
+    specs = Gathered.specs(cots, pairs and not held_in, tile)
+    for one in others:
+        args += [*one, *one]
+        specs += Gathered.specs(one, pairs, tile)
     got = call(
         "feed_back",
-        lambda *refs: feed_back_body(n, pairs, bool(beside), steps, *refs),
+        lambda *refs: feed_back_body(n, pairs, steps, held_in, len(others), *refs),
         (steps,),
-        (
-            cot,
-            slope,
-            normed,
-            gain,
-            bias,
-            up_weight,
-            down_weight,
-            *beside,
-            *(beside if pairs else ()),
-        ),
-        [rows_of((tile, full)), rows_of((tile, inner)), rows_of((tile, full))]
+        (*args, slope, normed, gain, bias, up_weight, down_weight),
+        specs
+        + [rows_of((tile, inner)), rows_of((tile, full))]
         + [fixed((8, full))] * 2
-        + [ANY] * 2
-        + (Gathered.specs(beside, pairs, tile) if beside else []),
-        [shape((length, inner), BF16), shape((8, inner), F32)]
+        + [ANY] * 2,
+        [shape((length, inner), BF16), shape((8, inner), F32), shape((8, width), F32)]
         + part_outs
-        + ([shape((length, full), BF16), shape((8, width), F32)] if beside else []),
-        [rows_of((tile, inner)), fixed((8, inner))]
+        + [shape((length, width), BF16)] * (2 * len(fetch)),
+        [rows_of((tile, inner)), fixed((8, inner)), fixed((8, width))]
         + part_specs
-        + ([rows_of((tile, full)), fixed((8, width))] if beside else []),
+        + [rows_of((tile, width))] * (2 * len(fetch)),
         scratch=[
             pltpu.VMEM((full, inner), BF16),
             pltpu.VMEM((inner, full), BF16),
+            pltpu.VMEM((tile, full), BF16),
             pltpu.VMEM((8, tile), F32),
-            pltpu.SemaphoreType.DMA((n + 1,)),
+            pltpu.SemaphoreType.DMA((2 * n,)),
         ]
-        + (Gathered.scratch(beside, pairs, steps) if beside else [])
+        + sum([Gathered.scratch(one, pairs, steps) for one in fetch], [])
         + parts.scratch(length, width),
         remote=pairs,
     )
-    return (*got[:2], got[2 : 2 + parts.count()], got[2 + parts.count() :])
+    got, shared = got[: 3 + parts.count()], got[3 + parts.count() :]
+    blocks = [
+        [one[0], shared[2 * i], one[1], shared[2 * i + 1]] for i, one in enumerate(fetch)
+    ]
+    return (*got[:3], got[3:], blocks)
 
 
 def norm_back(refs, n_parts, source, stat, sums, gain, full):
@@ -938,19 +925,24 @@
 def average_back_body(k, m, full, count, *refs):
     weights, parts, sums = refs[0], refs[1 : k + 1], refs[k + 1 : k + m + 1]
     source, stat, gain, hidden_grad, history = refs[k + m + 1 : k + m + 6]
-    grad_history, depth_sum, gain_sum, bias_sum = refs[-4:]
+    grad_history, depth_sum, gain_sum, bias_sum, held = refs[-5:]
     back, gain_part, bias_part = norm_back(parts, k, source, stat, sums, gain, full)
-    value = hidden_grad[...] + back
+    held[...] = hidden_grad[...] + back
     accumulate(gain_sum, gain_part)
     accumulate(bias_sum, bias_part)
-    lanes = value.shape[1] // 128
+    lanes = held.shape[1] // 128
+    chunk = min(32, held.shape[0])
+    folded = [0.0] * count
+    for t in range(held.shape[0] // chunk):
+        rows = slice(t * chunk, (t + 1) * chunk)
+        value = held[rows, :]
+        for j in range(count):
+            grad_history[j, rows, :] = (weights[j] * value).astype(BF16)
+            product = fold_rows(value * history[j, rows, :].astype(F32))
+            for c in range(lanes):
+                folded[j] = folded[j] + product[:, c * 128 : (c + 1) * 128]
     for j in range(count):
-        grad_history[j] = (weights[j] * value).astype(BF16)
-        product = fold_rows(value * history[j].astype(F32))
-        folded = product[:, 0:128]
-        for c in range(1, lanes):
-            folded += product[:, c * 128 : (c + 1) * 128]
-        accumulate(depth_sum.at[j], folded)
+        accumulate(depth_sum.at[j], folded[j])
 
 
 def average_back(weights, parts, source, stat, sums, gain, hidden_grad, history, row, made):
@@ -979,6 +971,7 @@
         specs,
         [shape(history.shape, BF16), shape((count, 8, 128), F32)] + [shape((8, width), F32)] * 2,
         [block, fixed((count, 8, 128))] + [fixed((8, width))] * 2,
+        scratch=[pltpu.VMEM((tile, width), F32)],
         **more,
     )
 
@@ -997,7 +990,7 @@
 
 def weight_grad(lefts, rights):
     rows, (length, high), wide = len(lefts), lefts[0].shape, rights[0].shape[1]
-    tall, across = divisor(high, 512), divisor(wide, 1024)
+    tall, across = divisor(high, 1024), divisor(wide, 1024)
     return call(
         "weight_grad",
         lambda *refs: weight_body(rows, *refs),
@@ -1007,6 +1000,34 @@
         + [pl.BlockSpec((length, across), lambda i, j: (0, j))] * rows,
         [shape((high, wide), BF16)],
         [pl.BlockSpec((tall, across), lambda i, j: (i, j))],
+    )[0]
+
+
+def weight_of_blocks_body(rows, n, me, *refs):
+    lefts, rights, out = refs[:rows], refs[rows:-1], refs[-1]
+    width = rights[0].shape[1]
+    turned = [left[...].T for left in lefts]
+    for j in range(n):
+        total = 0.0
+        for r in range(rows):
+            total += dot_nn(turned[r], rights[r * n + j][...])
+        out[:, place_of(me[0], j, width)] = total.astype(BF16)
+
+
+def weight_of_blocks(me, lefts, rights):
+    rows, n, (length, high) = len(lefts), len(rights[0]), lefts[0].shape
+    width = rights[0][0].shape[1]
+    tall = divisor(high, 512)
+    return call(
+        "weight_grad",
+        lambda *refs: weight_of_blocks_body(rows, n, *refs),
+        (high // tall,),
+        (me, *lefts, *sum(rights, [])),
+        [SMEM]
+        + [pl.BlockSpec((length, tall), lambda i: (0, i))] * rows
+        + [fixed((length, width))] * (rows * n),
+        [shape((high, n * width), BF16)],
+        [rows_of((tall, n * width))],
     )[0]
 
 
@@ -1158,10 +1179,12 @@
     outs = refs[len(refs) - len(groups) :]
     at = 0
     for out, group in zip(outs, groups):
-        for first, wide in group:
-            total = refs[at][0].astype(F32) + refs[at + 1][0].astype(F32)
+        for first, wide, count in group:
+            total = refs[at][0].astype(F32)
+            for ref in refs[at + 1 : at + count]:
+                total += ref[0].astype(F32)
             out[:, first : first + wide] = total
-            at += 2
+            at += count
 
 
 def finish(*groups):
@@ -1170,15 +1193,86 @@
     for group in groups:
         first, place = 0, []
         for one in group:
-            _, high, wide = one.held.shape
-            args += [one.held, one.coming]
-            specs += [pl.BlockSpec((1, high // steps, wide), lambda i: (0, i, 0))] * 2
-            place.append((first, wide))
+            terms = [one.held, one.coming] if isinstance(one, Spread) else [one[None]]
+            _, high, wide = terms[0].shape
+            args += terms
+            specs += [pl.BlockSpec((1, high // steps, wide), lambda i: (0, i, 0))] * len(terms)
+            place.append((first, wide, len(terms)))
             first += wide
         outs.append(shape((high, first), F32))
         out_specs.append(rows_of((high // steps, first)))
         places.append(place)
     return call("finish", lambda *refs: finish_body(places, *refs), (steps,), args, specs, outs, out_specs)
+
+
+def sums_body(groups, n, own, out, total, came, far, dp_sems, mp_sems):
+    me = {"dp": lax.axis_index("dp"), "mp": lax.axis_index("mp")}
+    peers = [("dp", b) for b in range(1, groups)] + [("mp", b) for b in range(1, n)]
+    barrier = pltpu.get_barrier_semaphore()
+    for axis, b in peers:
+        pl.semaphore_signal(
+            barrier, inc=1, device_id={axis: flip(me[axis], b)}, device_id_type=pl.DeviceIdType.MESH
+        )
+    pl.semaphore_wait(barrier, len(peers))
+
+    def copy(axis, b, source, target, sems):
+        return pltpu.make_async_remote_copy(
+            src_ref=source,
+            dst_ref=target.at[b - 1],
+            send_sem=sems.at[0, b - 1],
+            recv_sem=sems.at[1, b - 1],
+            device_id={axis: flip(me[axis], b)},
+            device_id_type=pl.DeviceIdType.MESH,
+        )
+
+    copies = [copy("dp", b, own, came, dp_sems) for b in range(1, groups)]
+    for one in copies:
+        one.start()
+    for one in copies:
+        one.wait()
+    value = own[...]
+    for b in range(groups - 1):
+        value = value + came[b]
+    out[...] = value
+    total[...] = value[-8:]
+    copies = [copy("mp", b, total, far, mp_sems) for b in range(1, n)]
+    for one in copies:
+        one.start()
+    for one in copies:
+        one.wait()
+    value = total[...]
+    for b in range(n - 1):
+        value = value + far[b]
+    out[-8:, :] = value
+
+
+def sums(vectors, depth):
+    groups, n = lax.axis_size("dp"), lax.axis_size("mp")
+    sizes = [v.size for v in vectors]
+    packed = jnp.concatenate(vectors)
+    packed = jnp.pad(packed, (0, -packed.size % 1024)).reshape(-1, 128)
+    packed = jnp.concatenate([packed, jnp.pad(depth[None], ((0, 7), (0, 128 - depth.size)))])
+    high = packed.shape[0]
+    got = call(
+        "sums",
+        lambda *refs: sums_body(groups, n, *refs),
+        (1,),
+        (packed,),
+        [fixed((high, 128))],
+        [shape((high, 128), F32)],
+        [fixed((high, 128))],
+        scratch=[
+            pltpu.VMEM((8, 128), F32),
+            pltpu.VMEM((groups - 1, high, 128), F32),
+            pltpu.VMEM((n - 1, 8, 128), F32),
+            pltpu.SemaphoreType.DMA((2, groups - 1)),
+            pltpu.SemaphoreType.DMA((2, n - 1)),
+        ],
+        remote=True,
+    )[0]
+    flat = got.reshape(-1)
+    ends = np.cumsum(sizes)
+    return [flat[end - size : end] for end, size in zip(ends, sizes)], got[-8, : depth.size]
 
 
 def output_body(rows, steps, *refs):
@@ -1274,20 +1368,6 @@
             return self.gather(weight)
         across = gate([across])[0]
         return [weight, self.over_core(weight), across, self.over_core(across)]
-
-
-def dp_total(vectors):
-    groups = lax.axis_size("dp")
-    sizes = [v.size for v in vectors]
-    packed = jnp.concatenate(vectors)
-    packed = jnp.pad(packed, (0, -packed.size % 1024)).reshape(-1, 128)
-    bit = 1
-    while bit < groups:
-        packed = packed + lax.ppermute(packed, "dp", [(i, i ^ bit) for i in range(groups)])
-        bit *= 2
-    packed = packed.reshape(-1)
-    ends = np.cumsum(sizes)
-    return [packed[end - size : end] for end, size in zip(ends, sizes)]
 
 
 def tables_of(length):
@@ -1335,14 +1415,14 @@
     spread = full % (128 * groups) == 0 and groups >= 4
     last = row_count - 1
 
-    Order.last, Order.names = None, 0
+    Order.last, Order.names, Order.cost = None, 0, 10**12
     vectors = jnp.stack([first_gain, first_bias, second_gain, second_bias])
     vectors = ring.gather_start(jnp.repeat(vectors, 8, 0))
     piece = ring.out_start(out_weight)
     cot_rows = [lax.slice_in_dim(cotangent, r * length, (r + 1) * length) for r in rows]
     none = [None] * row_count
     wide, low, xs, qkv, normed1, stat1 = (list(none) for _ in range(6))
-    attended, logs, heads, cots, cot_full = (list(none) for _ in range(5))
+    attended, logs, heads, cots = (list(none) for _ in range(4))
     hidden, normed2, stat2, activated, slope = (list(none) for _ in range(5))
     branch, up_grad, parts2, parts1 = (list(none) for _ in range(4))
     hidden_grad, grads, grad_full, qkv_grad = (list(none) for _ in range(4))
@@ -1372,7 +1452,7 @@
         )
         attended[r], logs[r] = attend(starts[r], qkv[r])
         heads[r] = ring.gather_start(attended[r])
-        if r == 0:
+        if r == last:
             out_w = ring.out_end(out_weight, across)
 
     for r in rows:
@@ -1389,92 +1469,81 @@
             up_bias8,
             up_weight,
             down_weight,
-            cots[r - 1] if r > 0 else (),
         )
-        hidden[r], normed2[r], stat2[r], activated[r], slope[r], parts, joined = got
+        hidden[r], normed2[r], stat2[r], activated[r], slope[r], parts = got
         branch[r] = ring.scatter(parts)[0]
-        if r > 0:
-            cot_full[r - 1], sums = joined
-            down_bias_sum += sums
-
-    def back(r, more=()):
-        return feed_back(
-            n, pairs, cot_full[r], slope[r], normed2[r], gain2, bias2, up_weight, down_weight, more
+
+    def back(r, others):
+        nonlocal up_bias_sum, down_bias_sum
+        up_grad[r], up_sum, cot_sum, parts, blocks = feed_back(
+            n, pairs, cots[r], others, slope[r], normed2[r], gain2, bias2, up_weight, down_weight
         )
-
-    def take(r, got):
-        nonlocal up_bias_sum
-        up_grad[r], up_sum, parts, joined = got
         up_bias_sum += up_sum
+        down_bias_sum += cot_sum
         parts2[r] = ring.scatter(parts, True)
-        return joined
-
-    cot_full[last], sums = take(0, back(0, cots[last]))
-    down_bias_sum += sums
-    if spread:
-        down = Spread(activated, cot_full, 1, (1, 2, 4))
-        down.first()
+        return blocks
+
+    def spread_over_dp(value, dim):
+        return lax.psum_scatter(value, "dp", scatter_dimension=dim, tiled=True)
+
+    blocks = back(0, cots[1:])
     if pairs:
+        cots = blocks
         branch[0][1] = gate(branch[0][1:])[0]
+    down_sum = spread_over_dp(weight_of_blocks(ring.me[None], activated, cots), 1)
     for r in rows[1:]:
-        take(r, back(r))
+        back(r, [])
 
     def hidden_step(r):
         nonlocal gain2_sum, bias2_sum
-        parts, sums = parts2[r]
+        parts, row_sums = parts2[r]
         hidden_grad[r], low_grad, gain_part, bias_part = hidden_back(
-            parts, cotangent, r, hidden[r], stat2[r], sums, own2, full
+            parts, cotangent, r, hidden[r], stat2[r], row_sums, own2, full
         )
         gain2_sum += gain_part
         bias2_sum += bias_part
         grads[r] = ring.gather_start(low_grad)
 
     hidden_step(0)
-    if spread:
-        up = [
-            Spread(normed2, up_grad, 0, (1, 2, 4), (0, 2)),
-            Spread(normed2, up_grad, 0, (2, 4, 1), (1, 2)),
-        ]
-        up[1].first()
-        if pairs:
-            branch[last][1] = gate(branch[last][1:])[0]
-        up[0].first()
-        down.keep()
+    up_sum = spread_over_dp(weight_grad(normed2, up_grad), 0)
+    if pairs:
+        branch[last][1] = gate(branch[last][1:])[0]
 
     for r in rows:
         grad_full[r], attended_grad = attended_back(n, pairs, grads[r], out_weight)
         if r < last:
             hidden_step(r + 1)
+        Order.cost = 10**4 if r < last else 10**12
         qkv_grad[r] = attend_back(starts[r], tables, qkv[r], attended_grad, logs[r])
+        Order.cost = 10**12
+        if r == last and spread:
+            qkv_sum = [
+                Spread(normed1, qkv_grad, 0, (1, 2, 4), (0, 2)),
+                Spread(normed1, qkv_grad, 0, (2, 4, 1), (1, 2)),
+            ]
+            qkv_sum[0].first()
+            qkv_sum[1].first()
         parts = project_back(n, pairs, qkv_grad[r], normed1[r], gain1, bias1, qkv_weight)
         parts1[r] = ring.scatter(parts, True)
-        if spread and r == 0:
-            up[1].keep_added()
-            advance(down)
 
     if spread:
-        qkv_sum = [
-            Spread(normed1, qkv_grad, 0, (1, 2, 4), (0, 2)),
-            Spread(normed1, qkv_grad, 0, (2, 4, 1), (1, 2)),
-        ]
         out_sum = Spread(attended, grad_full, 1, (2, 4, 1))
-        qkv_sum[0].first()
-        qkv_sum[1].first()
         out_sum.first()
-        up[0].keep_added()
-        advance(down, up[1])
-        out_sum.keep()
+    if pairs:
+        parts, row_sums = parts1[0]
+        parts[1], row_sums[1] = gate([parts[1], row_sums[1]])
+    down_sum = gate([down_sum])[0]
     made = output(branch, hidden, down_bias8)
 
     grad_history, depth_sum, gain1_sum, bias1_sum = None, 0.0, 0.0, 0.0
     for r in rows:
-        parts, sums = parts1[r]
+        parts, row_sums = parts1[r]
         grad_history, depth_part, gain_part, bias_part = average_back(
             depth_weights,
             parts,
             wide[r],
             stat1[r],
-            sums,
+            row_sums,
             (own1, full),
             hidden_grad[r],
             history,
@@ -1487,41 +1556,32 @@
         if r == 0 and spread:
             qkv_sum[0].keep_added()
             qkv_sum[1].keep_added()
-            advance(up[0], out_sum)
-
+            out_sum.keep()
+
+    Order.cost = 10**4
+    vectors = [up_bias_sum, down_bias_sum, gain2_sum, bias2_sum, gain1_sum, bias1_sum]
+    totals, depth_grad = sums([jnp.sum(v, 0) for v in vectors], jnp.sum(depth_sum, (1, 2)))
     if spread:
         advance(qkv_sum[0], qkv_sum[1], out_sum)
-        down_total, up_total, out_total, qkv_total = finish([down], up, [out_sum], qkv_sum)
+        advance(out_sum)
     else:
-        down_total, up_total, out_total, qkv_total = (
-            lax.psum_scatter(
-                weight_grad(*pair), "dp", scatter_dimension=dim, tiled=True
-            ).astype(F32)
-            for pair, dim in (
-                ((activated, cot_full), 1),
-                ((normed2, up_grad), 0),
-                ((attended, grad_full), 1),
-                ((normed1, qkv_grad), 0),
-            )
-        )
-
-    sums = [up_bias_sum, down_bias_sum, gain2_sum, bias2_sum, gain1_sum, bias1_sum]
-    depth_part = ring.total(jnp.sum(depth_sum, (1, 2)))
-    sums = dp_total([jnp.sum(v, 0) for v in sums] + [depth_part])
+        qkv_sum = [spread_over_dp(weight_grad(normed1, qkv_grad), 0)]
+        out_sum = spread_over_dp(weight_grad(attended, grad_full), 1)
+    down_total, up_total, out_total, qkv_total = finish([down_sum], [up_sum], [out_sum], qkv_sum)
     return (
         made,
         grad_history,
-        sums[6],
-        sums[4],
-        sums[5],
+        depth_grad,
+        totals[4],
+        totals[5],
         qkv_total,
         out_total,
-        sums[2],
-        sums[3],
+        totals[2],
+        totals[3],
         up_total,
-        sums[0],
+        totals[0],
         down_total,
-        sums[1],
+        totals[1],
     )
 
 

time: 769 us -> 675 us (0.88)
  waiting for transfers between devices: 185 us -> 107 us
  starting transfers between devices: 49.5 us -> 33.9 us
    ppermute x18 -> x9, waiting for transfers between devices: 115 us -> 70.6 us  [send(): lax.ppermute(value, 'dp', [(i, i ^ bit) for i in range(self.groups)])]
    ppermute x3 -> x0, waiting for transfers between devices: 37.8 us -> none  [dp_total(): lax.ppermute(packed, 'dp', [(i, i ^ bit) for i in range(groups)])]
    ppermute x18 -> x9, starting transfers between devices: 22.8 us -> 11.6 us  [send(): lax.ppermute(value, 'dp', [(i, i ^ bit) for i in range(self.groups)])]
    ppermute x21 -> x20, waiting for transfers between devices: 25.5 us -> 32.4 us  [over_chip(): return lax.ppermute(value, 'mp', self.chip)]
    ppermute x21 -> x20, starting transfers between devices: 23.8 us -> 21.2 us  [over_chip(): return lax.ppermute(value, 'mp', self.chip)]
    pallas_call x45 -> x42, Pallas kernels: 487 us -> 488 us  [call(): pl.pallas_call(without_extra, grid_spec=pltpu.PrefetchScalarGridSpec(num_...]
  transfers between devices with their start and end apart: 48 -> 36, of which waited for: 14 -> 9; matrix products, arithmetic and copies ran while one was open for 3% -> 3% of each run, Pallas kernels for 63% -> 72%
where the time goes in v5:
time: 675 us; the launch traced here: 671 us
  Pallas kernels  488 us (72%)
  waiting for transfers between devices  107 us (16%)
  starting transfers between devices  33.9 us (5%)
  local copies, waits for them, and re-layouts  19.8 us (3%)
  between operations  14.4 us (2%)
  other arithmetic  6.84 us (1%)
    pallas_call x42, Pallas kernels, call(): pl.pallas_call(without_extra, grid_spec=pltpu.PrefetchScalarGridSpec(num_...  488 us
    ppermute x9, waiting for transfers between devices, send(): lax.ppermute(value, 'dp', [(i, i ^ bit) for i in range(self.groups)])  70.6 us
    ppermute x20, waiting for transfers between devices, over_chip(): return lax.ppermute(value, 'mp', self.chip)  32.4 us
    ppermute x20, starting transfers between devices, over_chip(): return lax.ppermute(value, 'mp', self.chip)  21.2 us
  transfers between devices with their start and end apart: 36, of which 9 were waited for; matrix products, arithmetic and copies ran while one was open for 3% of the time, Pallas kernels for 72%

profile of v5, /device:TPU:0, one launch (start us, length us, event | category | flops | bytes accessed | tf_op | source)
XLA Modules:
  0.0 670.6 jit_solution(8172509125551268176)
XLA Ops:
  8.6 3.0 collective-permute-start.2
  13.8 8.0 %average.2 = (f32[1024,512]{1,0:T(8,128)}, bf16[1024,512]{1,0:T(8,128)(2,1)}) custom-call(f32[13]{0:T(128)} %refs_0_.7, bf16[13,2048,512]{2,1,0:T(8,128)(2,1)} %refs_9_.5), custom_call_target="tpu_custom_call" | custom-call | flops 999999995904 | bytes 100000000 | tf_op jit(solution)/shard_map/average/pallas_call | solution.py:57
  21.7 2.0 collective-permute-start
  27.1 7.8 %average.3 = (f32[1024,512]{1,0:T(8,128)}, bf16[1024,512]{1,0:T(8,128)(2,1)}) custom-call(f32[13]{0:T(128)} %refs_0_.7, bf16[13,2048,512]{2,1,0:T(8,128)(2,1)} %refs_9_.5, f32[32,512]{1,0:T(8,128)} %get-tuple-element.109.refs_2_), custom_call_target="tpu_custom_call" | custom-call | flops 999999995904 | bytes 100000000 | tf_op jit(solution)/shard_map/average/pallas_call | solution.py:57
  36.9 10.2 %collective-permute-done.refs_1_.refs_3_.refs_5_ = bf16[1024,512]{1,0:T(8,128)(2,1)} collective-permute-done((bf16[1024,512]{1,0:T(8,128)(2,1)}, bf16[1024,512]{1,0:T(8,128)(2,1)}, u32[]{:S(2)}, u32[]{:S(2)}) %collective-permute-start) | collective-permute-done | bytes 1048608 | tf_op jit(solution)/shard_map/ppermute | solution.py:1324
  48.9 17.9 %project.2 = (bf16[1024,1536]{1,0:T(8,128)(2,1)}, bf16[1024,2048]{1,0:T(8,128)(2,1)}, f32[1024,128]{1,0:T(8,128)}, bf16[1024,512]{1,0:T(8,128)(2,1)}, bf16[1024,512]{1,0:T(8,128)(2,1)}) custom-call(bf16[1024,512]{1,0:T(8,128)(2,1)} %get-tuple-element.107.refs_0_.refs_2_, bf16[1024,512]{1,0:T(8,128)(2,1)} %collective-permute-done.refs_1_.refs_3_.refs_5_, ...), custom_call_target="tpu_custom_call" | custom-call | flops 999999995904 | bytes 100000000 | tf_op jit(solution)/shard_map/project/pallas_call | solution.py:57
  67.4 10.1 %attend.2 = (bf16[1024,512]{1,0:T(8,128)(2,1)}, f32[4,8,1024]{2,1,0:T(8,128)}) custom-call(s32[8,1024]{1,0:T(8,128)} %broadcast_in_dim.50.refs_0_, bf16[1024,1536]{1,0:T(8,128)(2,1)} %get-tuple-element.112.refs_1_.refs_3_, f32[1024,128]{1,0:T(8,128)} %get-tuple-element.113.refs_2_.refs_6_), custom_call_target="tpu_custom_call" | custom-call | flops 999999995904 | bytes 100000000 | tf_op jit(solution)/shard_map/attend/pallas_call | solution.py:57
  77.7 17.9 %project.3 = (bf16[1024,1536]{1,0:T(8,128)(2,1)}, bf16[1024,2048]{1,0:T(8,128)(2,1)}, f32[1024,128]{1,0:T(8,128)}, bf16[1024,512]{1,0:T(8,128)(2,1)}, bf16[1024,512]{1,0:T(8,128)(2,1)}) custom-call(bf16[1024,512]{1,0:T(8,128)(2,1)} %gate.10.refs_9_.refs_0_.refs_2_, bf16[1024,512]{1,0:T(8,128)(2,1)} %collective-permute-done.7.refs_1_.refs_3_.refs_5_, ...), custom_call_target="tpu_custom_call" | custom-call | flops 999999995904 | bytes 100000000 | tf_op jit(solution)/shard_map/project/pallas_call | solution.py:57
  96.3 9.7 %attend.3 = (bf16[1024,512]{1,0:T(8,128)(2,1)}, f32[4,8,1024]{2,1,0:T(8,128)}) custom-call(s32[8,1024]{1,0:T(8,128)} %broadcast_in_dim.53.refs_0_, bf16[1024,1536]{1,0:T(8,128)(2,1)} %get-tuple-element.119.refs_1_.refs_3_, f32[1024,128]{1,0:T(8,128)} %get-tuple-element.120.refs_2_.refs_6_), custom_call_target="tpu_custom_call" | custom-call | flops 999999995904 | bytes 100000000 | tf_op jit(solution)/shard_map/attend/pallas_call | solution.py:57
  108.1 4.1 collective-permute-done.8.refs_10_
  112.9 40.9 %feed.2 = (f32[1024,512]{1,0:T(8,128)}, bf16[1024,2048]{1,0:T(8,128)(2,1)}, f32[1024,128]{1,0:T(8,128)}, bf16[1024,2048]{1,0:T(8,128)(2,1)}, bf16[1024,2048]{1,0...) custom-call(bf16[1024,512]{1,0:T(8,128)(2,1)} %get-tuple-element.114.refs_0_.refs_2_.refs_1_, ...), custom_call_target="tpu_custom_call" | custom-call | flops 999999995904 | bytes 100000000 | tf_op jit(solution)/shard_map/feed/pallas_call | solution.py:57
  154.1 1.8 collective-permute-start.11
  155.9 41.2 %feed.3 = (f32[1024,512]{1,0:T(8,128)}, bf16[1024,2048]{1,0:T(8,128)(2,1)}, f32[1024,128]{1,0:T(8,128)}, bf16[1024,2048]{1,0:T(8,128)(2,1)}, bf16[1024,2048]{1,0...) custom-call(bf16[1024,512]{1,0:T(8,128)(2,1)} %get-tuple-element.128.refs_0_.refs_2_, ...), custom_call_target="tpu_custom_call" | custom-call | flops 999999995904 | bytes 100000000 | tf_op jit(solution)/shard_map/feed/pallas_call | solution.py:57
  197.4 5.2 collective-permute-done.11.refs_5_.refs_7_.refs_9_.refs_2_
  202.6 32.8 %feed_back.2 = (bf16[1024,2048]{1,0:T(8,128)(2,1)}, f32[8,2048]{1,0:T(8,128)}, f32[8,512]{1,0:T(8,128)}, bf16[1024,512]{1,0:T(8,128)(2,1)}, bf16[1024,512]{1,0:T...) custom-call(bf16[1024,512]{1,0:T(8,128)(2,1)} %gate.12.refs_17_.refs, ...), custom_call_target="tpu_custom_call" | custom-call | flops 999999995904 | bytes 100000000 | tf_op jit(solution)/shard_map/feed_back/pallas_call | solution.py:57
  235.4 23.6 %weight_grad.2.refs_10_ = bf16[2048,2048]{1,0:T(8,128)(2,1)} custom-call(s32[1]{0:T(128)} %bitcast.7.refs_0_, bf16[1024,2048]{1,0:T(8,128)(2,1)} %get-tuple-element.141.refs_1_, bf16[1024,2048]{1,0:T(8,128)(2,1)} %get-tuple-element.142.refs_2_, bf16[1024,512]{1,0:T(8,128)(2,1)} %gate.12.refs_17_.refs_0_.refs_2_.refs_3_, ...), custom_call_target="tpu_custom_call" | custom-call | flops 999999995904 | bytes 100000000 | tf_op jit(solution)/shard_map/weight_grad/pallas_call | solution.py:57
  259.6 31.0 %feed_back.3 = (bf16[1024,2048]{1,0:T(8,128)(2,1)}, f32[8,2048]{1,0:T(8,128)}, f32[8,512]{1,0:T(8,128)}, bf16[1024,512]{1,0:T(8,128)(2,1)}, bf16[1024,512]{1,0:T(8,128)(2,1)}, /*index=5*/f32[8,1024]{1,0:T(8,128)}) custom-call(bf16[1024,512]{1,0:T(8,128)(2,1)} %gate.13.refs_17_.refs_4_.refs_6_.refs_7_.refs_0_, ...), custom_call_target="tpu_custom_call" | custom-call | flops 999999995904 | bytes 100000000 | tf_op jit(solution)/shard_map/feed_back/pallas_call | solution.py:57
  290.5 1.8 collective-permute-start.18
  292.6 1.8 collective-permute-start.17
  298.6 6.1 hidden_back.2
  304.7 23.6 %weight_grad.3.refs_1_ = bf16[2048,2048]{1,0:T(8,128)(2,1)} custom-call(bf16[1024,2048]{1,0:T(8,128)(2,1)} %get-tuple-element.127.refs_9_.refs_0_, bf16[1024,2048]{1,0:T(8,128)(2,1)} %get-tuple-element.136.refs_5_.refs_1_, bf16[1024,2048]{1,0:T(8,128)(2,1)} %get-tuple-element.137.refs_2_, bf16[1024,2048]{1,0:T(8,128)(2,1)} %get-tuple-element.145.refs_3_, ...), custom_call_target="tpu_custom_call" | custom-call | flops 999999995904 | bytes 100000000 | tf_op jit(solution)/shard_map/weight_grad/pallas_call | solution.py:57
  328.4 12.5 %collective-permute-done.16.refs_1_.refs_3_ = bf16[1024,512]{1,0:T(8,128)(2,1)} collective-permute-done((bf16[1024,512]{1,0:T(8,128)(2,1)}, bf16[1024,512]{1,0:T(8,128)(2,1)}, u32[]{:S(2)}, u32[]{:S(2)}) %collective-permute-start.16) | collective-permute-done | bytes 1048608 | tf_op jit(solution)/shard_map/ppermute | solution.py:1324
  340.9 9.0 %attended_back.2 = (bf16[1024,2048]{1,0:T(8,128)(2,1)}, bf16[1024,512]{1,0:T(8,128)(2,1)}) custom-call(bf16[1024,512]{1,0:T(8,128)(2,1)} %get-tuple-element.151.refs_0_.refs_2_, bf16[1024,512]{1,0:T(8,128)(2,1)} %collective-permute-done.16.refs_1_.refs_3_, bf16[1024,512]{1,0:T(8,128)(2,1)} %get-tuple-element.151.refs_0_.refs_2_, ...), custom_call_target="tpu_custom_call" | custom-call | flops 999999995904 | bytes 100000000 | tf_op jit(solution)/shard_map/attended_back/pallas_call | solution.py:57
  350.0 5.6 hidden_back.3
  355.6 12.5 %attend_back.2.refs_0_.refs_9_ = bf16[1024,1536]{1,0:T(8,128)(2,1)} custom-call(s32[8,1024]{1,0:T(8,128)} %broadcast_in_dim.50.refs_0_, f32[1024,128]{1,0:T(8,128)} %constant.22.clone.refs_6_.refs_1_, f32[1024,128]{1,0:T(8,128)} %constant.23.clone.refs_7_.refs_2_, bf16[1024,1536]{1,0:T(8,128)(2,1)} %get-tuple-element.112.refs_1_.refs_3_, ...), custom_call_target="tpu_custom_call" | custom-call | flops 10000 | bytes 1 | tf_op jit(solution)/shard_map/attend_back/pallas_call | solution.py:57
  369.3 15.9 %project_back.2 = (bf16[1024,512]{1,0:T(8,128)(2,1)}, bf16[1024,512]{1,0:T(8,128)(2,1)}, f32[8,1024]{1,0:T(8,128)}) custom-call(bf16[1024,1536]{1,0:T(8,128)(2,1)} %attend_back.2.refs_0_.refs_9_, bf16[1024,2048]{1,0:T(8,128)(2,1)} %get-tuple-element.157.refs_1_.refs_3_.refs_5_.refs_7_, f32[8,2048]{1,0:T(8,128)} %get-tuple-element.206.refs_4_.refs_2_, ...), custom_call_target="tpu_custom_call" | custom-call | flops 999999995904 | bytes 100000000 | tf_op jit(solution)/shard_map/project_back/pallas_call | solution.py:57
  389.9 4.4 collective-permute-done.21.refs_1_.refs_3_
  394.4 9.3 %attended_back.3 = (bf16[1024,2048]{1,0:T(8,128)(2,1)}, bf16[1024,512]{1,0:T(8,128)(2,1)}) custom-call(bf16[1024,512]{1,0:T(8,128)(2,1)} %get-tuple-element.161.refs_0_.refs_2_, bf16[1024,512]{1,0:T(8,128)(2,1)} %collective-permute-done.21.refs_1_.refs_3_, bf16[1024,512]{1,0:T(8,128)(2,1)} %get-tuple-element.161.refs_0_.refs_2_, ...), custom_call_target="tpu_custom_call" | custom-call | flops 999999995904 | bytes 100000000 | tf_op jit(solution)/shard_map/attended_back/pallas_call | solution.py:57
  403.6 12.4 %attend_back.3.refs_10_.refs_0_ = bf16[1024,1536]{1,0:T(8,128)(2,1)} custom-call(s32[8,1024]{1,0:T(8,128)} %broadcast_in_dim.53.refs_0_, f32[1024,128]{1,0:T(8,128)} %constant.22.clone.refs_6_.refs_1_, f32[1024,128]{1,0:T(8,128)} %constant.23.clone.refs_7_.refs_2_, bf16[1024,1536]{1,0:T(8,128)(2,1)} %get-tuple-element.119.refs_1_.refs_3_, ...), custom_call_target="tpu_custom_call" | custom-call | flops 999999995904 | bytes 100000000 | tf_op jit(solution)/shard_map/attend_back/pallas_call | solution.py:57
  416.0 9.6 %weight_blocks.6.refs_11_ = bf16[4,256,768]{2,1,0:T(8,128)(2,1)} custom-call(s32[1]{0:T(128)} %bitcast.8.refs_0_, bf16[1024,2048]{1,0:T(8,128)(2,1)} %get-tuple-element.157.refs_1_.refs_3_.refs_5_.refs_7_, bf16[1024,2048]{1,0:T(8,128)(2,1)} %get-tuple-element.164.refs_2_.refs_4_.refs_6_.refs_8_.refs_1_, ...), custom_call_target="tpu_custom_call" | custom-call | flops 999999995904 | bytes 100000000 | tf_op jit(solution)/shard_map/weight_blocks/pallas_call | solution.py:57
  425.7 9.7 %weight_blocks.7.refs_5_ = bf16[4,256,768]{2,1,0:T(8,128)(2,1)} custom-call(s32[1]{0:T(128)} %bitcast.8.refs_0_, bf16[1024,2048]{1,0:T(8,128)(2,1)} %get-tuple-element.157.refs_1_.refs_3_.refs_5_.refs_7_, bf16[1024,2048]{1,0:T(8,128)(2,1)} %get-tuple-element.164.refs_2_.refs_4_.refs_6_.refs_8_.refs_1_, ...), custom_call_target="tpu_custom_call" | custom-call | flops 999999995904 | bytes 100000000 | tf_op jit(solution)/shard_map/weight_blocks/pallas_call | solution.py:57
  438.5 15.7 %project_back.3 = (bf16[1024,512]{1,0:T(8,128)(2,1)}, bf16[1024,512]{1,0:T(8,128)(2,1)}, f32[8,1024]{1,0:T(8,128)}) custom-call(bf16[1024,1536]{1,0:T(8,128)(2,1)} %attend_back.3.refs_10_.refs_0_, bf16[1024,2048]{1,0:T(8,128)(2,1)} %get-tuple-element.164.refs_2_.refs_4_.refs_6_.refs_8_.refs_1_, f32[8,2048]{1,0:T(8,128)} %get-tuple-element.206.refs_4_.refs_2_, ...), custom_call_target="tpu_custom_call" | custom-call | flops 999999995904 | bytes 100000000 | tf_op jit(solution)/shard_map/project_back/pallas_call | solution.py:57
  455.5 6.2 weight_blocks.8.refs_2_
  464.2 6.4 output.1.refs_10_
  471.2 14.1 %average_back.2 = (bf16[13,2048,512]{2,1,0:T(8,128)(2,1)}, f32[13,8,128]{2,1,0:T(8,128)}, f32[8,512]{1,0:T(8,128)}, f32[8,512]{1,0:T(8,128)}) custom-call(f32[13]{0:T(128)} %refs_0_.7, bf16[1024,512]{1,0:T(8,128)(2,1)} %get-tuple-element.170.refs_1_, bf16[1024,512]{1,0:T(8,128)(2,1)} %get-tuple-element.171.refs_2_, ...), custom_call_target="tpu_custom_call" | custom-call | flops 999999995904 | bytes 100000000 | tf_op jit(solution)/shard_map/average_back/pallas_call | solution.py:57
  485.4 10.1 %weight_blocks.9 = (bf16[2,256,768]{2,1,0:T(8,128)(2,1)}, bf16[2,256,768]{2,1,0:T(8,128)(2,1)}) custom-call(s32[1]{0:T(128)} %bitcast.8.refs_0_, bf16[1024,2048]{1,0:T(8,128)(2,1)} %get-tuple-element.157.refs_1_.refs_3_.refs_5_.refs_7_, bf16[1024,2048]{1,0:T(8,128)(2,1)} %get-tuple-element.164.refs_2_.refs_4_.refs_6_.refs_8_.refs_1_, ...), custom_call_target="tpu_custom_call" | custom-call | flops 999999995904 | bytes 100000000 | tf_op jit(solution)/shard_map/weight_blocks/pallas_call | solution.py:57
  495.5 27.1 %collective-permute-done.24.refs_11_ = bf16[4,256,768]{2,1,0:T(8,128)(2,1)} collective-permute-done((bf16[4,256,768]{2,1,0:T(8,128)(2,1)}, bf16[4,256,768]{2,1,0:T(8,128)(2,1)}, u32[]{:S(2)}, u32[]{:S(2)}) %collective-permute-start.24) | collective-permute-done | bytes 1572896 | tf_op jit(solution)/shard_map/ppermute | solution.py:1141
  522.5 10.4 %weight_blocks.10 = (bf16[2,256,768]{2,1,0:T(8,128)(2,1)}, bf16[2,256,768]{2,1,0:T(8,128)(2,1)}) custom-call(s32[1]{0:T(128)} %bitcast.8.refs_0_, bf16[1024,2048]{1,0:T(8,128)(2,1)} %get-tuple-element.157.refs_1_.refs_3_.refs_5_.refs_7_, bf16[1024,2048]{1,0:T(8,128)(2,1)} %get-tuple-element.164.refs_2_.refs_4_.refs_6_.refs_8_.refs_1_, ...), custom_call_target="tpu_custom_call" | custom-call | flops 999999995904 | bytes 100000000 | tf_op jit(solution)/shard_map/weight_blocks/pallas_call | solution.py:57
  532.9 6.2 weight_blocks.11.refs_11_.refs_4_
  539.6 2.2 collective-permute-start.26
  541.9 14.5 %average_back.3 = (bf16[13,2048,512]{2,1,0:T(8,128)(2,1)}, f32[13,8,128]{2,1,0:T(8,128)}, f32[8,512]{1,0:T(8,128)}, f32[8,512]{1,0:T(8,128)}) custom-call(f32[13]{0:T(128)} %refs_0_.7, bf16[1024,512]{1,0:T(8,128)(2,1)} %get-tuple-element.167.refs_1_, bf16[1024,512]{1,0:T(8,128)(2,1)} %collective-permute-done.22.refs_2_, ...), custom_call_target="tpu_custom_call", output_to_operand_aliasing={{0}: (10, {})} | custom-call | flops 999999995904 | bytes 100000000 | tf_op jit(solution)/shard_map/average_back/pallas_call | solution.py:57
  561.3 37.4 %sums.1.refs_6_ = f32[48,128]{1,0:T(8,128)} custom-call(f32[48,128]{1,0:T(8,128)} %select_maximum_fusion.refs_0_, f32[8,512]{1,0:T(8,128)} %get-tuple-element.182.refs_1_), custom_call_target="tpu_custom_call" | custom-call | flops 10000 | bytes 1 | tf_op jit(solution)/shard_map/sums/pallas_call | solution.py:57
  598.7 4.6 fold.2
  603.3 3.1 collective-permute-start.29
  607.5 37.8 %collective-permute-done.29.refs_1_ = bf16[2,512,256]{2,1,0:T(8,128)(2,1)S(1)} collective-permute-done((bf16[2,512,256]{2,1,0:T(8,128)(2,1)}, bf16[2,512,256]{2,1,0:T(8,128)(2,1)S(1)}, u32[]{:S(2)}, u32[]{:S(2)}) %collective-permute-start.29) | collective-permute-done | bytes 524320 | tf_op jit(solution)/shard_map/ppermute | solution.py:1141
  646.0 3.3 fold.3
  653.7 4.2 collective-permute-done.30.refs_3_
  658.6 5.2 finish.1
  (148 shorter events, 46.5 us)
Async XLA Ops:
  7.2 100.6 %all-gather.2.cloned.1.call-start = ((), (), s32[]{:S(2)}) async-start(), calls=%async_computation.2 | async-start | bytes 2359296 | tf_op jit(solution)/shard_map/all_gather | solution.py:1364
  8.6 18.4 %collective-permute-start.2 = (f32[32,512]{1,0:T(8,128)}, f32[32,512]{1,0:T(8,128)}, u32[]{:S(2)}, u32[]{:S(2)}) collective-permute-start(f32[32,512]{1,0:T(8,128)} %broadcast_bitcast_fusion), channel_id=1, source_target_pairs={{0,2},{1,3},{2,0},{3,1},{4,6},{5,7},{6,4},{7,5},{8,10},{9,11},{10,... | collective-permute-start | bytes 196616 | tf_op jit(solution)/shard_map/ppermute | solution.py:1324
  11.6 23.6 %collective-permute-start.1 = (f32[32,512]{1,0:T(8,128)}, f32[32,512]{1,0:T(8,128)}, u32[]{:S(2)}, u32[]{:S(2)}) collective-permute-start(f32[32,512]{1,0:T(8,128)} %broadcast_bitcast_fusion), channel_id=1, source_target_pairs={{0,1},{1,0},{2,3},{3,2},{4,5},{5,4},{6,7},{7,6},{8,9},{9,8},{10,11... | collective-permute-start | bytes 196616 | tf_op jit(solution)/shard_map/ppermute | solution.py:1321
  11.6 96.5 %collective-permute-start.6 = (bf16[512,2048]{1,0:T(8,128)(2,1)}, bf16[512,2048]{1,0:T(8,128)(2,1)}, u32[]{:S(2)}, u32[]{:S(2)}) collective-permute-start(bf16[512,2048]{1,0:T(8,128)(2,1)} %refs_4_.10), channel_id=1, source_target_pairs={{0,1},{1,0},{2,3},{3,2},{4,5},{5,4},{6,7},{7,6},{8,9},{9,8},{10,11... | collective-permute-start | bytes 6291464 | tf_op jit(solution)/shard_map/ppermute | solution.py:1321
  13.8 13.2 %collective-permute-start.3 = (bf16[64,2048]{1,0:T(8,128)(2,1)}, bf16[64,2048]{1,0:T(8,128)(2,1)}, u32[]{:S(2)}, u32[]{:S(2)}) collective-permute-start(bf16[64,2048]{1,0:T(8,128)(2,1)} %constant_dynamic-slice_fusion), channel_id=1, source_target_pairs={{0,2},{1,3},{2,0},{3,1},{4,6},{5,7},{6,4},{7,5},{8,10},{9,11},{10,... | collective-permute-start | bytes 786440 | tf_op jit(solution)/shard_map/ppermute | solution.py:1324
  21.7 25.4 %collective-permute-start = (bf16[1024,512]{1,0:T(8,128)(2,1)}, bf16[1024,512]{1,0:T(8,128)(2,1)}, u32[]{:S(2)}, u32[]{:S(2)}) collective-permute-start(bf16[1024,512]{1,0:T(8,128)(2,1)} %get-tuple-element.107.refs_0_.refs_2_), channel_id=1, source_target_pairs={{0,2},{1,3},{2,0},{3,1},{4,6},{5,7},{6,4},{7,5},{8,10},{9,11},{10,... | collective-permute-start | bytes 3145736 | tf_op jit(solution)/shard_map/ppermute | solution.py:1324
  27.0 8.2 %collective-permute-start.4 = (f32[32,512]{1,0:T(8,128)}, f32[32,512]{1,0:T(8,128)}, u32[]{:S(2)}, u32[]{:S(2)}) collective-permute-start(f32[32,512]{1,0:T(8,128)} %get-tuple-element.109.refs_2_), channel_id=1, source_target_pairs={{0,1},{1,0},{2,3},{3,2},{4,5},{5,4},{6,7},{7,6},{8,9},{9,8},{10,11... | collective-permute-start | bytes 196616 | tf_op jit(solution)/shard_map/ppermute | solution.py:1321
  35.0 428.0 %reduce-scatter.3.cloned.1.call-start = ((), (), s32[]{:S(2)}) async-start(), calls=%async_computation.3 | async-start | bytes 9437184 | tf_op jit(solution)/shard_map/reduce_scatter | solution.py:1487
  47.1 30.6 %collective-permute-start.7 = (bf16[1024,512]{1,0:T(8,128)(2,1)}, bf16[1024,512]{1,0:T(8,128)(2,1)}, u32[]{:S(2)}, u32[]{:S(2)}) collective-permute-start(bf16[1024,512]{1,0:T(8,128)(2,1)} %gate.10.refs_9_.refs_0_.refs_2_), channel_id=1, source_target_pairs={{0,2},{1,3},{2,0},{3,1},{4,6},{5,7},{6,4},{7,5},{8,10},{9,11},{10,... | collective-permute-start | bytes 3145736 | tf_op jit(solution)/shard_map/ppermute | solution.py:1324
  48.9 17.9 %copy-start.17 = (s32[1,1024]{1,0:T(1,128)S(1)}, s32[1,1024]{1,0:T(1,128)}, u32[]{:S(2)}) copy-start(s32[1,1024]{1,0:T(1,128)} %get-tuple-element.213) | copy-start | bytes 12292
  77.5 30.6 %collective-permute-start.5 = (bf16[1024,512]{1,0:T(8,128)(2,1)}, bf16[1024,512]{1,0:T(8,128)(2,1)}, u32[]{:S(2)}, u32[]{:S(2)}) collective-permute-start(bf16[1024,512]{1,0:T(8,128)(2,1)} %get-tuple-element.114.refs_0_.refs_2_.refs_1_), channel_id=1, source_target_pairs={{0,2},{1,3},{2,0},{3,1},{4,6},{5,7},{6,4},{7,5},{8,10},{9,11},{10,... | collective-permute-start | bytes 3145736 | tf_op jit(solution)/shard_map/ppermute | solution.py:1324
  77.7 17.9 %copy-start.16 = (s32[1,1024]{1,0:T(1,128)S(1)}, s32[1,1024]{1,0:T(1,128)}, u32[]{:S(2)}) copy-start(s32[1,1024]{1,0:T(1,128)} %get-tuple-element.212) | copy-start | bytes 12292
  106.0 49.9 %collective-permute-start.12 = (bf16[1024,512]{1,0:T(8,128)(2,1)}, bf16[1024,512]{1,0:T(8,128)(2,1)}, u32[]{:S(2)}, u32[]{:S(2)}) collective-permute-start(bf16[1024,512]{1,0:T(8,128)(2,1)} %get-tuple-element.128.refs_0_.refs_2_), channel_id=1, source_target_pairs={{0,2},{1,3},{2,0},{3,1},{4,6},{5,7},{6,4},{7,5},{8,10},{9,11},{10,... | collective-permute-start | bytes 3145736 | tf_op jit(solution)/shard_map/ppermute | solution.py:1324
  107.8 4.5 collective-permute-start.8
  107.8 89.6 %collective-permute-start.10 = (bf16[1024,512]{1,0:T(8,128)(2,1)}, bf16[1024,512]{1,0:T(8,128)(2,1)}, u32[]{:S(2)}, u32[]{:S(2)}) collective-permute-start(bf16[1024,512]{1,0:T(8,128)(2,1)} %gate.12.refs_17_.refs_0_.refs_2_.refs_3_), channel_id=1, source_target_pairs={{0,2},{1,3},{2,0},{3,1},{4,6},{5,7},{6,4},{7,5},{8,10},{9,11},{10,... | collective-permute-start | bytes 3145736 | tf_op jit(solution)/shard_map/ppermute | solution.py:1324
  153.8 81.6 %collective-permute-start.9 = (bf16[1024,512]{1,0:T(8,128)(2,1)}, bf16[1024,512]{1,0:T(8,128)(2,1)}, u32[]{:S(2)}, u32[]{:S(2)}) collective-permute-start(bf16[1024,512]{1,0:T(8,128)(2,1)} %get-tuple-element.124), channel_id=1, source_target_pairs={{0,2},{1,3},{2,0},{3,1},{4,6},{5,7},{6,4},{7,5},{8,10},{9,11},{10,... | collective-permute-start | bytes 3145736 | tf_op jit(solution)/shard_map/ppermute | solution.py:1324
  154.1 48.5 %collective-permute-start.11 = (bf16[1024,512]{1,0:T(8,128)(2,1)}, bf16[1024,512]{1,0:T(8,128)(2,1)}, u32[]{:S(2)}, u32[]{:S(2)}) collective-permute-start(bf16[1024,512]{1,0:T(8,128)(2,1)} %gate.13.refs_17_.refs_4_.refs_6_.refs_7_.refs_0_), channel_id=1, source_target_pairs={{0,2},{1,3},{2,0},{3,1},{4,6},{5,7},{6,4},{7,5},{8,10},{9,11},{10,... | collective-permute-start | bytes 3145736 | tf_op jit(solution)/shard_map/ppermute | solution.py:1324
  197.1 131.3 %collective-permute-start.13 = (bf16[1024,512]{1,0:T(8,128)(2,1)}, bf16[1024,512]{1,0:T(8,128)(2,1)}, u32[]{:S(2)}, u32[]{:S(2)}) collective-permute-start(bf16[1024,512]{1,0:T(8,128)(2,1)} %get-tuple-element.135), channel_id=1, source_target_pairs={{0,2},{1,3},{2,0},{3,1},{4,6},{5,7},{6,4},{7,5},{8,10},{9,11},{10,... | collective-permute-start | bytes 3145736 | tf_op jit(solution)/shard_map/ppermute | solution.py:1324
  259.0 393.2 %reduce-scatter.5.cloned.1.call-start = ((), (), s32[]{:S(2)}) async-start(), calls=%async_computation.4 | async-start | bytes 9437184 | tf_op jit(solution)/shard_map/reduce_scatter | solution.py:1487
  259.2 38.7 %collective-permute-start.14 = (bf16[1024,512]{1,0:T(8,128)(2,1)}, bf16[1024,512]{1,0:T(8,128)(2,1)}, u32[]{:S(2)}, u32[]{:S(2)}) collective-permute-start(bf16[1024,512]{1,0:T(8,128)(2,1)} %get-tuple-element.147), channel_id=1, source_target_pairs={{0,2},{1,3},{2,0},{3,1},{4,6},{5,7},{6,4},{7,5},{8,10},{9,11},{10,... | collective-permute-start | bytes 3145736 | tf_op jit(solution)/shard_map/ppermute | solution.py:1324
  259.6 32.8 %copy-start.22 = (f32[8,1024]{1,0:T(8,128)S(1)}, f32[8,1024]{1,0:T(8,128)}, u32[]{:S(2)}) copy-start(f32[8,1024]{1,0:T(8,128)} %get-tuple-element.148.refs_2_) | copy-start | bytes 98308
  259.6 34.9 %copy-start.7 = (f32[8,2048]{1,0:T(8,128)S(1)}, f32[8,2048]{1,0:T(8,128)}, u32[]{:S(2)}) copy-start(f32[8,2048]{1,0:T(8,128)} %get-tuple-element.178) | copy-start | bytes 196612
  259.6 36.3 %copy-start.14 = (f32[8,512]{1,0:T(8,128)S(1)}, f32[8,512]{1,0:T(8,128)}, u32[]{:S(2)}) copy-start(f32[8,512]{1,0:T(8,128)} %get-tuple-element.132.refs_1_) | copy-start | bytes 49156
  259.6 38.4 %copy-start.19 = (f32[512]{0:T(512)S(1)}, f32[512]{0:T(512)}, u32[]{:S(2)}) copy-start(f32[512]{0:T(512)} %param.23) | copy-start | bytes 6148
  290.5 59.4 %collective-permute-start.18 = (f32[8,1024]{1,0:T(8,128)}, f32[8,1024]{1,0:T(8,128)}, u32[]{:S(2)}, u32[]{:S(2)}) collective-permute-start(f32[8,1024]{1,0:T(8,128)} %get-tuple-element.155.refs_2_), channel_id=1, source_target_pairs={{0,2},{1,3},{2,0},{3,1},{4,6},{5,7},{6,4},{7,5},{8,10},{9,11},{10,... | collective-permute-start | bytes 98312 | tf_op jit(solution)/shard_map/ppermute | solution.py:1324
  292.4 5.5 collective-permute-start.15
  292.6 57.3 %collective-permute-start.17 = (bf16[1024,512]{1,0:T(8,128)(2,1)}, bf16[1024,512]{1,0:T(8,128)(2,1)}, u32[]{:S(2)}, u32[]{:S(2)}) collective-permute-start(bf16[1024,512]{1,0:T(8,128)(2,1)} %get-tuple-element.154), channel_id=1, source_target_pairs={{0,2},{1,3},{2,0},{3,1},{4,6},{5,7},{6,4},{7,5},{8,10},{9,11},{10,... | collective-permute-start | bytes 3145736 | tf_op jit(solution)/shard_map/ppermute | solution.py:1324
  304.6 36.3 %collective-permute-start.16 = (bf16[1024,512]{1,0:T(8,128)(2,1)}, bf16[1024,512]{1,0:T(8,128)(2,1)}, u32[]{:S(2)}, u32[]{:S(2)}) collective-permute-start(bf16[1024,512]{1,0:T(8,128)(2,1)} %get-tuple-element.151.refs_0_.refs_2_), channel_id=1, source_target_pairs={{0,2},{1,3},{2,0},{3,1},{4,6},{5,7},{6,4},{7,5},{8,10},{9,11},{10,... | collective-permute-start | bytes 3145736 | tf_op jit(solution)/shard_map/ppermute | solution.py:1324
  368.0 26.3 %collective-permute-start.21 = (bf16[1024,512]{1,0:T(8,128)(2,1)}, bf16[1024,512]{1,0:T(8,128)(2,1)}, u32[]{:S(2)}, u32[]{:S(2)}) collective-permute-start(bf16[1024,512]{1,0:T(8,128)(2,1)} %get-tuple-element.161.refs_0_.refs_2_), channel_id=1, source_target_pairs={{0,2},{1,3},{2,0},{3,1},{4,6},{5,7},{6,4},{7,5},{8,10},{9,11},{10,... | collective-permute-start | bytes 3145736 | tf_op jit(solution)/shard_map/ppermute | solution.py:1324
  369.3 18.0 %copy-start.6 = (f32[8,512]{1,0:T(8,128)S(1)}, f32[8,512]{1,0:T(8,128)}, u32[]{:S(2)}) copy-start(f32[8,512]{1,0:T(8,128)} %get-tuple-element.156.refs_6_) | copy-start | bytes 49156
  369.3 18.0 %copy-start.13 = (f32[8,512]{1,0:T(8,128)S(1)}, f32[8,512]{1,0:T(8,128)}, u32[]{:S(2)}) copy-start(f32[8,512]{1,0:T(8,128)} %get-tuple-element.150.refs_4_) | copy-start | bytes 49156
  369.3 19.3 %copy-start.12 = (f32[8,512]{1,0:T(8,128)S(1)}, f32[8,512]{1,0:T(8,128)}, u32[]{:S(2)}) copy-start(f32[8,512]{1,0:T(8,128)} %get-tuple-element.180) | copy-start | bytes 49156
  369.3 19.3 %copy-start.15 = (f32[8,512]{1,0:T(8,128)S(1)}, f32[8,512]{1,0:T(8,128)}, u32[]{:S(2)}) copy-start(f32[8,512]{1,0:T(8,128)} %get-tuple-element.181) | copy-start | bytes 49156
  385.2 76.5 %collective-permute-start.20 = (f32[8,1024]{1,0:T(8,128)}, f32[8,1024]{1,0:T(8,128)}, u32[]{:S(2)}, u32[]{:S(2)}) collective-permute-start(f32[8,1024]{1,0:T(8,128)} %get-tuple-element.159.refs_5_.refs_3_), channel_id=1, source_target_pairs={{0,2},{1,3},{2,0},{3,1},{4,6},{5,7},{6,4},{7,5},{8,10},{9,11},{10,... | collective-permute-start | bytes 98312 | tf_op jit(solution)/shard_map/ppermute | solution.py:1324
  386.1 76.0 %collective-permute-start.19 = (bf16[1024,512]{1,0:T(8,128)(2,1)}, bf16[1024,512]{1,0:T(8,128)(2,1)}, u32[]{:S(2)}, u32[]{:S(2)}) collective-permute-start(bf16[1024,512]{1,0:T(8,128)(2,1)} %get-tuple-element.158), channel_id=1, source_target_pairs={{0,2},{1,3},{2,0},{3,1},{4,6},{5,7},{6,4},{7,5},{8,10},{9,11},{10,... | collective-permute-start | bytes 3145736 | tf_op jit(solution)/shard_map/ppermute | solution.py:1324
  435.4 50.0 %collective-permute-start.25 = (bf16[4,256,768]{2,1,0:T(8,128)(2,1)}, bf16[4,256,768]{2,1,0:T(8,128)(2,1)}, u32[]{:S(2)}, u32[]{:S(2)}) collective-permute-start(bf16[4,256,768]{2,1,0:T(8,128)(2,1)} %weight_blocks.6.refs_11_), channel_id=1, source_target_pairs={{0,4},{4,0},{8,12},{12,8},{16,20},{20,16},{24,28},{28,24},{1,5},{5... | collective-permute-start | bytes 4718600 | tf_op jit(solution)/shard_map/ppermute | solution.py:1141
  437.0 85.6 %collective-permute-start.24 = (bf16[4,256,768]{2,1,0:T(8,128)(2,1)}, bf16[4,256,768]{2,1,0:T(8,128)(2,1)}, u32[]{:S(2)}, u32[]{:S(2)}) collective-permute-start(bf16[4,256,768]{2,1,0:T(8,128)(2,1)} %weight_blocks.7.refs_5_), channel_id=1, source_target_pairs={{0,8},{4,12},{8,0},{12,4},{16,24},{20,28},{24,16},{28,20},{1,9},{5... | collective-permute-start | bytes 4718600 | tf_op jit(solution)/shard_map/ppermute | solution.py:1141
  454.2 87.6 %collective-permute-start.23 = (f32[8,1024]{1,0:T(8,128)}, f32[8,1024]{1,0:T(8,128)}, u32[]{:S(2)}, u32[]{:S(2)}) collective-permute-start(f32[8,1024]{1,0:T(8,128)} %get-tuple-element.165.refs_11_.refs_3_), channel_id=1, source_target_pairs={{0,2},{1,3},{2,0},{3,1},{4,6},{5,7},{6,4},{7,5},{8,10},{9,11},{10,... | collective-permute-start | bytes 98312 | tf_op jit(solution)/shard_map/ppermute | solution.py:1324
  461.7 137.0 %collective-permute-start.28 = (bf16[4,512,256]{2,1,0:T(8,128)(2,1)}, bf16[4,512,256]{2,1,0:T(8,128)(2,1)}, u32[]{:S(2)}, u32[]{:S(2)}) collective-permute-start(bf16[4,512,256]{2,1,0:T(8,128)(2,1)} %weight_blocks.8.refs_2_), channel_id=1, source_target_pairs={{0,8},{4,12},{8,0},{12,4},{16,24},{20,28},{24,16},{28,20},{1,9},{5... | collective-permute-start | bytes 3145736 | tf_op jit(solution)/shard_map/ppermute | solution.py:1141
  462.2 79.7 %collective-permute-start.22 = (bf16[1024,512]{1,0:T(8,128)(2,1)}, bf16[1024,512]{1,0:T(8,128)(2,1)}, u32[]{:S(2)}, u32[]{:S(2)}) collective-permute-start(bf16[1024,512]{1,0:T(8,128)(2,1)} %get-tuple-element.168), channel_id=1, source_target_pairs={{0,2},{1,3},{2,0},{3,1},{4,6},{5,7},{6,4},{7,5},{8,10},{9,11},{10,... | collective-permute-start | bytes 3145736 | tf_op jit(solution)/shard_map/ppermute | solution.py:1324
  539.1 59.6 %collective-permute-start.27 = (bf16[2,256,768]{2,1,0:T(8,128)(2,1)}, bf16[2,256,768]{2,1,0:T(8,128)(2,1)}, u32[]{:S(2)}, u32[]{:S(2)}) collective-permute-start(bf16[2,256,768]{2,1,0:T(8,128)(2,1)} %get-tuple-element.188), channel_id=1, source_target_pairs={{0,16},{4,20},{8,24},{12,28},{16,0},{20,4},{24,8},{28,12},{1,17},{... | collective-permute-start | bytes 2359304 | tf_op jit(solution)/shard_map/ppermute | solution.py:1141
  539.6 59.1 %collective-permute-start.26 = (bf16[2,256,768]{2,1,0:T(8,128)(2,1)}, bf16[2,256,768]{2,1,0:T(8,128)(2,1)}, u32[]{:S(2)}, u32[]{:S(2)}) collective-permute-start(bf16[2,256,768]{2,1,0:T(8,128)(2,1)} %get-tuple-element.187), channel_id=1, source_target_pairs={{0,8},{4,12},{8,0},{12,4},{16,24},{20,28},{24,16},{28,20},{1,9},{5... | collective-permute-start | bytes 2359304 | tf_op jit(solution)/shard_map/ppermute | solution.py:1141
  541.8 14.5 %copy-start.11 = (f32[8,512]{1,0:T(8,128)S(1)}, f32[8,512]{1,0:T(8,128)}, u32[]{:S(2)}) copy-start(f32[8,512]{1,0:T(8,128)} %get-tuple-element.183) | copy-start | bytes 49156
  541.8 17.9 %copy-start.8 = (f32[13,8,128]{2,1,0:T(8,128)S(1)}, f32[13,8,128]{2,1,0:T(8,128)}, u32[]{:S(2)}) copy-start(f32[13,8,128]{2,1,0:T(8,128)} %get-tuple-element.185) | copy-start | bytes 159748
  603.3 41.9 %collective-permute-start.29 = (bf16[2,512,256]{2,1,0:T(8,128)(2,1)}, bf16[2,512,256]{2,1,0:T(8,128)(2,1)S(1)}, u32[]{:S(2)}, u32[]{:S(2)}) collective-permute-start(bf16[2,512,256]{2,1,0:T(8,128)(2,1)} %get-tuple-element.190), channel_id=1, source_target_pairs={{0,16},{4,20},{8,24},{12,28},{16,0},{20,4},{24,8},{28,12},{1,17},{... | collective-permute-start | bytes 1572872 | tf_op jit(solution)/shard_map/ppermute | solution.py:1141
  607.0 46.6 %collective-permute-start.31 = (bf16[1,256,768]{2,1,0:T(8,128)(2,1)}, bf16[1,256,768]{2,1,0:T(8,128)(2,1)S(1)}, u32[]{:S(2)}, u32[]{:S(2)}) collective-permute-start(bf16[1,256,768]{2,1,0:T(8,128)(2,1)} %get-tuple-element.194), channel_id=1, source_target_pairs={{0,16},{4,20},{8,24},{12,28},{16,0},{20,4},{24,8},{28,12},{1,17},{... | collective-permute-start | bytes 1179656 | tf_op jit(solution)/shard_map/ppermute | solution.py:1141
  607.0 46.6 %collective-permute-start.32 = (bf16[1,256,768]{2,1,0:T(8,128)(2,1)}, bf16[1,256,768]{2,1,0:T(8,128)(2,1)S(1)}, u32[]{:S(2)}, u32[]{:S(2)}) collective-permute-start(bf16[1,256,768]{2,1,0:T(8,128)(2,1)} %get-tuple-element.196), channel_id=1, source_target_pairs={{0,4},{4,0},{8,12},{12,8},{16,20},{20,16},{24,28},{28,24},{1,5},{5... | collective-permute-start | bytes 1179656 | tf_op jit(solution)/shard_map/ppermute | solution.py:1141
  649.3 8.5 %collective-permute-start.30 = (bf16[1,512,256]{2,1,0:T(8,128)(2,1)}, bf16[1,512,256]{2,1,0:T(8,128)(2,1)S(1)}, u32[]{:S(2)}, u32[]{:S(2)}) collective-permute-start(bf16[1,512,256]{2,1,0:T(8,128)(2,1)} %get-tuple-element.193), channel_id=1, source_target_pairs={{0,4},{4,0},{8,12},{12,8},{16,20},{20,16},{24,28},{28,24},{1,5},{5... | collective-permute-start | bytes 786440 | tf_op jit(solution)/shard_map/ppermute | solution.py:1141
  (12 other events, 57.8 us)
Sparse Core Ops, SparseCore 0:
  35.1 49.7 all-gather.1
  259.1 149.6 reduce-scatter.2
  412.9 215.2 reduce-scatter.4

commit v6 on v5

--- a/solution.py
+++ b/solution.py
@@ -32,10 +32,13 @@
     return lax.dot_general(a, b, (((0,), (0,)), ((), ())), preferred_element_type=F32)
 
 
+LARGE, TINY = 10**12, 10**4
+
+
 class Order:
     last = None
     names = 0
-    cost = 10**12
+    cost = LARGE
 
     @staticmethod
     def name(remote):
@@ -689,45 +692,65 @@
     return row_stats(total, weighted)
 
 
-def feed_back_body(n, pairs, steps, held_in, passed, *refs):
-    count = n if held_in or not pairs else 4
-    cots, refs = Gathered(refs[:count], pairs and not held_in, steps), refs[count:]
-    others = []
-    for _ in range(passed):
-        others.append(Gathered(refs[:4], pairs, steps))
-        refs = refs[4:]
+def join_body(count, steps, *refs):
+    gathered = [Gathered(refs[4 * i : 4 * i + 4], True, steps) for i in range(count)]
+    outs, scratch = refs[4 * count : 5 * count], refs[5 * count :]
+    for i, one in enumerate(gathered):
+        one.attach(scratch[2 * i : 2 * i + 2])
+    me = lax.axis_index("mp")
+
+    def work(wait):
+        for one, out in zip(gathered, outs):
+            for j, block in enumerate(one.refs()):
+                out[:, place_of(me, j, block.shape[1])] = block[...]
+
+    with_weights([], work, True, gathered)
+
+
+def join(gathered, full):
+    length = gathered[0][0].shape[0]
+    tile = min(256, length)
+    steps = length // tile
+    args, specs, scratch = [], [], []
+    for one in gathered:
+        args += [*one, *one]
+        specs += Gathered.specs(one, True, tile)
+        scratch += Gathered.scratch(one, True, steps)
+    return call(
+        "join",
+        lambda *refs: join_body(len(gathered), steps, *refs),
+        (steps,),
+        args,
+        specs,
+        [shape((length, full), BF16)] * len(gathered),
+        [rows_of((tile, full))] * len(gathered),
+        scratch=scratch,
+        remote=True,
+    )
+
+
+def feed_back_body(n, pairs, steps, *refs):
+    cot, refs = refs[0], refs[1:]
     slope, normed, gain, bias, up_weight, down_weight, up_grad, up_bias_sum, cot_sum = refs[:9]
     refs = refs[9:]
     parts = Scattered(pairs, n, steps, True)
     part_outs, refs = refs[: parts.count()], refs[parts.count() :]
-    fetched = ([] if held_in or not pairs else [cots]) + others
-    shared, refs = refs[: 2 * len(fetched)], refs[2 * len(fetched) :]
-    up_held, down_held, joined, row_sums, sems, *refs = refs
-    for one in fetched:
-        one.attach(refs[:2])
-        refs = refs[2:]
+    up_held, down_held, row_sums, sems, *refs = refs
     parts.attach(part_outs, refs)
     me = lax.axis_index("mp")
     inner = up_held.shape[1]
     width = gain.shape[1] // n
     step = divisor(inner, 512)
-    down_copies = col_blocks(me, n, width, down_weight, down_held, sems, n)
+    down_copies = [pltpu.make_async_copy(down_weight, down_held, sems.at[n])]
     up_copies = row_blocks(me, n, width, up_weight, up_held, sems, 0)
 
     def work(wait):
-        blocks = cots.refs()
-        for j, block in enumerate(blocks):
-            joined[:, j * width : (j + 1) * width] = block[...]
-        for i, one in enumerate(fetched):
-            there = blocks if one is cots else one.refs()
-            shared[2 * i][...] = there[1][...]
-            shared[2 * i + 1][...] = there[3][...]
-        accumulate(cot_sum, fold_rows(blocks[0][...].astype(F32)))
+        accumulate(cot_sum, fold_rows(cot[:, place_of(me, 0, width)].astype(F32)))
         wait(down_copies)
         bias_parts = []
         for c in range(inner // step):
             part = slice(c * step, (c + 1) * step)
-            value = dot_nt(joined[...], down_held[part, :]) * slope[:, part].astype(F32)
+            value = dot_nt(cot[...], down_held[part, :]) * slope[:, part].astype(F32)
             low = value.astype(BF16)
             up_grad[:, part] = low
             bias_parts.append(fold_rows(low.astype(F32)))
@@ -743,57 +766,38 @@
             me,
         )
 
-    with_weights(down_copies + up_copies, work, pairs, fetched)
+    with_weights(down_copies + up_copies, work, pairs)
     parts.finish(row_sums[...])
 
 
-def feed_back(n, pairs, cots, others, slope, normed, gain, bias, up_weight, down_weight):
+def feed_back(n, pairs, cot, slope, normed, gain, bias, up_weight, down_weight):
     length, full = normed.shape
     width = full // n
     inner = up_weight.shape[1]
     tile = min(256, length)
     steps = length // tile
-    held_in = pairs and len(cots) == n
-    others = others if pairs else []
-    fetch = ([] if held_in or not pairs else [cots]) + others
     parts = Scattered(pairs, n, steps, True)
     part_outs, part_specs = parts.outs(length, width)
-    args = [*cots, *(cots if pairs and not held_in else ())]
-    specs = Gathered.specs(cots, pairs and not held_in, tile)
-    for one in others:
-        args += [*one, *one]
-        specs += Gathered.specs(one, pairs, tile)
     got = call(
         "feed_back",
-        lambda *refs: feed_back_body(n, pairs, steps, held_in, len(others), *refs),
+        lambda *refs: feed_back_body(n, pairs, steps, *refs),
         (steps,),
-        (*args, slope, normed, gain, bias, up_weight, down_weight),
-        specs
-        + [rows_of((tile, inner)), rows_of((tile, full))]
+        (cot, slope, normed, gain, bias, up_weight, down_weight),
+        [rows_of((tile, full)), rows_of((tile, inner)), rows_of((tile, full))]
         + [fixed((8, full))] * 2
         + [ANY] * 2,
-        [shape((length, inner), BF16), shape((8, inner), F32), shape((8, width), F32)]
-        + part_outs
-        + [shape((length, width), BF16)] * (2 * len(fetch)),
-        [rows_of((tile, inner)), fixed((8, inner)), fixed((8, width))]
-        + part_specs
-        + [rows_of((tile, width))] * (2 * len(fetch)),
+        [shape((length, inner), BF16), shape((8, inner), F32), shape((8, width), F32)] + part_outs,
+        [rows_of((tile, inner)), fixed((8, inner)), fixed((8, width))] + part_specs,
         scratch=[
             pltpu.VMEM((full, inner), BF16),
             pltpu.VMEM((inner, full), BF16),
-            pltpu.VMEM((tile, full), BF16),
             pltpu.VMEM((8, tile), F32),
-            pltpu.SemaphoreType.DMA((2 * n,)),
+            pltpu.SemaphoreType.DMA((n + 1,)),
         ]
-        + sum([Gathered.scratch(one, pairs, steps) for one in fetch], [])
         + parts.scratch(length, width),
         remote=pairs,
     )
-    got, shared = got[: 3 + parts.count()], got[3 + parts.count() :]
-    blocks = [
-        [one[0], shared[2 * i], one[1], shared[2 * i + 1]] for i, one in enumerate(fetch)
-    ]
-    return (*got[:3], got[3:], blocks)
+    return (*got[:3], got[3:])
 
 
 def norm_back(refs, n_parts, source, stat, sums, gain, full):
@@ -1000,34 +1004,6 @@
         + [pl.BlockSpec((length, across), lambda i, j: (0, j))] * rows,
         [shape((high, wide), BF16)],
         [pl.BlockSpec((tall, across), lambda i, j: (i, j))],
-    )[0]
-
-
-def weight_of_blocks_body(rows, n, me, *refs):
-    lefts, rights, out = refs[:rows], refs[rows:-1], refs[-1]
-    width = rights[0].shape[1]
-    turned = [left[...].T for left in lefts]
-    for j in range(n):
-        total = 0.0
-        for r in range(rows):
-            total += dot_nn(turned[r], rights[r * n + j][...])
-        out[:, place_of(me[0], j, width)] = total.astype(BF16)
-
-
-def weight_of_blocks(me, lefts, rights):
-    rows, n, (length, high) = len(lefts), len(rights[0]), lefts[0].shape
-    width = rights[0][0].shape[1]
-    tall = divisor(high, 512)
-    return call(
-        "weight_grad",
-        lambda *refs: weight_of_blocks_body(rows, n, *refs),
-        (high // tall,),
-        (me, *lefts, *sum(rights, [])),
-        [SMEM]
-        + [pl.BlockSpec((length, tall), lambda i: (0, i))] * rows
-        + [fixed((length, width))] * (rows * n),
-        [shape((high, n * width), BF16)],
-        [rows_of((tall, n * width))],
     )[0]
 
 
@@ -1415,7 +1391,7 @@
     spread = full % (128 * groups) == 0 and groups >= 4
     last = row_count - 1
 
-    Order.last, Order.names, Order.cost = None, 0, 10**12
+    Order.last, Order.names, Order.cost = None, 0, LARGE
     vectors = jnp.stack([first_gain, first_bias, second_gain, second_bias])
     vectors = ring.gather_start(jnp.repeat(vectors, 8, 0))
     piece = ring.out_start(out_weight)
@@ -1473,26 +1449,27 @@
         hidden[r], normed2[r], stat2[r], activated[r], slope[r], parts = got
         branch[r] = ring.scatter(parts)[0]
 
-    def back(r, others):
-        nonlocal up_bias_sum, down_bias_sum
-        up_grad[r], up_sum, cot_sum, parts, blocks = feed_back(
-            n, pairs, cots[r], others, slope[r], normed2[r], gain2, bias2, up_weight, down_weight
+    def spread_over_dp(value, dim):
+        return lax.psum_scatter(value, "dp", scatter_dimension=dim, tiled=True)
+
+    if pairs:
+        cot_full = join(cots, full)
+        branch[0][1] = gate(branch[0][1:])[0]
+    else:
+        cot_full = [lax.all_gather(v, "mp", axis=1, tiled=True) for v in cot_rows]
+    if spread:
+        down_sum = Spread(activated, cot_full, 1, (1, 2, 4))
+        down_sum.first()
+
+    for r in rows:
+        up_grad[r], up_sum, cot_sum, parts = feed_back(
+            n, pairs, cot_full[r], slope[r], normed2[r], gain2, bias2, up_weight, down_weight
         )
         up_bias_sum += up_sum
         down_bias_sum += cot_sum
         parts2[r] = ring.scatter(parts, True)
-        return blocks
-
-    def spread_over_dp(value, dim):
-        return lax.psum_scatter(value, "dp", scatter_dimension=dim, tiled=True)
-
-    blocks = back(0, cots[1:])
-    if pairs:
-        cots = blocks
-        branch[0][1] = gate(branch[0][1:])[0]
-    down_sum = spread_over_dp(weight_of_blocks(ring.me[None], activated, cots), 1)
-    for r in rows[1:]:
-        back(r, [])
+        if r == 0 and pairs:
+            branch[last][1] = gate(branch[last][1:])[0]
 
     def hidden_step(r):
         nonlocal gain2_sum, bias2_sum
@@ -1505,34 +1482,31 @@
         grads[r] = ring.gather_start(low_grad)
 
     hidden_step(0)
-    up_sum = spread_over_dp(weight_grad(normed2, up_grad), 0)
-    if pairs:
-        branch[last][1] = gate(branch[last][1:])[0]
+    if spread:
+        up_sum = Spread(normed2, up_grad, 0, (1, 2, 4))
+        up_sum.first()
+
+        down_sum.keep_added()
 
     for r in rows:
         grad_full[r], attended_grad = attended_back(n, pairs, grads[r], out_weight)
         if r < last:
             hidden_step(r + 1)
-        Order.cost = 10**4 if r < last else 10**12
         qkv_grad[r] = attend_back(starts[r], tables, qkv[r], attended_grad, logs[r])
-        Order.cost = 10**12
         if r == last and spread:
-            qkv_sum = [
-                Spread(normed1, qkv_grad, 0, (1, 2, 4), (0, 2)),
-                Spread(normed1, qkv_grad, 0, (2, 4, 1), (1, 2)),
-            ]
-            qkv_sum[0].first()
-            qkv_sum[1].first()
+            advance(down_sum)
+            qkv_sum = Spread(normed1, qkv_grad, 0, (1, 2, 4))
+            qkv_sum.first()
+        if r > 0 and pairs:
+            parts, row_sums = parts1[r - 1]
+            parts[1], row_sums[1] = gate([parts[1], row_sums[1]])
         parts = project_back(n, pairs, qkv_grad[r], normed1[r], gain1, bias1, qkv_weight)
         parts1[r] = ring.scatter(parts, True)
 
     if spread:
-        out_sum = Spread(attended, grad_full, 1, (2, 4, 1))
+        up_sum.keep_added()
+        out_sum = Spread(attended, grad_full, 1, (1, 2, 4))
         out_sum.first()
-    if pairs:
-        parts, row_sums = parts1[0]
-        parts[1], row_sums[1] = gate([parts[1], row_sums[1]])
-    down_sum = gate([down_sum])[0]
     made = output(branch, hidden, down_bias8)
 
     grad_history, depth_sum, gain1_sum, bias1_sum = None, 0.0, 0.0, 0.0
@@ -1553,21 +1527,26 @@
         depth_sum += depth_part
         gain1_sum += gain_part
         bias1_sum += bias_part
-        if r == 0 and spread:
-            qkv_sum[0].keep_added()
-            qkv_sum[1].keep_added()
-            out_sum.keep()
-
-    Order.cost = 10**4
+        if r == 0:
+            if pairs:
+                parts, row_sums = parts1[last]
+                parts[1], row_sums[1] = gate([parts[1], row_sums[1]])
+            if spread:
+                qkv_sum.keep_added()
+
+    if spread:
+        down_sum.coming = gate([down_sum.coming])[0]
+        advance(up_sum)
+        out_sum.keep_added()
+        advance(qkv_sum, out_sum)
+    else:
+        qkv_sum = spread_over_dp(weight_grad(normed1, qkv_grad), 0)
+        out_sum = spread_over_dp(weight_grad(attended, grad_full), 1)
+        down_sum = spread_over_dp(weight_grad(activated, cot_full), 1)
+        up_sum = spread_over_dp(weight_grad(normed2, up_grad), 0)
+    down_total, up_total, out_total, qkv_total = finish([down_sum], [up_sum], [out_sum], [qkv_sum])
     vectors = [up_bias_sum, down_bias_sum, gain2_sum, bias2_sum, gain1_sum, bias1_sum]
     totals, depth_grad = sums([jnp.sum(v, 0) for v in vectors], jnp.sum(depth_sum, (1, 2)))
-    if spread:
-        advance(qkv_sum[0], qkv_sum[1], out_sum)
-        advance(out_sum)
-    else:
-        qkv_sum = [spread_over_dp(weight_grad(normed1, qkv_grad), 0)]
-        out_sum = spread_over_dp(weight_grad(attended, grad_full), 1)
-    down_total, up_total, out_total, qkv_total = finish([down_sum], [up_sum], [out_sum], qkv_sum)
     return (
         made,
         grad_history,

time: 675 us -> 696 us (1.031)
  waiting for transfers between devices: 107 us -> 144 us
  Pallas kernels: 488 us -> 473 us
    ppermute x9 -> x12, waiting for transfers between devices: 70.6 us -> 117 us  [send(): lax.ppermute(value, 'dp', [(i, i ^ bit) for i in range(self.groups)])]
    pallas_call x42 -> x45, Pallas kernels: 488 us -> 473 us  [call(): pl.pallas_call(without_extra, grid_spec=pltpu.PrefetchScalarGridSpec(num_...]
    ppermute x20, waiting for transfers between devices: 32.4 us -> 22.6 us  [over_chip(): return lax.ppermute(value, 'mp', self.chip)]
    ppermute x9 -> x12, starting transfers between devices: 11.6 us -> 16.6 us  [send(): lax.ppermute(value, 'dp', [(i, i ^ bit) for i in range(self.groups)])]
  transfers between devices with their start and end apart: 36 -> 37, of which waited for: 9 -> 10; matrix products, arithmetic and copies ran while one was open for 3% -> 2% of each run, Pallas kernels for 72% -> 66%
where the time goes in v6:
time: 696 us; the launch traced here: 692 us
  Pallas kernels  473 us (68%)
  waiting for transfers between devices  144 us (21%)
  starting transfers between devices  40.3 us (6%)
  between operations  14.8 us (2%)
  local copies, waits for them, and re-layouts  14.5 us (2%)
    pallas_call x45, Pallas kernels, call(): pl.pallas_call(without_extra, grid_spec=pltpu.PrefetchScalarGridSpec(num_...  473 us
    ppermute x12, waiting for transfers between devices, send(): lax.ppermute(value, 'dp', [(i, i ^ bit) for i in range(self.groups)])  117 us
    ppermute x20, starting transfers between devices, over_chip(): return lax.ppermute(value, 'mp', self.chip)  23.1 us
    ppermute x20, waiting for transfers between devices, over_chip(): return lax.ppermute(value, 'mp', self.chip)  22.6 us
    ppermute x12, starting transfers between devices, send(): lax.ppermute(value, 'dp', [(i, i ^ bit) for i in range(self.groups)])  16.6 us
  transfers between devices with their start and end apart: 37, of which 10 were waited for; matrix products, arithmetic and copies ran while one was open for 2% of the time, Pallas kernels for 66%

profile of v6, /device:TPU:0, one launch (start us, length us, event | category | flops | bytes accessed | tf_op | source)
XLA Modules:
  0.0 692.1 jit_solution(8178450311820784085)
XLA Ops:
  8.6 3.0 collective-permute-start.2
  13.7 8.0 %average.2 = (f32[1024,512]{1,0:T(8,128)}, bf16[1024,512]{1,0:T(8,128)(2,1)}) custom-call(f32[13]{0:T(128)} %refs_0_.7, bf16[13,2048,512]{2,1,0:T(8,128)(2,1)} %refs_9_.3), custom_call_target="tpu_custom_call" | custom-call | flops 999999995904 | bytes 100000000 | tf_op jit(solution)/shard_map/average/pallas_call | solution.py:60
  21.7 2.0 collective-permute-start
  27.1 7.8 %average.3 = (f32[1024,512]{1,0:T(8,128)}, bf16[1024,512]{1,0:T(8,128)(2,1)}) custom-call(f32[13]{0:T(128)} %refs_0_.7, bf16[13,2048,512]{2,1,0:T(8,128)(2,1)} %refs_9_.3, f32[32,512]{1,0:T(8,128)} %get-tuple-element.113.refs_2_), custom_call_target="tpu_custom_call" | custom-call | flops 999999995904 | bytes 100000000 | tf_op jit(solution)/shard_map/average/pallas_call | solution.py:60
  36.7 10.5 %collective-permute-done.refs_1_.refs_3_.refs_5_ = bf16[1024,512]{1,0:T(8,128)(2,1)} collective-permute-done((bf16[1024,512]{1,0:T(8,128)(2,1)}, bf16[1024,512]{1,0:T(8,128)(2,1)}, u32[]{:S(2)}, u32[]{:S(2)}) %collective-permute-start) | collective-permute-done | bytes 1048608 | tf_op jit(solution)/shard_map/ppermute | solution.py:1300
  48.8 18.1 %project.2 = (bf16[1024,1536]{1,0:T(8,128)(2,1)}, bf16[1024,2048]{1,0:T(8,128)(2,1)}, f32[1024,128]{1,0:T(8,128)}, bf16[1024,512]{1,0:T(8,128)(2,1)}, bf16[1024,512]{1,0:T(8,128)(2,1)}) custom-call(bf16[1024,512]{1,0:T(8,128)(2,1)} %get-tuple-element.111.refs_0_.refs_2_, bf16[1024,512]{1,0:T(8,128)(2,1)} %collective-permute-done.refs_1_.refs_3_.refs_5_, ...), custom_call_target="tpu_custom_call" | custom-call | flops 999999995904 | bytes 100000000 | tf_op jit(solution)/shard_map/project/pallas_call | solution.py:60
  67.6 10.1 %attend.2 = (bf16[1024,512]{1,0:T(8,128)(2,1)}, f32[4,8,1024]{2,1,0:T(8,128)}) custom-call(s32[8,1024]{1,0:T(8,128)} %broadcast_in_dim.19.refs_0_, bf16[1024,1536]{1,0:T(8,128)(2,1)} %get-tuple-element.116.refs_1_.refs_3_, f32[1024,128]{1,0:T(8,128)} %get-tuple-element.117.refs_2_.refs_6_), custom_call_target="tpu_custom_call" | custom-call | flops 999999995904 | bytes 100000000 | tf_op jit(solution)/shard_map/attend/pallas_call | solution.py:60
  77.9 17.9 %project.3 = (bf16[1024,1536]{1,0:T(8,128)(2,1)}, bf16[1024,2048]{1,0:T(8,128)(2,1)}, f32[1024,128]{1,0:T(8,128)}, bf16[1024,512]{1,0:T(8,128)(2,1)}, bf16[1024,512]{1,0:T(8,128)(2,1)}) custom-call(bf16[1024,512]{1,0:T(8,128)(2,1)} %gate.11.refs_9_.refs_0_.refs_2_, bf16[1024,512]{1,0:T(8,128)(2,1)} %collective-permute-done.7.refs_1_.refs_3_.refs_5_, ...), custom_call_target="tpu_custom_call" | custom-call | flops 999999995904 | bytes 100000000 | tf_op jit(solution)/shard_map/project/pallas_call | solution.py:60
  96.5 9.7 %attend.3 = (bf16[1024,512]{1,0:T(8,128)(2,1)}, f32[4,8,1024]{2,1,0:T(8,128)}) custom-call(s32[8,1024]{1,0:T(8,128)} %broadcast_in_dim.22.refs_0_, bf16[1024,1536]{1,0:T(8,128)(2,1)} %get-tuple-element.123.refs_1_.refs_3_, f32[1024,128]{1,0:T(8,128)} %get-tuple-element.124.refs_2_.refs_6_), custom_call_target="tpu_custom_call" | custom-call | flops 999999995904 | bytes 100000000 | tf_op jit(solution)/shard_map/attend/pallas_call | solution.py:60
  108.3 4.1 collective-permute-done.8.refs_10_
  113.1 40.8 %feed.2 = (f32[1024,512]{1,0:T(8,128)}, bf16[1024,2048]{1,0:T(8,128)(2,1)}, f32[1024,128]{1,0:T(8,128)}, bf16[1024,2048]{1,0:T(8,128)(2,1)}, bf16[1024,2048]{1,0...) custom-call(bf16[1024,512]{1,0:T(8,128)(2,1)} %get-tuple-element.118.refs_0_.refs_2_.refs_1_, ...), custom_call_target="tpu_custom_call" | custom-call | flops 999999995904 | bytes 100000000 | tf_op jit(solution)/shard_map/feed/pallas_call | solution.py:60
  154.2 1.8 collective-permute-start.9
  156.0 41.1 %feed.3 = (f32[1024,512]{1,0:T(8,128)}, bf16[1024,2048]{1,0:T(8,128)(2,1)}, f32[1024,128]{1,0:T(8,128)}, bf16[1024,2048]{1,0:T(8,128)(2,1)}, bf16[1024,2048]{1,0...) custom-call(bf16[1024,512]{1,0:T(8,128)(2,1)} %get-tuple-element.130.refs_0_.refs_2_, ...), custom_call_target="tpu_custom_call" | custom-call | flops 999999995904 | bytes 100000000 | tf_op jit(solution)/shard_map/feed/pallas_call | solution.py:60
  197.4 11.3 %join.1 = (bf16[1024,2048]{1,0:T(8,128)(2,1)}, bf16[1024,2048]{1,0:T(8,128)(2,1)}) custom-call(bf16[1024,512]{1,0:T(8,128)(2,1)} %gate.13.refs_17_.refs_0_.refs_2_, bf16[1024,512]{1,0:T(8,128)(2,1)} %collective-permute-done.10.refs_1_.refs_3_, bf16[1024,512]{1,0:T(8,128)(2,1)} %gate.13.refs_17_.refs_0_.refs_2_, ...), custom_call_target="tpu_custom_call" | custom-call | flops 999999995904 | bytes 100000000 | tf_op jit(solution)/shard_map/join/pallas_call | solution.py:60
  208.7 13.6 %weight_blocks.8.refs_7_ = bf16[4,2048,256]{2,1,0:T(8,128)(2,1)} custom-call(s32[1]{0:T(128)} %bitcast.7.refs_0_, bf16[1024,2048]{1,0:T(8,128)(2,1)} %get-tuple-element.140.refs_1_, bf16[1024,2048]{1,0:T(8,128)(2,1)} %get-tuple-element.141.refs_2_, bf16[1024,2048]{1,0:T(8,128)(2,1)} %get-tuple-element.134.refs_1_.refs_3_.refs_5_.refs_7_.refs_9_.refs_0_, ...), custom_call_target="tpu_custom_call" | custom-call | flops 999999995904 | bytes 100000000 | tf_op jit(solution)/shard_map/weight_blocks/pallas_call | solution.py:60
  224.0 30.4 %feed_back.2 = (bf16[1024,2048]{1,0:T(8,128)(2,1)}, f32[8,2048]{1,0:T(8,128)}, f32[8,512]{1,0:T(8,128)}, bf16[1024,512]{1,0:T(8,128)(2,1)}, bf16[1024,512]{1,0:T(8,128)(2,1)}, /*index=5*/f32[8,1024]{1,0:T(8,128)}) custom-call(bf16[1024,2048]{1,0:T(8,128)(2,1)} %get-tuple-element.134.refs_1_.refs_3_.refs_5_.refs_7_.refs_9_.refs_0_, ...), custom_call_target="tpu_custom_call" | custom-call | flops 999999995904 | bytes 100000000 | tf_op jit(solution)/shard_map/feed_back/pallas_call | solution.py:60
  256.5 30.6 %feed_back.3 = (bf16[1024,2048]{1,0:T(8,128)(2,1)}, f32[8,2048]{1,0:T(8,128)}, f32[8,512]{1,0:T(8,128)}, bf16[1024,512]{1,0:T(8,128)(2,1)}, bf16[1024,512]{1,0:T(8,128)(2,1)}, /*index=5*/f32[8,1024]{1,0:T(8,128)}) custom-call(bf16[1024,2048]{1,0:T(8,128)(2,1)} %get-tuple-element.142.refs_4_.refs_6_.refs_8_.refs_10_.refs_0_, ...), custom_call_target="tpu_custom_call" | custom-call | flops 999999995904 | bytes 100000000 | tf_op jit(solution)/shard_map/feed_back/pallas_call | solution.py:60
  291.3 5.7 hidden_back.2
  298.6 14.7 %weight_blocks.9.refs_12_ = bf16[4,256,2048]{2,1,0:T(8,128)(2,1)} custom-call(s32[1]{0:T(128)} %bitcast.7.refs_0_, bf16[1024,2048]{1,0:T(8,128)(2,1)} %get-tuple-element.139.refs_2_.refs_1_.refs_3_.refs_5_.refs_7_, bf16[1024,2048]{1,0:T(8,128)(2,1)} %get-tuple-element.148.refs_2_.refs_4_.refs_6_.refs_8_, ...), custom_call_target="tpu_custom_call" | custom-call | flops 999999995904 | bytes 100000000 | tf_op jit(solution)/shard_map/weight_blocks/pallas_call | solution.py:60
  315.3 14.3 %weight_blocks.10 = (bf16[2,2048,256]{2,1,0:T(8,128)(2,1)}, bf16[2,2048,256]{2,1,0:T(8,128)(2,1)}) custom-call(s32[1]{0:T(128)} %bitcast.7.refs_0_, bf16[1024,2048]{1,0:T(8,128)(2,1)} %get-tuple-element.140.refs_1_, bf16[1024,2048]{1,0:T(8,128)(2,1)} %get-tuple-element.141.refs_2_, ...), custom_call_target="tpu_custom_call" | custom-call | flops 999999995904 | bytes 100000000 | tf_op jit(solution)/shard_map/weight_blocks/pallas_call | solution.py:60
  329.5 6.5 collective-permute-done.16.refs_1_.refs_3_
  336.1 9.0 %attended_back.2 = (bf16[1024,2048]{1,0:T(8,128)(2,1)}, bf16[1024,512]{1,0:T(8,128)(2,1)}) custom-call(bf16[1024,512]{1,0:T(8,128)(2,1)} %get-tuple-element.150.refs_0_.refs_2_, bf16[1024,512]{1,0:T(8,128)(2,1)} %collective-permute-done.16.refs_1_.refs_3_, bf16[1024,512]{1,0:T(8,128)(2,1)} %get-tuple-element.150.refs_0_.refs_2_, ...), custom_call_target="tpu_custom_call" | custom-call | flops 999999995904 | bytes 100000000 | tf_op jit(solution)/shard_map/attended_back/pallas_call | solution.py:60
  345.1 5.7 hidden_back.3
  350.8 12.4 %attend_back.2.refs_0_.refs_9_ = bf16[1024,1536]{1,0:T(8,128)(2,1)} custom-call(s32[8,1024]{1,0:T(8,128)} %broadcast_in_dim.19.refs_0_, f32[1024,128]{1,0:T(8,128)} %constant.19.clone.refs_6_.refs_1_, f32[1024,128]{1,0:T(8,128)} %constant.20.clone.refs_7_.refs_2_, bf16[1024,1536]{1,0:T(8,128)(2,1)} %get-tuple-element.116.refs_1_.refs_3_, ...), custom_call_target="tpu_custom_call" | custom-call | flops 999999995904 | bytes 100000000 | tf_op jit(solution)/shard_map/attend_back/pallas_call | solution.py:60
  366.3 15.5 %project_back.2 = (bf16[1024,512]{1,0:T(8,128)(2,1)}, bf16[1024,512]{1,0:T(8,128)(2,1)}, f32[8,1024]{1,0:T(8,128)}) custom-call(bf16[1024,1536]{1,0:T(8,128)(2,1)} %attend_back.2.refs_0_.refs_9_, bf16[1024,2048]{1,0:T(8,128)(2,1)} %get-tuple-element.162.refs_1_.refs_3_.refs_5_.refs_7_, f32[8,2048]{1,0:T(8,128)} %get-tuple-element.214.refs_4_.refs_2_, ...), custom_call_target="tpu_custom_call" | custom-call | flops 999999995904 | bytes 100000000 | tf_op jit(solution)/shard_map/project_back/pallas_call | solution.py:60
  383.9 5.6 collective-permute-done.20.refs_1_.refs_3_
  389.5 9.1 %attended_back.3 = (bf16[1024,2048]{1,0:T(8,128)(2,1)}, bf16[1024,512]{1,0:T(8,128)(2,1)}) custom-call(bf16[1024,512]{1,0:T(8,128)(2,1)} %get-tuple-element.160.refs_0_.refs_2_, bf16[1024,512]{1,0:T(8,128)(2,1)} %collective-permute-done.20.refs_1_.refs_3_, bf16[1024,512]{1,0:T(8,128)(2,1)} %get-tuple-element.160.refs_0_.refs_2_, ...), custom_call_target="tpu_custom_call" | custom-call | flops 999999995904 | bytes 100000000 | tf_op jit(solution)/shard_map/attended_back/pallas_call | solution.py:60
  398.6 12.6 %attend_back.3.refs_2_.refs_10_.refs_0_ = bf16[1024,1536]{1,0:T(8,128)(2,1)} custom-call(s32[8,1024]{1,0:T(8,128)} %broadcast_in_dim.22.refs_0_, f32[1024,128]{1,0:T(8,128)} %constant.19.clone.refs_6_.refs_1_, f32[1024,128]{1,0:T(8,128)} %constant.20.clone.refs_7_.refs_2_, bf16[1024,1536]{1,0:T(8,128)(2,1)} %get-tuple-element.123.refs_1_.refs_3_, ...), custom_call_target="tpu_custom_call" | custom-call | flops 999999995904 | bytes 100000000 | tf_op jit(solution)/shard_map/attend_back/pallas_call | solution.py:60
  412.5 4.2 fold.3
  416.7 12.3 %weight_blocks.11.refs_2_ = bf16[4,256,1536]{2,1,0:T(8,128)(2,1)} custom-call(s32[1]{0:T(128)} %bitcast.7.refs_0_, bf16[1024,2048]{1,0:T(8,128)(2,1)} %get-tuple-element.162.refs_1_.refs_3_.refs_5_.refs_7_, bf16[1024,2048]{1,0:T(8,128)(2,1)} %get-tuple-element.166.refs_2_.refs_4_.refs_6_.refs_8_.refs_1_, ...), custom_call_target="tpu_custom_call" | custom-call | flops 999999995904 | bytes 100000000 | tf_op jit(solution)/shard_map/weight_blocks/pallas_call | solution.py:60
  429.5 15.5 %project_back.3 = (bf16[1024,512]{1,0:T(8,128)(2,1)}, bf16[1024,512]{1,0:T(8,128)(2,1)}, f32[8,1024]{1,0:T(8,128)}) custom-call(bf16[1024,1536]{1,0:T(8,128)(2,1)} %attend_back.3.refs_2_.refs_10_.refs_0_, bf16[1024,2048]{1,0:T(8,128)(2,1)} %get-tuple-element.166.refs_2_.refs_4_.refs_6_.refs_8_.refs_1_, f32[8,2048]{1,0:T(8,128)} %get-tuple-element.214.refs_4_.refs_2_, ...), custom_call_target="tpu_custom_call" | custom-call | flops 999999995904 | bytes 100000000 | tf_op jit(solution)/shard_map/project_back/pallas_call | solution.py:60
  447.2 2.5 collective-permute-start.28
  449.7 15.3 %weight_blocks.12 = (bf16[2,256,2048]{2,1,0:T(8,128)(2,1)}, bf16[2,256,2048]{2,1,0:T(8,128)(2,1)}) custom-call(s32[1]{0:T(128)} %bitcast.7.refs_0_, bf16[1024,2048]{1,0:T(8,128)(2,1)} %get-tuple-element.139.refs_2_.refs_1_.refs_3_.refs_5_.refs_7_, bf16[1024,2048]{1,0:T(8,128)(2,1)} %get-tuple-element.148.refs_2_.refs_4_.refs_6_.refs_8_, ...), custom_call_target="tpu_custom_call" | custom-call | flops 999999995904 | bytes 100000000 | tf_op jit(solution)/shard_map/weight_blocks/pallas_call | solution.py:60
  465.1 6.2 weight_blocks.13.refs_7_
  473.4 6.3 output.1.refs_10_
  480.3 14.1 %average_back.2 = (bf16[13,2048,512]{2,1,0:T(8,128)(2,1)}, f32[13,8,128]{2,1,0:T(8,128)}, f32[8,512]{1,0:T(8,128)}, f32[8,512]{1,0:T(8,128)}) custom-call(f32[13]{0:T(128)} %refs_0_.7, bf16[1024,512]{1,0:T(8,128)(2,1)} %get-tuple-element.175.refs_1_, bf16[1024,512]{1,0:T(8,128)(2,1)} %get-tuple-element.176.refs_2_, ...), custom_call_target="tpu_custom_call" | custom-call | flops 999999995904 | bytes 100000000 | tf_op jit(solution)/shard_map/average_back/pallas_call | solution.py:60
  496.1 4.2 collective-permute-done.27.refs_11_
  500.3 12.6 %weight_blocks.14 = (bf16[2,256,1536]{2,1,0:T(8,128)(2,1)}, bf16[2,256,1536]{2,1,0:T(8,128)(2,1)}) custom-call(s32[1]{0:T(128)} %bitcast.7.refs_0_, bf16[1024,2048]{1,0:T(8,128)(2,1)} %get-tuple-element.162.refs_1_.refs_3_.refs_5_.refs_7_, bf16[1024,2048]{1,0:T(8,128)(2,1)} %get-tuple-element.166.refs_2_.refs_4_.refs_6_.refs_8_.refs_1_, ...), custom_call_target="tpu_custom_call" | custom-call | flops 999999995904 | bytes 100000000 | tf_op jit(solution)/shard_map/weight_blocks/pallas_call | solution.py:60
  514.5 14.3 %average_back.3 = (bf16[13,2048,512]{2,1,0:T(8,128)(2,1)}, f32[13,8,128]{2,1,0:T(8,128)}, f32[8,512]{1,0:T(8,128)}, f32[8,512]{1,0:T(8,128)}) custom-call(f32[13]{0:T(128)} %refs_0_.7, bf16[1024,512]{1,0:T(8,128)(2,1)} %get-tuple-element.173.refs_1_, bf16[1024,512]{1,0:T(8,128)(2,1)} %get-tuple-element.179.refs_2_, ...), custom_call_target="tpu_custom_call", output_to_operand_aliasing={{0}: (10, {})} | custom-call | flops 999999995904 | bytes 100000000 | tf_op jit(solution)/shard_map/average_back/pallas_call | solution.py:60
  528.9 14.6 %collective-permute-done.29.refs_1_ = bf16[2,256,2048]{2,1,0:T(8,128)(2,1)} collective-permute-done((bf16[2,256,2048]{2,1,0:T(8,128)(2,1)}, bf16[2,256,2048]{2,1,0:T(8,128)(2,1)}, u32[]{:S(2)}, u32[]{:S(2)}) %collective-permute-start.29) | collective-permute-done | bytes 2097184 | tf_op jit(solution)/shard_map/ppermute | solution.py:1117
  543.4 4.2 fold.4
  547.7 6.4 weight_blocks.15
  556.7 52.3 %collective-permute-done.33.refs_3_ = bf16[2,512,256]{2,1,0:T(8,128)(2,1)S(1)} collective-permute-done((bf16[2,512,256]{2,1,0:T(8,128)(2,1)}, bf16[2,512,256]{2,1,0:T(8,128)(2,1)S(1)}, u32[]{:S(2)}, u32[]{:S(2)}) %collective-permute-start.33) | collective-permute-done | bytes 524320 | tf_op jit(solution)/shard_map/ppermute | solution.py:1117
  609.8 4.2 fold.5
  614.8 2.3 collective-permute-start.34
  617.9 43.1 %collective-permute-done.34.refs_5_ = bf16[1,512,256]{2,1,0:T(8,128)(2,1)S(1)} collective-permute-done((bf16[1,512,256]{2,1,0:T(8,128)(2,1)}, bf16[1,512,256]{2,1,0:T(8,128)(2,1)S(1)}, u32[]{:S(2)}, u32[]{:S(2)}) %collective-permute-start.34) | collective-permute-done | bytes 262176 | tf_op jit(solution)/shard_map/ppermute | solution.py:1117
  662.0 5.7 finish.1
  667.7 13.5 %sums.1 = f32[48,128]{1,0:T(8,128)} custom-call(f32[48,128]{1,0:T(8,128)} %select_maximum_fusion.refs_0_, f32[512,256]{1,0:T(8,128)} %get-tuple-element.104.refs_1_), custom_call_target="tpu_custom_call" | custom-call | flops 999999995904 | bytes 100000000 | tf_op jit(solution)/shard_map/sums/pallas_call | solution.py:60
  (158 shorter events, 51.8 us)
Async XLA Ops:
  7.2 100.8 %all-gather.2.cloned.1.call-start = ((), (), s32[]{:S(2)}) async-start(), calls=%async_computation | async-start | bytes 2359296 | tf_op jit(solution)/shard_map/all_gather | solution.py:1340
  8.6 18.4 %collective-permute-start.2 = (f32[32,512]{1,0:T(8,128)}, f32[32,512]{1,0:T(8,128)}, u32[]{:S(2)}, u32[]{:S(2)}) collective-permute-start(f32[32,512]{1,0:T(8,128)} %broadcast_bitcast_fusion), channel_id=1, source_target_pairs={{0,2},{1,3},{2,0},{3,1},{4,6},{5,7},{6,4},{7,5},{8,10},{9,11},{10,... | collective-permute-start | bytes 196616 | tf_op jit(solution)/shard_map/ppermute | solution.py:1300
  11.6 23.4 %collective-permute-start.1 = (f32[32,512]{1,0:T(8,128)}, f32[32,512]{1,0:T(8,128)}, u32[]{:S(2)}, u32[]{:S(2)}) collective-permute-start(f32[32,512]{1,0:T(8,128)} %broadcast_bitcast_fusion), channel_id=1, source_target_pairs={{0,1},{1,0},{2,3},{3,2},{4,5},{5,4},{6,7},{7,6},{8,9},{9,8},{10,11... | collective-permute-start | bytes 196616 | tf_op jit(solution)/shard_map/ppermute | solution.py:1297
  11.6 96.8 %collective-permute-start.6 = (bf16[512,2048]{1,0:T(8,128)(2,1)}, bf16[512,2048]{1,0:T(8,128)(2,1)}, u32[]{:S(2)}, u32[]{:S(2)}) collective-permute-start(bf16[512,2048]{1,0:T(8,128)(2,1)} %refs_4_.10), channel_id=1, source_target_pairs={{0,1},{1,0},{2,3},{3,2},{4,5},{5,4},{6,7},{7,6},{8,9},{9,8},{10,11... | collective-permute-start | bytes 6291464 | tf_op jit(solution)/shard_map/ppermute | solution.py:1297
  13.7 13.3 %collective-permute-start.3 = (bf16[64,2048]{1,0:T(8,128)(2,1)}, bf16[64,2048]{1,0:T(8,128)(2,1)}, u32[]{:S(2)}, u32[]{:S(2)}) collective-permute-start(bf16[64,2048]{1,0:T(8,128)(2,1)} %constant_dynamic-slice_fusion), channel_id=1, source_target_pairs={{0,2},{1,3},{2,0},{3,1},{4,6},{5,7},{6,4},{7,5},{8,10},{9,11},{10,... | collective-permute-start | bytes 786440 | tf_op jit(solution)/shard_map/ppermute | solution.py:1300
  13.7 10.0 %copy-start = (bf16[2048,512]{1,0:T(8,128)(2,1)S(1)}, bf16[2048,512]{1,0:T(8,128)(2,1)}, u32[]{:S(2)}) copy-start(bf16[2048,512]{1,0:T(8,128)(2,1)} %refs_4_.8) | copy-start | bytes 6291460
  21.7 25.4 %collective-permute-start = (bf16[1024,512]{1,0:T(8,128)(2,1)}, bf16[1024,512]{1,0:T(8,128)(2,1)}, u32[]{:S(2)}, u32[]{:S(2)}) collective-permute-start(bf16[1024,512]{1,0:T(8,128)(2,1)} %get-tuple-element.111.refs_0_.refs_2_), channel_id=1, source_target_pairs={{0,2},{1,3},{2,0},{3,1},{4,6},{5,7},{6,4},{7,5},{8,10},{9,11},{10,... | collective-permute-start | bytes 3145736 | tf_op jit(solution)/shard_map/ppermute | solution.py:1300
  27.0 8.0 %collective-permute-start.4 = (f32[32,512]{1,0:T(8,128)}, f32[32,512]{1,0:T(8,128)}, u32[]{:S(2)}, u32[]{:S(2)}) collective-permute-start(f32[32,512]{1,0:T(8,128)} %get-tuple-element.113.refs_2_), channel_id=1, source_target_pairs={{0,1},{1,0},{2,3},{3,2},{4,5},{5,4},{6,7},{7,6},{8,9},{9,8},{10,11... | collective-permute-start | bytes 196616 | tf_op jit(solution)/shard_map/ppermute | solution.py:1297
  47.1 30.8 %collective-permute-start.7 = (bf16[1024,512]{1,0:T(8,128)(2,1)}, bf16[1024,512]{1,0:T(8,128)(2,1)}, u32[]{:S(2)}, u32[]{:S(2)}) collective-permute-start(bf16[1024,512]{1,0:T(8,128)(2,1)} %gate.11.refs_9_.refs_0_.refs_2_), channel_id=1, source_target_pairs={{0,2},{1,3},{2,0},{3,1},{4,6},{5,7},{6,4},{7,5},{8,10},{9,11},{10,... | collective-permute-start | bytes 3145736 | tf_op jit(solution)/shard_map/ppermute | solution.py:1300
  48.8 18.1 %copy-start.19 = (s32[1,1024]{1,0:T(1,128)S(1)}, s32[1,1024]{1,0:T(1,128)}, u32[]{:S(2)}) copy-start(s32[1,1024]{1,0:T(1,128)} %get-tuple-element.221) | copy-start | bytes 12292
  77.7 30.6 %collective-permute-start.5 = (bf16[1024,512]{1,0:T(8,128)(2,1)}, bf16[1024,512]{1,0:T(8,128)(2,1)}, u32[]{:S(2)}, u32[]{:S(2)}) collective-permute-start(bf16[1024,512]{1,0:T(8,128)(2,1)} %get-tuple-element.118.refs_0_.refs_2_.refs_1_), channel_id=1, source_target_pairs={{0,2},{1,3},{2,0},{3,1},{4,6},{5,7},{6,4},{7,5},{8,10},{9,11},{10,... | collective-permute-start | bytes 3145736 | tf_op jit(solution)/shard_map/ppermute | solution.py:1300
  77.9 17.9 %copy-start.18 = (s32[1,1024]{1,0:T(1,128)S(1)}, s32[1,1024]{1,0:T(1,128)}, u32[]{:S(2)}) copy-start(s32[1,1024]{1,0:T(1,128)} %get-tuple-element.220) | copy-start | bytes 12292
  106.2 49.8 %collective-permute-start.12 = (bf16[1024,512]{1,0:T(8,128)(2,1)}, bf16[1024,512]{1,0:T(8,128)(2,1)}, u32[]{:S(2)}, u32[]{:S(2)}) collective-permute-start(bf16[1024,512]{1,0:T(8,128)(2,1)} %get-tuple-element.130.refs_0_.refs_2_), channel_id=1, source_target_pairs={{0,2},{1,3},{2,0},{3,1},{4,6},{5,7},{6,4},{7,5},{8,10},{9,11},{10,... | collective-permute-start | bytes 3145736 | tf_op jit(solution)/shard_map/ppermute | solution.py:1300
  108.0 4.5 collective-permute-start.8
  108.0 89.4 %collective-permute-start.10 = (bf16[1024,512]{1,0:T(8,128)(2,1)}, bf16[1024,512]{1,0:T(8,128)(2,1)}, u32[]{:S(2)}, u32[]{:S(2)}) collective-permute-start(bf16[1024,512]{1,0:T(8,128)(2,1)} %gate.13.refs_17_.refs_0_.refs_2_), channel_id=1, source_target_pairs={{0,2},{1,3},{2,0},{3,1},{4,6},{5,7},{6,4},{7,5},{8,10},{9,11},{10,... | collective-permute-start | bytes 3145736 | tf_op jit(solution)/shard_map/ppermute | solution.py:1300
  153.9 43.5 %collective-permute-start.11 = (bf16[1024,512]{1,0:T(8,128)(2,1)}, bf16[1024,512]{1,0:T(8,128)(2,1)}, u32[]{:S(2)}, u32[]{:S(2)}) collective-permute-start(bf16[1024,512]{1,0:T(8,128)(2,1)} %gate.14.refs_17_.refs_4_.refs_6_), channel_id=1, source_target_pairs={{0,2},{1,3},{2,0},{3,1},{4,6},{5,7},{6,4},{7,5},{8,10},{9,11},{10,... | collective-permute-start | bytes 3145736 | tf_op jit(solution)/shard_map/ppermute | solution.py:1300
  154.2 54.5 %collective-permute-start.9 = (bf16[1024,512]{1,0:T(8,128)(2,1)}, bf16[1024,512]{1,0:T(8,128)(2,1)}, u32[]{:S(2)}, u32[]{:S(2)}) collective-permute-start(bf16[1024,512]{1,0:T(8,128)(2,1)} %get-tuple-element.128), channel_id=1, source_target_pairs={{0,2},{1,3},{2,0},{3,1},{4,6},{5,7},{6,4},{7,5},{8,10},{9,11},{10,... | collective-permute-start | bytes 3145736 | tf_op jit(solution)/shard_map/ppermute | solution.py:1300
  197.1 59.4 %collective-permute-start.13 = (bf16[1024,512]{1,0:T(8,128)(2,1)}, bf16[1024,512]{1,0:T(8,128)(2,1)}, u32[]{:S(2)}, u32[]{:S(2)}) collective-permute-start(bf16[1024,512]{1,0:T(8,128)(2,1)} %get-tuple-element.137), channel_id=1, source_target_pairs={{0,2},{1,3},{2,0},{3,1},{4,6},{5,7},{6,4},{7,5},{8,10},{9,11},{10,... | collective-permute-start | bytes 3145736 | tf_op jit(solution)/shard_map/ppermute | solution.py:1300
  222.3 93.0 %collective-permute-start.17 = (bf16[4,2048,256]{2,1,0:T(8,128)(2,1)}, bf16[4,2048,256]{2,1,0:T(8,128)(2,1)}, u32[]{:S(2)}, u32[]{:S(2)}) collective-permute-start(bf16[4,2048,256]{2,1,0:T(8,128)(2,1)} %weight_blocks.8.refs_7_), channel_id=1, source_target_pairs={{0,4},{4,0},{8,12},{12,8},{16,20},{20,16},{24,28},{28,24},{1,5},{5... | collective-permute-start | bytes 12582920 | tf_op jit(solution)/shard_map/ppermute | solution.py:1117
  254.4 36.3 %collective-permute-start.14 = (bf16[1024,512]{1,0:T(8,128)(2,1)}, bf16[1024,512]{1,0:T(8,128)(2,1)}, u32[]{:S(2)}, u32[]{:S(2)}) collective-permute-start(bf16[1024,512]{1,0:T(8,128)(2,1)} %get-tuple-element.145), channel_id=1, source_target_pairs={{0,2},{1,3},{2,0},{3,1},{4,6},{5,7},{6,4},{7,5},{8,10},{9,11},{10,... | collective-permute-start | bytes 3145736 | tf_op jit(solution)/shard_map/ppermute | solution.py:1300
  256.1 34.6 %collective-permute-start.15 = (f32[8,1024]{1,0:T(8,128)}, f32[8,1024]{1,0:T(8,128)}, u32[]{:S(2)}, u32[]{:S(2)}) collective-permute-start(f32[8,1024]{1,0:T(8,128)} %get-tuple-element.146.refs_2_), channel_id=1, source_target_pairs={{0,2},{1,3},{2,0},{3,1},{4,6},{5,7},{6,4},{7,5},{8,10},{9,11},{10,... | collective-permute-start | bytes 98312 | tf_op jit(solution)/shard_map/ppermute | solution.py:1300
  256.5 32.7 %copy-start.1 = (f32[8,2048]{1,0:T(8,128)S(1)}, f32[8,2048]{1,0:T(8,128)}, u32[]{:S(2)}) copy-start(f32[8,2048]{1,0:T(8,128)} %get-tuple-element.185) | copy-start | bytes 196612
  256.5 34.2 %copy-start.22 = (f32[512]{0:T(512)S(1)}, f32[512]{0:T(512)}, u32[]{:S(2)}) copy-start(f32[512]{0:T(512)} %param.23) | copy-start | bytes 6148
  287.1 58.0 %collective-permute-start.18 = (bf16[1024,512]{1,0:T(8,128)(2,1)}, bf16[1024,512]{1,0:T(8,128)(2,1)}, u32[]{:S(2)}, u32[]{:S(2)}) collective-permute-start(bf16[1024,512]{1,0:T(8,128)(2,1)} %get-tuple-element.157), channel_id=1, source_target_pairs={{0,2},{1,3},{2,0},{3,1},{4,6},{5,7},{6,4},{7,5},{8,10},{9,11},{10,... | collective-permute-start | bytes 3145736 | tf_op jit(solution)/shard_map/ppermute | solution.py:1300
  288.7 56.3 %collective-permute-start.19 = (f32[8,1024]{1,0:T(8,128)}, f32[8,1024]{1,0:T(8,128)}, u32[]{:S(2)}, u32[]{:S(2)}) collective-permute-start(f32[8,1024]{1,0:T(8,128)} %get-tuple-element.158.refs_2_), channel_id=1, source_target_pairs={{0,2},{1,3},{2,0},{3,1},{4,6},{5,7},{6,4},{7,5},{8,10},{9,11},{10,... | collective-permute-start | bytes 98312 | tf_op jit(solution)/shard_map/ppermute | solution.py:1300
  297.0 39.1 %collective-permute-start.16 = (bf16[1024,512]{1,0:T(8,128)(2,1)}, bf16[1024,512]{1,0:T(8,128)(2,1)}, u32[]{:S(2)}, u32[]{:S(2)}) collective-permute-start(bf16[1024,512]{1,0:T(8,128)(2,1)} %get-tuple-element.150.refs_0_.refs_2_), channel_id=1, source_target_pairs={{0,2},{1,3},{2,0},{3,1},{4,6},{5,7},{6,4},{7,5},{8,10},{9,11},{10,... | collective-permute-start | bytes 3145736 | tf_op jit(solution)/shard_map/ppermute | solution.py:1300
  313.3 136.5 %collective-permute-start.21 = (bf16[4,256,2048]{2,1,0:T(8,128)(2,1)}, bf16[4,256,2048]{2,1,0:T(8,128)(2,1)}, u32[]{:S(2)}, u32[]{:S(2)}) collective-permute-start(bf16[4,256,2048]{2,1,0:T(8,128)(2,1)} %weight_blocks.9.refs_12_), channel_id=1, source_target_pairs={{0,4},{4,0},{8,12},{12,8},{16,20},{20,16},{24,28},{28,24},{1,5},{5... | collective-permute-start | bytes 12582920 | tf_op jit(solution)/shard_map/ppermute | solution.py:1117
  363.1 26.3 %collective-permute-start.20 = (bf16[1024,512]{1,0:T(8,128)(2,1)}, bf16[1024,512]{1,0:T(8,128)(2,1)}, u32[]{:S(2)}, u32[]{:S(2)}) collective-permute-start(bf16[1024,512]{1,0:T(8,128)(2,1)} %get-tuple-element.160.refs_0_.refs_2_), channel_id=1, source_target_pairs={{0,2},{1,3},{2,0},{3,1},{4,6},{5,7},{6,4},{7,5},{8,10},{9,11},{10,... | collective-permute-start | bytes 3145736 | tf_op jit(solution)/shard_map/ppermute | solution.py:1300
  364.7 47.7 %collective-permute-start.24 = (bf16[2,2048,256]{2,1,0:T(8,128)(2,1)}, bf16[2,2048,256]{2,1,0:T(8,128)(2,1)}, u32[]{:S(2)}, u32[]{:S(2)}) collective-permute-start(bf16[2,2048,256]{2,1,0:T(8,128)(2,1)} %get-tuple-element.168), channel_id=1, source_target_pairs={{0,8},{4,12},{8,0},{12,4},{16,24},{20,28},{24,16},{28,20},{1,9},{5... | collective-permute-start | bytes 6291464 | tf_op jit(solution)/shard_map/ppermute | solution.py:1117
  381.8 47.7 %collective-permute-start.22 = (bf16[1024,512]{1,0:T(8,128)(2,1)}, bf16[1024,512]{1,0:T(8,128)(2,1)}, u32[]{:S(2)}, u32[]{:S(2)}) collective-permute-start(bf16[1024,512]{1,0:T(8,128)(2,1)} %get-tuple-element.167), channel_id=1, source_target_pairs={{0,2},{1,3},{2,0},{3,1},{4,6},{5,7},{6,4},{7,5},{8,10},{9,11},{10,... | collective-permute-start | bytes 3145736 | tf_op jit(solution)/shard_map/ppermute | solution.py:1300
  382.3 47.2 %collective-permute-start.23 = (f32[8,1024]{1,0:T(8,128)}, f32[8,1024]{1,0:T(8,128)}, u32[]{:S(2)}, u32[]{:S(2)}) collective-permute-start(f32[8,1024]{1,0:T(8,128)} %get-tuple-element.163.refs_5_.refs_3_), channel_id=1, source_target_pairs={{0,2},{1,3},{2,0},{3,1},{4,6},{5,7},{6,4},{7,5},{8,10},{9,11},{10,... | collective-permute-start | bytes 98312 | tf_op jit(solution)/shard_map/ppermute | solution.py:1300
  429.0 71.4 %collective-permute-start.27 = (bf16[4,256,1536]{2,1,0:T(8,128)(2,1)}, bf16[4,256,1536]{2,1,0:T(8,128)(2,1)}, u32[]{:S(2)}, u32[]{:S(2)}) collective-permute-start(bf16[4,256,1536]{2,1,0:T(8,128)(2,1)} %weight_blocks.11.refs_2_), channel_id=1, source_target_pairs={{0,4},{4,0},{8,12},{12,8},{16,20},{20,16},{24,28},{28,24},{1,5},{5... | collective-permute-start | bytes 9437192 | tf_op jit(solution)/shard_map/ppermute | solution.py:1117
  445.1 51.1 %collective-permute-start.25 = (bf16[1024,512]{1,0:T(8,128)(2,1)}, bf16[1024,512]{1,0:T(8,128)(2,1)}, u32[]{:S(2)}, u32[]{:S(2)}) collective-permute-start(bf16[1024,512]{1,0:T(8,128)(2,1)} %get-tuple-element.174), channel_id=1, source_target_pairs={{0,2},{1,3},{2,0},{3,1},{4,6},{5,7},{6,4},{7,5},{8,10},{9,11},{10,... | collective-permute-start | bytes 3145736 | tf_op jit(solution)/shard_map/ppermute | solution.py:1300
  445.4 49.0 %collective-permute-start.26 = (f32[8,1024]{1,0:T(8,128)}, f32[8,1024]{1,0:T(8,128)}, u32[]{:S(2)}, u32[]{:S(2)}) collective-permute-start(f32[8,1024]{1,0:T(8,128)} %get-tuple-element.171.refs_12_.refs_3_), channel_id=1, source_target_pairs={{0,2},{1,3},{2,0},{3,1},{4,6},{5,7},{6,4},{7,5},{8,10},{9,11},{10,... | collective-permute-start | bytes 98312 | tf_op jit(solution)/shard_map/ppermute | solution.py:1300
  447.2 81.7 %collective-permute-start.28 = (bf16[1,2048,256]{2,1,0:T(8,128)(2,1)}, bf16[1,2048,256]{2,1,0:T(8,128)(2,1)}, u32[]{:S(2)}, u32[]{:S(2)}) collective-permute-start(bf16[1,2048,256]{2,1,0:T(8,128)(2,1)} %get-tuple-element.194), channel_id=1, source_target_pairs={{0,16},{4,20},{8,24},{12,28},{16,0},{20,4},{24,8},{28,12},{1,17},{... | collective-permute-start | bytes 3145736 | tf_op jit(solution)/shard_map/ppermute | solution.py:1117
  471.3 76.3 %collective-permute-start.32 = (bf16[4,512,256]{2,1,0:T(8,128)(2,1)}, bf16[4,512,256]{2,1,0:T(8,128)(2,1)}, u32[]{:S(2)}, u32[]{:S(2)}) collective-permute-start(bf16[4,512,256]{2,1,0:T(8,128)(2,1)} %weight_blocks.13.refs_7_), channel_id=1, source_target_pairs={{0,4},{4,0},{8,12},{12,8},{16,20},{20,16},{24,28},{28,24},{1,5},{5... | collective-permute-start | bytes 3145736 | tf_op jit(solution)/shard_map/ppermute | solution.py:1117
  494.5 49.0 %collective-permute-start.29 = (bf16[2,256,2048]{2,1,0:T(8,128)(2,1)}, bf16[2,256,2048]{2,1,0:T(8,128)(2,1)}, u32[]{:S(2)}, u32[]{:S(2)}) collective-permute-start(bf16[2,256,2048]{2,1,0:T(8,128)(2,1)} %get-tuple-element.195), channel_id=1, source_target_pairs={{0,8},{4,12},{8,0},{12,4},{16,24},{20,28},{24,16},{28,20},{1,9},{5... | collective-permute-start | bytes 6291464 | tf_op jit(solution)/shard_map/ppermute | solution.py:1117
  513.0 96.0 %collective-permute-start.31 = (bf16[2,256,1536]{2,1,0:T(8,128)(2,1)}, bf16[2,256,1536]{2,1,0:T(8,128)(2,1)}, u32[]{:S(2)}, u32[]{:S(2)}) collective-permute-start(bf16[2,256,1536]{2,1,0:T(8,128)(2,1)} %get-tuple-element.198), channel_id=1, source_target_pairs={{0,8},{4,12},{8,0},{12,4},{16,24},{20,28},{24,16},{28,20},{1,9},{5... | collective-permute-start | bytes 4718600 | tf_op jit(solution)/shard_map/ppermute | solution.py:1117
  547.6 8.0 %copy-start.6 = (f32[2048]{0:T(1024)S(1)}, f32[2048]{0:T(1024)}, u32[]{:S(2)}) copy-start(f32[2048]{0:T(1024)} %add_reduce_fusion) | copy-start | bytes 24580
  547.6 8.1 %copy-start.8 = (f32[8,512]{1,0:T(8,128)S(1)}, f32[8,512]{1,0:T(8,128)}, u32[]{:S(2)}) copy-start(f32[8,512]{1,0:T(8,128)} %get-tuple-element.153.refs_11_) | copy-start | bytes 49156
  547.7 8.1 %copy-start.9 = (f32[8,512]{1,0:T(8,128)S(1)}, f32[8,512]{1,0:T(8,128)}, u32[]{:S(2)}) copy-start(f32[8,512]{1,0:T(8,128)} %get-tuple-element.187) | copy-start | bytes 49156
  547.7 8.1 %copy-start.10 = (f32[8,512]{1,0:T(8,128)S(1)}, f32[8,512]{1,0:T(8,128)}, u32[]{:S(2)}) copy-start(f32[8,512]{1,0:T(8,128)} %get-tuple-element.161.refs_6_) | copy-start | bytes 49156
  547.7 8.1 %copy-start.11 = (f32[8,512]{1,0:T(8,128)S(1)}, f32[8,512]{1,0:T(8,128)}, u32[]{:S(2)}) copy-start(f32[8,512]{1,0:T(8,128)} %get-tuple-element.188) | copy-start | bytes 49156
  554.1 54.9 %collective-permute-start.33 = (bf16[2,512,256]{2,1,0:T(8,128)(2,1)}, bf16[2,512,256]{2,1,0:T(8,128)(2,1)S(1)}, u32[]{:S(2)}, u32[]{:S(2)}) collective-permute-start(bf16[2,512,256]{2,1,0:T(8,128)(2,1)} %get-tuple-element.200), channel_id=1, source_target_pairs={{0,8},{4,12},{8,0},{12,4},{16,24},{20,28},{24,16},{28,20},{1,9},{5... | collective-permute-start | bytes 1572872 | tf_op jit(solution)/shard_map/ppermute | solution.py:1117
  556.3 52.6 %copy-start.4 = (f32[4608]{0:T(1024)}, f32[4608]{0:T(1024)S(1)}, u32[]{:S(2)}) copy-start(f32[4608]{0:T(1024)S(1)} %constant_dynamic-update-slice_fusion.3) | copy-start | bytes 55300
  556.4 61.6 %collective-permute-start.30 = (bf16[1,256,2048]{2,1,0:T(8,128)(2,1)}, bf16[1,256,2048]{2,1,0:T(8,128)(2,1)}, u32[]{:S(2)}, u32[]{:S(2)}) collective-permute-start(bf16[1,256,2048]{2,1,0:T(8,128)(2,1)} %get-tuple-element.197), channel_id=1, source_target_pairs={{0,16},{4,20},{8,24},{12,28},{16,0},{20,4},{24,8},{28,12},{1,17},{... | collective-permute-start | bytes 3145736 | tf_op jit(solution)/shard_map/ppermute | solution.py:1117
  614.0 47.0 %collective-permute-start.35 = (bf16[1,256,1536]{2,1,0:T(8,128)(2,1)}, bf16[1,256,1536]{2,1,0:T(8,128)(2,1)S(1)}, u32[]{:S(2)}, u32[]{:S(2)}) collective-permute-start(bf16[1,256,1536]{2,1,0:T(8,128)(2,1)} %get-tuple-element.204), channel_id=1, source_target_pairs={{0,16},{4,20},{8,24},{12,28},{16,0},{20,4},{24,8},{28,12},{1,17},{... | collective-permute-start | bytes 2359304 | tf_op jit(solution)/shard_map/ppermute | solution.py:1117
  614.8 46.2 %collective-permute-start.34 = (bf16[1,512,256]{2,1,0:T(8,128)(2,1)}, bf16[1,512,256]{2,1,0:T(8,128)(2,1)S(1)}, u32[]{:S(2)}, u32[]{:S(2)}) collective-permute-start(bf16[1,512,256]{2,1,0:T(8,128)(2,1)} %get-tuple-element.202), channel_id=1, source_target_pairs={{0,16},{4,20},{8,24},{12,28},{16,0},{20,4},{24,8},{28,12},{1,17},{... | collective-permute-start | bytes 786440 | tf_op jit(solution)/shard_map/ppermute | solution.py:1117
  (17 other events, 85.1 us)
Sparse Core Ops, SparseCore 0:
  35.1 49.6 all-gather.1

commit v7 on v6

--- a/solution.py
+++ b/solution.py
@@ -197,6 +197,33 @@
         return [self.blocks[0], self.came.at[0, rows, :], self.blocks[1], self.came.at[1, rows, :]]
 
 
+EXTRA = 16
+
+
+def pack(sums, width):
+    rows = []
+    for s in range(2):
+        rest = sums[s : s + 1, :]
+        for _ in range(3):
+            piece = rest.astype(BF16).astype(F32)
+            rest = rest - piece
+            rows += [piece[:, h : h + width] for h in range(0, sums.shape[1], width)]
+    assert len(rows) <= EXTRA
+    rows += [jnp.zeros((1, width), F32)] * (EXTRA - len(rows))
+    return jnp.concatenate(rows).astype(BF16)
+
+
+def unpack(packed, target):
+    width = packed.shape[1]
+    per = target.shape[1] // width
+    value = packed[...].astype(F32)
+    for s in range(2):
+        for h in range(per):
+            at = [(3 * s + p) * per + h for p in range(3)]
+            total = value[at[0] : at[0] + 1] + value[at[1] : at[1] + 1] + value[at[2] : at[2] + 1]
+            target[s : s + 1, h * width : (h + 1) * width] = total
+
+
 class Scattered:
     def __init__(self, pairs, n, steps, with_sums):
         self.pairs, self.n, self.steps, self.with_sums = pairs, n, steps, with_sums
@@ -204,10 +231,11 @@
     def outs(self, length, width):
         tile = length // self.steps
         if self.pairs:
-            outs = [shape((length, width), BF16), sent((length, width), BF16)]
-            specs = [fixed((length, width))] * 2
+            high = length + EXTRA * self.with_sums
+            outs = [shape((length, width), BF16), sent((high, width), BF16)]
+            specs = [fixed((length, width)), fixed((high, width))]
             if self.with_sums:
-                outs, specs = outs + [sent((8, length), F32)], specs + [fixed((8, length))]
+                outs, specs = outs + [shape((8, length), F32)], specs + [fixed((8, length))]
             return outs, specs
         outs, specs = [shape((length, width), BF16)] * self.n, [rows_of((tile, width))] * self.n
         if self.with_sums:
@@ -283,6 +311,9 @@
         @pl.when(step == self.steps - 1)
         def _():
             self.take(step)
+            if self.with_sums:
+                length, width = self.out[0].shape
+                self.out[1][length:, :] = pack(self.out[2][...], width)
 
 
 def with_weights(copies, work, remote=False, gathered=()):
@@ -804,7 +835,18 @@
     grad = refs[0][...].astype(F32)
     for ref in refs[1:n_parts]:
         grad += ref[...].astype(F32)
-    columns = sum(one[...] for one in sums).T
+    columns = sums[0][...]
+    if len(sums) > 1:
+        packed, far = sums[1:]
+
+        @pl.when(pl.program_id(0) == 0)
+        def _():
+            far[...] = jnp.zeros_like(far)
+            unpack(packed, far)
+
+        tile = refs[0].shape[0]
+        columns += far[:, pl.ds(pl.multiple_of(pl.program_id(0) * tile, tile), tile)]
+    columns = columns.T
     mean, inv = stat[:, 0:1], stat[:, 1:2]
     scaled = (source[...] - mean) * inv
     back = inv * (
@@ -813,9 +855,15 @@
     return back, fold_rows(grad * scaled), fold_rows(grad)
 
 
+def sum_specs(sums, tile, length):
+    far = [pl.BlockSpec((EXTRA, v.shape[1]), lambda i: (length // EXTRA, 0)) for v in sums[1:]]
+    return [cols_of((8, tile)), *far]
+
+
 def hidden_back_body(k, m, full, *refs):
     parts, sums = refs[:k], refs[k : k + m]
-    cot, hidden, stat, gain, wide, low, gain_sum, bias_sum = refs[k + m :]
+    cot, hidden, stat, gain, wide, low, gain_sum, bias_sum, *more = refs[k + m :]
+    sums = (*sums, *more)
     back, gain_part, bias_part = norm_back(parts, k, hidden, stat, sums, gain, full)
     value = cot[...].astype(F32) + back
     wide[...] = value
@@ -834,7 +882,7 @@
         (steps,),
         (*parts, *sums, cotangent, hidden, stat, gain),
         [rows_of((tile, width))] * k
-        + [cols_of((8, tile))] * m
+        + sum_specs(sums, tile, length)
         + [
             pl.BlockSpec((tile, width), lambda i: (row * steps + i, 0)),
             rows_of((tile, width)),
@@ -843,6 +891,7 @@
         ],
         [shape((length, width), F32), sent((length, width), BF16)] + [shape((8, width), F32)] * 2,
         [rows_of((tile, width))] * 2 + [fixed((8, width))] * 2,
+        scratch=[pltpu.VMEM((8, length), F32)] * (m - 1),
     )
 
 
@@ -929,6 +978,8 @@
 def average_back_body(k, m, full, count, *refs):
     weights, parts, sums = refs[0], refs[1 : k + 1], refs[k + 1 : k + m + 1]
     source, stat, gain, hidden_grad, history = refs[k + m + 1 : k + m + 6]
+    refs, more = (refs[:-1], refs[-1:]) if m > 1 else (refs, ())
+    sums = (*sums, *more)
     grad_history, depth_sum, gain_sum, bias_sum, held = refs[-5:]
     back, gain_part, bias_part = norm_back(parts, k, source, stat, sums, gain, full)
     held[...] = hidden_grad[...] + back
@@ -960,7 +1011,7 @@
     specs = (
         [SMEM]
         + [rows_of((tile, width))] * k
-        + [cols_of((8, tile))] * m
+        + sum_specs(sums, tile, length)
         + [rows_of((tile, width)), rows_of((tile, 128)), fixed((8, width)), rows_of((tile, width)), block]
     )
     more = {}
@@ -975,7 +1026,7 @@
         specs,
         [shape(history.shape, BF16), shape((count, 8, 128), F32)] + [shape((8, width), F32)] * 2,
         [block, fixed((count, 8, 128))] + [fixed((8, width))] * 2,
-        scratch=[pltpu.VMEM((tile, width), F32)],
+        scratch=[pltpu.VMEM((tile, width), F32)] + [pltpu.VMEM((8, length), F32)] * (m - 1),
         **more,
     )
 
@@ -1316,7 +1367,8 @@
     def scatter(self, parts, sums=False):
         parts, extra = (parts[:-1], parts[-1:]) if sums else (parts, [])
         if self.pairs:
-            return [parts[0], self.over_chip(parts[1])], [*extra, *map(self.over_chip, extra)]
+            came = self.over_chip(parts[1])
+            return [parts[0], came], [*extra, came] if sums else []
         stacked = jnp.stack([part.astype(F32) for part in parts])
         ordered = jnp.take(stacked, self.me ^ jnp.arange(self.n), axis=0)
         total = lax.psum_scatter(ordered, "mp", scatter_dimension=0, tiled=False)
@@ -1495,16 +1547,21 @@
         qkv_grad[r] = attend_back(starts[r], tables, qkv[r], attended_grad, logs[r])
         if r == last and spread:
             advance(down_sum)
-            qkv_sum = Spread(normed1, qkv_grad, 0, (1, 2, 4))
-            qkv_sum.first()
+            qkv_sum = [
+                Spread(normed1, qkv_grad, 0, (1, 2, 4), (0, 2)),
+                Spread(normed1, qkv_grad, 0, (1, 2, 4), (1, 2)),
+            ]
+            qkv_sum[0].first()
+            up_sum.keep_added()
+            qkv_sum[1].first()
         if r > 0 and pairs:
             parts, row_sums = parts1[r - 1]
-            parts[1], row_sums[1] = gate([parts[1], row_sums[1]])
+            parts[1] = row_sums[1] = gate([parts[1]])[0]
         parts = project_back(n, pairs, qkv_grad[r], normed1[r], gain1, bias1, qkv_weight)
         parts1[r] = ring.scatter(parts, True)
 
     if spread:
-        up_sum.keep_added()
+        down_sum.coming = gate([down_sum.coming])[0]
         out_sum = Spread(attended, grad_full, 1, (1, 2, 4))
         out_sum.first()
     made = output(branch, hidden, down_bias8)
@@ -1530,23 +1587,27 @@
         if r == 0:
             if pairs:
                 parts, row_sums = parts1[last]
-                parts[1], row_sums[1] = gate([parts[1], row_sums[1]])
+                parts[1] = row_sums[1] = gate([parts[1]])[0]
             if spread:
-                qkv_sum.keep_added()
-
+                qkv_sum[0].keep_added()
+                advance(up_sum)
+
+    Order.cost = TINY
+    vectors = [up_bias_sum, down_bias_sum, gain2_sum, bias2_sum, gain1_sum, bias1_sum]
+    vectors, depth_part = [jnp.sum(v, 0) for v in vectors], jnp.sum(depth_sum, (1, 2))
     if spread:
-        down_sum.coming = gate([down_sum.coming])[0]
-        advance(up_sum)
+        qkv_sum[1].keep_added()
         out_sum.keep_added()
-        advance(qkv_sum, out_sum)
+        up_sum.coming = gate([up_sum.coming])[0]
+        advance(qkv_sum[0])
+        advance(qkv_sum[1], out_sum)
     else:
-        qkv_sum = spread_over_dp(weight_grad(normed1, qkv_grad), 0)
+        qkv_sum = [spread_over_dp(weight_grad(normed1, qkv_grad), 0)]
         out_sum = spread_over_dp(weight_grad(attended, grad_full), 1)
         down_sum = spread_over_dp(weight_grad(activated, cot_full), 1)
         up_sum = spread_over_dp(weight_grad(normed2, up_grad), 0)
-    down_total, up_total, out_total, qkv_total = finish([down_sum], [up_sum], [out_sum], [qkv_sum])
-    vectors = [up_bias_sum, down_bias_sum, gain2_sum, bias2_sum, gain1_sum, bias1_sum]
-    totals, depth_grad = sums([jnp.sum(v, 0) for v in vectors], jnp.sum(depth_sum, (1, 2)))
+    down_total, up_total, out_total, qkv_total = finish([down_sum], [up_sum], [out_sum], qkv_sum)
+    totals, depth_grad = sums(vectors, depth_part)
     return (
         made,
         grad_history,

time: 696 us -> 679 us (0.976)
  waiting for transfers between devices: 144 us -> 114 us
  Pallas kernels: 473 us -> 490 us
    ppermute x12 -> x15, waiting for transfers between devices: 117 us -> 82.9 us  [send(): lax.ppermute(value, 'dp', [(i, i ^ bit) for i in range(self.groups)])]
    pallas_call x45 -> x49, Pallas kernels: 473 us -> 490 us  [call(): pl.pallas_call(without_extra, grid_spec=pltpu.PrefetchScalarGridSpec(num_...]
    ppermute x20 -> x16, starting transfers between devices: 23.1 us -> 17.9 us  [over_chip(): return lax.ppermute(value, 'mp', self.chip)]
    ppermute x20 -> x16, waiting for transfers between devices: 22.6 us -> 26.8 us  [over_chip(): return lax.ppermute(value, 'mp', self.chip)]
    ppermute x12 -> x15, starting transfers between devices: 16.6 us -> 16.1 us  [send(): lax.ppermute(value, 'dp', [(i, i ^ bit) for i in range(self.groups)])]
  transfers between devices with their start and end apart: 37 -> 36, of which waited for: 10 -> 10; matrix products, arithmetic and copies ran while one was open for 2% -> 2% of each run, Pallas kernels for 66% -> 69%
where the time goes in v7:
time: 679 us; the launch traced here: 675 us
  Pallas kernels  490 us (72%)
  waiting for transfers between devices  114 us (17%)
  starting transfers between devices  34.6 us (5%)
  between operations  14.8 us (2%)
  local copies, waits for them, and re-layouts  14.7 us (2%)
    pallas_call x49, Pallas kernels, call(): pl.pallas_call(without_extra, grid_spec=pltpu.PrefetchScalarGridSpec(num_...  490 us
    ppermute x15, waiting for transfers between devices, send(): lax.ppermute(value, 'dp', [(i, i ^ bit) for i in range(self.groups)])  82.9 us
    ppermute x16, waiting for transfers between devices, over_chip(): return lax.ppermute(value, 'mp', self.chip)  26.8 us
    ppermute x16, starting transfers between devices, over_chip(): return lax.ppermute(value, 'mp', self.chip)  17.9 us
    ppermute x15, starting transfers between devices, send(): lax.ppermute(value, 'dp', [(i, i ^ bit) for i in range(self.groups)])  16.1 us
  transfers between devices with their start and end apart: 36, of which 10 were waited for; matrix products, arithmetic and copies ran while one was open for 2% of the time, Pallas kernels for 69%

profile of v7, /device:TPU:0, one launch (start us, length us, event | category | flops | bytes accessed | tf_op | source)
XLA Modules:
  0.0 674.9 jit_solution(12515511447388406056)
XLA Ops:
  8.6 3.0 collective-permute-start.2
  13.8 8.0 %average.2 = (f32[1024,512]{1,0:T(8,128)}, bf16[1024,512]{1,0:T(8,128)(2,1)}) custom-call(f32[13]{0:T(128)} %refs_0_.7, bf16[13,2048,512]{2,1,0:T(8,128)(2,1)} %refs_9_.3), custom_call_target="tpu_custom_call" | custom-call | flops 999999995904 | bytes 100000000 | tf_op jit(solution)/shard_map/average/pallas_call | solution.py:60
  27.0 7.8 %average.3 = (f32[1024,512]{1,0:T(8,128)}, bf16[1024,512]{1,0:T(8,128)(2,1)}) custom-call(f32[13]{0:T(128)} %refs_0_.7, bf16[13,2048,512]{2,1,0:T(8,128)(2,1)} %refs_9_.3, f32[32,512]{1,0:T(8,128)} %get-tuple-element.113.refs_2_), custom_call_target="tpu_custom_call" | custom-call | flops 999999995904 | bytes 100000000 | tf_op jit(solution)/shard_map/average/pallas_call | solution.py:60
  36.6 10.5 %collective-permute-done.refs_1_.refs_3_.refs_5_ = bf16[1024,512]{1,0:T(8,128)(2,1)} collective-permute-done((bf16[1024,512]{1,0:T(8,128)(2,1)}, bf16[1024,512]{1,0:T(8,128)(2,1)}, u32[]{:S(2)}, u32[]{:S(2)}) %collective-permute-start) | collective-permute-done | bytes 1048608 | tf_op jit(solution)/shard_map/ppermute | solution.py:1351
  48.9 18.1 %project.2 = (bf16[1024,1536]{1,0:T(8,128)(2,1)}, bf16[1024,2048]{1,0:T(8,128)(2,1)}, f32[1024,128]{1,0:T(8,128)}, bf16[1024,512]{1,0:T(8,128)(2,1)}, bf16[1024,512]{1,0:T(8,128)(2,1)}) custom-call(bf16[1024,512]{1,0:T(8,128)(2,1)} %get-tuple-element.111.refs_0_.refs_2_, bf16[1024,512]{1,0:T(8,128)(2,1)} %collective-permute-done.refs_1_.refs_3_.refs_5_, ...), custom_call_target="tpu_custom_call" | custom-call | flops 999999995904 | bytes 100000000 | tf_op jit(solution)/shard_map/project/pallas_call | solution.py:60
  67.6 10.1 %attend.2 = (bf16[1024,512]{1,0:T(8,128)(2,1)}, f32[4,8,1024]{2,1,0:T(8,128)}) custom-call(s32[8,1024]{1,0:T(8,128)} %broadcast_in_dim.19.refs_0_, bf16[1024,1536]{1,0:T(8,128)(2,1)} %get-tuple-element.116.refs_1_.refs_3_, f32[1024,128]{1,0:T(8,128)} %get-tuple-element.117.refs_2_.refs_6_), custom_call_target="tpu_custom_call" | custom-call | flops 999999995904 | bytes 100000000 | tf_op jit(solution)/shard_map/attend/pallas_call | solution.py:60
  78.0 17.9 %project.3 = (bf16[1024,1536]{1,0:T(8,128)(2,1)}, bf16[1024,2048]{1,0:T(8,128)(2,1)}, f32[1024,128]{1,0:T(8,128)}, bf16[1024,512]{1,0:T(8,128)(2,1)}, bf16[1024,512]{1,0:T(8,128)(2,1)}) custom-call(bf16[1024,512]{1,0:T(8,128)(2,1)} %gate.12.refs_9_.refs_0_.refs_2_, bf16[1024,512]{1,0:T(8,128)(2,1)} %collective-permute-done.7.refs_1_.refs_3_.refs_5_, ...), custom_call_target="tpu_custom_call" | custom-call | flops 999999995904 | bytes 100000000 | tf_op jit(solution)/shard_map/project/pallas_call | solution.py:60
  96.5 9.7 %attend.3 = (bf16[1024,512]{1,0:T(8,128)(2,1)}, f32[4,8,1024]{2,1,0:T(8,128)}) custom-call(s32[8,1024]{1,0:T(8,128)} %broadcast_in_dim.22.refs_0_, bf16[1024,1536]{1,0:T(8,128)(2,1)} %get-tuple-element.123.refs_1_.refs_3_, f32[1024,128]{1,0:T(8,128)} %get-tuple-element.124.refs_2_.refs_6_), custom_call_target="tpu_custom_call" | custom-call | flops 999999995904 | bytes 100000000 | tf_op jit(solution)/shard_map/attend/pallas_call | solution.py:60
  108.3 4.1 collective-permute-done.8.refs_10_
  113.1 40.7 %feed.2 = (f32[1024,512]{1,0:T(8,128)}, bf16[1024,2048]{1,0:T(8,128)(2,1)}, f32[1024,128]{1,0:T(8,128)}, bf16[1024,2048]{1,0:T(8,128)(2,1)}, bf16[1024,2048]{1,0...) custom-call(bf16[1024,512]{1,0:T(8,128)(2,1)} %get-tuple-element.118.refs_0_.refs_2_.refs_1_, ...), custom_call_target="tpu_custom_call" | custom-call | flops 999999995904 | bytes 100000000 | tf_op jit(solution)/shard_map/feed/pallas_call | solution.py:60
  156.0 41.1 %feed.3 = (f32[1024,512]{1,0:T(8,128)}, bf16[1024,2048]{1,0:T(8,128)(2,1)}, f32[1024,128]{1,0:T(8,128)}, bf16[1024,2048]{1,0:T(8,128)(2,1)}, bf16[1024,2048]{1,0...) custom-call(bf16[1024,512]{1,0:T(8,128)(2,1)} %get-tuple-element.130.refs_0_.refs_2_, ...), custom_call_target="tpu_custom_call" | custom-call | flops 999999995904 | bytes 100000000 | tf_op jit(solution)/shard_map/feed/pallas_call | solution.py:60
  197.4 5.3 collective-permute-done.11.refs_5_.refs_7_
  202.7 11.3 %join.1 = (bf16[1024,2048]{1,0:T(8,128)(2,1)}, bf16[1024,2048]{1,0:T(8,128)(2,1)}) custom-call(bf16[1024,512]{1,0:T(8,128)(2,1)} %gate.14.refs_17_.refs_0_.refs_2_, bf16[1024,512]{1,0:T(8,128)(2,1)} %collective-permute-done.10.refs_1_.refs_3_, bf16[1024,512]{1,0:T(8,128)(2,1)} %gate.14.refs_17_.refs_0_.refs_2_, ...), custom_call_target="tpu_custom_call" | custom-call | flops 999999995904 | bytes 100000000 | tf_op jit(solution)/shard_map/join/pallas_call | solution.py:60
  214.0 13.5 %weight_blocks.10.refs_7_ = bf16[4,2048,256]{2,1,0:T(8,128)(2,1)} custom-call(s32[1]{0:T(128)} %bitcast.7.refs_0_, bf16[1024,2048]{1,0:T(8,128)(2,1)} %get-tuple-element.140.refs_1_, bf16[1024,2048]{1,0:T(8,128)(2,1)} %get-tuple-element.141.refs_2_, bf16[1024,2048]{1,0:T(8,128)(2,1)} %get-tuple-element.134.refs_1_.refs_3_.refs_5_.refs_7_.refs_9_.refs_0_, ...), custom_call_target="tpu_custom_call" | custom-call | flops 999999995904 | bytes 100000000 | tf_op jit(solution)/shard_map/weight_blocks/pallas_call | solution.py:60
  229.0 30.5 %feed_back.2 = (bf16[1024,2048]{1,0:T(8,128)(2,1)}, f32[8,2048]{1,0:T(8,128)}, f32[8,512]{1,0:T(8,128)}, bf16[1024,512]{1,0:T(8,128)(2,1)}, bf16[1040,512]{1,0:T(8,128)(2,1)}, /*index=5*/f32[8,1024]{1,0:T(8,128)}) custom-call(bf16[1024,2048]{1,0:T(8,128)(2,1)} %get-tuple-element.134.refs_1_.refs_3_.refs_5_.refs_7_.refs_9_.refs_0_, ...), custom_call_target="tpu_custom_call" | custom-call | flops 999999995904 | bytes 100000000 | tf_op jit(solution)/shard_map/feed_back/pallas_call | solution.py:60
  260.1 30.7 %feed_back.3 = (bf16[1024,2048]{1,0:T(8,128)(2,1)}, f32[8,2048]{1,0:T(8,128)}, f32[8,512]{1,0:T(8,128)}, bf16[1024,512]{1,0:T(8,128)(2,1)}, bf16[1040,512]{1,0:T(8,128)(2,1)}, /*index=5*/f32[8,1024]{1,0:T(8,128)}) custom-call(bf16[1024,2048]{1,0:T(8,128)(2,1)} %get-tuple-element.142.refs_4_.refs_6_.refs_8_.refs_10_.refs_0_, ...), custom_call_target="tpu_custom_call" | custom-call | flops 999999995904 | bytes 100000000 | tf_op jit(solution)/shard_map/feed_back/pallas_call | solution.py:60
  295.8 5.8 hidden_back.2
  302.2 14.6 %weight_blocks.11.refs_12_ = bf16[4,256,2048]{2,1,0:T(8,128)(2,1)} custom-call(s32[1]{0:T(128)} %bitcast.7.refs_0_, bf16[1024,2048]{1,0:T(8,128)(2,1)} %get-tuple-element.139.refs_2_.refs_1_.refs_3_.refs_5_.refs_7_, bf16[1024,2048]{1,0:T(8,128)(2,1)} %get-tuple-element.148.refs_2_.refs_4_.refs_6_.refs_8_, ...), custom_call_target="tpu_custom_call" | custom-call | flops 999999995904 | bytes 100000000 | tf_op jit(solution)/shard_map/weight_blocks/pallas_call | solution.py:60
  317.2 4.1 collective-permute-done.16.refs_11_
  321.3 14.2 %weight_blocks.12 = (bf16[2,2048,256]{2,1,0:T(8,128)(2,1)}, bf16[2,2048,256]{2,1,0:T(8,128)(2,1)}) custom-call(s32[1]{0:T(128)} %bitcast.7.refs_0_, bf16[1024,2048]{1,0:T(8,128)(2,1)} %get-tuple-element.140.refs_1_, bf16[1024,2048]{1,0:T(8,128)(2,1)} %get-tuple-element.141.refs_2_, ...), custom_call_target="tpu_custom_call" | custom-call | flops 999999995904 | bytes 100000000 | tf_op jit(solution)/shard_map/weight_blocks/pallas_call | solution.py:60
  339.4 9.0 %attended_back.2 = (bf16[1024,2048]{1,0:T(8,128)(2,1)}, bf16[1024,512]{1,0:T(8,128)(2,1)}) custom-call(bf16[1024,512]{1,0:T(8,128)(2,1)} %get-tuple-element.150.refs_0_.refs_2_, bf16[1024,512]{1,0:T(8,128)(2,1)} %collective-permute-done.15.refs_1_.refs_3_, bf16[1024,512]{1,0:T(8,128)(2,1)} %get-tuple-element.150.refs_0_.refs_2_, ...), custom_call_target="tpu_custom_call" | custom-call | flops 999999995904 | bytes 100000000 | tf_op jit(solution)/shard_map/attended_back/pallas_call | solution.py:60
  348.5 5.8 hidden_back.3
  354.3 12.4 %attend_back.2.refs_0_.refs_9_ = bf16[1024,1536]{1,0:T(8,128)(2,1)} custom-call(s32[8,1024]{1,0:T(8,128)} %broadcast_in_dim.19.refs_0_, f32[1024,128]{1,0:T(8,128)} %constant.19.clone.refs_6_.refs_1_, f32[1024,128]{1,0:T(8,128)} %constant.20.clone.refs_7_.refs_2_, bf16[1024,1536]{1,0:T(8,128)(2,1)} %get-tuple-element.116.refs_1_.refs_3_, ...), custom_call_target="tpu_custom_call" | custom-call | flops 999999995904 | bytes 100000000 | tf_op jit(solution)/shard_map/attend_back/pallas_call | solution.py:60
  368.2 15.6 %project_back.2 = (bf16[1024,512]{1,0:T(8,128)(2,1)}, bf16[1040,512]{1,0:T(8,128)(2,1)}, f32[8,1024]{1,0:T(8,128)}) custom-call(bf16[1024,1536]{1,0:T(8,128)(2,1)} %attend_back.2.refs_0_.refs_9_, bf16[1024,2048]{1,0:T(8,128)(2,1)} %get-tuple-element.162.refs_1_.refs_3_.refs_5_.refs_7_, f32[8,2048]{1,0:T(8,128)} %get-tuple-element.214.refs_4_.refs_2_, ...), custom_call_target="tpu_custom_call" | custom-call | flops 999999995904 | bytes 100000000 | tf_op jit(solution)/shard_map/project_back/pallas_call | solution.py:60
  384.3 8.7 %collective-permute-done.18.refs_1_.refs_3_ = bf16[1024,512]{1,0:T(8,128)(2,1)} collective-permute-done((bf16[1024,512]{1,0:T(8,128)(2,1)}, bf16[1024,512]{1,0:T(8,128)(2,1)}, u32[]{:S(2)}, u32[]{:S(2)}) %collective-permute-start.18) | collective-permute-done | bytes 1048608 | tf_op jit(solution)/shard_map/ppermute | solution.py:1351
  393.0 9.1 %attended_back.3 = (bf16[1024,2048]{1,0:T(8,128)(2,1)}, bf16[1024,512]{1,0:T(8,128)(2,1)}) custom-call(bf16[1024,512]{1,0:T(8,128)(2,1)} %get-tuple-element.160.refs_0_.refs_2_, bf16[1024,512]{1,0:T(8,128)(2,1)} %collective-permute-done.18.refs_1_.refs_3_, bf16[1024,512]{1,0:T(8,128)(2,1)} %get-tuple-element.160.refs_0_.refs_2_, ...), custom_call_target="tpu_custom_call" | custom-call | flops 999999995904 | bytes 100000000 | tf_op jit(solution)/shard_map/attended_back/pallas_call | solution.py:60
  402.1 12.6 %attend_back.3.refs_2_.refs_10_.refs_0_ = bf16[1024,1536]{1,0:T(8,128)(2,1)} custom-call(s32[8,1024]{1,0:T(8,128)} %broadcast_in_dim.22.refs_0_, f32[1024,128]{1,0:T(8,128)} %constant.19.clone.refs_6_.refs_1_, f32[1024,128]{1,0:T(8,128)} %constant.20.clone.refs_7_.refs_2_, bf16[1024,1536]{1,0:T(8,128)(2,1)} %get-tuple-element.123.refs_1_.refs_3_, ...), custom_call_target="tpu_custom_call" | custom-call | flops 999999995904 | bytes 100000000 | tf_op jit(solution)/shard_map/attend_back/pallas_call | solution.py:60
  414.7 4.2 fold.4
  421.5 9.6 %weight_blocks.13.refs_12_ = bf16[4,256,768]{2,1,0:T(8,128)(2,1)} custom-call(s32[1]{0:T(128)} %bitcast.7.refs_0_, bf16[1024,2048]{1,0:T(8,128)(2,1)} %get-tuple-element.162.refs_1_.refs_3_.refs_5_.refs_7_, bf16[1024,2048]{1,0:T(8,128)(2,1)} %get-tuple-element.168.refs_2_.refs_4_.refs_6_.refs_8_.refs_1_, ...), custom_call_target="tpu_custom_call" | custom-call | flops 999999995904 | bytes 100000000 | tf_op jit(solution)/shard_map/weight_blocks/pallas_call | solution.py:60
  431.6 15.1 %weight_blocks.14 = (bf16[2,256,2048]{2,1,0:T(8,128)(2,1)}, bf16[2,256,2048]{2,1,0:T(8,128)(2,1)}) custom-call(s32[1]{0:T(128)} %bitcast.7.refs_0_, bf16[1024,2048]{1,0:T(8,128)(2,1)} %get-tuple-element.139.refs_2_.refs_1_.refs_3_.refs_5_.refs_7_, bf16[1024,2048]{1,0:T(8,128)(2,1)} %get-tuple-element.148.refs_2_.refs_4_.refs_6_.refs_8_, ...), custom_call_target="tpu_custom_call" | custom-call | flops 999999995904 | bytes 100000000 | tf_op jit(solution)/shard_map/weight_blocks/pallas_call | solution.py:60
  446.7 9.7 %weight_blocks.15.refs_1_ = bf16[4,256,768]{2,1,0:T(8,128)(2,1)} custom-call(s32[1]{0:T(128)} %bitcast.7.refs_0_, bf16[1024,2048]{1,0:T(8,128)(2,1)} %get-tuple-element.162.refs_1_.refs_3_.refs_5_.refs_7_, bf16[1024,2048]{1,0:T(8,128)(2,1)} %get-tuple-element.168.refs_2_.refs_4_.refs_6_.refs_8_.refs_1_, ...), custom_call_target="tpu_custom_call" | custom-call | flops 999999995904 | bytes 100000000 | tf_op jit(solution)/shard_map/weight_blocks/pallas_call | solution.py:60
  457.9 15.7 %project_back.3 = (bf16[1024,512]{1,0:T(8,128)(2,1)}, bf16[1040,512]{1,0:T(8,128)(2,1)}, f32[8,1024]{1,0:T(8,128)}) custom-call(bf16[1024,1536]{1,0:T(8,128)(2,1)} %attend_back.3.refs_2_.refs_10_.refs_0_, bf16[1024,2048]{1,0:T(8,128)(2,1)} %get-tuple-element.168.refs_2_.refs_4_.refs_6_.refs_8_.refs_1_, f32[8,2048]{1,0:T(8,128)} %get-tuple-element.214.refs_4_.refs_2_, ...), custom_call_target="tpu_custom_call" | custom-call | flops 999999995904 | bytes 100000000 | tf_op jit(solution)/shard_map/project_back/pallas_call | solution.py:60
  476.8 6.2 weight_blocks.16.refs_7_
  484.2 6.4 output.1.refs_10_
  491.2 14.4 %average_back.2 = (bf16[13,2048,512]{2,1,0:T(8,128)(2,1)}, f32[13,8,128]{2,1,0:T(8,128)}, f32[8,512]{1,0:T(8,128)}, f32[8,512]{1,0:T(8,128)}) custom-call(f32[13]{0:T(128)} %refs_0_.7, bf16[1024,512]{1,0:T(8,128)(2,1)} %get-tuple-element.175.refs_1_, bf16[1040,512]{1,0:T(8,128)(2,1)} %gate.18.refs_5_.refs_2_.refs_4_, ...), custom_call_target="tpu_custom_call" | custom-call | flops 999999995904 | bytes 100000000 | tf_op jit(solution)/shard_map/average_back/pallas_call | solution.py:60
  505.7 10.0 %weight_blocks.17 = (bf16[2,256,768]{2,1,0:T(8,128)(2,1)}, bf16[2,256,768]{2,1,0:T(8,128)(2,1)}) custom-call(s32[1]{0:T(128)} %bitcast.7.refs_0_, bf16[1024,2048]{1,0:T(8,128)(2,1)} %get-tuple-element.162.refs_1_.refs_3_.refs_5_.refs_7_, bf16[1024,2048]{1,0:T(8,128)(2,1)} %get-tuple-element.168.refs_2_.refs_4_.refs_6_.refs_8_.refs_1_, ...), custom_call_target="tpu_custom_call" | custom-call | flops 999999995904 | bytes 100000000 | tf_op jit(solution)/shard_map/weight_blocks/pallas_call | solution.py:60
  516.1 7.9 %collective-permute-done.24.refs_1_ = bf16[2,256,2048]{2,1,0:T(8,128)(2,1)} collective-permute-done((bf16[2,256,2048]{2,1,0:T(8,128)(2,1)}, bf16[2,256,2048]{2,1,0:T(8,128)(2,1)}, u32[]{:S(2)}, u32[]{:S(2)}) %collective-permute-start.24) | collective-permute-done | bytes 2097184 | tf_op jit(solution)/shard_map/ppermute | solution.py:1168
  524.0 4.2 fold.5
  528.5 14.7 %average_back.3 = (bf16[13,2048,512]{2,1,0:T(8,128)(2,1)}, f32[13,8,128]{2,1,0:T(8,128)}, f32[8,512]{1,0:T(8,128)}, f32[8,512]{1,0:T(8,128)}) custom-call(f32[13]{0:T(128)} %refs_0_.7, bf16[1024,512]{1,0:T(8,128)(2,1)} %get-tuple-element.173.refs_1_, bf16[1040,512]{1,0:T(8,128)(2,1)} %gate.20.refs_12_.refs_2_.refs_4_, ...), custom_call_target="tpu_custom_call", output_to_operand_aliasing={{0}: (10, {})} | custom-call | flops 999999995904 | bytes 100000000 | tf_op jit(solution)/shard_map/average_back/pallas_call | solution.py:60
  543.3 10.0 %weight_blocks.18 = (bf16[2,256,768]{2,1,0:T(8,128)(2,1)}, bf16[2,256,768]{2,1,0:T(8,128)(2,1)}) custom-call(s32[1]{0:T(128)} %bitcast.7.refs_0_, bf16[1024,2048]{1,0:T(8,128)(2,1)} %get-tuple-element.162.refs_1_.refs_3_.refs_5_.refs_7_, bf16[1024,2048]{1,0:T(8,128)(2,1)} %get-tuple-element.168.refs_2_.refs_4_.refs_6_.refs_8_.refs_1_, ...), custom_call_target="tpu_custom_call" | custom-call | flops 10000 | bytes 1 | tf_op jit(solution)/shard_map/weight_blocks/pallas_call | solution.py:60
  555.0 6.4 weight_blocks.19
  562.0 13.5 %collective-permute-done.26.refs_0_ = bf16[1,256,2048]{2,1,0:T(8,128)(2,1)} collective-permute-done((bf16[1,256,2048]{2,1,0:T(8,128)(2,1)}, bf16[1,256,2048]{2,1,0:T(8,128)(2,1)}, u32[]{:S(2)}, u32[]{:S(2)}) %collective-permute-start.26) | collective-permute-done | bytes 1048608 | tf_op jit(solution)/shard_map/ppermute | solution.py:1168
  575.5 3.5 fold.6
  579.0 16.3 %collective-permute-done.30.refs_3_ = bf16[2,512,256]{2,1,0:T(8,128)(2,1)S(1)} collective-permute-done((bf16[2,512,256]{2,1,0:T(8,128)(2,1)}, bf16[2,512,256]{2,1,0:T(8,128)(2,1)S(1)}, u32[]{:S(2)}, u32[]{:S(2)}) %collective-permute-start.30) | collective-permute-done | bytes 524320 | tf_op jit(solution)/shard_map/ppermute | solution.py:1168
  596.3 3.8 fold.7
  604.0 41.1 %collective-permute-done.32.refs_5_ = bf16[1,512,256]{2,1,0:T(8,128)(2,1)S(1)} collective-permute-done((bf16[1,512,256]{2,1,0:T(8,128)(2,1)}, bf16[1,512,256]{2,1,0:T(8,128)(2,1)S(1)}, u32[]{:S(2)}, u32[]{:S(2)}) %collective-permute-start.32) | collective-permute-done | bytes 262176 | tf_op jit(solution)/shard_map/ppermute | solution.py:1168
  646.1 5.7 finish.1
  651.8 12.1 %sums.1 = f32[48,128]{1,0:T(8,128)} custom-call(f32[48,128]{1,0:T(8,128)} %select_maximum_fusion.refs_0_, f32[512,256]{1,0:T(8,128)} %get-tuple-element.104.refs_1_), custom_call_target="tpu_custom_call" | custom-call | flops 10000 | bytes 1 | tf_op jit(solution)/shard_map/sums/pallas_call | solution.py:60
  (160 shorter events, 55.2 us)
Async XLA Ops:
  7.2 100.8 %all-gather.2.cloned.1.call-start = ((), (), s32[]{:S(2)}) async-start(), calls=%async_computation | async-start | bytes 2359296 | tf_op jit(solution)/shard_map/all_gather | solution.py:1392
  8.6 18.3 %collective-permute-start.2 = (f32[32,512]{1,0:T(8,128)}, f32[32,512]{1,0:T(8,128)}, u32[]{:S(2)}, u32[]{:S(2)}) collective-permute-start(f32[32,512]{1,0:T(8,128)} %broadcast_bitcast_fusion), channel_id=1, source_target_pairs={{0,2},{1,3},{2,0},{3,1},{4,6},{5,7},{6,4},{7,5},{8,10},{9,11},{10,... | collective-permute-start | bytes 196616 | tf_op jit(solution)/shard_map/ppermute | solution.py:1351
  11.6 23.3 %collective-permute-start.1 = (f32[32,512]{1,0:T(8,128)}, f32[32,512]{1,0:T(8,128)}, u32[]{:S(2)}, u32[]{:S(2)}) collective-permute-start(f32[32,512]{1,0:T(8,128)} %broadcast_bitcast_fusion), channel_id=1, source_target_pairs={{0,1},{1,0},{2,3},{3,2},{4,5},{5,4},{6,7},{7,6},{8,9},{9,8},{10,11... | collective-permute-start | bytes 196616 | tf_op jit(solution)/shard_map/ppermute | solution.py:1348
  11.6 96.8 %collective-permute-start.6 = (bf16[512,2048]{1,0:T(8,128)(2,1)}, bf16[512,2048]{1,0:T(8,128)(2,1)}, u32[]{:S(2)}, u32[]{:S(2)}) collective-permute-start(bf16[512,2048]{1,0:T(8,128)(2,1)} %refs_4_.10), channel_id=1, source_target_pairs={{0,1},{1,0},{2,3},{3,2},{4,5},{5,4},{6,7},{7,6},{8,9},{9,8},{10,11... | collective-permute-start | bytes 6291464 | tf_op jit(solution)/shard_map/ppermute | solution.py:1348
  13.8 13.2 %collective-permute-start.3 = (bf16[64,2048]{1,0:T(8,128)(2,1)}, bf16[64,2048]{1,0:T(8,128)(2,1)}, u32[]{:S(2)}, u32[]{:S(2)}) collective-permute-start(bf16[64,2048]{1,0:T(8,128)(2,1)} %constant_dynamic-slice_fusion), channel_id=1, source_target_pairs={{0,2},{1,3},{2,0},{3,1},{4,6},{5,7},{6,4},{7,5},{8,10},{9,11},{10,... | collective-permute-start | bytes 786440 | tf_op jit(solution)/shard_map/ppermute | solution.py:1351
  13.8 10.0 %copy-start = (bf16[2048,512]{1,0:T(8,128)(2,1)S(1)}, bf16[2048,512]{1,0:T(8,128)(2,1)}, u32[]{:S(2)}) copy-start(bf16[2048,512]{1,0:T(8,128)(2,1)} %refs_4_.8) | copy-start | bytes 6291460
  21.7 25.4 %collective-permute-start = (bf16[1024,512]{1,0:T(8,128)(2,1)}, bf16[1024,512]{1,0:T(8,128)(2,1)}, u32[]{:S(2)}, u32[]{:S(2)}) collective-permute-start(bf16[1024,512]{1,0:T(8,128)(2,1)} %get-tuple-element.111.refs_0_.refs_2_), channel_id=1, source_target_pairs={{0,2},{1,3},{2,0},{3,1},{4,6},{5,7},{6,4},{7,5},{8,10},{9,11},{10,... | collective-permute-start | bytes 3145736 | tf_op jit(solution)/shard_map/ppermute | solution.py:1351
  27.0 8.0 %collective-permute-start.4 = (f32[32,512]{1,0:T(8,128)}, f32[32,512]{1,0:T(8,128)}, u32[]{:S(2)}, u32[]{:S(2)}) collective-permute-start(f32[32,512]{1,0:T(8,128)} %get-tuple-element.113.refs_2_), channel_id=1, source_target_pairs={{0,1},{1,0},{2,3},{3,2},{4,5},{5,4},{6,7},{7,6},{8,9},{9,8},{10,11... | collective-permute-start | bytes 196616 | tf_op jit(solution)/shard_map/ppermute | solution.py:1348
  47.1 30.8 %collective-permute-start.7 = (bf16[1024,512]{1,0:T(8,128)(2,1)}, bf16[1024,512]{1,0:T(8,128)(2,1)}, u32[]{:S(2)}, u32[]{:S(2)}) collective-permute-start(bf16[1024,512]{1,0:T(8,128)(2,1)} %gate.12.refs_9_.refs_0_.refs_2_), channel_id=1, source_target_pairs={{0,2},{1,3},{2,0},{3,1},{4,6},{5,7},{6,4},{7,5},{8,10},{9,11},{10,... | collective-permute-start | bytes 3145736 | tf_op jit(solution)/shard_map/ppermute | solution.py:1351
  48.9 18.1 %copy-start.21 = (s32[1,1024]{1,0:T(1,128)S(1)}, s32[1,1024]{1,0:T(1,128)}, u32[]{:S(2)}) copy-start(s32[1,1024]{1,0:T(1,128)} %get-tuple-element.221) | copy-start | bytes 12292
  77.7 30.7 %collective-permute-start.5 = (bf16[1024,512]{1,0:T(8,128)(2,1)}, bf16[1024,512]{1,0:T(8,128)(2,1)}, u32[]{:S(2)}, u32[]{:S(2)}) collective-permute-start(bf16[1024,512]{1,0:T(8,128)(2,1)} %get-tuple-element.118.refs_0_.refs_2_.refs_1_), channel_id=1, source_target_pairs={{0,2},{1,3},{2,0},{3,1},{4,6},{5,7},{6,4},{7,5},{8,10},{9,11},{10,... | collective-permute-start | bytes 3145736 | tf_op jit(solution)/shard_map/ppermute | solution.py:1351
  78.0 17.9 %copy-start.20 = (s32[1,1024]{1,0:T(1,128)S(1)}, s32[1,1024]{1,0:T(1,128)}, u32[]{:S(2)}) copy-start(s32[1,1024]{1,0:T(1,128)} %get-tuple-element.220) | copy-start | bytes 12292
  106.2 49.8 %collective-permute-start.12 = (bf16[1024,512]{1,0:T(8,128)(2,1)}, bf16[1024,512]{1,0:T(8,128)(2,1)}, u32[]{:S(2)}, u32[]{:S(2)}) collective-permute-start(bf16[1024,512]{1,0:T(8,128)(2,1)} %get-tuple-element.130.refs_0_.refs_2_), channel_id=1, source_target_pairs={{0,2},{1,3},{2,0},{3,1},{4,6},{5,7},{6,4},{7,5},{8,10},{9,11},{10,... | collective-permute-start | bytes 3145736 | tf_op jit(solution)/shard_map/ppermute | solution.py:1351
  108.0 4.5 collective-permute-start.8
  108.0 89.4 %collective-permute-start.10 = (bf16[1024,512]{1,0:T(8,128)(2,1)}, bf16[1024,512]{1,0:T(8,128)(2,1)}, u32[]{:S(2)}, u32[]{:S(2)}) collective-permute-start(bf16[1024,512]{1,0:T(8,128)(2,1)} %gate.14.refs_17_.refs_0_.refs_2_), channel_id=1, source_target_pairs={{0,2},{1,3},{2,0},{3,1},{4,6},{5,7},{6,4},{7,5},{8,10},{9,11},{10,... | collective-permute-start | bytes 3145736 | tf_op jit(solution)/shard_map/ppermute | solution.py:1351
  153.9 60.1 %collective-permute-start.9 = (bf16[1024,512]{1,0:T(8,128)(2,1)}, bf16[1024,512]{1,0:T(8,128)(2,1)}, u32[]{:S(2)}, u32[]{:S(2)}) collective-permute-start(bf16[1024,512]{1,0:T(8,128)(2,1)} %get-tuple-element.128), channel_id=1, source_target_pairs={{0,2},{1,3},{2,0},{3,1},{4,6},{5,7},{6,4},{7,5},{8,10},{9,11},{10,... | collective-permute-start | bytes 3145736 | tf_op jit(solution)/shard_map/ppermute | solution.py:1351
  154.2 48.5 %collective-permute-start.11 = (bf16[1024,512]{1,0:T(8,128)(2,1)}, bf16[1024,512]{1,0:T(8,128)(2,1)}, u32[]{:S(2)}, u32[]{:S(2)}) collective-permute-start(bf16[1024,512]{1,0:T(8,128)(2,1)} %gate.15.refs_17_.refs_4_.refs_6_), channel_id=1, source_target_pairs={{0,2},{1,3},{2,0},{3,1},{4,6},{5,7},{6,4},{7,5},{8,10},{9,11},{10,... | collective-permute-start | bytes 3145736 | tf_op jit(solution)/shard_map/ppermute | solution.py:1351
  197.1 63.0 %collective-permute-start.13 = (bf16[1024,512]{1,0:T(8,128)(2,1)}, bf16[1024,512]{1,0:T(8,128)(2,1)}, u32[]{:S(2)}, u32[]{:S(2)}) collective-permute-start(bf16[1024,512]{1,0:T(8,128)(2,1)} %get-tuple-element.137), channel_id=1, source_target_pairs={{0,2},{1,3},{2,0},{3,1},{4,6},{5,7},{6,4},{7,5},{8,10},{9,11},{10,... | collective-permute-start | bytes 3145736 | tf_op jit(solution)/shard_map/ppermute | solution.py:1351
  227.6 93.7 %collective-permute-start.16 = (bf16[4,2048,256]{2,1,0:T(8,128)(2,1)}, bf16[4,2048,256]{2,1,0:T(8,128)(2,1)}, u32[]{:S(2)}, u32[]{:S(2)}) collective-permute-start(bf16[4,2048,256]{2,1,0:T(8,128)(2,1)} %weight_blocks.10.refs_7_), channel_id=1, source_target_pairs={{0,4},{4,0},{8,12},{12,8},{16,20},{20,16},{24,28},{28,24},{1,5},{5... | collective-permute-start | bytes 12582920 | tf_op jit(solution)/shard_map/ppermute | solution.py:1168
  259.5 35.7 %collective-permute-start.14 = (bf16[1040,512]{1,0:T(8,128)(2,1)}, bf16[1040,512]{1,0:T(8,128)(2,1)}, u32[]{:S(2)}, u32[]{:S(2)}) collective-permute-start(bf16[1040,512]{1,0:T(8,128)(2,1)} %get-tuple-element.145), channel_id=1, source_target_pairs={{0,2},{1,3},{2,0},{3,1},{4,6},{5,7},{6,4},{7,5},{8,10},{9,11},{10,... | collective-permute-start | bytes 3194888 | tf_op jit(solution)/shard_map/ppermute | solution.py:1351
  260.1 32.4 %copy-start.19 = (f32[8,512]{1,0:T(8,128)S(1)}, f32[8,512]{1,0:T(8,128)}, u32[]{:S(2)}) copy-start(f32[8,512]{1,0:T(8,128)} %get-tuple-element.143.refs_1_) | copy-start | bytes 49156
  260.1 33.7 %copy-start.7 = (f32[8,2048]{1,0:T(8,128)S(1)}, f32[8,2048]{1,0:T(8,128)}, u32[]{:S(2)}) copy-start(f32[8,2048]{1,0:T(8,128)} %get-tuple-element.184) | copy-start | bytes 196612
  260.1 35.1 %copy-start.24 = (f32[512]{0:T(512)S(1)}, f32[512]{0:T(512)}, u32[]{:S(2)}) copy-start(f32[512]{0:T(512)} %param.23) | copy-start | bytes 6148
  290.8 57.7 %collective-permute-start.17 = (bf16[1040,512]{1,0:T(8,128)(2,1)}, bf16[1040,512]{1,0:T(8,128)(2,1)}, u32[]{:S(2)}, u32[]{:S(2)}) collective-permute-start(bf16[1040,512]{1,0:T(8,128)(2,1)} %get-tuple-element.157), channel_id=1, source_target_pairs={{0,2},{1,3},{2,0},{3,1},{4,6},{5,7},{6,4},{7,5},{8,10},{9,11},{10,... | collective-permute-start | bytes 3194888 | tf_op jit(solution)/shard_map/ppermute | solution.py:1351
  301.6 37.8 %collective-permute-start.15 = (bf16[1024,512]{1,0:T(8,128)(2,1)}, bf16[1024,512]{1,0:T(8,128)(2,1)}, u32[]{:S(2)}, u32[]{:S(2)}) collective-permute-start(bf16[1024,512]{1,0:T(8,128)(2,1)} %get-tuple-element.150.refs_0_.refs_2_), channel_id=1, source_target_pairs={{0,2},{1,3},{2,0},{3,1},{4,6},{5,7},{6,4},{7,5},{8,10},{9,11},{10,... | collective-permute-start | bytes 3145736 | tf_op jit(solution)/shard_map/ppermute | solution.py:1351
  316.8 114.8 %collective-permute-start.22 = (bf16[4,256,2048]{2,1,0:T(8,128)(2,1)}, bf16[4,256,2048]{2,1,0:T(8,128)(2,1)}, u32[]{:S(2)}, u32[]{:S(2)}) collective-permute-start(bf16[4,256,2048]{2,1,0:T(8,128)(2,1)} %weight_blocks.11.refs_12_), channel_id=1, source_target_pairs={{0,4},{4,0},{8,12},{12,8},{16,20},{20,16},{24,28},{28,24},{1,5},{5... | collective-permute-start | bytes 12582920 | tf_op jit(solution)/shard_map/ppermute | solution.py:1168
  335.5 79.1 %collective-permute-start.19 = (bf16[2,2048,256]{2,1,0:T(8,128)(2,1)}, bf16[2,2048,256]{2,1,0:T(8,128)(2,1)}, u32[]{:S(2)}, u32[]{:S(2)}) collective-permute-start(bf16[2,2048,256]{2,1,0:T(8,128)(2,1)} %get-tuple-element.165), channel_id=1, source_target_pairs={{0,8},{4,12},{8,0},{12,4},{16,24},{20,28},{24,16},{28,20},{1,9},{5... | collective-permute-start | bytes 6291464 | tf_op jit(solution)/shard_map/ppermute | solution.py:1168
  366.7 26.3 %collective-permute-start.18 = (bf16[1024,512]{1,0:T(8,128)(2,1)}, bf16[1024,512]{1,0:T(8,128)(2,1)}, u32[]{:S(2)}, u32[]{:S(2)}) collective-permute-start(bf16[1024,512]{1,0:T(8,128)(2,1)} %get-tuple-element.160.refs_0_.refs_2_), channel_id=1, source_target_pairs={{0,2},{1,3},{2,0},{3,1},{4,6},{5,7},{6,4},{7,5},{8,10},{9,11},{10,... | collective-permute-start | bytes 3145736 | tf_op jit(solution)/shard_map/ppermute | solution.py:1351
  383.8 74.1 %collective-permute-start.21 = (bf16[1040,512]{1,0:T(8,128)(2,1)}, bf16[1040,512]{1,0:T(8,128)(2,1)}, u32[]{:S(2)}, u32[]{:S(2)}) collective-permute-start(bf16[1040,512]{1,0:T(8,128)(2,1)} %get-tuple-element.169), channel_id=1, source_target_pairs={{0,2},{1,3},{2,0},{3,1},{4,6},{5,7},{6,4},{7,5},{8,10},{9,11},{10,... | collective-permute-start | bytes 3194888 | tf_op jit(solution)/shard_map/ppermute | solution.py:1351
  418.9 57.9 %collective-permute-start.20 = (bf16[1,2048,256]{2,1,0:T(8,128)(2,1)}, bf16[1,2048,256]{2,1,0:T(8,128)(2,1)}, u32[]{:S(2)}, u32[]{:S(2)}) collective-permute-start(bf16[1,2048,256]{2,1,0:T(8,128)(2,1)} %get-tuple-element.167), channel_id=1, source_target_pairs={{0,16},{4,20},{8,24},{12,28},{16,0},{20,4},{24,8},{28,12},{1,17},{... | collective-permute-start | bytes 3145736 | tf_op jit(solution)/shard_map/ppermute | solution.py:1168
  431.0 74.6 %collective-permute-start.25 = (bf16[4,256,768]{2,1,0:T(8,128)(2,1)}, bf16[4,256,768]{2,1,0:T(8,128)(2,1)}, u32[]{:S(2)}, u32[]{:S(2)}) collective-permute-start(bf16[4,256,768]{2,1,0:T(8,128)(2,1)} %weight_blocks.13.refs_12_), channel_id=1, source_target_pairs={{0,4},{4,0},{8,12},{12,8},{16,20},{20,16},{24,28},{28,24},{1,5},{5... | collective-permute-start | bytes 4718600 | tf_op jit(solution)/shard_map/ppermute | solution.py:1168
  456.4 86.9 %collective-permute-start.28 = (bf16[4,256,768]{2,1,0:T(8,128)(2,1)}, bf16[4,256,768]{2,1,0:T(8,128)(2,1)}, u32[]{:S(2)}, u32[]{:S(2)}) collective-permute-start(bf16[4,256,768]{2,1,0:T(8,128)(2,1)} %weight_blocks.15.refs_1_), channel_id=1, source_target_pairs={{0,4},{4,0},{8,12},{12,8},{16,20},{20,16},{24,28},{28,24},{1,5},{5... | collective-permute-start | bytes 4718600 | tf_op jit(solution)/shard_map/ppermute | solution.py:1168
  473.6 32.1 %collective-permute-start.23 = (bf16[1040,512]{1,0:T(8,128)(2,1)}, bf16[1040,512]{1,0:T(8,128)(2,1)}, u32[]{:S(2)}, u32[]{:S(2)}) collective-permute-start(bf16[1040,512]{1,0:T(8,128)(2,1)} %get-tuple-element.174), channel_id=1, source_target_pairs={{0,2},{1,3},{2,0},{3,1},{4,6},{5,7},{6,4},{7,5},{8,10},{9,11},{10,... | collective-permute-start | bytes 3194888 | tf_op jit(solution)/shard_map/ppermute | solution.py:1351
  475.2 48.8 %collective-permute-start.24 = (bf16[2,256,2048]{2,1,0:T(8,128)(2,1)}, bf16[2,256,2048]{2,1,0:T(8,128)(2,1)}, u32[]{:S(2)}, u32[]{:S(2)}) collective-permute-start(bf16[2,256,2048]{2,1,0:T(8,128)(2,1)} %get-tuple-element.180), channel_id=1, source_target_pairs={{0,8},{4,12},{8,0},{12,4},{16,24},{20,28},{24,16},{28,20},{1,9},{5... | collective-permute-start | bytes 6291464 | tf_op jit(solution)/shard_map/ppermute | solution.py:1168
  483.0 71.9 %collective-permute-start.27 = (bf16[4,512,256]{2,1,0:T(8,128)(2,1)}, bf16[4,512,256]{2,1,0:T(8,128)(2,1)}, u32[]{:S(2)}, u32[]{:S(2)}) collective-permute-start(bf16[4,512,256]{2,1,0:T(8,128)(2,1)} %weight_blocks.16.refs_7_), channel_id=1, source_target_pairs={{0,4},{4,0},{8,12},{12,8},{16,20},{20,16},{24,28},{28,24},{1,5},{5... | collective-permute-start | bytes 3145736 | tf_op jit(solution)/shard_map/ppermute | solution.py:1168
  515.7 59.8 %collective-permute-start.31 = (bf16[2,256,768]{2,1,0:T(8,128)(2,1)}, bf16[2,256,768]{2,1,0:T(8,128)(2,1)}, u32[]{:S(2)}, u32[]{:S(2)}) collective-permute-start(bf16[2,256,768]{2,1,0:T(8,128)(2,1)} %get-tuple-element.198), channel_id=1, source_target_pairs={{0,8},{4,12},{8,0},{12,4},{16,24},{20,28},{24,16},{28,20},{1,9},{5... | collective-permute-start | bytes 2359304 | tf_op jit(solution)/shard_map/ppermute | solution.py:1168
  528.2 47.3 %collective-permute-start.26 = (bf16[1,256,2048]{2,1,0:T(8,128)(2,1)}, bf16[1,256,2048]{2,1,0:T(8,128)(2,1)}, u32[]{:S(2)}, u32[]{:S(2)}) collective-permute-start(bf16[1,256,2048]{2,1,0:T(8,128)(2,1)} %get-tuple-element.193), channel_id=1, source_target_pairs={{0,16},{4,20},{8,24},{12,28},{16,0},{20,4},{24,8},{28,12},{1,17},{... | collective-permute-start | bytes 3145736 | tf_op jit(solution)/shard_map/ppermute | solution.py:1168
  543.2 11.6 %copy-start.10 = (f32[2048]{0:T(1024)S(1)}, f32[2048]{0:T(1024)}, u32[]{:S(2)}) copy-start(f32[2048]{0:T(1024)} %add_reduce_fusion) | copy-start | bytes 24580
  543.3 11.6 %copy-start.23 = (f32[512]{0:T(512)S(1)}, f32[512]{0:T(512)}, u32[]{:S(2)}) copy-start(f32[512]{0:T(512)} %add_reduce_fusion.6) | copy-start | bytes 6148
  553.3 42.0 %collective-permute-start.29 = (bf16[2,256,768]{2,1,0:T(8,128)(2,1)}, bf16[2,256,768]{2,1,0:T(8,128)(2,1)S(1)}, u32[]{:S(2)}, u32[]{:S(2)}) collective-permute-start(bf16[2,256,768]{2,1,0:T(8,128)(2,1)} %get-tuple-element.196), channel_id=1, source_target_pairs={{0,8},{4,12},{8,0},{12,4},{16,24},{20,28},{24,16},{28,20},{1,9},{5... | collective-permute-start | bytes 2359304 | tf_op jit(solution)/shard_map/ppermute | solution.py:1168
  554.9 7.0 %copy-start.6 = (f32[8,512]{1,0:T(8,128)S(1)}, f32[8,512]{1,0:T(8,128)}, u32[]{:S(2)}) copy-start(f32[8,512]{1,0:T(8,128)} %get-tuple-element.188.refs_12_) | copy-start | bytes 49156
  561.3 34.0 %collective-permute-start.30 = (bf16[2,512,256]{2,1,0:T(8,128)(2,1)}, bf16[2,512,256]{2,1,0:T(8,128)(2,1)S(1)}, u32[]{:S(2)}, u32[]{:S(2)}) collective-permute-start(bf16[2,512,256]{2,1,0:T(8,128)(2,1)} %get-tuple-element.197), channel_id=1, source_target_pairs={{0,8},{4,12},{8,0},{12,4},{16,24},{20,28},{24,16},{28,20},{1,9},{5... | collective-permute-start | bytes 1572872 | tf_op jit(solution)/shard_map/ppermute | solution.py:1168
  579.0 21.2 %copy-start.27 = (bf16[1,256,768]{2,1,0:T(8,128)(2,1)S(1)}, bf16[1,256,768]{2,1,0:T(8,128)(2,1)}, u32[]{:S(2)}) copy-start(bf16[1,256,768]{2,1,0:T(8,128)(2,1)} %get-tuple-element.202) | copy-start | bytes 1179652
  579.0 24.2 %copy-start.8 = (f32[13,8,128]{2,1,0:T(8,128)S(1)}, f32[13,8,128]{2,1,0:T(8,128)}, u32[]{:S(2)}) copy-start(f32[13,8,128]{2,1,0:T(8,128)} %get-tuple-element.191) | copy-start | bytes 159748
  579.0 24.2 %copy-start.9 = (f32[13,8,128]{2,1,0:T(8,128)S(1)}, f32[13,8,128]{2,1,0:T(8,128)}, u32[]{:S(2)}) copy-start(f32[13,8,128]{2,1,0:T(8,128)} %get-tuple-element.192) | copy-start | bytes 159748
  600.2 44.9 %collective-permute-start.34 = (bf16[1,256,768]{2,1,0:T(8,128)(2,1)}, bf16[1,256,768]{2,1,0:T(8,128)(2,1)S(1)}, u32[]{:S(2)}, u32[]{:S(2)}) collective-permute-start(bf16[1,256,768]{2,1,0:T(8,128)(2,1)} %get-tuple-element.204), channel_id=1, source_target_pairs={{0,16},{4,20},{8,24},{12,28},{16,0},{20,4},{24,8},{28,12},{1,17},{... | collective-permute-start | bytes 1179656 | tf_op jit(solution)/shard_map/ppermute | solution.py:1168
  600.2 44.9 %collective-permute-start.33 = (bf16[1,256,768]{2,1,0:T(8,128)(2,1)S(1)}, bf16[1,256,768]{2,1,0:T(8,128)(2,1)S(1)}, u32[]{:S(2)}, u32[]{:S(2)}) collective-permute-start(bf16[1,256,768]{2,1,0:T(8,128)(2,1)S(1)} %copy-done.27), channel_id=1, source_target_pairs={{0,16},{4,20},{8,24},{12,28},{16,0},{20,4},{24,8},{28,12},{1,17},{... | collective-permute-start | bytes 1179656 | tf_op jit(solution)/shard_map/ppermute | solution.py:1168
  603.1 42.0 %collective-permute-start.32 = (bf16[1,512,256]{2,1,0:T(8,128)(2,1)}, bf16[1,512,256]{2,1,0:T(8,128)(2,1)S(1)}, u32[]{:S(2)}, u32[]{:S(2)}) collective-permute-start(bf16[1,512,256]{2,1,0:T(8,128)(2,1)} %get-tuple-element.201), channel_id=1, source_target_pairs={{0,16},{4,20},{8,24},{12,28},{16,0},{20,4},{24,8},{28,12},{1,17},{... | collective-permute-start | bytes 786440 | tf_op jit(solution)/shard_map/ppermute | solution.py:1168
  (16 other events, 74.1 us)
Sparse Core Ops, SparseCore 0:
  35.0 49.6 all-gather.1

commit v8 on v7

--- a/solution.py
+++ b/solution.py
@@ -1509,9 +1509,7 @@
         branch[0][1] = gate(branch[0][1:])[0]
     else:
         cot_full = [lax.all_gather(v, "mp", axis=1, tiled=True) for v in cot_rows]
-    if spread:
-        down_sum = Spread(activated, cot_full, 1, (1, 2, 4))
-        down_sum.first()
+    down_sum = spread_over_dp(weight_grad(activated, cot_full), 1)
 
     for r in rows:
         up_grad[r], up_sum, cot_sum, parts = feed_back(
@@ -1537,23 +1535,19 @@
     if spread:
         up_sum = Spread(normed2, up_grad, 0, (1, 2, 4))
         up_sum.first()
-
-        down_sum.keep_added()
+    made = output(branch, hidden, down_bias8)
+    for r in rows[1:]:
+        hidden_step(r)
 
     for r in rows:
         grad_full[r], attended_grad = attended_back(n, pairs, grads[r], out_weight)
-        if r < last:
-            hidden_step(r + 1)
         qkv_grad[r] = attend_back(starts[r], tables, qkv[r], attended_grad, logs[r])
         if r == last and spread:
-            advance(down_sum)
             qkv_sum = [
                 Spread(normed1, qkv_grad, 0, (1, 2, 4), (0, 2)),
                 Spread(normed1, qkv_grad, 0, (1, 2, 4), (1, 2)),
             ]
             qkv_sum[0].first()
-            up_sum.keep_added()
-            qkv_sum[1].first()
         if r > 0 and pairs:
             parts, row_sums = parts1[r - 1]
             parts[1] = row_sums[1] = gate([parts[1]])[0]
@@ -1561,10 +1555,11 @@
         parts1[r] = ring.scatter(parts, True)
 
     if spread:
-        down_sum.coming = gate([down_sum.coming])[0]
+        down_sum = gate([down_sum])[0]
+        up_sum.keep_added()
+        qkv_sum[1].first()
         out_sum = Spread(attended, grad_full, 1, (1, 2, 4))
         out_sum.first()
-    made = output(branch, hidden, down_bias8)
 
     grad_history, depth_sum, gain1_sum, bias1_sum = None, 0.0, 0.0, 0.0
     for r in rows:
@@ -1600,14 +1595,14 @@
         out_sum.keep_added()
         up_sum.coming = gate([up_sum.coming])[0]
         advance(qkv_sum[0])
+        totals, depth_grad = sums(vectors, depth_part)
         advance(qkv_sum[1], out_sum)
     else:
         qkv_sum = [spread_over_dp(weight_grad(normed1, qkv_grad), 0)]
         out_sum = spread_over_dp(weight_grad(attended, grad_full), 1)
-        down_sum = spread_over_dp(weight_grad(activated, cot_full), 1)
         up_sum = spread_over_dp(weight_grad(normed2, up_grad), 0)
+        totals, depth_grad = sums(vectors, depth_part)
     down_total, up_total, out_total, qkv_total = finish([down_sum], [up_sum], [out_sum], qkv_sum)
-    totals, depth_grad = sums(vectors, depth_part)
     return (
         made,
         grad_history,

time: 679 us -> 676 us (level)
  waiting for transfers between devices: 114 us -> 95.9 us
  Pallas kernels: 490 us -> 500 us
  local copies, waits for them, and re-layouts: 14.7 us -> 22.3 us
    pallas_call x49 -> x47, Pallas kernels: 490 us -> 500 us  [call(): pl.pallas_call(without_extra, grid_spec=pltpu.PrefetchScalarGridSpec(num_...]
    ppermute x15 -> x12, waiting for transfers between devices: 82.9 us -> 73.4 us  [send(): lax.ppermute(value, 'dp', [(i, i ^ bit) for i in range(self.groups)])]
    ppermute x16, waiting for transfers between devices: 26.8 us -> 18.2 us  [over_chip(): return lax.ppermute(value, 'mp', self.chip)]
    ppermute x15 -> x12, starting transfers between devices: 16.1 us -> 13.7 us  [send(): lax.ppermute(value, 'dp', [(i, i ^ bit) for i in range(self.groups)])]
  transfers between devices with their start and end apart: 36 -> 34, of which waited for: 10 -> 10; matrix products, arithmetic and copies ran while one was open for 2% -> 4% of each run, Pallas kernels for 69% -> 73%
where the time goes in v8:
time: 676 us; the launch traced here: 671 us
  Pallas kernels  500 us (74%)
  waiting for transfers between devices  95.9 us (14%)
  starting transfers between devices  32.4 us (5%)
  local copies, waits for them, and re-layouts  22.3 us (3%)
  between operations  14.7 us (2%)
    pallas_call x47, Pallas kernels, call(): pl.pallas_call(without_extra, grid_spec=pltpu.PrefetchScalarGridSpec(num_...  500 us
    ppermute x12, waiting for transfers between devices, send(): lax.ppermute(value, 'dp', [(i, i ^ bit) for i in range(self.groups)])  73.4 us
    ppermute x16, waiting for transfers between devices, over_chip(): return lax.ppermute(value, 'mp', self.chip)  18.2 us
    ppermute x16, starting transfers between devices, over_chip(): return lax.ppermute(value, 'mp', self.chip)  17.8 us
    ppermute x12, starting transfers between devices, send(): lax.ppermute(value, 'dp', [(i, i ^ bit) for i in range(self.groups)])  13.7 us
  transfers between devices with their start and end apart: 34, of which 10 were waited for; matrix products, arithmetic and copies ran while one was open for 4% of the time, Pallas kernels for 73%

profile of v8, /device:TPU:0, one launch (start us, length us, event | category | flops | bytes accessed | tf_op | source)
XLA Modules:
  0.0 671.4 jit_solution(17218728571817748123)
XLA Ops:
  8.6 3.0 collective-permute-start.2
  13.8 8.0 %average.2 = (f32[1024,512]{1,0:T(8,128)}, bf16[1024,512]{1,0:T(8,128)(2,1)}) custom-call(f32[13]{0:T(128)} %refs_0_.7, bf16[13,2048,512]{2,1,0:T(8,128)(2,1)} %refs_9_.3), custom_call_target="tpu_custom_call" | custom-call | flops 999999995904 | bytes 100000000 | tf_op jit(solution)/shard_map/average/pallas_call | solution.py:60
  27.1 7.8 %average.3 = (f32[1024,512]{1,0:T(8,128)}, bf16[1024,512]{1,0:T(8,128)(2,1)}) custom-call(f32[13]{0:T(128)} %refs_0_.7, bf16[13,2048,512]{2,1,0:T(8,128)(2,1)} %refs_9_.3, f32[32,512]{1,0:T(8,128)} %get-tuple-element.109.refs_2_), custom_call_target="tpu_custom_call" | custom-call | flops 999999995904 | bytes 100000000 | tf_op jit(solution)/shard_map/average/pallas_call | solution.py:60
  36.9 10.2 %collective-permute-done.refs_1_.refs_3_.refs_5_ = bf16[1024,512]{1,0:T(8,128)(2,1)} collective-permute-done((bf16[1024,512]{1,0:T(8,128)(2,1)}, bf16[1024,512]{1,0:T(8,128)(2,1)}, u32[]{:S(2)}, u32[]{:S(2)}) %collective-permute-start) | collective-permute-done | bytes 1048608 | tf_op jit(solution)/shard_map/ppermute | solution.py:1351
  48.9 17.9 %project.2 = (bf16[1024,1536]{1,0:T(8,128)(2,1)}, bf16[1024,2048]{1,0:T(8,128)(2,1)}, f32[1024,128]{1,0:T(8,128)}, bf16[1024,512]{1,0:T(8,128)(2,1)}, bf16[1024,512]{1,0:T(8,128)(2,1)}) custom-call(bf16[1024,512]{1,0:T(8,128)(2,1)} %get-tuple-element.107.refs_0_.refs_2_, bf16[1024,512]{1,0:T(8,128)(2,1)} %collective-permute-done.refs_1_.refs_3_.refs_5_, ...), custom_call_target="tpu_custom_call" | custom-call | flops 999999995904 | bytes 100000000 | tf_op jit(solution)/shard_map/project/pallas_call | solution.py:60
  67.4 10.1 %attend.2 = (bf16[1024,512]{1,0:T(8,128)(2,1)}, f32[4,8,1024]{2,1,0:T(8,128)}) custom-call(s32[8,1024]{1,0:T(8,128)} %broadcast_in_dim.21.refs_0_, bf16[1024,1536]{1,0:T(8,128)(2,1)} %get-tuple-element.112.refs_1_.refs_3_, f32[1024,128]{1,0:T(8,128)} %get-tuple-element.113.refs_2_.refs_6_), custom_call_target="tpu_custom_call" | custom-call | flops 999999995904 | bytes 100000000 | tf_op jit(solution)/shard_map/attend/pallas_call | solution.py:60
  77.8 18.0 %project.3 = (bf16[1024,1536]{1,0:T(8,128)(2,1)}, bf16[1024,2048]{1,0:T(8,128)(2,1)}, f32[1024,128]{1,0:T(8,128)}, bf16[1024,512]{1,0:T(8,128)(2,1)}, bf16[1024,512]{1,0:T(8,128)(2,1)}) custom-call(bf16[1024,512]{1,0:T(8,128)(2,1)} %gate.12.refs_9_.refs_0_.refs_2_, bf16[1024,512]{1,0:T(8,128)(2,1)} %collective-permute-done.7.refs_1_.refs_3_.refs_5_, ...), custom_call_target="tpu_custom_call" | custom-call | flops 999999995904 | bytes 100000000 | tf_op jit(solution)/shard_map/project/pallas_call | solution.py:60
  96.4 9.7 %attend.3 = (bf16[1024,512]{1,0:T(8,128)(2,1)}, f32[4,8,1024]{2,1,0:T(8,128)}) custom-call(s32[8,1024]{1,0:T(8,128)} %broadcast_in_dim.24.refs_0_, bf16[1024,1536]{1,0:T(8,128)(2,1)} %get-tuple-element.119.refs_1_.refs_3_, f32[1024,128]{1,0:T(8,128)} %get-tuple-element.120.refs_2_.refs_6_), custom_call_target="tpu_custom_call" | custom-call | flops 999999995904 | bytes 100000000 | tf_op jit(solution)/shard_map/attend/pallas_call | solution.py:60
  108.3 4.1 collective-permute-done.8.refs_10_
  113.0 40.8 %feed.2 = (f32[1024,512]{1,0:T(8,128)}, bf16[1024,2048]{1,0:T(8,128)(2,1)}, f32[1024,128]{1,0:T(8,128)}, bf16[1024,2048]{1,0:T(8,128)(2,1)}, bf16[1024,2048]{1,0...) custom-call(bf16[1024,512]{1,0:T(8,128)(2,1)} %get-tuple-element.114.refs_0_.refs_2_.refs_1_, ...), custom_call_target="tpu_custom_call" | custom-call | flops 999999995904 | bytes 100000000 | tf_op jit(solution)/shard_map/feed/pallas_call | solution.py:60
  156.0 41.1 %feed.3 = (f32[1024,512]{1,0:T(8,128)}, bf16[1024,2048]{1,0:T(8,128)(2,1)}, f32[1024,128]{1,0:T(8,128)}, bf16[1024,2048]{1,0:T(8,128)(2,1)}, bf16[1024,2048]{1,0...) custom-call(bf16[1024,512]{1,0:T(8,128)(2,1)} %get-tuple-element.126.refs_0_.refs_2_, ...), custom_call_target="tpu_custom_call" | custom-call | flops 999999995904 | bytes 100000000 | tf_op jit(solution)/shard_map/feed/pallas_call | solution.py:60
  197.4 5.3 collective-permute-done.11.refs_5_.refs_7_
  202.7 11.2 %join.1 = (bf16[1024,2048]{1,0:T(8,128)(2,1)}, bf16[1024,2048]{1,0:T(8,128)(2,1)}) custom-call(bf16[1024,512]{1,0:T(8,128)(2,1)} %gate.14.refs_17_.refs_0_.refs_2_, bf16[1024,512]{1,0:T(8,128)(2,1)} %collective-permute-done.10.refs_1_.refs_3_, bf16[1024,512]{1,0:T(8,128)(2,1)} %gate.14.refs_17_.refs_0_.refs_2_, ...), custom_call_target="tpu_custom_call" | custom-call | flops 999999995904 | bytes 100000000 | tf_op jit(solution)/shard_map/join/pallas_call | solution.py:60
  213.9 23.1 %weight_grad.1.refs_7_ = bf16[2048,2048]{1,0:T(8,128)(2,1)} custom-call(bf16[1024,2048]{1,0:T(8,128)(2,1)} %get-tuple-element.136.refs_0_, bf16[1024,2048]{1,0:T(8,128)(2,1)} %get-tuple-element.137.refs_1_, bf16[1024,2048]{1,0:T(8,128)(2,1)} %get-tuple-element.130.refs_1_.refs_2_.refs_0_, bf16[1024,2048]{1,0:T(8,128)(2,1)} %get-tuple-element.138.refs_3_.refs_0_, ...), custom_call_target="tpu_custom_call" | custom-call | flops 999999995904 | bytes 100000000 | tf_op jit(solution)/shard_map/weight_grad/pallas_call | solution.py:60
  237.0 31.1 %feed_back.2 = (bf16[1024,2048]{1,0:T(8,128)(2,1)}, f32[8,2048]{1,0:T(8,128)}, f32[8,512]{1,0:T(8,128)}, bf16[1024,512]{1,0:T(8,128)(2,1)}, bf16[1040,512]{1,0:T(8,128)(2,1)}, /*index=5*/f32[8,1024]{1,0:T(8,128)}) custom-call(bf16[1024,2048]{1,0:T(8,128)(2,1)} %get-tuple-element.130.refs_1_.refs_2_.refs_0_, bf16[1024,2048]{1,0:T(8,128)(2,1)} %get-tuple-element.134.refs_1_, ...), custom_call_target="tpu_custom_call" | custom-call | flops 999999995904 | bytes 100000000 | tf_op jit(solution)/shard_map/feed_back/pallas_call | solution.py:60
  268.2 31.1 %feed_back.3 = (bf16[1024,2048]{1,0:T(8,128)(2,1)}, f32[8,2048]{1,0:T(8,128)}, f32[8,512]{1,0:T(8,128)}, bf16[1024,512]{1,0:T(8,128)(2,1)}, bf16[1040,512]{1,0:T(8,128)(2,1)}, /*index=5*/f32[8,1024]{1,0:T(8,128)}) custom-call(bf16[1024,2048]{1,0:T(8,128)(2,1)} %get-tuple-element.138.refs_3_.refs_0_, bf16[1024,2048]{1,0:T(8,128)(2,1)} %get-tuple-element.142.refs_1_, ...), custom_call_target="tpu_custom_call" | custom-call | flops 999999995904 | bytes 100000000 | tf_op jit(solution)/shard_map/feed_back/pallas_call | solution.py:60
  305.4 5.9 hidden_back.2
  311.5 14.7 %weight_blocks.8.refs_7_ = bf16[4,256,2048]{2,1,0:T(8,128)(2,1)} custom-call(s32[1]{0:T(128)} %bitcast.7.refs_0_, bf16[1024,2048]{1,0:T(8,128)(2,1)} %get-tuple-element.135.refs_2_.refs_1_.refs_3_.refs_5_.refs_7_, bf16[1024,2048]{1,0:T(8,128)(2,1)} %get-tuple-element.140.refs_2_.refs_4_.refs_6_.refs_8_, ...), custom_call_target="tpu_custom_call" | custom-call | flops 999999995904 | bytes 100000000 | tf_op jit(solution)/shard_map/weight_blocks/pallas_call | solution.py:60
  328.0 6.8 %output.1.refs_8_ = bf16[2048,512]{1,0:T(8,128)(2,1)} custom-call(f32[1024,512]{1,0:T(8,128)} %get-tuple-element.122.refs_5_.refs_0_, bf16[1024,512]{1,0:T(8,128)(2,1)} %get-tuple-element.123.refs_1_, bf16[1024,512]{1,0:T(8,128)(2,1)} %gate.16.refs_4_.refs_2_, f32[1024,512]{1,0:T(8,128)} %get-tuple-element.131.refs_3_.refs_5_, ...), custom_call_target="tpu_custom_call" | custom-call | flops 999999995904 | bytes 100000000 | tf_op jit(solution)/shard_map/output/pallas_call | solution.py:60
  334.8 5.8 hidden_back.3
  345.8 2.7 collective-permute-done.17.refs_1_.refs_3_
  348.6 9.1 %attended_back.2 = (bf16[1024,2048]{1,0:T(8,128)(2,1)}, bf16[1024,512]{1,0:T(8,128)(2,1)}) custom-call(bf16[1024,512]{1,0:T(8,128)(2,1)} %get-tuple-element.153.refs_0_.refs_2_, bf16[1024,512]{1,0:T(8,128)(2,1)} %collective-permute-done.17.refs_1_.refs_3_, bf16[1024,512]{1,0:T(8,128)(2,1)} %get-tuple-element.153.refs_0_.refs_2_, ...), custom_call_target="tpu_custom_call" | custom-call | flops 999999995904 | bytes 100000000 | tf_op jit(solution)/shard_map/attended_back/pallas_call | solution.py:60
  357.6 12.4 %attend_back.2.refs_0_.refs_9_ = bf16[1024,1536]{1,0:T(8,128)(2,1)} custom-call(s32[8,1024]{1,0:T(8,128)} %broadcast_in_dim.21.refs_0_, f32[1024,128]{1,0:T(8,128)} %constant.19.clone.refs_6_.refs_1_, f32[1024,128]{1,0:T(8,128)} %constant.20.clone.refs_7_.refs_2_, bf16[1024,1536]{1,0:T(8,128)(2,1)} %get-tuple-element.112.refs_1_.refs_3_, ...), custom_call_target="tpu_custom_call" | custom-call | flops 999999995904 | bytes 100000000 | tf_op jit(solution)/shard_map/attend_back/pallas_call | solution.py:60
  370.0 15.6 %project_back.2 = (bf16[1024,512]{1,0:T(8,128)(2,1)}, bf16[1040,512]{1,0:T(8,128)(2,1)}, f32[8,1024]{1,0:T(8,128)}) custom-call(bf16[1024,1536]{1,0:T(8,128)(2,1)} %attend_back.2.refs_0_.refs_9_, bf16[1024,2048]{1,0:T(8,128)(2,1)} %get-tuple-element.156.refs_1_.refs_3_.refs_5_.refs_7_, f32[8,2048]{1,0:T(8,128)} %get-tuple-element.206.refs_4_.refs_2_, ...), custom_call_target="tpu_custom_call" | custom-call | flops 999999995904 | bytes 100000000 | tf_op jit(solution)/shard_map/project_back/pallas_call | solution.py:60
  387.5 9.0 %attended_back.3 = (bf16[1024,2048]{1,0:T(8,128)(2,1)}, bf16[1024,512]{1,0:T(8,128)(2,1)}) custom-call(bf16[1024,512]{1,0:T(8,128)(2,1)} %get-tuple-element.152.refs_0_.refs_2_, bf16[1024,512]{1,0:T(8,128)(2,1)} %collective-permute-done.16.refs_1_.refs_3_, bf16[1024,512]{1,0:T(8,128)(2,1)} %get-tuple-element.152.refs_0_.refs_2_, ...), custom_call_target="tpu_custom_call" | custom-call | flops 999999995904 | bytes 100000000 | tf_op jit(solution)/shard_map/attended_back/pallas_call | solution.py:60
  396.5 12.6 %attend_back.3.refs_10_.refs_0_ = bf16[1024,1536]{1,0:T(8,128)(2,1)} custom-call(s32[8,1024]{1,0:T(8,128)} %broadcast_in_dim.24.refs_0_, f32[1024,128]{1,0:T(8,128)} %constant.19.clone.refs_6_.refs_1_, f32[1024,128]{1,0:T(8,128)} %constant.20.clone.refs_7_.refs_2_, bf16[1024,1536]{1,0:T(8,128)(2,1)} %get-tuple-element.119.refs_1_.refs_3_, ...), custom_call_target="tpu_custom_call" | custom-call | flops 999999995904 | bytes 100000000 | tf_op jit(solution)/shard_map/attend_back/pallas_call | solution.py:60
  409.1 9.6 %weight_blocks.9.refs_1_ = bf16[4,256,768]{2,1,0:T(8,128)(2,1)} custom-call(s32[1]{0:T(128)} %bitcast.7.refs_0_, bf16[1024,2048]{1,0:T(8,128)(2,1)} %get-tuple-element.156.refs_1_.refs_3_.refs_5_.refs_7_, bf16[1024,2048]{1,0:T(8,128)(2,1)} %get-tuple-element.159.refs_2_.refs_4_.refs_6_.refs_8_.refs_1_, ...), custom_call_target="tpu_custom_call" | custom-call | flops 999999995904 | bytes 100000000 | tf_op jit(solution)/shard_map/weight_blocks/pallas_call | solution.py:60
  419.9 15.6 %project_back.3 = (bf16[1024,512]{1,0:T(8,128)(2,1)}, bf16[1040,512]{1,0:T(8,128)(2,1)}, f32[8,1024]{1,0:T(8,128)}) custom-call(bf16[1024,1536]{1,0:T(8,128)(2,1)} %attend_back.3.refs_10_.refs_0_, bf16[1024,2048]{1,0:T(8,128)(2,1)} %get-tuple-element.159.refs_2_.refs_4_.refs_6_.refs_8_.refs_1_, f32[8,2048]{1,0:T(8,128)} %get-tuple-element.206.refs_4_.refs_2_, ...), custom_call_target="tpu_custom_call" | custom-call | flops 999999995904 | bytes 100000000 | tf_op jit(solution)/shard_map/project_back/pallas_call | solution.py:60
  435.9 2.6 collective-permute-done.20.refs_11_
  438.5 15.1 %weight_blocks.10 = (bf16[2,256,2048]{2,1,0:T(8,128)(2,1)}, bf16[2,256,2048]{2,1,0:T(8,128)(2,1)}) custom-call(s32[1]{0:T(128)} %bitcast.7.refs_0_, bf16[1024,2048]{1,0:T(8,128)(2,1)} %get-tuple-element.135.refs_2_.refs_1_.refs_3_.refs_5_.refs_7_, bf16[1024,2048]{1,0:T(8,128)(2,1)} %get-tuple-element.140.refs_2_.refs_4_.refs_6_.refs_8_, ...), custom_call_target="tpu_custom_call" | custom-call | flops 999999995904 | bytes 100000000 | tf_op jit(solution)/shard_map/weight_blocks/pallas_call | solution.py:60
  453.6 9.9 %weight_blocks.11.refs_11_ = bf16[4,256,768]{2,1,0:T(8,128)(2,1)} custom-call(s32[1]{0:T(128)} %bitcast.7.refs_0_, bf16[1024,2048]{1,0:T(8,128)(2,1)} %get-tuple-element.156.refs_1_.refs_3_.refs_5_.refs_7_, bf16[1024,2048]{1,0:T(8,128)(2,1)} %get-tuple-element.159.refs_2_.refs_4_.refs_6_.refs_8_.refs_1_, ...), custom_call_target="tpu_custom_call" | custom-call | flops 999999995904 | bytes 100000000 | tf_op jit(solution)/shard_map/weight_blocks/pallas_call | solution.py:60
  465.0 6.2 weight_blocks.12.refs_10_
  472.4 14.4 %average_back.2 = (bf16[13,2048,512]{2,1,0:T(8,128)(2,1)}, f32[13,8,128]{2,1,0:T(8,128)}, f32[8,512]{1,0:T(8,128)}, f32[8,512]{1,0:T(8,128)}) custom-call(f32[13]{0:T(128)} %refs_0_.7, bf16[1024,512]{1,0:T(8,128)(2,1)} %get-tuple-element.163.refs_1_, bf16[1040,512]{1,0:T(8,128)(2,1)} %gate.18.refs_5_.refs_2_.refs_4_, ...), custom_call_target="tpu_custom_call" | custom-call | flops 999999995904 | bytes 100000000 | tf_op jit(solution)/shard_map/average_back/pallas_call | solution.py:60
  486.9 10.0 %weight_blocks.13 = (bf16[2,256,768]{2,1,0:T(8,128)(2,1)}, bf16[2,256,768]{2,1,0:T(8,128)(2,1)}) custom-call(s32[1]{0:T(128)} %bitcast.7.refs_0_, bf16[1024,2048]{1,0:T(8,128)(2,1)} %get-tuple-element.156.refs_1_.refs_3_.refs_5_.refs_7_, bf16[1024,2048]{1,0:T(8,128)(2,1)} %get-tuple-element.159.refs_2_.refs_4_.refs_6_.refs_8_.refs_1_, ...), custom_call_target="tpu_custom_call" | custom-call | flops 999999995904 | bytes 100000000 | tf_op jit(solution)/shard_map/weight_blocks/pallas_call | solution.py:60
  498.7 21.8 %collective-permute-done.21.refs_1_ = bf16[2,256,2048]{2,1,0:T(8,128)(2,1)} collective-permute-done((bf16[2,256,2048]{2,1,0:T(8,128)(2,1)}, bf16[2,256,2048]{2,1,0:T(8,128)(2,1)}, u32[]{:S(2)}, u32[]{:S(2)}) %collective-permute-start.21) | collective-permute-done | bytes 2097184 | tf_op jit(solution)/shard_map/ppermute | solution.py:1168
  520.5 4.2 fold.3
  525.9 14.7 %average_back.3 = (bf16[13,2048,512]{2,1,0:T(8,128)(2,1)}, f32[13,8,128]{2,1,0:T(8,128)}, f32[8,512]{1,0:T(8,128)}, f32[8,512]{1,0:T(8,128)}) custom-call(f32[13]{0:T(128)} %refs_0_.7, bf16[1024,512]{1,0:T(8,128)(2,1)} %get-tuple-element.161.refs_1_, bf16[1040,512]{1,0:T(8,128)(2,1)} %gate.20.refs_12_.refs_2_.refs_4_, ...), custom_call_target="tpu_custom_call", output_to_operand_aliasing={{0}: (10, {})} | custom-call | flops 999999995904 | bytes 100000000 | tf_op jit(solution)/shard_map/average_back/pallas_call | solution.py:60
  540.7 10.0 %weight_blocks.14 = (bf16[2,256,768]{2,1,0:T(8,128)(2,1)}, bf16[2,256,768]{2,1,0:T(8,128)(2,1)}) custom-call(s32[1]{0:T(128)} %bitcast.7.refs_0_, bf16[1024,2048]{1,0:T(8,128)(2,1)} %get-tuple-element.156.refs_1_.refs_3_.refs_5_.refs_7_, bf16[1024,2048]{1,0:T(8,128)(2,1)} %get-tuple-element.159.refs_2_.refs_4_.refs_6_.refs_8_.refs_1_, ...), custom_call_target="tpu_custom_call" | custom-call | flops 10000 | bytes 1 | tf_op jit(solution)/shard_map/weight_blocks/pallas_call | solution.py:60
  550.8 6.4 weight_blocks.15
  557.2 2.0 collective-permute-start.28
  562.7 6.7 %collective-permute-done.24.refs_0_ = bf16[1,256,2048]{2,1,0:T(8,128)(2,1)} collective-permute-done((bf16[1,256,2048]{2,1,0:T(8,128)(2,1)}, bf16[1,256,2048]{2,1,0:T(8,128)(2,1)}, u32[]{:S(2)}, u32[]{:S(2)}) %collective-permute-start.24) | collective-permute-done | bytes 1048608 | tf_op jit(solution)/shard_map/ppermute | solution.py:1168
  569.5 3.5 fold.4
  573.0 29.4 %sums.1.refs_4_ = f32[48,128]{1,0:T(8,128)} custom-call(f32[48,128]{1,0:T(8,128)} %select_maximum_fusion.refs_0_, bf16[1,256,768]{2,1,0:T(8,128)(2,1)} %get-tuple-element.189.refs_1_.refs_5_), custom_call_target="tpu_custom_call" | custom-call | flops 10000 | bytes 1 | tf_op jit(solution)/shard_map/sums/pallas_call | solution.py:60
  605.4 3.8 fold.5
  615.7 26.3 %collective-permute-done.29.refs_4_ = bf16[1,512,256]{2,1,0:T(8,128)(2,1)S(1)} collective-permute-done((bf16[1,512,256]{2,1,0:T(8,128)(2,1)}, bf16[1,512,256]{2,1,0:T(8,128)(2,1)S(1)}, u32[]{:S(2)}, u32[]{:S(2)}) %collective-permute-start.29) | collective-permute-done | bytes 262176 | tf_op jit(solution)/shard_map/ppermute | solution.py:1168
  642.0 8.4 %collective-permute-done.31.refs_8_ = bf16[1,256,768]{2,1,0:T(8,128)(2,1)S(1)} collective-permute-done((bf16[1,256,768]{2,1,0:T(8,128)(2,1)}, bf16[1,256,768]{2,1,0:T(8,128)(2,1)S(1)}, u32[]{:S(2)}, u32[]{:S(2)}) %collective-permute-start.31) | collective-permute-done | bytes 393248 | tf_op jit(solution)/shard_map/ppermute | solution.py:1168
  650.5 7.6 %collective-permute-done.30.refs_6_ = bf16[1,256,768]{2,1,0:T(8,128)(2,1)S(1)} collective-permute-done((bf16[1,256,768]{2,1,0:T(8,128)(2,1)S(1)}, bf16[1,256,768]{2,1,0:T(8,128)(2,1)S(1)}, u32[]{:S(2)}, u32[]{:S(2)}) %collective-permute-start.30) | collective-permute-done | bytes 393248 | tf_op jit(solution)/shard_map/ppermute | solution.py:1168
  658.8 5.5 finish.1
  (149 shorter events, 55.7 us)
Async XLA Ops:
  7.2 100.7 %all-gather.2.cloned.1.call-start = ((), (), s32[]{:S(2)}) async-start(), calls=%async_computation.1 | async-start | bytes 2359296 | tf_op jit(solution)/shard_map/all_gather | solution.py:1392
  8.6 18.4 %collective-permute-start.2 = (f32[32,512]{1,0:T(8,128)}, f32[32,512]{1,0:T(8,128)}, u32[]{:S(2)}, u32[]{:S(2)}) collective-permute-start(f32[32,512]{1,0:T(8,128)} %broadcast_bitcast_fusion), channel_id=1, source_target_pairs={{0,2},{1,3},{2,0},{3,1},{4,6},{5,7},{6,4},{7,5},{8,10},{9,11},{10,... | collective-permute-start | bytes 196616 | tf_op jit(solution)/shard_map/ppermute | solution.py:1351
  11.6 23.6 %collective-permute-start.1 = (f32[32,512]{1,0:T(8,128)}, f32[32,512]{1,0:T(8,128)}, u32[]{:S(2)}, u32[]{:S(2)}) collective-permute-start(f32[32,512]{1,0:T(8,128)} %broadcast_bitcast_fusion), channel_id=1, source_target_pairs={{0,1},{1,0},{2,3},{3,2},{4,5},{5,4},{6,7},{7,6},{8,9},{9,8},{10,11... | collective-permute-start | bytes 196616 | tf_op jit(solution)/shard_map/ppermute | solution.py:1348
  11.6 96.7 %collective-permute-start.6 = (bf16[512,2048]{1,0:T(8,128)(2,1)}, bf16[512,2048]{1,0:T(8,128)(2,1)}, u32[]{:S(2)}, u32[]{:S(2)}) collective-permute-start(bf16[512,2048]{1,0:T(8,128)(2,1)} %refs_4_.10), channel_id=1, source_target_pairs={{0,1},{1,0},{2,3},{3,2},{4,5},{5,4},{6,7},{7,6},{8,9},{9,8},{10,11... | collective-permute-start | bytes 6291464 | tf_op jit(solution)/shard_map/ppermute | solution.py:1348
  13.8 13.3 %collective-permute-start.3 = (bf16[64,2048]{1,0:T(8,128)(2,1)}, bf16[64,2048]{1,0:T(8,128)(2,1)}, u32[]{:S(2)}, u32[]{:S(2)}) collective-permute-start(bf16[64,2048]{1,0:T(8,128)(2,1)} %constant_dynamic-slice_fusion), channel_id=1, source_target_pairs={{0,2},{1,3},{2,0},{3,1},{4,6},{5,7},{6,4},{7,5},{8,10},{9,11},{10,... | collective-permute-start | bytes 786440 | tf_op jit(solution)/shard_map/ppermute | solution.py:1351
  13.8 10.0 %copy-start = (bf16[2048,512]{1,0:T(8,128)(2,1)S(1)}, bf16[2048,512]{1,0:T(8,128)(2,1)}, u32[]{:S(2)}) copy-start(bf16[2048,512]{1,0:T(8,128)(2,1)} %refs_4_.7) | copy-start | bytes 6291460
  21.7 25.4 %collective-permute-start = (bf16[1024,512]{1,0:T(8,128)(2,1)}, bf16[1024,512]{1,0:T(8,128)(2,1)}, u32[]{:S(2)}, u32[]{:S(2)}) collective-permute-start(bf16[1024,512]{1,0:T(8,128)(2,1)} %get-tuple-element.107.refs_0_.refs_2_), channel_id=1, source_target_pairs={{0,2},{1,3},{2,0},{3,1},{4,6},{5,7},{6,4},{7,5},{8,10},{9,11},{10,... | collective-permute-start | bytes 3145736 | tf_op jit(solution)/shard_map/ppermute | solution.py:1351
  27.0 8.2 %collective-permute-start.4 = (f32[32,512]{1,0:T(8,128)}, f32[32,512]{1,0:T(8,128)}, u32[]{:S(2)}, u32[]{:S(2)}) collective-permute-start(f32[32,512]{1,0:T(8,128)} %get-tuple-element.109.refs_2_), channel_id=1, source_target_pairs={{0,1},{1,0},{2,3},{3,2},{4,5},{5,4},{6,7},{7,6},{8,9},{9,8},{10,11... | collective-permute-start | bytes 196616 | tf_op jit(solution)/shard_map/ppermute | solution.py:1348
  35.0 400.9 %reduce-scatter.2.cloned.1.call-start = ((), (), s32[]{:S(2)}) async-start(), calls=%async_computation.2 | async-start | bytes 9437184 | tf_op jit(solution)/shard_map/reduce_scatter | solution.py:1505
  47.1 30.6 %collective-permute-start.7 = (bf16[1024,512]{1,0:T(8,128)(2,1)}, bf16[1024,512]{1,0:T(8,128)(2,1)}, u32[]{:S(2)}, u32[]{:S(2)}) collective-permute-start(bf16[1024,512]{1,0:T(8,128)(2,1)} %gate.12.refs_9_.refs_0_.refs_2_), channel_id=1, source_target_pairs={{0,2},{1,3},{2,0},{3,1},{4,6},{5,7},{6,4},{7,5},{8,10},{9,11},{10,... | collective-permute-start | bytes 3145736 | tf_op jit(solution)/shard_map/ppermute | solution.py:1351
  48.9 17.9 %copy-start.18 = (s32[1,1024]{1,0:T(1,128)S(1)}, s32[1,1024]{1,0:T(1,128)}, u32[]{:S(2)}) copy-start(s32[1,1024]{1,0:T(1,128)} %get-tuple-element.213) | copy-start | bytes 12292
  77.5 30.8 %collective-permute-start.5 = (bf16[1024,512]{1,0:T(8,128)(2,1)}, bf16[1024,512]{1,0:T(8,128)(2,1)}, u32[]{:S(2)}, u32[]{:S(2)}) collective-permute-start(bf16[1024,512]{1,0:T(8,128)(2,1)} %get-tuple-element.114.refs_0_.refs_2_.refs_1_), channel_id=1, source_target_pairs={{0,2},{1,3},{2,0},{3,1},{4,6},{5,7},{6,4},{7,5},{8,10},{9,11},{10,... | collective-permute-start | bytes 3145736 | tf_op jit(solution)/shard_map/ppermute | solution.py:1351
  77.8 18.0 %copy-start.17 = (s32[1,1024]{1,0:T(1,128)S(1)}, s32[1,1024]{1,0:T(1,128)}, u32[]{:S(2)}) copy-start(s32[1,1024]{1,0:T(1,128)} %get-tuple-element.212) | copy-start | bytes 12292
  106.1 49.8 %collective-permute-start.12 = (bf16[1024,512]{1,0:T(8,128)(2,1)}, bf16[1024,512]{1,0:T(8,128)(2,1)}, u32[]{:S(2)}, u32[]{:S(2)}) collective-permute-start(bf16[1024,512]{1,0:T(8,128)(2,1)} %get-tuple-element.126.refs_0_.refs_2_), channel_id=1, source_target_pairs={{0,2},{1,3},{2,0},{3,1},{4,6},{5,7},{6,4},{7,5},{8,10},{9,11},{10,... | collective-permute-start | bytes 3145736 | tf_op jit(solution)/shard_map/ppermute | solution.py:1351
  107.9 4.5 collective-permute-start.8
  107.9 89.5 %collective-permute-start.10 = (bf16[1024,512]{1,0:T(8,128)(2,1)}, bf16[1024,512]{1,0:T(8,128)(2,1)}, u32[]{:S(2)}, u32[]{:S(2)}) collective-permute-start(bf16[1024,512]{1,0:T(8,128)(2,1)} %gate.14.refs_17_.refs_0_.refs_2_), channel_id=1, source_target_pairs={{0,2},{1,3},{2,0},{3,1},{4,6},{5,7},{6,4},{7,5},{8,10},{9,11},{10,... | collective-permute-start | bytes 3145736 | tf_op jit(solution)/shard_map/ppermute | solution.py:1351
  153.8 60.1 %collective-permute-start.9 = (bf16[1024,512]{1,0:T(8,128)(2,1)}, bf16[1024,512]{1,0:T(8,128)(2,1)}, u32[]{:S(2)}, u32[]{:S(2)}) collective-permute-start(bf16[1024,512]{1,0:T(8,128)(2,1)} %get-tuple-element.124), channel_id=1, source_target_pairs={{0,2},{1,3},{2,0},{3,1},{4,6},{5,7},{6,4},{7,5},{8,10},{9,11},{10,... | collective-permute-start | bytes 3145736 | tf_op jit(solution)/shard_map/ppermute | solution.py:1351
  154.2 48.5 %collective-permute-start.11 = (bf16[1024,512]{1,0:T(8,128)(2,1)}, bf16[1024,512]{1,0:T(8,128)(2,1)}, u32[]{:S(2)}, u32[]{:S(2)}) collective-permute-start(bf16[1024,512]{1,0:T(8,128)(2,1)} %gate.15.refs_17_.refs_4_.refs_6_), channel_id=1, source_target_pairs={{0,2},{1,3},{2,0},{3,1},{4,6},{5,7},{6,4},{7,5},{8,10},{9,11},{10,... | collective-permute-start | bytes 3145736 | tf_op jit(solution)/shard_map/ppermute | solution.py:1351
  197.1 71.1 %collective-permute-start.13 = (bf16[1024,512]{1,0:T(8,128)(2,1)}, bf16[1024,512]{1,0:T(8,128)(2,1)}, u32[]{:S(2)}, u32[]{:S(2)}) collective-permute-start(bf16[1024,512]{1,0:T(8,128)(2,1)} %get-tuple-element.133), channel_id=1, source_target_pairs={{0,2},{1,3},{2,0},{3,1},{4,6},{5,7},{6,4},{7,5},{8,10},{9,11},{10,... | collective-permute-start | bytes 3145736 | tf_op jit(solution)/shard_map/ppermute | solution.py:1351
  268.1 36.6 %collective-permute-start.14 = (bf16[1040,512]{1,0:T(8,128)(2,1)}, bf16[1040,512]{1,0:T(8,128)(2,1)}, u32[]{:S(2)}, u32[]{:S(2)}) collective-permute-start(bf16[1040,512]{1,0:T(8,128)(2,1)} %get-tuple-element.145), channel_id=1, source_target_pairs={{0,2},{1,3},{2,0},{3,1},{4,6},{5,7},{6,4},{7,5},{8,10},{9,11},{10,... | collective-permute-start | bytes 3194888 | tf_op jit(solution)/shard_map/ppermute | solution.py:1351
  268.2 33.0 %copy-start.7 = (f32[8,2048]{1,0:T(8,128)S(1)}, f32[8,2048]{1,0:T(8,128)}, u32[]{:S(2)}) copy-start(f32[8,2048]{1,0:T(8,128)} %get-tuple-element.176) | copy-start | bytes 196612
  268.2 34.5 %copy-start.16 = (f32[8,512]{1,0:T(8,128)S(1)}, f32[8,512]{1,0:T(8,128)}, u32[]{:S(2)}) copy-start(f32[8,512]{1,0:T(8,128)} %get-tuple-element.139.refs_1_) | copy-start | bytes 49156
  268.2 36.5 %copy-start.20 = (f32[512]{0:T(512)S(1)}, f32[512]{0:T(512)}, u32[]{:S(2)}) copy-start(f32[512]{0:T(512)} %param.23) | copy-start | bytes 6148
  299.4 35.4 %collective-permute-start.15 = (bf16[1040,512]{1,0:T(8,128)(2,1)}, bf16[1040,512]{1,0:T(8,128)(2,1)}, u32[]{:S(2)}, u32[]{:S(2)}) collective-permute-start(bf16[1040,512]{1,0:T(8,128)(2,1)} %get-tuple-element.150), channel_id=1, source_target_pairs={{0,2},{1,3},{2,0},{3,1},{4,6},{5,7},{6,4},{7,5},{8,10},{9,11},{10,... | collective-permute-start | bytes 3194888 | tf_op jit(solution)/shard_map/ppermute | solution.py:1351
  311.2 37.3 %collective-permute-start.17 = (bf16[1024,512]{1,0:T(8,128)(2,1)}, bf16[1024,512]{1,0:T(8,128)(2,1)}, u32[]{:S(2)}, u32[]{:S(2)}) collective-permute-start(bf16[1024,512]{1,0:T(8,128)(2,1)} %get-tuple-element.153.refs_0_.refs_2_), channel_id=1, source_target_pairs={{0,2},{1,3},{2,0},{3,1},{4,6},{5,7},{6,4},{7,5},{8,10},{9,11},{10,... | collective-permute-start | bytes 3145736 | tf_op jit(solution)/shard_map/ppermute | solution.py:1351
  311.5 16.0 %copy-start.22 = (f32[512]{0:T(512)S(1)}, f32[512]{0:T(512)}, u32[]{:S(2)}) copy-start(f32[512]{0:T(512)} %param.28) | copy-start | bytes 6148
  326.2 112.3 %collective-permute-start.20 = (bf16[4,256,2048]{2,1,0:T(8,128)(2,1)}, bf16[4,256,2048]{2,1,0:T(8,128)(2,1)}, u32[]{:S(2)}, u32[]{:S(2)}) collective-permute-start(bf16[4,256,2048]{2,1,0:T(8,128)(2,1)} %weight_blocks.8.refs_7_), channel_id=1, source_target_pairs={{0,4},{4,0},{8,12},{12,8},{16,20},{20,16},{24,28},{28,24},{1,5},{5... | collective-permute-start | bytes 12582920 | tf_op jit(solution)/shard_map/ppermute | solution.py:1168
  340.7 46.8 %collective-permute-start.16 = (bf16[1024,512]{1,0:T(8,128)(2,1)}, bf16[1024,512]{1,0:T(8,128)(2,1)}, u32[]{:S(2)}, u32[]{:S(2)}) collective-permute-start(bf16[1024,512]{1,0:T(8,128)(2,1)} %get-tuple-element.152.refs_0_.refs_2_), channel_id=1, source_target_pairs={{0,2},{1,3},{2,0},{3,1},{4,6},{5,7},{6,4},{7,5},{8,10},{9,11},{10,... | collective-permute-start | bytes 3145736 | tf_op jit(solution)/shard_map/ppermute | solution.py:1351
  385.6 34.3 %collective-permute-start.18 = (bf16[1040,512]{1,0:T(8,128)(2,1)}, bf16[1040,512]{1,0:T(8,128)(2,1)}, u32[]{:S(2)}, u32[]{:S(2)}) collective-permute-start(bf16[1040,512]{1,0:T(8,128)(2,1)} %get-tuple-element.160), channel_id=1, source_target_pairs={{0,2},{1,3},{2,0},{3,1},{4,6},{5,7},{6,4},{7,5},{8,10},{9,11},{10,... | collective-permute-start | bytes 3194888 | tf_op jit(solution)/shard_map/ppermute | solution.py:1351
  418.7 68.1 %collective-permute-start.22 = (bf16[4,256,768]{2,1,0:T(8,128)(2,1)}, bf16[4,256,768]{2,1,0:T(8,128)(2,1)}, u32[]{:S(2)}, u32[]{:S(2)}) collective-permute-start(bf16[4,256,768]{2,1,0:T(8,128)(2,1)} %weight_blocks.9.refs_1_), channel_id=1, source_target_pairs={{0,4},{4,0},{8,12},{12,8},{16,20},{20,16},{24,28},{28,24},{1,5},{5... | collective-permute-start | bytes 4718600 | tf_op jit(solution)/shard_map/ppermute | solution.py:1168
  435.4 51.4 %collective-permute-start.19 = (bf16[1040,512]{1,0:T(8,128)(2,1)}, bf16[1040,512]{1,0:T(8,128)(2,1)}, u32[]{:S(2)}, u32[]{:S(2)}) collective-permute-start(bf16[1040,512]{1,0:T(8,128)(2,1)} %get-tuple-element.162), channel_id=1, source_target_pairs={{0,2},{1,3},{2,0},{3,1},{4,6},{5,7},{6,4},{7,5},{8,10},{9,11},{10,... | collective-permute-start | bytes 3194888 | tf_op jit(solution)/shard_map/ppermute | solution.py:1351
  463.5 77.2 %collective-permute-start.26 = (bf16[4,256,768]{2,1,0:T(8,128)(2,1)}, bf16[4,256,768]{2,1,0:T(8,128)(2,1)}, u32[]{:S(2)}, u32[]{:S(2)}) collective-permute-start(bf16[4,256,768]{2,1,0:T(8,128)(2,1)} %weight_blocks.11.refs_11_), channel_id=1, source_target_pairs={{0,4},{4,0},{8,12},{12,8},{16,20},{20,16},{24,28},{28,24},{1,5},{5... | collective-permute-start | bytes 4718600 | tf_op jit(solution)/shard_map/ppermute | solution.py:1168
  471.1 79.6 %collective-permute-start.25 = (bf16[4,512,256]{2,1,0:T(8,128)(2,1)}, bf16[4,512,256]{2,1,0:T(8,128)(2,1)}, u32[]{:S(2)}, u32[]{:S(2)}) collective-permute-start(bf16[4,512,256]{2,1,0:T(8,128)(2,1)} %weight_blocks.12.refs_10_), channel_id=1, source_target_pairs={{0,4},{4,0},{8,12},{12,8},{16,20},{20,16},{24,28},{28,24},{1,5},{5... | collective-permute-start | bytes 3145736 | tf_op jit(solution)/shard_map/ppermute | solution.py:1168
  471.7 48.9 %collective-permute-start.21 = (bf16[2,256,2048]{2,1,0:T(8,128)(2,1)}, bf16[2,256,2048]{2,1,0:T(8,128)(2,1)}, u32[]{:S(2)}, u32[]{:S(2)}) collective-permute-start(bf16[2,256,2048]{2,1,0:T(8,128)(2,1)} %get-tuple-element.172), channel_id=1, source_target_pairs={{0,8},{4,12},{8,0},{12,4},{16,24},{20,28},{24,16},{28,20},{1,9},{5... | collective-permute-start | bytes 6291464 | tf_op jit(solution)/shard_map/ppermute | solution.py:1168
  496.9 72.6 %collective-permute-start.23 = (bf16[2,256,768]{2,1,0:T(8,128)(2,1)}, bf16[2,256,768]{2,1,0:T(8,128)(2,1)}, u32[]{:S(2)}, u32[]{:S(2)}) collective-permute-start(bf16[2,256,768]{2,1,0:T(8,128)(2,1)} %get-tuple-element.185), channel_id=1, source_target_pairs={{0,8},{4,12},{8,0},{12,4},{16,24},{20,28},{24,16},{28,20},{1,9},{5... | collective-permute-start | bytes 2359304 | tf_op jit(solution)/shard_map/ppermute | solution.py:1168
  524.7 44.8 %collective-permute-start.24 = (bf16[1,256,2048]{2,1,0:T(8,128)(2,1)}, bf16[1,256,2048]{2,1,0:T(8,128)(2,1)}, u32[]{:S(2)}, u32[]{:S(2)}) collective-permute-start(bf16[1,256,2048]{2,1,0:T(8,128)(2,1)} %get-tuple-element.186), channel_id=1, source_target_pairs={{0,16},{4,20},{8,24},{12,28},{16,0},{20,4},{24,8},{28,12},{1,17},{... | collective-permute-start | bytes 3145736 | tf_op jit(solution)/shard_map/ppermute | solution.py:1168
  550.7 8.6 %copy-start.6 = (f32[8,512]{1,0:T(8,128)S(1)}, f32[8,512]{1,0:T(8,128)}, u32[]{:S(2)}) copy-start(f32[8,512]{1,0:T(8,128)} %get-tuple-element.180.refs_12_) | copy-start | bytes 49156
  550.7 8.6 %copy-start.11 = (f32[8,512]{1,0:T(8,128)S(1)}, f32[8,512]{1,0:T(8,128)}, u32[]{:S(2)}) copy-start(f32[8,512]{1,0:T(8,128)} %get-tuple-element.169.refs_1_) | copy-start | bytes 49156
  550.7 8.6 %copy-start.12 = (f32[8,512]{1,0:T(8,128)S(1)}, f32[8,512]{1,0:T(8,128)}, u32[]{:S(2)}) copy-start(f32[8,512]{1,0:T(8,128)} %get-tuple-element.181) | copy-start | bytes 49156
  550.8 11.2 %copy-start.8 = (f32[13,8,128]{2,1,0:T(8,128)S(1)}, f32[13,8,128]{2,1,0:T(8,128)}, u32[]{:S(2)}) copy-start(f32[13,8,128]{2,1,0:T(8,128)} %get-tuple-element.183) | copy-start | bytes 159748
  550.8 11.2 %copy-start.9 = (f32[13,8,128]{2,1,0:T(8,128)S(1)}, f32[13,8,128]{2,1,0:T(8,128)}, u32[]{:S(2)}) copy-start(f32[13,8,128]{2,1,0:T(8,128)} %get-tuple-element.184) | copy-start | bytes 159748
  557.2 46.6 %collective-permute-start.28 = (bf16[2,512,256]{2,1,0:T(8,128)(2,1)}, bf16[2,512,256]{2,1,0:T(8,128)(2,1)S(1)}, u32[]{:S(2)}, u32[]{:S(2)}) collective-permute-start(bf16[2,512,256]{2,1,0:T(8,128)(2,1)} %get-tuple-element.191), channel_id=1, source_target_pairs={{0,8},{4,12},{8,0},{12,4},{16,24},{20,28},{24,16},{28,20},{1,9},{5... | collective-permute-start | bytes 1572872 | tf_op jit(solution)/shard_map/ppermute | solution.py:1168
  559.2 44.6 %collective-permute-start.27 = (bf16[2,256,768]{2,1,0:T(8,128)(2,1)S(1)}, bf16[2,256,768]{2,1,0:T(8,128)(2,1)S(1)}, u32[]{:S(2)}, u32[]{:S(2)}) collective-permute-start(bf16[2,256,768]{2,1,0:T(8,128)(2,1)S(1)} %copy-done.23), channel_id=1, source_target_pairs={{0,8},{4,12},{8,0},{12,4},{16,24},{20,28},{24,16},{28,20},{1,9},{5... | collective-permute-start | bytes 2359304 | tf_op jit(solution)/shard_map/ppermute | solution.py:1168
  573.0 39.2 %copy-start.24 = (bf16[1,256,768]{2,1,0:T(8,128)(2,1)S(1)}, bf16[1,256,768]{2,1,0:T(8,128)(2,1)}, u32[]{:S(2)}) copy-start(bf16[1,256,768]{2,1,0:T(8,128)(2,1)} %get-tuple-element.194) | copy-start | bytes 1179652
  609.3 32.8 %collective-permute-start.29 = (bf16[1,512,256]{2,1,0:T(8,128)(2,1)}, bf16[1,512,256]{2,1,0:T(8,128)(2,1)S(1)}, u32[]{:S(2)}, u32[]{:S(2)}) collective-permute-start(bf16[1,512,256]{2,1,0:T(8,128)(2,1)} %get-tuple-element.193), channel_id=1, source_target_pairs={{0,16},{4,20},{8,24},{12,28},{16,0},{20,4},{24,8},{28,12},{1,17},{... | collective-permute-start | bytes 786440 | tf_op jit(solution)/shard_map/ppermute | solution.py:1168
  610.3 40.1 %collective-permute-start.31 = (bf16[1,256,768]{2,1,0:T(8,128)(2,1)}, bf16[1,256,768]{2,1,0:T(8,128)(2,1)S(1)}, u32[]{:S(2)}, u32[]{:S(2)}) collective-permute-start(bf16[1,256,768]{2,1,0:T(8,128)(2,1)} %get-tuple-element.196), channel_id=1, source_target_pairs={{0,16},{4,20},{8,24},{12,28},{16,0},{20,4},{24,8},{28,12},{1,17},{... | collective-permute-start | bytes 1179656 | tf_op jit(solution)/shard_map/ppermute | solution.py:1168
  612.2 45.8 %collective-permute-start.30 = (bf16[1,256,768]{2,1,0:T(8,128)(2,1)S(1)}, bf16[1,256,768]{2,1,0:T(8,128)(2,1)S(1)}, u32[]{:S(2)}, u32[]{:S(2)}) collective-permute-start(bf16[1,256,768]{2,1,0:T(8,128)(2,1)S(1)} %copy-done.24), channel_id=1, source_target_pairs={{0,16},{4,20},{8,24},{12,28},{16,0},{20,4},{24,8},{28,12},{1,17},{... | collective-permute-start | bytes 1179656 | tf_op jit(solution)/shard_map/ppermute | solution.py:1168
  642.0 16.0 %copy-start.5 = (bf16[1,512,256]{2,1,0:T(8,128)(2,1)}, bf16[1,512,256]{2,1,0:T(8,128)(2,1)S(1)}, u32[]{:S(2)}) copy-start(bf16[1,512,256]{2,1,0:T(8,128)(2,1)S(1)} %collective-permute-done.29.refs_4_) | copy-start | bytes 786436
  (11 other events, 57.3 us)
Sparse Core Ops, SparseCore 0:
  35.1 49.6 all-gather.1
  237.1 162.7 reduce-scatter.1

commit v9 on v8

--- a/solution.py
+++ b/solution.py
@@ -1541,6 +1541,9 @@
 
     for r in rows:
         grad_full[r], attended_grad = attended_back(n, pairs, grads[r], out_weight)
+        if r == last and spread:
+            out_sum = Spread(attended, grad_full, 1, (2, 4, 1))
+            out_sum.first()
         qkv_grad[r] = attend_back(starts[r], tables, qkv[r], attended_grad, logs[r])
         if r == last and spread:
             qkv_sum = [
@@ -1556,10 +1559,9 @@
 
     if spread:
         down_sum = gate([down_sum])[0]
+        out_sum.keep_added()
         up_sum.keep_added()
         qkv_sum[1].first()
-        out_sum = Spread(attended, grad_full, 1, (1, 2, 4))
-        out_sum.first()
 
     grad_history, depth_sum, gain1_sum, bias1_sum = None, 0.0, 0.0, 0.0
     for r in rows:
@@ -1585,18 +1587,16 @@
                 parts[1] = row_sums[1] = gate([parts[1]])[0]
             if spread:
                 qkv_sum[0].keep_added()
-                advance(up_sum)
-
-    Order.cost = TINY
+                out_sum.coming = gate([out_sum.coming])[0]
+
     vectors = [up_bias_sum, down_bias_sum, gain2_sum, bias2_sum, gain1_sum, bias1_sum]
     vectors, depth_part = [jnp.sum(v, 0) for v in vectors], jnp.sum(depth_sum, (1, 2))
     if spread:
+        advance(up_sum)
         qkv_sum[1].keep_added()
-        out_sum.keep_added()
-        up_sum.coming = gate([up_sum.coming])[0]
         advance(qkv_sum[0])
+        advance(qkv_sum[1], out_sum)
         totals, depth_grad = sums(vectors, depth_part)
-        advance(qkv_sum[1], out_sum)
     else:
         qkv_sum = [spread_over_dp(weight_grad(normed1, qkv_grad), 0)]
         out_sum = spread_over_dp(weight_grad(attended, grad_full), 1)

time: 676 us -> 670 us (level)
  waiting for transfers between devices: 95.9 us -> 59.4 us
  Pallas kernels: 500 us -> 529 us
    ppermute x12, waiting for transfers between devices: 73.4 us -> 24 us  [send(): lax.ppermute(value, 'dp', [(i, i ^ bit) for i in range(self.groups)])]
    pallas_call x47, Pallas kernels: 500 us -> 529 us  [call(): pl.pallas_call(without_extra, grid_spec=pltpu.PrefetchScalarGridSpec(num_...]
    ppermute x16, waiting for transfers between devices: 18.2 us -> 31.2 us  [over_chip(): return lax.ppermute(value, 'mp', self.chip)]
  transfers between devices with their start and end apart: 34 -> 34, of which waited for: 10 -> 8; matrix products, arithmetic and copies ran while one was open for 4% -> 4% of each run, Pallas kernels for 73% -> 79%
where the time goes in v9:
time: 670 us; the launch traced here: 666 us
  Pallas kernels  529 us (79%)
  waiting for transfers between devices  59.4 us (9%)
  starting transfers between devices  34.9 us (5%)
  local copies, waits for them, and re-layouts  19.8 us (3%)
  between operations  14.7 us (2%)
  other arithmetic  7.54 us (1%)
    pallas_call x47, Pallas kernels, call(): pl.pallas_call(without_extra, grid_spec=pltpu.PrefetchScalarGridSpec(num_...  529 us
    ppermute x16, waiting for transfers between devices, over_chip(): return lax.ppermute(value, 'mp', self.chip)  31.2 us
    ppermute x12, waiting for transfers between devices, send(): lax.ppermute(value, 'dp', [(i, i ^ bit) for i in range(self.groups)])  24 us
    ppermute x16, starting transfers between devices, over_chip(): return lax.ppermute(value, 'mp', self.chip)  19 us
    ppermute x12, starting transfers between devices, send(): lax.ppermute(value, 'dp', [(i, i ^ bit) for i in range(self.groups)])  15 us
  transfers between devices with their start and end apart: 34, of which 8 were waited for; matrix products, arithmetic and copies ran while one was open for 4% of the time, Pallas kernels for 79%

profile of v9, /device:TPU:0, one launch (start us, length us, event | category | flops | bytes accessed | tf_op | source)
XLA Modules:
  0.0 665.7 jit_solution(7946926779568437461)
XLA Ops:
  8.6 3.0 collective-permute-start.2
  13.8 8.0 %average.2 = (f32[1024,512]{1,0:T(8,128)}, bf16[1024,512]{1,0:T(8,128)(2,1)}) custom-call(f32[13]{0:T(128)} %refs_0_.7, bf16[13,2048,512]{2,1,0:T(8,128)(2,1)} %refs_9_.3), custom_call_target="tpu_custom_call" | custom-call | flops 999999995904 | bytes 100000000 | tf_op jit(solution)/shard_map/average/pallas_call | solution.py:60
  21.7 2.0 collective-permute-start
  27.0 7.8 %average.3 = (f32[1024,512]{1,0:T(8,128)}, bf16[1024,512]{1,0:T(8,128)(2,1)}) custom-call(f32[13]{0:T(128)} %refs_0_.7, bf16[13,2048,512]{2,1,0:T(8,128)(2,1)} %refs_9_.3, f32[32,512]{1,0:T(8,128)} %get-tuple-element.109.refs_2_), custom_call_target="tpu_custom_call" | custom-call | flops 999999995904 | bytes 100000000 | tf_op jit(solution)/shard_map/average/pallas_call | solution.py:60
  36.8 10.3 %collective-permute-done.refs_1_.refs_3_.refs_5_ = bf16[1024,512]{1,0:T(8,128)(2,1)} collective-permute-done((bf16[1024,512]{1,0:T(8,128)(2,1)}, bf16[1024,512]{1,0:T(8,128)(2,1)}, u32[]{:S(2)}, u32[]{:S(2)}) %collective-permute-start) | collective-permute-done | bytes 1048608 | tf_op jit(solution)/shard_map/ppermute | solution.py:1351
  48.8 17.9 %project.2 = (bf16[1024,1536]{1,0:T(8,128)(2,1)}, bf16[1024,2048]{1,0:T(8,128)(2,1)}, f32[1024,128]{1,0:T(8,128)}, bf16[1024,512]{1,0:T(8,128)(2,1)}, bf16[1024,512]{1,0:T(8,128)(2,1)}) custom-call(bf16[1024,512]{1,0:T(8,128)(2,1)} %get-tuple-element.107.refs_0_.refs_2_, bf16[1024,512]{1,0:T(8,128)(2,1)} %collective-permute-done.refs_1_.refs_3_.refs_5_, ...), custom_call_target="tpu_custom_call" | custom-call | flops 999999995904 | bytes 100000000 | tf_op jit(solution)/shard_map/project/pallas_call | solution.py:60
  67.4 10.1 %attend.2 = (bf16[1024,512]{1,0:T(8,128)(2,1)}, f32[4,8,1024]{2,1,0:T(8,128)}) custom-call(s32[8,1024]{1,0:T(8,128)} %broadcast_in_dim.21.refs_0_, bf16[1024,1536]{1,0:T(8,128)(2,1)} %get-tuple-element.112.refs_1_.refs_3_, f32[1024,128]{1,0:T(8,128)} %get-tuple-element.113.refs_2_.refs_6_), custom_call_target="tpu_custom_call" | custom-call | flops 999999995904 | bytes 100000000 | tf_op jit(solution)/shard_map/attend/pallas_call | solution.py:60
  77.8 18.0 %project.3 = (bf16[1024,1536]{1,0:T(8,128)(2,1)}, bf16[1024,2048]{1,0:T(8,128)(2,1)}, f32[1024,128]{1,0:T(8,128)}, bf16[1024,512]{1,0:T(8,128)(2,1)}, bf16[1024,512]{1,0:T(8,128)(2,1)}) custom-call(bf16[1024,512]{1,0:T(8,128)(2,1)} %gate.12.refs_9_.refs_0_.refs_2_, bf16[1024,512]{1,0:T(8,128)(2,1)} %collective-permute-done.7.refs_1_.refs_3_.refs_5_, ...), custom_call_target="tpu_custom_call" | custom-call | flops 999999995904 | bytes 100000000 | tf_op jit(solution)/shard_map/project/pallas_call | solution.py:60
  96.5 9.7 %attend.3 = (bf16[1024,512]{1,0:T(8,128)(2,1)}, f32[4,8,1024]{2,1,0:T(8,128)}) custom-call(s32[8,1024]{1,0:T(8,128)} %broadcast_in_dim.24.refs_0_, bf16[1024,1536]{1,0:T(8,128)(2,1)} %get-tuple-element.119.refs_1_.refs_3_, f32[1024,128]{1,0:T(8,128)} %get-tuple-element.120.refs_2_.refs_6_), custom_call_target="tpu_custom_call" | custom-call | flops 999999995904 | bytes 100000000 | tf_op jit(solution)/shard_map/attend/pallas_call | solution.py:60
  108.3 4.1 collective-permute-done.8.refs_10_
  113.1 40.8 %feed.2 = (f32[1024,512]{1,0:T(8,128)}, bf16[1024,2048]{1,0:T(8,128)(2,1)}, f32[1024,128]{1,0:T(8,128)}, bf16[1024,2048]{1,0:T(8,128)(2,1)}, bf16[1024,2048]{1,0...) custom-call(bf16[1024,512]{1,0:T(8,128)(2,1)} %get-tuple-element.114.refs_0_.refs_2_.refs_1_, ...), custom_call_target="tpu_custom_call" | custom-call | flops 999999995904 | bytes 100000000 | tf_op jit(solution)/shard_map/feed/pallas_call | solution.py:60
  156.0 41.2 %feed.3 = (f32[1024,512]{1,0:T(8,128)}, bf16[1024,2048]{1,0:T(8,128)(2,1)}, f32[1024,128]{1,0:T(8,128)}, bf16[1024,2048]{1,0:T(8,128)(2,1)}, bf16[1024,2048]{1,0...) custom-call(bf16[1024,512]{1,0:T(8,128)(2,1)} %get-tuple-element.126.refs_0_.refs_2_, ...), custom_call_target="tpu_custom_call" | custom-call | flops 999999995904 | bytes 100000000 | tf_op jit(solution)/shard_map/feed/pallas_call | solution.py:60
  197.6 5.2 collective-permute-done.11.refs_5_.refs_7_
  202.8 11.2 %join.1 = (bf16[1024,2048]{1,0:T(8,128)(2,1)}, bf16[1024,2048]{1,0:T(8,128)(2,1)}) custom-call(bf16[1024,512]{1,0:T(8,128)(2,1)} %gate.14.refs_17_.refs_0_.refs_2_, bf16[1024,512]{1,0:T(8,128)(2,1)} %collective-permute-done.10.refs_1_.refs_3_, bf16[1024,512]{1,0:T(8,128)(2,1)} %gate.14.refs_17_.refs_0_.refs_2_, ...), custom_call_target="tpu_custom_call" | custom-call | flops 999999995904 | bytes 100000000 | tf_op jit(solution)/shard_map/join/pallas_call | solution.py:60
  214.0 23.1 %weight_grad.1.refs_7_ = bf16[2048,2048]{1,0:T(8,128)(2,1)} custom-call(bf16[1024,2048]{1,0:T(8,128)(2,1)} %get-tuple-element.136.refs_0_, bf16[1024,2048]{1,0:T(8,128)(2,1)} %get-tuple-element.137.refs_1_, bf16[1024,2048]{1,0:T(8,128)(2,1)} %get-tuple-element.130.refs_1_.refs_2_.refs_0_, bf16[1024,2048]{1,0:T(8,128)(2,1)} %get-tuple-element.138.refs_3_.refs_0_, ...), custom_call_target="tpu_custom_call" | custom-call | flops 999999995904 | bytes 100000000 | tf_op jit(solution)/shard_map/weight_grad/pallas_call | solution.py:60
  237.1 31.0 %feed_back.2 = (bf16[1024,2048]{1,0:T(8,128)(2,1)}, f32[8,2048]{1,0:T(8,128)}, f32[8,512]{1,0:T(8,128)}, bf16[1024,512]{1,0:T(8,128)(2,1)}, bf16[1040,512]{1,0:T(8,128)(2,1)}, /*index=5*/f32[8,1024]{1,0:T(8,128)}) custom-call(bf16[1024,2048]{1,0:T(8,128)(2,1)} %get-tuple-element.130.refs_1_.refs_2_.refs_0_, bf16[1024,2048]{1,0:T(8,128)(2,1)} %get-tuple-element.134.refs_1_, ...), custom_call_target="tpu_custom_call" | custom-call | flops 999999995904 | bytes 100000000 | tf_op jit(solution)/shard_map/feed_back/pallas_call | solution.py:60
  268.3 31.1 %feed_back.3 = (bf16[1024,2048]{1,0:T(8,128)(2,1)}, f32[8,2048]{1,0:T(8,128)}, f32[8,512]{1,0:T(8,128)}, bf16[1024,512]{1,0:T(8,128)(2,1)}, bf16[1040,512]{1,0:T(8,128)(2,1)}, /*index=5*/f32[8,1024]{1,0:T(8,128)}) custom-call(bf16[1024,2048]{1,0:T(8,128)(2,1)} %get-tuple-element.138.refs_3_.refs_0_, bf16[1024,2048]{1,0:T(8,128)(2,1)} %get-tuple-element.142.refs_1_, ...), custom_call_target="tpu_custom_call" | custom-call | flops 999999995904 | bytes 100000000 | tf_op jit(solution)/shard_map/feed_back/pallas_call | solution.py:60
  305.4 5.9 hidden_back.2
  311.5 14.7 %weight_blocks.8.refs_7_ = bf16[4,256,2048]{2,1,0:T(8,128)(2,1)} custom-call(s32[1]{0:T(128)} %bitcast.7.refs_0_, bf16[1024,2048]{1,0:T(8,128)(2,1)} %get-tuple-element.135.refs_2_.refs_1_.refs_3_.refs_5_.refs_7_, bf16[1024,2048]{1,0:T(8,128)(2,1)} %get-tuple-element.140.refs_2_.refs_4_.refs_6_.refs_8_, ...), custom_call_target="tpu_custom_call" | custom-call | flops 999999995904 | bytes 100000000 | tf_op jit(solution)/shard_map/weight_blocks/pallas_call | solution.py:60
  328.2 6.7 %output.1.refs_8_ = bf16[2048,512]{1,0:T(8,128)(2,1)} custom-call(f32[1024,512]{1,0:T(8,128)} %get-tuple-element.122.refs_5_.refs_0_, bf16[1024,512]{1,0:T(8,128)(2,1)} %get-tuple-element.123.refs_1_, bf16[1024,512]{1,0:T(8,128)(2,1)} %gate.16.refs_4_.refs_2_, f32[1024,512]{1,0:T(8,128)} %get-tuple-element.131.refs_3_.refs_5_, ...), custom_call_target="tpu_custom_call" | custom-call | flops 999999995904 | bytes 100000000 | tf_op jit(solution)/shard_map/output/pallas_call | solution.py:60
  334.9 5.9 hidden_back.3
  345.9 2.7 collective-permute-done.17.refs_1_.refs_3_
  348.6 9.0 %attended_back.2 = (bf16[1024,2048]{1,0:T(8,128)(2,1)}, bf16[1024,512]{1,0:T(8,128)(2,1)}) custom-call(bf16[1024,512]{1,0:T(8,128)(2,1)} %get-tuple-element.153.refs_0_.refs_2_, bf16[1024,512]{1,0:T(8,128)(2,1)} %collective-permute-done.17.refs_1_.refs_3_, bf16[1024,512]{1,0:T(8,128)(2,1)} %get-tuple-element.153.refs_0_.refs_2_, ...), custom_call_target="tpu_custom_call" | custom-call | flops 999999995904 | bytes 100000000 | tf_op jit(solution)/shard_map/attended_back/pallas_call | solution.py:60
  357.6 12.4 %attend_back.2.refs_0_.refs_9_ = bf16[1024,1536]{1,0:T(8,128)(2,1)} custom-call(s32[8,1024]{1,0:T(8,128)} %broadcast_in_dim.21.refs_0_, f32[1024,128]{1,0:T(8,128)} %constant.19.clone.refs_6_.refs_1_, f32[1024,128]{1,0:T(8,128)} %constant.20.clone.refs_7_.refs_2_, bf16[1024,1536]{1,0:T(8,128)(2,1)} %get-tuple-element.112.refs_1_.refs_3_, ...), custom_call_target="tpu_custom_call" | custom-call | flops 999999995904 | bytes 100000000 | tf_op jit(solution)/shard_map/attend_back/pallas_call | solution.py:60
  370.0 15.6 %project_back.2 = (bf16[1024,512]{1,0:T(8,128)(2,1)}, bf16[1040,512]{1,0:T(8,128)(2,1)}, f32[8,1024]{1,0:T(8,128)}) custom-call(bf16[1024,1536]{1,0:T(8,128)(2,1)} %attend_back.2.refs_0_.refs_9_, bf16[1024,2048]{1,0:T(8,128)(2,1)} %get-tuple-element.156.refs_1_.refs_3_.refs_5_.refs_7_, f32[8,2048]{1,0:T(8,128)} %get-tuple-element.206.refs_4_.refs_2_, ...), custom_call_target="tpu_custom_call" | custom-call | flops 999999995904 | bytes 100000000 | tf_op jit(solution)/shard_map/project_back/pallas_call | solution.py:60
  385.6 9.1 %attended_back.3 = (bf16[1024,2048]{1,0:T(8,128)(2,1)}, bf16[1024,512]{1,0:T(8,128)(2,1)}) custom-call(bf16[1024,512]{1,0:T(8,128)(2,1)} %get-tuple-element.152.refs_0_.refs_2_, bf16[1024,512]{1,0:T(8,128)(2,1)} %collective-permute-done.16.refs_1_.refs_3_, bf16[1024,512]{1,0:T(8,128)(2,1)} %get-tuple-element.152.refs_0_.refs_2_, ...), custom_call_target="tpu_custom_call" | custom-call | flops 999999995904 | bytes 100000000 | tf_op jit(solution)/shard_map/attended_back/pallas_call | solution.py:60
  394.8 6.2 weight_blocks.9.refs_6_
  401.0 12.6 %attend_back.3.refs_10_.refs_0_ = bf16[1024,1536]{1,0:T(8,128)(2,1)} custom-call(s32[8,1024]{1,0:T(8,128)} %broadcast_in_dim.24.refs_0_, f32[1024,128]{1,0:T(8,128)} %constant.19.clone.refs_6_.refs_1_, f32[1024,128]{1,0:T(8,128)} %constant.20.clone.refs_7_.refs_2_, bf16[1024,1536]{1,0:T(8,128)(2,1)} %get-tuple-element.119.refs_1_.refs_3_, ...), custom_call_target="tpu_custom_call" | custom-call | flops 999999995904 | bytes 100000000 | tf_op jit(solution)/shard_map/attend_back/pallas_call | solution.py:60
  416.9 9.6 %weight_blocks.10.refs_1_ = bf16[4,256,768]{2,1,0:T(8,128)(2,1)} custom-call(s32[1]{0:T(128)} %bitcast.7.refs_0_, bf16[1024,2048]{1,0:T(8,128)(2,1)} %get-tuple-element.156.refs_1_.refs_3_.refs_5_.refs_7_, bf16[1024,2048]{1,0:T(8,128)(2,1)} %get-tuple-element.161.refs_2_.refs_4_.refs_6_.refs_8_.refs_1_, ...), custom_call_target="tpu_custom_call" | custom-call | flops 999999995904 | bytes 100000000 | tf_op jit(solution)/shard_map/weight_blocks/pallas_call | solution.py:60
  428.0 13.0 %collective-permute-done.18.refs_0_ = bf16[1040,512]{1,0:T(8,128)(2,1)} collective-permute-done((bf16[1040,512]{1,0:T(8,128)(2,1)}, bf16[1040,512]{1,0:T(8,128)(2,1)}, u32[]{:S(2)}, u32[]{:S(2)}) %collective-permute-start.18) | collective-permute-done | bytes 1064992 | tf_op jit(solution)/shard_map/ppermute | solution.py:1351
  441.0 15.6 %project_back.3 = (bf16[1024,512]{1,0:T(8,128)(2,1)}, bf16[1040,512]{1,0:T(8,128)(2,1)}, f32[8,1024]{1,0:T(8,128)}) custom-call(bf16[1024,1536]{1,0:T(8,128)(2,1)} %attend_back.3.refs_10_.refs_0_, bf16[1024,2048]{1,0:T(8,128)(2,1)} %get-tuple-element.161.refs_2_.refs_4_.refs_6_.refs_8_.refs_1_, f32[8,2048]{1,0:T(8,128)} %get-tuple-element.206.refs_4_.refs_2_, ...), custom_call_target="tpu_custom_call" | custom-call | flops 999999995904 | bytes 100000000 | tf_op jit(solution)/shard_map/project_back/pallas_call | solution.py:60
  458.4 6.4 weight_blocks.11
  464.8 2.7 collective-permute-start.22
  467.5 15.3 %weight_blocks.12 = (bf16[2,256,2048]{2,1,0:T(8,128)(2,1)}, bf16[2,256,2048]{2,1,0:T(8,128)(2,1)}) custom-call(s32[1]{0:T(128)} %bitcast.7.refs_0_, bf16[1024,2048]{1,0:T(8,128)(2,1)} %get-tuple-element.135.refs_2_.refs_1_.refs_3_.refs_5_.refs_7_, bf16[1024,2048]{1,0:T(8,128)(2,1)} %get-tuple-element.140.refs_2_.refs_4_.refs_6_.refs_8_, ...), custom_call_target="tpu_custom_call" | custom-call | flops 999999995904 | bytes 100000000 | tf_op jit(solution)/shard_map/weight_blocks/pallas_call | solution.py:60
  482.8 9.7 %weight_blocks.13.refs_10_ = bf16[4,256,768]{2,1,0:T(8,128)(2,1)} custom-call(s32[1]{0:T(128)} %bitcast.7.refs_0_, bf16[1024,2048]{1,0:T(8,128)(2,1)} %get-tuple-element.156.refs_1_.refs_3_.refs_5_.refs_7_, bf16[1024,2048]{1,0:T(8,128)(2,1)} %get-tuple-element.161.refs_2_.refs_4_.refs_6_.refs_8_.refs_1_, ...), custom_call_target="tpu_custom_call" | custom-call | flops 999999995904 | bytes 100000000 | tf_op jit(solution)/shard_map/weight_blocks/pallas_call | solution.py:60
  495.0 14.4 %average_back.2 = (bf16[13,2048,512]{2,1,0:T(8,128)(2,1)}, f32[13,8,128]{2,1,0:T(8,128)}, f32[8,512]{1,0:T(8,128)}, f32[8,512]{1,0:T(8,128)}) custom-call(f32[13]{0:T(128)} %refs_0_.7, bf16[1024,512]{1,0:T(8,128)(2,1)} %get-tuple-element.165.refs_1_, bf16[1040,512]{1,0:T(8,128)(2,1)} %gate.18.refs_5_.refs_2_.refs_4_, ...), custom_call_target="tpu_custom_call" | custom-call | flops 999999995904 | bytes 100000000 | tf_op jit(solution)/shard_map/average_back/pallas_call | solution.py:60
  509.5 10.0 %weight_blocks.14 = (bf16[2,256,768]{2,1,0:T(8,128)(2,1)}, bf16[2,256,768]{2,1,0:T(8,128)(2,1)}) custom-call(s32[1]{0:T(128)} %bitcast.7.refs_0_, bf16[1024,2048]{1,0:T(8,128)(2,1)} %get-tuple-element.156.refs_1_.refs_3_.refs_5_.refs_7_, bf16[1024,2048]{1,0:T(8,128)(2,1)} %get-tuple-element.161.refs_2_.refs_4_.refs_6_.refs_8_.refs_1_, ...), custom_call_target="tpu_custom_call" | custom-call | flops 999999995904 | bytes 100000000 | tf_op jit(solution)/shard_map/weight_blocks/pallas_call | solution.py:60
  521.2 14.7 %average_back.3 = (bf16[13,2048,512]{2,1,0:T(8,128)(2,1)}, f32[13,8,128]{2,1,0:T(8,128)}, f32[8,512]{1,0:T(8,128)}, f32[8,512]{1,0:T(8,128)}) custom-call(f32[13]{0:T(128)} %refs_0_.7, bf16[1024,512]{1,0:T(8,128)(2,1)} %get-tuple-element.163.refs_1_, bf16[1040,512]{1,0:T(8,128)(2,1)} %gate.20.refs_12_.refs_2_.refs_4_, ...), custom_call_target="tpu_custom_call", output_to_operand_aliasing={{0}: (10, {})} | custom-call | flops 999999995904 | bytes 100000000 | tf_op jit(solution)/shard_map/average_back/pallas_call | solution.py:60
  540.9 2.0 collective-permute-done.25.refs_1_
  542.9 4.2 fold.3
  547.1 10.0 %weight_blocks.15 = (bf16[2,256,768]{2,1,0:T(8,128)(2,1)}, bf16[2,256,768]{2,1,0:T(8,128)(2,1)}) custom-call(s32[1]{0:T(128)} %bitcast.7.refs_0_, bf16[1024,2048]{1,0:T(8,128)(2,1)} %get-tuple-element.156.refs_1_.refs_3_.refs_5_.refs_7_, bf16[1024,2048]{1,0:T(8,128)(2,1)} %get-tuple-element.161.refs_2_.refs_4_.refs_6_.refs_8_.refs_1_, ...), custom_call_target="tpu_custom_call" | custom-call | flops 999999995904 | bytes 100000000 | tf_op jit(solution)/shard_map/weight_blocks/pallas_call | solution.py:60
  557.5 1.9 collective-permute-done.27.refs_1_
  559.4 3.5 fold.4
  563.0 2.8 collective-permute-start.28
  565.8 20.0 %collective-permute-done.26.refs_1_ = bf16[2,256,768]{2,1,0:T(8,128)(2,1)} collective-permute-done((bf16[2,256,768]{2,1,0:T(8,128)(2,1)}, bf16[2,256,768]{2,1,0:T(8,128)(2,1)}, u32[]{:S(2)}, u32[]{:S(2)}) %collective-permute-start.26) | collective-permute-done | bytes 786464 | tf_op jit(solution)/shard_map/ppermute | solution.py:1168
  585.8 3.8 fold.5
  590.7 58.5 %sums.1.refs_9_ = f32[48,128]{1,0:T(8,128)} custom-call(f32[48,128]{1,0:T(8,128)} %select_maximum_fusion.refs_0_, bf16[1,512,256]{2,1,0:T(8,128)(2,1)} %get-tuple-element.191.refs_1_.refs_3_), custom_call_target="tpu_custom_call" | custom-call | flops 999999995904 | bytes 100000000 | tf_op jit(solution)/shard_map/sums/pallas_call | solution.py:60
  653.1 5.5 finish.1
  (129 shorter events, 51.8 us)
Async XLA Ops:
  7.2 100.8 %all-gather.2.cloned.1.call-start = ((), (), s32[]{:S(2)}) async-start(), calls=%async_computation.1 | async-start | bytes 2359296 | tf_op jit(solution)/shard_map/all_gather | solution.py:1392
  8.6 18.4 %collective-permute-start.2 = (f32[32,512]{1,0:T(8,128)}, f32[32,512]{1,0:T(8,128)}, u32[]{:S(2)}, u32[]{:S(2)}) collective-permute-start(f32[32,512]{1,0:T(8,128)} %broadcast_bitcast_fusion), channel_id=1, source_target_pairs={{0,2},{1,3},{2,0},{3,1},{4,6},{5,7},{6,4},{7,5},{8,10},{9,11},{10,... | collective-permute-start | bytes 196616 | tf_op jit(solution)/shard_map/ppermute | solution.py:1351
  11.6 23.6 %collective-permute-start.1 = (f32[32,512]{1,0:T(8,128)}, f32[32,512]{1,0:T(8,128)}, u32[]{:S(2)}, u32[]{:S(2)}) collective-permute-start(f32[32,512]{1,0:T(8,128)} %broadcast_bitcast_fusion), channel_id=1, source_target_pairs={{0,1},{1,0},{2,3},{3,2},{4,5},{5,4},{6,7},{7,6},{8,9},{9,8},{10,11... | collective-permute-start | bytes 196616 | tf_op jit(solution)/shard_map/ppermute | solution.py:1348
  11.6 96.8 %collective-permute-start.6 = (bf16[512,2048]{1,0:T(8,128)(2,1)}, bf16[512,2048]{1,0:T(8,128)(2,1)}, u32[]{:S(2)}, u32[]{:S(2)}) collective-permute-start(bf16[512,2048]{1,0:T(8,128)(2,1)} %refs_4_.10), channel_id=1, source_target_pairs={{0,1},{1,0},{2,3},{3,2},{4,5},{5,4},{6,7},{7,6},{8,9},{9,8},{10,11... | collective-permute-start | bytes 6291464 | tf_op jit(solution)/shard_map/ppermute | solution.py:1348
  13.7 13.2 %collective-permute-start.3 = (bf16[64,2048]{1,0:T(8,128)(2,1)}, bf16[64,2048]{1,0:T(8,128)(2,1)}, u32[]{:S(2)}, u32[]{:S(2)}) collective-permute-start(bf16[64,2048]{1,0:T(8,128)(2,1)} %constant_dynamic-slice_fusion), channel_id=1, source_target_pairs={{0,2},{1,3},{2,0},{3,1},{4,6},{5,7},{6,4},{7,5},{8,10},{9,11},{10,... | collective-permute-start | bytes 786440 | tf_op jit(solution)/shard_map/ppermute | solution.py:1351
  13.7 10.0 %copy-start = (bf16[2048,512]{1,0:T(8,128)(2,1)S(1)}, bf16[2048,512]{1,0:T(8,128)(2,1)}, u32[]{:S(2)}) copy-start(bf16[2048,512]{1,0:T(8,128)(2,1)} %refs_4_.7) | copy-start | bytes 6291460
  21.7 25.4 %collective-permute-start = (bf16[1024,512]{1,0:T(8,128)(2,1)}, bf16[1024,512]{1,0:T(8,128)(2,1)}, u32[]{:S(2)}, u32[]{:S(2)}) collective-permute-start(bf16[1024,512]{1,0:T(8,128)(2,1)} %get-tuple-element.107.refs_0_.refs_2_), channel_id=1, source_target_pairs={{0,2},{1,3},{2,0},{3,1},{4,6},{5,7},{6,4},{7,5},{8,10},{9,11},{10,... | collective-permute-start | bytes 3145736 | tf_op jit(solution)/shard_map/ppermute | solution.py:1351
  27.0 8.2 %collective-permute-start.4 = (f32[32,512]{1,0:T(8,128)}, f32[32,512]{1,0:T(8,128)}, u32[]{:S(2)}, u32[]{:S(2)}) collective-permute-start(f32[32,512]{1,0:T(8,128)} %get-tuple-element.109.refs_2_), channel_id=1, source_target_pairs={{0,1},{1,0},{2,3},{3,2},{4,5},{5,4},{6,7},{7,6},{8,9},{9,8},{10,11... | collective-permute-start | bytes 196616 | tf_op jit(solution)/shard_map/ppermute | solution.py:1348
  34.9 423.5 %reduce-scatter.2.cloned.1.call-start = ((), (), s32[]{:S(2)}) async-start(), calls=%async_computation.2 | async-start | bytes 9437184 | tf_op jit(solution)/shard_map/reduce_scatter | solution.py:1505
  47.1 30.7 %collective-permute-start.7 = (bf16[1024,512]{1,0:T(8,128)(2,1)}, bf16[1024,512]{1,0:T(8,128)(2,1)}, u32[]{:S(2)}, u32[]{:S(2)}) collective-permute-start(bf16[1024,512]{1,0:T(8,128)(2,1)} %gate.12.refs_9_.refs_0_.refs_2_), channel_id=1, source_target_pairs={{0,2},{1,3},{2,0},{3,1},{4,6},{5,7},{6,4},{7,5},{8,10},{9,11},{10,... | collective-permute-start | bytes 3145736 | tf_op jit(solution)/shard_map/ppermute | solution.py:1351
  48.8 18.0 %copy-start.10 = (s32[1,1024]{1,0:T(1,128)S(1)}, s32[1,1024]{1,0:T(1,128)}, u32[]{:S(2)}) copy-start(s32[1,1024]{1,0:T(1,128)} %get-tuple-element.213) | copy-start | bytes 12292
  77.5 30.8 %collective-permute-start.5 = (bf16[1024,512]{1,0:T(8,128)(2,1)}, bf16[1024,512]{1,0:T(8,128)(2,1)}, u32[]{:S(2)}, u32[]{:S(2)}) collective-permute-start(bf16[1024,512]{1,0:T(8,128)(2,1)} %get-tuple-element.114.refs_0_.refs_2_.refs_1_), channel_id=1, source_target_pairs={{0,2},{1,3},{2,0},{3,1},{4,6},{5,7},{6,4},{7,5},{8,10},{9,11},{10,... | collective-permute-start | bytes 3145736 | tf_op jit(solution)/shard_map/ppermute | solution.py:1351
  77.8 18.0 %copy-start.9 = (s32[1,1024]{1,0:T(1,128)S(1)}, s32[1,1024]{1,0:T(1,128)}, u32[]{:S(2)}) copy-start(s32[1,1024]{1,0:T(1,128)} %get-tuple-element.212) | copy-start | bytes 12292
  106.2 49.8 %collective-permute-start.12 = (bf16[1024,512]{1,0:T(8,128)(2,1)}, bf16[1024,512]{1,0:T(8,128)(2,1)}, u32[]{:S(2)}, u32[]{:S(2)}) collective-permute-start(bf16[1024,512]{1,0:T(8,128)(2,1)} %get-tuple-element.126.refs_0_.refs_2_), channel_id=1, source_target_pairs={{0,2},{1,3},{2,0},{3,1},{4,6},{5,7},{6,4},{7,5},{8,10},{9,11},{10,... | collective-permute-start | bytes 3145736 | tf_op jit(solution)/shard_map/ppermute | solution.py:1351
  108.0 4.5 collective-permute-start.8
  108.0 4.5 copy-start.11
  108.0 89.6 %collective-permute-start.10 = (bf16[1024,512]{1,0:T(8,128)(2,1)}, bf16[1024,512]{1,0:T(8,128)(2,1)}, u32[]{:S(2)}, u32[]{:S(2)}) collective-permute-start(bf16[1024,512]{1,0:T(8,128)(2,1)} %gate.14.refs_17_.refs_0_.refs_2_), channel_id=1, source_target_pairs={{0,2},{1,3},{2,0},{3,1},{4,6},{5,7},{6,4},{7,5},{8,10},{9,11},{10,... | collective-permute-start | bytes 3145736 | tf_op jit(solution)/shard_map/ppermute | solution.py:1351
  153.9 60.1 %collective-permute-start.9 = (bf16[1024,512]{1,0:T(8,128)(2,1)}, bf16[1024,512]{1,0:T(8,128)(2,1)}, u32[]{:S(2)}, u32[]{:S(2)}) collective-permute-start(bf16[1024,512]{1,0:T(8,128)(2,1)} %get-tuple-element.124), channel_id=1, source_target_pairs={{0,2},{1,3},{2,0},{3,1},{4,6},{5,7},{6,4},{7,5},{8,10},{9,11},{10,... | collective-permute-start | bytes 3145736 | tf_op jit(solution)/shard_map/ppermute | solution.py:1351
  154.3 48.5 %collective-permute-start.11 = (bf16[1024,512]{1,0:T(8,128)(2,1)}, bf16[1024,512]{1,0:T(8,128)(2,1)}, u32[]{:S(2)}, u32[]{:S(2)}) collective-permute-start(bf16[1024,512]{1,0:T(8,128)(2,1)} %gate.15.refs_17_.refs_4_.refs_6_), channel_id=1, source_target_pairs={{0,2},{1,3},{2,0},{3,1},{4,6},{5,7},{6,4},{7,5},{8,10},{9,11},{10,... | collective-permute-start | bytes 3145736 | tf_op jit(solution)/shard_map/ppermute | solution.py:1351
  197.2 71.0 %collective-permute-start.13 = (bf16[1024,512]{1,0:T(8,128)(2,1)}, bf16[1024,512]{1,0:T(8,128)(2,1)}, u32[]{:S(2)}, u32[]{:S(2)}) collective-permute-start(bf16[1024,512]{1,0:T(8,128)(2,1)} %get-tuple-element.133), channel_id=1, source_target_pairs={{0,2},{1,3},{2,0},{3,1},{4,6},{5,7},{6,4},{7,5},{8,10},{9,11},{10,... | collective-permute-start | bytes 3145736 | tf_op jit(solution)/shard_map/ppermute | solution.py:1351
  268.1 36.7 %collective-permute-start.14 = (bf16[1040,512]{1,0:T(8,128)(2,1)}, bf16[1040,512]{1,0:T(8,128)(2,1)}, u32[]{:S(2)}, u32[]{:S(2)}) collective-permute-start(bf16[1040,512]{1,0:T(8,128)(2,1)} %get-tuple-element.145), channel_id=1, source_target_pairs={{0,2},{1,3},{2,0},{3,1},{4,6},{5,7},{6,4},{7,5},{8,10},{9,11},{10,... | collective-permute-start | bytes 3194888 | tf_op jit(solution)/shard_map/ppermute | solution.py:1351
  268.2 33.1 %copy-start.1 = (f32[8,2048]{1,0:T(8,128)S(1)}, f32[8,2048]{1,0:T(8,128)}, u32[]{:S(2)}) copy-start(f32[8,2048]{1,0:T(8,128)} %get-tuple-element.176) | copy-start | bytes 196612
  268.3 34.5 %copy-start.8 = (f32[8,512]{1,0:T(8,128)S(1)}, f32[8,512]{1,0:T(8,128)}, u32[]{:S(2)}) copy-start(f32[8,512]{1,0:T(8,128)} %get-tuple-element.139.refs_1_) | copy-start | bytes 49156
  268.3 36.5 %copy-start.12 = (f32[512]{0:T(512)S(1)}, f32[512]{0:T(512)}, u32[]{:S(2)}) copy-start(f32[512]{0:T(512)} %param.23) | copy-start | bytes 6148
  299.4 35.4 %collective-permute-start.15 = (bf16[1040,512]{1,0:T(8,128)(2,1)}, bf16[1040,512]{1,0:T(8,128)(2,1)}, u32[]{:S(2)}, u32[]{:S(2)}) collective-permute-start(bf16[1040,512]{1,0:T(8,128)(2,1)} %get-tuple-element.150), channel_id=1, source_target_pairs={{0,2},{1,3},{2,0},{3,1},{4,6},{5,7},{6,4},{7,5},{8,10},{9,11},{10,... | collective-permute-start | bytes 3194888 | tf_op jit(solution)/shard_map/ppermute | solution.py:1351
  311.3 37.3 %collective-permute-start.17 = (bf16[1024,512]{1,0:T(8,128)(2,1)}, bf16[1024,512]{1,0:T(8,128)(2,1)}, u32[]{:S(2)}, u32[]{:S(2)}) collective-permute-start(bf16[1024,512]{1,0:T(8,128)(2,1)} %get-tuple-element.153.refs_0_.refs_2_), channel_id=1, source_target_pairs={{0,2},{1,3},{2,0},{3,1},{4,6},{5,7},{6,4},{7,5},{8,10},{9,11},{10,... | collective-permute-start | bytes 3145736 | tf_op jit(solution)/shard_map/ppermute | solution.py:1351
  311.5 16.1 %copy-start.14 = (f32[512]{0:T(512)S(1)}, f32[512]{0:T(512)}, u32[]{:S(2)}) copy-start(f32[512]{0:T(512)} %param.28) | copy-start | bytes 6148
  326.3 141.2 %collective-permute-start.20 = (bf16[4,256,2048]{2,1,0:T(8,128)(2,1)}, bf16[4,256,2048]{2,1,0:T(8,128)(2,1)}, u32[]{:S(2)}, u32[]{:S(2)}) collective-permute-start(bf16[4,256,2048]{2,1,0:T(8,128)(2,1)} %weight_blocks.8.refs_7_), channel_id=1, source_target_pairs={{0,4},{4,0},{8,12},{12,8},{16,20},{20,16},{24,28},{28,24},{1,5},{5... | collective-permute-start | bytes 12582920 | tf_op jit(solution)/shard_map/ppermute | solution.py:1168
  334.8 7.7 %copy-start.4 = (f32[8,512]{1,0:T(8,128)S(1)}, f32[8,512]{1,0:T(8,128)}, u32[]{:S(2)}) copy-start(f32[8,512]{1,0:T(8,128)} %get-tuple-element.148.refs_11_) | copy-start | bytes 49156
  334.8 7.7 %copy-start.5 = (f32[8,512]{1,0:T(8,128)S(1)}, f32[8,512]{1,0:T(8,128)}, u32[]{:S(2)}) copy-start(f32[8,512]{1,0:T(8,128)} %get-tuple-element.178) | copy-start | bytes 49156
  340.7 44.9 %collective-permute-start.16 = (bf16[1024,512]{1,0:T(8,128)(2,1)}, bf16[1024,512]{1,0:T(8,128)(2,1)}, u32[]{:S(2)}, u32[]{:S(2)}) collective-permute-start(bf16[1024,512]{1,0:T(8,128)(2,1)} %get-tuple-element.152.refs_0_.refs_2_), channel_id=1, source_target_pairs={{0,2},{1,3},{2,0},{3,1},{4,6},{5,7},{6,4},{7,5},{8,10},{9,11},{10,... | collective-permute-start | bytes 3145736 | tf_op jit(solution)/shard_map/ppermute | solution.py:1351
  413.6 44.9 %collective-permute-start.21 = (bf16[4,512,256]{2,1,0:T(8,128)(2,1)}, bf16[4,512,256]{2,1,0:T(8,128)(2,1)}, u32[]{:S(2)}, u32[]{:S(2)}) collective-permute-start(bf16[4,512,256]{2,1,0:T(8,128)(2,1)} %weight_blocks.9.refs_6_), channel_id=1, source_target_pairs={{0,8},{4,12},{8,0},{12,4},{16,24},{20,28},{24,16},{28,20},{1,9},{5... | collective-permute-start | bytes 3145736 | tf_op jit(solution)/shard_map/ppermute | solution.py:1168
  415.2 25.8 %collective-permute-start.18 = (bf16[1040,512]{1,0:T(8,128)(2,1)}, bf16[1040,512]{1,0:T(8,128)(2,1)}, u32[]{:S(2)}, u32[]{:S(2)}) collective-permute-start(bf16[1040,512]{1,0:T(8,128)(2,1)} %get-tuple-element.162), channel_id=1, source_target_pairs={{0,2},{1,3},{2,0},{3,1},{4,6},{5,7},{6,4},{7,5},{8,10},{9,11},{10,... | collective-permute-start | bytes 3194888 | tf_op jit(solution)/shard_map/ppermute | solution.py:1351
  426.5 83.0 %collective-permute-start.23 = (bf16[4,256,768]{2,1,0:T(8,128)(2,1)}, bf16[4,256,768]{2,1,0:T(8,128)(2,1)}, u32[]{:S(2)}, u32[]{:S(2)}) collective-permute-start(bf16[4,256,768]{2,1,0:T(8,128)(2,1)} %weight_blocks.10.refs_1_), channel_id=1, source_target_pairs={{0,4},{4,0},{8,12},{12,8},{16,20},{20,16},{24,28},{28,24},{1,5},{5... | collective-permute-start | bytes 4718600 | tf_op jit(solution)/shard_map/ppermute | solution.py:1168
  456.6 52.9 %collective-permute-start.19 = (bf16[1040,512]{1,0:T(8,128)(2,1)}, bf16[1040,512]{1,0:T(8,128)(2,1)}, u32[]{:S(2)}, u32[]{:S(2)}) collective-permute-start(bf16[1040,512]{1,0:T(8,128)(2,1)} %get-tuple-element.164), channel_id=1, source_target_pairs={{0,2},{1,3},{2,0},{3,1},{4,6},{5,7},{6,4},{7,5},{8,10},{9,11},{10,... | collective-permute-start | bytes 3194888 | tf_op jit(solution)/shard_map/ppermute | solution.py:1351
  464.8 56.4 %collective-permute-start.22 = (bf16[2,512,256]{2,1,0:T(8,128)(2,1)}, bf16[2,512,256]{2,1,0:T(8,128)(2,1)}, u32[]{:S(2)}, u32[]{:S(2)}) collective-permute-start(bf16[2,512,256]{2,1,0:T(8,128)(2,1)} %get-tuple-element.173), channel_id=1, source_target_pairs={{0,16},{4,20},{8,24},{12,28},{16,0},{20,4},{24,8},{28,12},{1,17},{... | collective-permute-start | bytes 1572872 | tf_op jit(solution)/shard_map/ppermute | solution.py:1168
  482.8 11.6 %copy-start.13 = (f32[512]{0:T(512)S(1)}, f32[512]{0:T(512)}, u32[]{:S(2)}) copy-start(f32[512]{0:T(512)} %param.19) | copy-start | bytes 6148
  492.5 54.6 %collective-permute-start.24 = (bf16[4,256,768]{2,1,0:T(8,128)(2,1)}, bf16[4,256,768]{2,1,0:T(8,128)(2,1)}, u32[]{:S(2)}, u32[]{:S(2)}) collective-permute-start(bf16[4,256,768]{2,1,0:T(8,128)(2,1)} %weight_blocks.13.refs_10_), channel_id=1, source_target_pairs={{0,4},{4,0},{8,12},{12,8},{16,20},{20,16},{24,28},{28,24},{1,5},{5... | collective-permute-start | bytes 4718600 | tf_op jit(solution)/shard_map/ppermute | solution.py:1168
  494.1 48.9 %collective-permute-start.25 = (bf16[2,256,2048]{2,1,0:T(8,128)(2,1)}, bf16[2,256,2048]{2,1,0:T(8,128)(2,1)}, u32[]{:S(2)}, u32[]{:S(2)}) collective-permute-start(bf16[2,256,2048]{2,1,0:T(8,128)(2,1)} %get-tuple-element.185), channel_id=1, source_target_pairs={{0,8},{4,12},{8,0},{12,4},{16,24},{20,28},{24,16},{28,20},{1,9},{5... | collective-permute-start | bytes 6291464 | tf_op jit(solution)/shard_map/ppermute | solution.py:1168
  519.5 39.9 %collective-permute-start.27 = (bf16[2,256,768]{2,1,0:T(8,128)(2,1)}, bf16[2,256,768]{2,1,0:T(8,128)(2,1)}, u32[]{:S(2)}, u32[]{:S(2)}) collective-permute-start(bf16[2,256,768]{2,1,0:T(8,128)(2,1)} %get-tuple-element.189), channel_id=1, source_target_pairs={{0,8},{4,12},{8,0},{12,4},{16,24},{20,28},{24,16},{28,20},{1,9},{5... | collective-permute-start | bytes 2359304 | tf_op jit(solution)/shard_map/ppermute | solution.py:1168
  521.1 14.8 %copy-start.6 = (f32[8,512]{1,0:T(8,128)S(1)}, f32[8,512]{1,0:T(8,128)}, u32[]{:S(2)}) copy-start(f32[8,512]{1,0:T(8,128)} %get-tuple-element.170.refs_1_) | copy-start | bytes 49156
  521.1 14.8 %copy-start.7 = (f32[8,512]{1,0:T(8,128)S(1)}, f32[8,512]{1,0:T(8,128)}, u32[]{:S(2)}) copy-start(f32[8,512]{1,0:T(8,128)} %get-tuple-element.181) | copy-start | bytes 49156
  521.2 18.2 %copy-start.2 = (f32[13,8,128]{2,1,0:T(8,128)S(1)}, f32[13,8,128]{2,1,0:T(8,128)}, u32[]{:S(2)}) copy-start(f32[13,8,128]{2,1,0:T(8,128)} %get-tuple-element.183) | copy-start | bytes 159748
  557.1 28.7 %collective-permute-start.26 = (bf16[2,256,768]{2,1,0:T(8,128)(2,1)}, bf16[2,256,768]{2,1,0:T(8,128)(2,1)}, u32[]{:S(2)}, u32[]{:S(2)}) collective-permute-start(bf16[2,256,768]{2,1,0:T(8,128)(2,1)} %get-tuple-element.188), channel_id=1, source_target_pairs={{0,8},{4,12},{8,0},{12,4},{16,24},{20,28},{24,16},{28,20},{1,9},{5... | collective-permute-start | bytes 2359304 | tf_op jit(solution)/shard_map/ppermute | solution.py:1168
  562.9 90.1 %collective-permute-start.30 = (bf16[1,256,768]{2,1,0:T(8,128)(2,1)}, bf16[1,256,768]{2,1,0:T(8,128)(2,1)}, u32[]{:S(2)}, u32[]{:S(2)}) collective-permute-start(bf16[1,256,768]{2,1,0:T(8,128)(2,1)} %get-tuple-element.194), channel_id=1, source_target_pairs={{0,16},{4,20},{8,24},{12,28},{16,0},{20,4},{24,8},{28,12},{1,17},{... | collective-permute-start | bytes 1179656 | tf_op jit(solution)/shard_map/ppermute | solution.py:1168
  563.0 90.0 %collective-permute-start.28 = (bf16[1,256,2048]{2,1,0:T(8,128)(2,1)}, bf16[1,256,2048]{2,1,0:T(8,128)(2,1)}, u32[]{:S(2)}, u32[]{:S(2)}) collective-permute-start(bf16[1,256,2048]{2,1,0:T(8,128)(2,1)} %get-tuple-element.192), channel_id=1, source_target_pairs={{0,16},{4,20},{8,24},{12,28},{16,0},{20,4},{24,8},{28,12},{1,17},{... | collective-permute-start | bytes 3145736 | tf_op jit(solution)/shard_map/ppermute | solution.py:1168
  589.6 63.4 %collective-permute-start.29 = (bf16[1,512,256]{2,1,0:T(8,128)(2,1)}, bf16[1,512,256]{2,1,0:T(8,128)(2,1)}, u32[]{:S(2)}, u32[]{:S(2)}) collective-permute-start(bf16[1,512,256]{2,1,0:T(8,128)(2,1)} %get-tuple-element.193), channel_id=1, source_target_pairs={{0,4},{4,0},{8,12},{12,8},{16,20},{20,16},{24,28},{28,24},{1,5},{5... | collective-permute-start | bytes 786440 | tf_op jit(solution)/shard_map/ppermute | solution.py:1168
  590.1 62.9 %collective-permute-start.31 = (bf16[1,256,768]{2,1,0:T(8,128)(2,1)}, bf16[1,256,768]{2,1,0:T(8,128)(2,1)}, u32[]{:S(2)}, u32[]{:S(2)}) collective-permute-start(bf16[1,256,768]{2,1,0:T(8,128)(2,1)} %get-tuple-element.196), channel_id=1, source_target_pairs={{0,16},{4,20},{8,24},{12,28},{16,0},{20,4},{24,8},{28,12},{1,17},{... | collective-permute-start | bytes 1179656 | tf_op jit(solution)/shard_map/ppermute | solution.py:1168
  (1 other events, 3.5 us)
Sparse Core Ops, SparseCore 0:
  35.0 49.6 all-gather.1
  237.2 162.7 reduce-scatter.1

commit v10 on v9

--- a/solution.py
+++ b/solution.py
@@ -1551,16 +1551,16 @@
                 Spread(normed1, qkv_grad, 0, (1, 2, 4), (1, 2)),
             ]
             qkv_sum[0].first()
+        parts = project_back(n, pairs, qkv_grad[r], normed1[r], gain1, bias1, qkv_weight)
+        parts1[r] = ring.scatter(parts, True)
         if r > 0 and pairs:
             parts, row_sums = parts1[r - 1]
             parts[1] = row_sums[1] = gate([parts[1]])[0]
-        parts = project_back(n, pairs, qkv_grad[r], normed1[r], gain1, bias1, qkv_weight)
-        parts1[r] = ring.scatter(parts, True)
 
     if spread:
         down_sum = gate([down_sum])[0]
+        up_sum.keep_added()
         out_sum.keep_added()
-        up_sum.keep_added()
         qkv_sum[1].first()
 
     grad_history, depth_sum, gain1_sum, bias1_sum = None, 0.0, 0.0, 0.0
@@ -1589,20 +1589,21 @@
                 qkv_sum[0].keep_added()
                 out_sum.coming = gate([out_sum.coming])[0]
 
+    Order.cost = TINY
     vectors = [up_bias_sum, down_bias_sum, gain2_sum, bias2_sum, gain1_sum, bias1_sum]
     vectors, depth_part = [jnp.sum(v, 0) for v in vectors], jnp.sum(depth_sum, (1, 2))
     if spread:
         advance(up_sum)
         qkv_sum[1].keep_added()
         advance(qkv_sum[0])
+        up_sum.coming = gate([up_sum.coming])[0]
         advance(qkv_sum[1], out_sum)
-        totals, depth_grad = sums(vectors, depth_part)
     else:
         qkv_sum = [spread_over_dp(weight_grad(normed1, qkv_grad), 0)]
         out_sum = spread_over_dp(weight_grad(attended, grad_full), 1)
         up_sum = spread_over_dp(weight_grad(normed2, up_grad), 0)
-        totals, depth_grad = sums(vectors, depth_part)
     down_total, up_total, out_total, qkv_total = finish([down_sum], [up_sum], [out_sum], qkv_sum)
+    totals, depth_grad = sums(vectors, depth_part)
     return (
         made,
         grad_history,

time: 670 us -> 666 us (level)
  waiting for transfers between devices: 59.4 us -> 111 us
  Pallas kernels: 529 us -> 484 us
    ppermute x12, waiting for transfers between devices: 24 us -> 82 us  [send(): lax.ppermute(value, 'dp', [(i, i ^ bit) for i in range(self.groups)])]
    pallas_call x47 -> x48, Pallas kernels: 529 us -> 484 us  [call(): pl.pallas_call(without_extra, grid_spec=pltpu.PrefetchScalarGridSpec(num_...]
  transfers between devices with their start and end apart: 34 -> 34, of which waited for: 8 -> 9; matrix products, arithmetic and copies ran while one was open for 4% -> 2% of each run, Pallas kernels for 79% -> 70%
where the time goes in v10:
time: 666 us; the launch traced here: 662 us
  Pallas kernels  484 us (73%)
  waiting for transfers between devices  111 us (17%)
  starting transfers between devices  32.1 us (5%)
  local copies, waits for them, and re-layouts  16.3 us (2%)
  between operations  14.9 us (2%)
    pallas_call x48, Pallas kernels, call(): pl.pallas_call(without_extra, grid_spec=pltpu.PrefetchScalarGridSpec(num_...  484 us
    ppermute x12, waiting for transfers between devices, send(): lax.ppermute(value, 'dp', [(i, i ^ bit) for i in range(self.groups)])  82 us
    ppermute x16, waiting for transfers between devices, over_chip(): return lax.ppermute(value, 'mp', self.chip)  24.8 us
    ppermute x16, starting transfers between devices, over_chip(): return lax.ppermute(value, 'mp', self.chip)  17.5 us
    ppermute x12, starting transfers between devices, send(): lax.ppermute(value, 'dp', [(i, i ^ bit) for i in range(self.groups)])  13.8 us
  transfers between devices with their start and end apart: 34, of which 9 were waited for; matrix products, arithmetic and copies ran while one was open for 2% of the time, Pallas kernels for 70%

profile of v10, /device:TPU:0, one launch (start us, length us, event | category | flops | bytes accessed | tf_op | source)
XLA Modules:
  0.0 662.4 jit_solution(15675144426936481303)
XLA Ops:
  8.6 3.0 collective-permute-start.2
  13.8 8.0 %average.2 = (f32[1024,512]{1,0:T(8,128)}, bf16[1024,512]{1,0:T(8,128)(2,1)}) custom-call(f32[13]{0:T(128)} %refs_0_.7, bf16[13,2048,512]{2,1,0:T(8,128)(2,1)} %refs_9_.3), custom_call_target="tpu_custom_call" | custom-call | flops 999999995904 | bytes 100000000 | tf_op jit(solution)/shard_map/average/pallas_call | solution.py:60
  27.1 7.8 %average.3 = (f32[1024,512]{1,0:T(8,128)}, bf16[1024,512]{1,0:T(8,128)(2,1)}) custom-call(f32[13]{0:T(128)} %refs_0_.7, bf16[13,2048,512]{2,1,0:T(8,128)(2,1)} %refs_9_.3, f32[32,512]{1,0:T(8,128)} %get-tuple-element.109.refs_2_), custom_call_target="tpu_custom_call" | custom-call | flops 999999995904 | bytes 100000000 | tf_op jit(solution)/shard_map/average/pallas_call | solution.py:60
  36.9 10.2 %collective-permute-done.refs_1_.refs_3_.refs_5_ = bf16[1024,512]{1,0:T(8,128)(2,1)} collective-permute-done((bf16[1024,512]{1,0:T(8,128)(2,1)}, bf16[1024,512]{1,0:T(8,128)(2,1)}, u32[]{:S(2)}, u32[]{:S(2)}) %collective-permute-start) | collective-permute-done | bytes 1048608 | tf_op jit(solution)/shard_map/ppermute | solution.py:1351
  48.9 17.9 %project.2 = (bf16[1024,1536]{1,0:T(8,128)(2,1)}, bf16[1024,2048]{1,0:T(8,128)(2,1)}, f32[1024,128]{1,0:T(8,128)}, bf16[1024,512]{1,0:T(8,128)(2,1)}, bf16[1024,512]{1,0:T(8,128)(2,1)}) custom-call(bf16[1024,512]{1,0:T(8,128)(2,1)} %get-tuple-element.107.refs_0_.refs_2_, bf16[1024,512]{1,0:T(8,128)(2,1)} %collective-permute-done.refs_1_.refs_3_.refs_5_, ...), custom_call_target="tpu_custom_call" | custom-call | flops 999999995904 | bytes 100000000 | tf_op jit(solution)/shard_map/project/pallas_call | solution.py:60
  67.4 10.1 %attend.2 = (bf16[1024,512]{1,0:T(8,128)(2,1)}, f32[4,8,1024]{2,1,0:T(8,128)}) custom-call(s32[8,1024]{1,0:T(8,128)} %broadcast_in_dim.21.refs_0_, bf16[1024,1536]{1,0:T(8,128)(2,1)} %get-tuple-element.112.refs_1_.refs_3_, f32[1024,128]{1,0:T(8,128)} %get-tuple-element.113.refs_2_.refs_6_), custom_call_target="tpu_custom_call" | custom-call | flops 999999995904 | bytes 100000000 | tf_op jit(solution)/shard_map/attend/pallas_call | solution.py:60
  77.8 18.0 %project.3 = (bf16[1024,1536]{1,0:T(8,128)(2,1)}, bf16[1024,2048]{1,0:T(8,128)(2,1)}, f32[1024,128]{1,0:T(8,128)}, bf16[1024,512]{1,0:T(8,128)(2,1)}, bf16[1024,512]{1,0:T(8,128)(2,1)}) custom-call(bf16[1024,512]{1,0:T(8,128)(2,1)} %gate.13.refs_9_.refs_0_.refs_2_, bf16[1024,512]{1,0:T(8,128)(2,1)} %collective-permute-done.7.refs_1_.refs_3_.refs_5_, ...), custom_call_target="tpu_custom_call" | custom-call | flops 999999995904 | bytes 100000000 | tf_op jit(solution)/shard_map/project/pallas_call | solution.py:60
  96.4 9.7 %attend.3 = (bf16[1024,512]{1,0:T(8,128)(2,1)}, f32[4,8,1024]{2,1,0:T(8,128)}) custom-call(s32[8,1024]{1,0:T(8,128)} %broadcast_in_dim.24.refs_0_, bf16[1024,1536]{1,0:T(8,128)(2,1)} %get-tuple-element.119.refs_1_.refs_3_, f32[1024,128]{1,0:T(8,128)} %get-tuple-element.120.refs_2_.refs_6_), custom_call_target="tpu_custom_call" | custom-call | flops 999999995904 | bytes 100000000 | tf_op jit(solution)/shard_map/attend/pallas_call | solution.py:60
  108.2 4.1 collective-permute-done.8.refs_10_
  113.0 40.9 %feed.2 = (f32[1024,512]{1,0:T(8,128)}, bf16[1024,2048]{1,0:T(8,128)(2,1)}, f32[1024,128]{1,0:T(8,128)}, bf16[1024,2048]{1,0:T(8,128)(2,1)}, bf16[1024,2048]{1,0...) custom-call(bf16[1024,512]{1,0:T(8,128)(2,1)} %get-tuple-element.114.refs_0_.refs_2_.refs_1_, ...), custom_call_target="tpu_custom_call" | custom-call | flops 999999995904 | bytes 100000000 | tf_op jit(solution)/shard_map/feed/pallas_call | solution.py:60
  156.0 41.1 %feed.3 = (f32[1024,512]{1,0:T(8,128)}, bf16[1024,2048]{1,0:T(8,128)(2,1)}, f32[1024,128]{1,0:T(8,128)}, bf16[1024,2048]{1,0:T(8,128)(2,1)}, bf16[1024,2048]{1,0...) custom-call(bf16[1024,512]{1,0:T(8,128)(2,1)} %get-tuple-element.126.refs_0_.refs_2_, ...), custom_call_target="tpu_custom_call" | custom-call | flops 999999995904 | bytes 100000000 | tf_op jit(solution)/shard_map/feed/pallas_call | solution.py:60
  197.5 5.3 collective-permute-done.11.refs_5_.refs_7_
  202.7 11.2 %join.1 = (bf16[1024,2048]{1,0:T(8,128)(2,1)}, bf16[1024,2048]{1,0:T(8,128)(2,1)}) custom-call(bf16[1024,512]{1,0:T(8,128)(2,1)} %gate.15.refs_17_.refs_0_.refs_2_, bf16[1024,512]{1,0:T(8,128)(2,1)} %collective-permute-done.10.refs_1_.refs_3_, bf16[1024,512]{1,0:T(8,128)(2,1)} %gate.15.refs_17_.refs_0_.refs_2_, ...), custom_call_target="tpu_custom_call" | custom-call | flops 999999995904 | bytes 100000000 | tf_op jit(solution)/shard_map/join/pallas_call | solution.py:60
  214.0 23.1 %weight_grad.1.refs_7_ = bf16[2048,2048]{1,0:T(8,128)(2,1)} custom-call(bf16[1024,2048]{1,0:T(8,128)(2,1)} %get-tuple-element.136.refs_0_, bf16[1024,2048]{1,0:T(8,128)(2,1)} %get-tuple-element.137.refs_1_, bf16[1024,2048]{1,0:T(8,128)(2,1)} %get-tuple-element.130.refs_1_.refs_2_.refs_0_, bf16[1024,2048]{1,0:T(8,128)(2,1)} %get-tuple-element.138.refs_3_.refs_0_, ...), custom_call_target="tpu_custom_call" | custom-call | flops 999999995904 | bytes 100000000 | tf_op jit(solution)/shard_map/weight_grad/pallas_call | solution.py:60
  237.1 31.0 %feed_back.2 = (bf16[1024,2048]{1,0:T(8,128)(2,1)}, f32[8,2048]{1,0:T(8,128)}, f32[8,512]{1,0:T(8,128)}, bf16[1024,512]{1,0:T(8,128)(2,1)}, bf16[1040,512]{1,0:T(8,128)(2,1)}, /*index=5*/f32[8,1024]{1,0:T(8,128)}) custom-call(bf16[1024,2048]{1,0:T(8,128)(2,1)} %get-tuple-element.130.refs_1_.refs_2_.refs_0_, bf16[1024,2048]{1,0:T(8,128)(2,1)} %get-tuple-element.134.refs_1_, ...), custom_call_target="tpu_custom_call" | custom-call | flops 999999995904 | bytes 100000000 | tf_op jit(solution)/shard_map/feed_back/pallas_call | solution.py:60
  268.2 31.1 %feed_back.3 = (bf16[1024,2048]{1,0:T(8,128)(2,1)}, f32[8,2048]{1,0:T(8,128)}, f32[8,512]{1,0:T(8,128)}, bf16[1024,512]{1,0:T(8,128)(2,1)}, bf16[1040,512]{1,0:T(8,128)(2,1)}, /*index=5*/f32[8,1024]{1,0:T(8,128)}) custom-call(bf16[1024,2048]{1,0:T(8,128)(2,1)} %get-tuple-element.138.refs_3_.refs_0_, bf16[1024,2048]{1,0:T(8,128)(2,1)} %get-tuple-element.142.refs_1_, ...), custom_call_target="tpu_custom_call" | custom-call | flops 999999995904 | bytes 100000000 | tf_op jit(solution)/shard_map/feed_back/pallas_call | solution.py:60
  301.7 5.9 hidden_back.2
  307.9 14.8 %weight_blocks.8.refs_7_ = bf16[4,256,2048]{2,1,0:T(8,128)(2,1)} custom-call(s32[1]{0:T(128)} %bitcast.7.refs_0_, bf16[1024,2048]{1,0:T(8,128)(2,1)} %get-tuple-element.135.refs_2_.refs_1_.refs_3_.refs_5_.refs_7_, bf16[1024,2048]{1,0:T(8,128)(2,1)} %get-tuple-element.140.refs_2_.refs_4_.refs_6_.refs_8_, ...), custom_call_target="tpu_custom_call" | custom-call | flops 999999995904 | bytes 100000000 | tf_op jit(solution)/shard_map/weight_blocks/pallas_call | solution.py:60
  324.7 6.9 %output.1.refs_8_ = bf16[2048,512]{1,0:T(8,128)(2,1)} custom-call(f32[1024,512]{1,0:T(8,128)} %get-tuple-element.122.refs_5_.refs_0_, bf16[1024,512]{1,0:T(8,128)(2,1)} %get-tuple-element.123.refs_1_, bf16[1024,512]{1,0:T(8,128)(2,1)} %gate.17.refs_4_.refs_2_, f32[1024,512]{1,0:T(8,128)} %get-tuple-element.131.refs_3_.refs_5_, ...), custom_call_target="tpu_custom_call" | custom-call | flops 999999995904 | bytes 100000000 | tf_op jit(solution)/shard_map/output/pallas_call | solution.py:60
  331.6 5.9 hidden_back.3
  339.2 9.3 %collective-permute-done.17.refs_1_.refs_3_ = bf16[1024,512]{1,0:T(8,128)(2,1)} collective-permute-done((bf16[1024,512]{1,0:T(8,128)(2,1)}, bf16[1024,512]{1,0:T(8,128)(2,1)}, u32[]{:S(2)}, u32[]{:S(2)}) %collective-permute-start.17) | collective-permute-done | bytes 1048608 | tf_op jit(solution)/shard_map/ppermute | solution.py:1351
  348.4 9.0 %attended_back.2 = (bf16[1024,2048]{1,0:T(8,128)(2,1)}, bf16[1024,512]{1,0:T(8,128)(2,1)}) custom-call(bf16[1024,512]{1,0:T(8,128)(2,1)} %get-tuple-element.153.refs_0_.refs_2_, bf16[1024,512]{1,0:T(8,128)(2,1)} %collective-permute-done.17.refs_1_.refs_3_, bf16[1024,512]{1,0:T(8,128)(2,1)} %get-tuple-element.153.refs_0_.refs_2_, ...), custom_call_target="tpu_custom_call" | custom-call | flops 999999995904 | bytes 100000000 | tf_op jit(solution)/shard_map/attended_back/pallas_call | solution.py:60
  357.5 12.4 %attend_back.2.refs_0_.refs_9_ = bf16[1024,1536]{1,0:T(8,128)(2,1)} custom-call(s32[8,1024]{1,0:T(8,128)} %broadcast_in_dim.21.refs_0_, f32[1024,128]{1,0:T(8,128)} %constant.19.clone.refs_6_.refs_1_, f32[1024,128]{1,0:T(8,128)} %constant.20.clone.refs_7_.refs_2_, bf16[1024,1536]{1,0:T(8,128)(2,1)} %get-tuple-element.112.refs_1_.refs_3_, ...), custom_call_target="tpu_custom_call" | custom-call | flops 999999995904 | bytes 100000000 | tf_op jit(solution)/shard_map/attend_back/pallas_call | solution.py:60
  369.9 15.6 %project_back.2 = (bf16[1024,512]{1,0:T(8,128)(2,1)}, bf16[1040,512]{1,0:T(8,128)(2,1)}, f32[8,1024]{1,0:T(8,128)}) custom-call(bf16[1024,1536]{1,0:T(8,128)(2,1)} %attend_back.2.refs_0_.refs_9_, bf16[1024,2048]{1,0:T(8,128)(2,1)} %get-tuple-element.156.refs_1_.refs_3_.refs_5_.refs_7_, f32[8,2048]{1,0:T(8,128)} %get-tuple-element.206.refs_4_.refs_2_, ...), custom_call_target="tpu_custom_call" | custom-call | flops 999999995904 | bytes 100000000 | tf_op jit(solution)/shard_map/project_back/pallas_call | solution.py:60
  385.5 9.2 %attended_back.3 = (bf16[1024,2048]{1,0:T(8,128)(2,1)}, bf16[1024,512]{1,0:T(8,128)(2,1)}) custom-call(bf16[1024,512]{1,0:T(8,128)(2,1)} %get-tuple-element.152.refs_0_.refs_2_, bf16[1024,512]{1,0:T(8,128)(2,1)} %collective-permute-done.16.refs_1_.refs_3_, bf16[1024,512]{1,0:T(8,128)(2,1)} %get-tuple-element.152.refs_0_.refs_2_, ...), custom_call_target="tpu_custom_call" | custom-call | flops 999999995904 | bytes 100000000 | tf_op jit(solution)/shard_map/attended_back/pallas_call | solution.py:60
  394.7 6.2 weight_blocks.9.refs_6_
  400.9 12.6 %attend_back.3.refs_10_.refs_0_ = bf16[1024,1536]{1,0:T(8,128)(2,1)} custom-call(s32[8,1024]{1,0:T(8,128)} %broadcast_in_dim.24.refs_0_, f32[1024,128]{1,0:T(8,128)} %constant.19.clone.refs_6_.refs_1_, f32[1024,128]{1,0:T(8,128)} %constant.20.clone.refs_7_.refs_2_, bf16[1024,1536]{1,0:T(8,128)(2,1)} %get-tuple-element.119.refs_1_.refs_3_, ...), custom_call_target="tpu_custom_call" | custom-call | flops 999999995904 | bytes 100000000 | tf_op jit(solution)/shard_map/attend_back/pallas_call | solution.py:60
  416.9 9.6 %weight_blocks.10.refs_5_ = bf16[4,256,768]{2,1,0:T(8,128)(2,1)} custom-call(s32[1]{0:T(128)} %bitcast.7.refs_0_, bf16[1024,2048]{1,0:T(8,128)(2,1)} %get-tuple-element.156.refs_1_.refs_3_.refs_5_.refs_7_, bf16[1024,2048]{1,0:T(8,128)(2,1)} %get-tuple-element.161.refs_2_.refs_4_.refs_6_.refs_8_.refs_1_, ...), custom_call_target="tpu_custom_call" | custom-call | flops 999999995904 | bytes 100000000 | tf_op jit(solution)/shard_map/weight_blocks/pallas_call | solution.py:60
  428.0 15.6 %project_back.3 = (bf16[1024,512]{1,0:T(8,128)(2,1)}, bf16[1040,512]{1,0:T(8,128)(2,1)}, f32[8,1024]{1,0:T(8,128)}) custom-call(bf16[1024,1536]{1,0:T(8,128)(2,1)} %attend_back.3.refs_10_.refs_0_, bf16[1024,2048]{1,0:T(8,128)(2,1)} %get-tuple-element.161.refs_2_.refs_4_.refs_6_.refs_8_.refs_1_, f32[8,2048]{1,0:T(8,128)} %get-tuple-element.206.refs_4_.refs_2_, ...), custom_call_target="tpu_custom_call" | custom-call | flops 999999995904 | bytes 100000000 | tf_op jit(solution)/shard_map/project_back/pallas_call | solution.py:60
  443.9 15.3 %weight_blocks.11 = (bf16[2,256,2048]{2,1,0:T(8,128)(2,1)}, bf16[2,256,2048]{2,1,0:T(8,128)(2,1)}) custom-call(s32[1]{0:T(128)} %bitcast.7.refs_0_, bf16[1024,2048]{1,0:T(8,128)(2,1)} %get-tuple-element.135.refs_2_.refs_1_.refs_3_.refs_5_.refs_7_, bf16[1024,2048]{1,0:T(8,128)(2,1)} %get-tuple-element.140.refs_2_.refs_4_.refs_6_.refs_8_, ...), custom_call_target="tpu_custom_call" | custom-call | flops 999999995904 | bytes 100000000 | tf_op jit(solution)/shard_map/weight_blocks/pallas_call | solution.py:60
  459.2 6.4 weight_blocks.12
  465.6 2.6 collective-permute-start.22
  468.1 9.7 %weight_blocks.13.refs_10_ = bf16[4,256,768]{2,1,0:T(8,128)(2,1)} custom-call(s32[1]{0:T(128)} %bitcast.7.refs_0_, bf16[1024,2048]{1,0:T(8,128)(2,1)} %get-tuple-element.156.refs_1_.refs_3_.refs_5_.refs_7_, bf16[1024,2048]{1,0:T(8,128)(2,1)} %get-tuple-element.161.refs_2_.refs_4_.refs_6_.refs_8_.refs_1_, ...), custom_call_target="tpu_custom_call" | custom-call | flops 999999995904 | bytes 100000000 | tf_op jit(solution)/shard_map/weight_blocks/pallas_call | solution.py:60
  479.5 14.4 %average_back.2 = (bf16[13,2048,512]{2,1,0:T(8,128)(2,1)}, f32[13,8,128]{2,1,0:T(8,128)}, f32[8,512]{1,0:T(8,128)}, f32[8,512]{1,0:T(8,128)}) custom-call(f32[13]{0:T(128)} %refs_0_.7, bf16[1024,512]{1,0:T(8,128)(2,1)} %get-tuple-element.164.refs_1_, bf16[1040,512]{1,0:T(8,128)(2,1)} %gate.19.refs_1_.refs_2_.refs_4_, ...), custom_call_target="tpu_custom_call" | custom-call | flops 999999995904 | bytes 100000000 | tf_op jit(solution)/shard_map/average_back/pallas_call | solution.py:60
  493.9 10.3 %weight_blocks.14 = (bf16[2,256,768]{2,1,0:T(8,128)(2,1)}, bf16[2,256,768]{2,1,0:T(8,128)(2,1)}) custom-call(s32[1]{0:T(128)} %bitcast.7.refs_0_, bf16[1024,2048]{1,0:T(8,128)(2,1)} %get-tuple-element.156.refs_1_.refs_3_.refs_5_.refs_7_, bf16[1024,2048]{1,0:T(8,128)(2,1)} %get-tuple-element.161.refs_2_.refs_4_.refs_6_.refs_8_.refs_1_, ...), custom_call_target="tpu_custom_call" | custom-call | flops 999999995904 | bytes 100000000 | tf_op jit(solution)/shard_map/weight_blocks/pallas_call | solution.py:60
  504.2 14.5 %average_back.3 = (bf16[13,2048,512]{2,1,0:T(8,128)(2,1)}, f32[13,8,128]{2,1,0:T(8,128)}, f32[8,512]{1,0:T(8,128)}, f32[8,512]{1,0:T(8,128)}) custom-call(f32[13]{0:T(128)} %refs_0_.7, bf16[1024,512]{1,0:T(8,128)(2,1)} %get-tuple-element.162.refs_1_, bf16[1040,512]{1,0:T(8,128)(2,1)} %gate.21.refs_12_.refs_2_.refs_4_, ...), custom_call_target="tpu_custom_call", output_to_operand_aliasing={{0}: (10, {})} | custom-call | flops 999999995904 | bytes 100000000 | tf_op jit(solution)/shard_map/average_back/pallas_call | solution.py:60
  518.8 18.0 %collective-permute-done.24.refs_1_ = bf16[2,256,2048]{2,1,0:T(8,128)(2,1)} collective-permute-done((bf16[2,256,2048]{2,1,0:T(8,128)(2,1)}, bf16[2,256,2048]{2,1,0:T(8,128)(2,1)}, u32[]{:S(2)}, u32[]{:S(2)}) %collective-permute-start.24) | collective-permute-done | bytes 2097184 | tf_op jit(solution)/shard_map/ppermute | solution.py:1168
  536.8 4.2 fold.3
  541.2 10.0 %weight_blocks.15 = (bf16[2,256,768]{2,1,0:T(8,128)(2,1)}, bf16[2,256,768]{2,1,0:T(8,128)(2,1)}) custom-call(s32[1]{0:T(128)} %bitcast.7.refs_0_, bf16[1024,2048]{1,0:T(8,128)(2,1)} %get-tuple-element.156.refs_1_.refs_3_.refs_5_.refs_7_, bf16[1024,2048]{1,0:T(8,128)(2,1)} %get-tuple-element.161.refs_2_.refs_4_.refs_6_.refs_8_.refs_1_, ...), custom_call_target="tpu_custom_call" | custom-call | flops 10000 | bytes 1 | tf_op jit(solution)/shard_map/weight_blocks/pallas_call | solution.py:60
  553.4 28.2 %collective-permute-done.26.refs_1_ = bf16[2,256,768]{2,1,0:T(8,128)(2,1)S(1)} collective-permute-done((bf16[2,256,768]{2,1,0:T(8,128)(2,1)S(1)}, bf16[2,256,768]{2,1,0:T(8,128)(2,1)S(1)}, u32[]{:S(2)}, u32[]{:S(2)}) %collective-permute-start.26) | collective-permute-done | bytes 786464 | tf_op jit(solution)/shard_map/ppermute | solution.py:1168
  582.5 3.5 fold.4
  585.9 3.0 collective-permute-start.30
  589.9 18.5 %collective-permute-done.28.refs_1_ = bf16[2,256,768]{2,1,0:T(8,128)(2,1)S(1)} collective-permute-done((bf16[2,256,768]{2,1,0:T(8,128)(2,1)}, bf16[2,256,768]{2,1,0:T(8,128)(2,1)S(1)}, u32[]{:S(2)}, u32[]{:S(2)}) %collective-permute-start.28) | collective-permute-done | bytes 786464 | tf_op jit(solution)/shard_map/ppermute | solution.py:1168
  609.3 3.8 fold.5
  614.6 6.2 collective-permute-done.29.refs_4_
  620.8 11.1 %collective-permute-done.31.refs_8_ = bf16[1,256,768]{2,1,0:T(8,128)(2,1)S(1)} collective-permute-done((bf16[1,256,768]{2,1,0:T(8,128)(2,1)}, bf16[1,256,768]{2,1,0:T(8,128)(2,1)S(1)}, u32[]{:S(2)}, u32[]{:S(2)}) %collective-permute-start.31) | collective-permute-done | bytes 393248 | tf_op jit(solution)/shard_map/ppermute | solution.py:1168
  632.7 5.5 finish.1
  638.2 13.3 %sums.1 = f32[48,128]{1,0:T(8,128)} custom-call(f32[48,128]{1,0:T(8,128)} %select_maximum_fusion.refs_0_, f32[512,256]{1,0:T(8,128)} %get-tuple-element.100.refs_1_), custom_call_target="tpu_custom_call" | custom-call | flops 10000 | bytes 1 | tf_op jit(solution)/shard_map/sums/pallas_call | solution.py:60
  (158 shorter events, 43.7 us)
Async XLA Ops:
  7.2 100.7 %all-gather.2.cloned.1.call-start = ((), (), s32[]{:S(2)}) async-start(), calls=%async_computation.1 | async-start | bytes 2359296 | tf_op jit(solution)/shard_map/all_gather | solution.py:1392
  8.6 18.4 %collective-permute-start.2 = (f32[32,512]{1,0:T(8,128)}, f32[32,512]{1,0:T(8,128)}, u32[]{:S(2)}, u32[]{:S(2)}) collective-permute-start(f32[32,512]{1,0:T(8,128)} %broadcast_bitcast_fusion), channel_id=1, source_target_pairs={{0,2},{1,3},{2,0},{3,1},{4,6},{5,7},{6,4},{7,5},{8,10},{9,11},{10,... | collective-permute-start | bytes 196616 | tf_op jit(solution)/shard_map/ppermute | solution.py:1351
  11.6 23.6 %collective-permute-start.1 = (f32[32,512]{1,0:T(8,128)}, f32[32,512]{1,0:T(8,128)}, u32[]{:S(2)}, u32[]{:S(2)}) collective-permute-start(f32[32,512]{1,0:T(8,128)} %broadcast_bitcast_fusion), channel_id=1, source_target_pairs={{0,1},{1,0},{2,3},{3,2},{4,5},{5,4},{6,7},{7,6},{8,9},{9,8},{10,11... | collective-permute-start | bytes 196616 | tf_op jit(solution)/shard_map/ppermute | solution.py:1348
  11.6 96.7 %collective-permute-start.6 = (bf16[512,2048]{1,0:T(8,128)(2,1)}, bf16[512,2048]{1,0:T(8,128)(2,1)}, u32[]{:S(2)}, u32[]{:S(2)}) collective-permute-start(bf16[512,2048]{1,0:T(8,128)(2,1)} %refs_4_.10), channel_id=1, source_target_pairs={{0,1},{1,0},{2,3},{3,2},{4,5},{5,4},{6,7},{7,6},{8,9},{9,8},{10,11... | collective-permute-start | bytes 6291464 | tf_op jit(solution)/shard_map/ppermute | solution.py:1348
  13.8 13.3 %collective-permute-start.3 = (bf16[64,2048]{1,0:T(8,128)(2,1)}, bf16[64,2048]{1,0:T(8,128)(2,1)}, u32[]{:S(2)}, u32[]{:S(2)}) collective-permute-start(bf16[64,2048]{1,0:T(8,128)(2,1)} %constant_dynamic-slice_fusion), channel_id=1, source_target_pairs={{0,2},{1,3},{2,0},{3,1},{4,6},{5,7},{6,4},{7,5},{8,10},{9,11},{10,... | collective-permute-start | bytes 786440 | tf_op jit(solution)/shard_map/ppermute | solution.py:1351
  21.7 25.4 %collective-permute-start = (bf16[1024,512]{1,0:T(8,128)(2,1)}, bf16[1024,512]{1,0:T(8,128)(2,1)}, u32[]{:S(2)}, u32[]{:S(2)}) collective-permute-start(bf16[1024,512]{1,0:T(8,128)(2,1)} %get-tuple-element.107.refs_0_.refs_2_), channel_id=1, source_target_pairs={{0,2},{1,3},{2,0},{3,1},{4,6},{5,7},{6,4},{7,5},{8,10},{9,11},{10,... | collective-permute-start | bytes 3145736 | tf_op jit(solution)/shard_map/ppermute | solution.py:1351
  27.0 8.2 %collective-permute-start.4 = (f32[32,512]{1,0:T(8,128)}, f32[32,512]{1,0:T(8,128)}, u32[]{:S(2)}, u32[]{:S(2)}) collective-permute-start(f32[32,512]{1,0:T(8,128)} %get-tuple-element.109.refs_2_), channel_id=1, source_target_pairs={{0,1},{1,0},{2,3},{3,2},{4,5},{5,4},{6,7},{7,6},{8,9},{9,8},{10,11... | collective-permute-start | bytes 196616 | tf_op jit(solution)/shard_map/ppermute | solution.py:1348
  35.0 408.9 %reduce-scatter.2.cloned.1.call-start = ((), (), s32[]{:S(2)}) async-start(), calls=%async_computation.2 | async-start | bytes 9437184 | tf_op jit(solution)/shard_map/reduce_scatter | solution.py:1505
  47.1 30.6 %collective-permute-start.7 = (bf16[1024,512]{1,0:T(8,128)(2,1)}, bf16[1024,512]{1,0:T(8,128)(2,1)}, u32[]{:S(2)}, u32[]{:S(2)}) collective-permute-start(bf16[1024,512]{1,0:T(8,128)(2,1)} %gate.13.refs_9_.refs_0_.refs_2_), channel_id=1, source_target_pairs={{0,2},{1,3},{2,0},{3,1},{4,6},{5,7},{6,4},{7,5},{8,10},{9,11},{10,... | collective-permute-start | bytes 3145736 | tf_op jit(solution)/shard_map/ppermute | solution.py:1351
  48.9 17.9 %copy-start.23 = (s32[1,1024]{1,0:T(1,128)S(1)}, s32[1,1024]{1,0:T(1,128)}, u32[]{:S(2)}) copy-start(s32[1,1024]{1,0:T(1,128)} %get-tuple-element.213) | copy-start | bytes 12292
  77.5 30.7 %collective-permute-start.5 = (bf16[1024,512]{1,0:T(8,128)(2,1)}, bf16[1024,512]{1,0:T(8,128)(2,1)}, u32[]{:S(2)}, u32[]{:S(2)}) collective-permute-start(bf16[1024,512]{1,0:T(8,128)(2,1)} %get-tuple-element.114.refs_0_.refs_2_.refs_1_), channel_id=1, source_target_pairs={{0,2},{1,3},{2,0},{3,1},{4,6},{5,7},{6,4},{7,5},{8,10},{9,11},{10,... | collective-permute-start | bytes 3145736 | tf_op jit(solution)/shard_map/ppermute | solution.py:1351
  77.8 18.0 %copy-start.22 = (s32[1,1024]{1,0:T(1,128)S(1)}, s32[1,1024]{1,0:T(1,128)}, u32[]{:S(2)}) copy-start(s32[1,1024]{1,0:T(1,128)} %get-tuple-element.212) | copy-start | bytes 12292
  106.1 49.9 %collective-permute-start.12 = (bf16[1024,512]{1,0:T(8,128)(2,1)}, bf16[1024,512]{1,0:T(8,128)(2,1)}, u32[]{:S(2)}, u32[]{:S(2)}) collective-permute-start(bf16[1024,512]{1,0:T(8,128)(2,1)} %get-tuple-element.126.refs_0_.refs_2_), channel_id=1, source_target_pairs={{0,2},{1,3},{2,0},{3,1},{4,6},{5,7},{6,4},{7,5},{8,10},{9,11},{10,... | collective-permute-start | bytes 3145736 | tf_op jit(solution)/shard_map/ppermute | solution.py:1351
  107.9 4.5 collective-permute-start.8
  107.9 89.5 %collective-permute-start.10 = (bf16[1024,512]{1,0:T(8,128)(2,1)}, bf16[1024,512]{1,0:T(8,128)(2,1)}, u32[]{:S(2)}, u32[]{:S(2)}) collective-permute-start(bf16[1024,512]{1,0:T(8,128)(2,1)} %gate.15.refs_17_.refs_0_.refs_2_), channel_id=1, source_target_pairs={{0,2},{1,3},{2,0},{3,1},{4,6},{5,7},{6,4},{7,5},{8,10},{9,11},{10,... | collective-permute-start | bytes 3145736 | tf_op jit(solution)/shard_map/ppermute | solution.py:1351
  153.9 60.1 %collective-permute-start.9 = (bf16[1024,512]{1,0:T(8,128)(2,1)}, bf16[1024,512]{1,0:T(8,128)(2,1)}, u32[]{:S(2)}, u32[]{:S(2)}) collective-permute-start(bf16[1024,512]{1,0:T(8,128)(2,1)} %get-tuple-element.124), channel_id=1, source_target_pairs={{0,2},{1,3},{2,0},{3,1},{4,6},{5,7},{6,4},{7,5},{8,10},{9,11},{10,... | collective-permute-start | bytes 3145736 | tf_op jit(solution)/shard_map/ppermute | solution.py:1351
  154.2 48.5 %collective-permute-start.11 = (bf16[1024,512]{1,0:T(8,128)(2,1)}, bf16[1024,512]{1,0:T(8,128)(2,1)}, u32[]{:S(2)}, u32[]{:S(2)}) collective-permute-start(bf16[1024,512]{1,0:T(8,128)(2,1)} %gate.16.refs_17_.refs_4_.refs_6_), channel_id=1, source_target_pairs={{0,2},{1,3},{2,0},{3,1},{4,6},{5,7},{6,4},{7,5},{8,10},{9,11},{10,... | collective-permute-start | bytes 3145736 | tf_op jit(solution)/shard_map/ppermute | solution.py:1351
  197.1 71.0 %collective-permute-start.13 = (bf16[1024,512]{1,0:T(8,128)(2,1)}, bf16[1024,512]{1,0:T(8,128)(2,1)}, u32[]{:S(2)}, u32[]{:S(2)}) collective-permute-start(bf16[1024,512]{1,0:T(8,128)(2,1)} %get-tuple-element.133), channel_id=1, source_target_pairs={{0,2},{1,3},{2,0},{3,1},{4,6},{5,7},{6,4},{7,5},{8,10},{9,11},{10,... | collective-permute-start | bytes 3145736 | tf_op jit(solution)/shard_map/ppermute | solution.py:1351
  268.1 33.1 %collective-permute-start.14 = (bf16[1040,512]{1,0:T(8,128)(2,1)}, bf16[1040,512]{1,0:T(8,128)(2,1)}, u32[]{:S(2)}, u32[]{:S(2)}) collective-permute-start(bf16[1040,512]{1,0:T(8,128)(2,1)} %get-tuple-element.145), channel_id=1, source_target_pairs={{0,2},{1,3},{2,0},{3,1},{4,6},{5,7},{6,4},{7,5},{8,10},{9,11},{10,... | collective-permute-start | bytes 3194888 | tf_op jit(solution)/shard_map/ppermute | solution.py:1351
  268.2 33.0 %copy-start.25 = (f32[512]{0:T(512)S(1)}, f32[512]{0:T(512)}, u32[]{:S(2)}) copy-start(f32[512]{0:T(512)} %param.23) | copy-start | bytes 6148
  299.3 32.3 %collective-permute-start.15 = (bf16[1040,512]{1,0:T(8,128)(2,1)}, bf16[1040,512]{1,0:T(8,128)(2,1)}, u32[]{:S(2)}, u32[]{:S(2)}) collective-permute-start(bf16[1040,512]{1,0:T(8,128)(2,1)} %get-tuple-element.150), channel_id=1, source_target_pairs={{0,2},{1,3},{2,0},{3,1},{4,6},{5,7},{6,4},{7,5},{8,10},{9,11},{10,... | collective-permute-start | bytes 3194888 | tf_op jit(solution)/shard_map/ppermute | solution.py:1351
  307.6 40.8 %collective-permute-start.17 = (bf16[1024,512]{1,0:T(8,128)(2,1)}, bf16[1024,512]{1,0:T(8,128)(2,1)}, u32[]{:S(2)}, u32[]{:S(2)}) collective-permute-start(bf16[1024,512]{1,0:T(8,128)(2,1)} %get-tuple-element.153.refs_0_.refs_2_), channel_id=1, source_target_pairs={{0,2},{1,3},{2,0},{3,1},{4,6},{5,7},{6,4},{7,5},{8,10},{9,11},{10,... | collective-permute-start | bytes 3145736 | tf_op jit(solution)/shard_map/ppermute | solution.py:1351
  307.9 16.2 %copy-start.27 = (f32[512]{0:T(512)S(1)}, f32[512]{0:T(512)}, u32[]{:S(2)}) copy-start(f32[512]{0:T(512)} %param.28) | copy-start | bytes 6148
  322.7 121.2 %collective-permute-start.21 = (bf16[4,256,2048]{2,1,0:T(8,128)(2,1)}, bf16[4,256,2048]{2,1,0:T(8,128)(2,1)}, u32[]{:S(2)}, u32[]{:S(2)}) collective-permute-start(bf16[4,256,2048]{2,1,0:T(8,128)(2,1)} %weight_blocks.8.refs_7_), channel_id=1, source_target_pairs={{0,4},{4,0},{8,12},{12,8},{16,20},{20,16},{24,28},{28,24},{1,5},{5... | collective-permute-start | bytes 12582920 | tf_op jit(solution)/shard_map/ppermute | solution.py:1168
  337.5 48.0 %collective-permute-start.16 = (bf16[1024,512]{1,0:T(8,128)(2,1)}, bf16[1024,512]{1,0:T(8,128)(2,1)}, u32[]{:S(2)}, u32[]{:S(2)}) collective-permute-start(bf16[1024,512]{1,0:T(8,128)(2,1)} %get-tuple-element.152.refs_0_.refs_2_), channel_id=1, source_target_pairs={{0,2},{1,3},{2,0},{3,1},{4,6},{5,7},{6,4},{7,5},{8,10},{9,11},{10,... | collective-permute-start | bytes 3145736 | tf_op jit(solution)/shard_map/ppermute | solution.py:1351
  413.5 45.7 %collective-permute-start.20 = (bf16[4,512,256]{2,1,0:T(8,128)(2,1)}, bf16[4,512,256]{2,1,0:T(8,128)(2,1)}, u32[]{:S(2)}, u32[]{:S(2)}) collective-permute-start(bf16[4,512,256]{2,1,0:T(8,128)(2,1)} %weight_blocks.9.refs_6_), channel_id=1, source_target_pairs={{0,8},{4,12},{8,0},{12,4},{16,24},{20,28},{24,16},{28,20},{1,9},{5... | collective-permute-start | bytes 3145736 | tf_op jit(solution)/shard_map/ppermute | solution.py:1168
  415.1 28.7 %collective-permute-start.19 = (bf16[1040,512]{1,0:T(8,128)(2,1)}, bf16[1040,512]{1,0:T(8,128)(2,1)}, u32[]{:S(2)}, u32[]{:S(2)}) collective-permute-start(bf16[1040,512]{1,0:T(8,128)(2,1)} %get-tuple-element.165), channel_id=1, source_target_pairs={{0,2},{1,3},{2,0},{3,1},{4,6},{5,7},{6,4},{7,5},{8,10},{9,11},{10,... | collective-permute-start | bytes 3194888 | tf_op jit(solution)/shard_map/ppermute | solution.py:1351
  426.4 67.5 %collective-permute-start.23 = (bf16[4,256,768]{2,1,0:T(8,128)(2,1)}, bf16[4,256,768]{2,1,0:T(8,128)(2,1)}, u32[]{:S(2)}, u32[]{:S(2)}) collective-permute-start(bf16[4,256,768]{2,1,0:T(8,128)(2,1)} %weight_blocks.10.refs_5_), channel_id=1, source_target_pairs={{0,4},{4,0},{8,12},{12,8},{16,20},{20,16},{24,28},{28,24},{1,5},{5... | collective-permute-start | bytes 4718600 | tf_op jit(solution)/shard_map/ppermute | solution.py:1168
  443.5 50.4 %collective-permute-start.18 = (bf16[1040,512]{1,0:T(8,128)(2,1)}, bf16[1040,512]{1,0:T(8,128)(2,1)}, u32[]{:S(2)}, u32[]{:S(2)}) collective-permute-start(bf16[1040,512]{1,0:T(8,128)(2,1)} %get-tuple-element.163), channel_id=1, source_target_pairs={{0,2},{1,3},{2,0},{3,1},{4,6},{5,7},{6,4},{7,5},{8,10},{9,11},{10,... | collective-permute-start | bytes 3194888 | tf_op jit(solution)/shard_map/ppermute | solution.py:1351
  465.6 38.6 %collective-permute-start.22 = (bf16[2,512,256]{2,1,0:T(8,128)(2,1)}, bf16[2,512,256]{2,1,0:T(8,128)(2,1)}, u32[]{:S(2)}, u32[]{:S(2)}) collective-permute-start(bf16[2,512,256]{2,1,0:T(8,128)(2,1)} %get-tuple-element.173), channel_id=1, source_target_pairs={{0,16},{4,20},{8,24},{12,28},{16,0},{20,4},{24,8},{28,12},{1,17},{... | collective-permute-start | bytes 1572872 | tf_op jit(solution)/shard_map/ppermute | solution.py:1168
  477.8 63.4 %collective-permute-start.27 = (bf16[4,256,768]{2,1,0:T(8,128)(2,1)}, bf16[4,256,768]{2,1,0:T(8,128)(2,1)}, u32[]{:S(2)}, u32[]{:S(2)}) collective-permute-start(bf16[4,256,768]{2,1,0:T(8,128)(2,1)} %weight_blocks.13.refs_10_), channel_id=1, source_target_pairs={{0,4},{4,0},{8,12},{12,8},{16,20},{20,16},{24,28},{28,24},{1,5},{5... | collective-permute-start | bytes 4718600 | tf_op jit(solution)/shard_map/ppermute | solution.py:1168
  478.5 58.3 %collective-permute-start.24 = (bf16[2,256,2048]{2,1,0:T(8,128)(2,1)}, bf16[2,256,2048]{2,1,0:T(8,128)(2,1)}, u32[]{:S(2)}, u32[]{:S(2)}) collective-permute-start(bf16[2,256,2048]{2,1,0:T(8,128)(2,1)} %get-tuple-element.185), channel_id=1, source_target_pairs={{0,8},{4,12},{8,0},{12,4},{16,24},{20,28},{24,16},{28,20},{1,9},{5... | collective-permute-start | bytes 6291464 | tf_op jit(solution)/shard_map/ppermute | solution.py:1168
  518.7 22.3 %copy-start.20 = (f32[8,512]{1,0:T(8,128)S(1)}, f32[8,512]{1,0:T(8,128)}, u32[]{:S(2)}) copy-start(f32[8,512]{1,0:T(8,128)} %get-tuple-element.139.refs_1_) | copy-start | bytes 49156
  518.7 22.3 %copy-start.21 = (f32[8,512]{1,0:T(8,128)S(1)}, f32[8,512]{1,0:T(8,128)}, u32[]{:S(2)}) copy-start(f32[8,512]{1,0:T(8,128)} %get-tuple-element.147.refs_8_) | copy-start | bytes 49156
  518.7 22.3 %copy-start.8 = (f32[8,2048]{1,0:T(8,128)S(1)}, f32[8,2048]{1,0:T(8,128)}, u32[]{:S(2)}) copy-start(f32[8,2048]{1,0:T(8,128)} %get-tuple-element.176) | copy-start | bytes 196612
  518.7 22.3 %copy-start.9 = (f32[8,2048]{1,0:T(8,128)S(1)}, f32[8,2048]{1,0:T(8,128)}, u32[]{:S(2)}) copy-start(f32[8,2048]{1,0:T(8,128)} %get-tuple-element.177) | copy-start | bytes 196612
  518.7 22.4 %copy-start.28 = (bf16[2,256,768]{2,1,0:T(8,128)(2,1)S(1)}, bf16[2,256,768]{2,1,0:T(8,128)(2,1)}, u32[]{:S(2)}) copy-start(bf16[2,256,768]{2,1,0:T(8,128)(2,1)} %get-tuple-element.188) | copy-start | bytes 2359300
  541.0 47.9 %collective-permute-start.25 = (bf16[1,256,2048]{2,1,0:T(8,128)(2,1)}, bf16[1,256,2048]{2,1,0:T(8,128)(2,1)S(1)}, u32[]{:S(2)}, u32[]{:S(2)}) collective-permute-start(bf16[1,256,2048]{2,1,0:T(8,128)(2,1)} %get-tuple-element.187), channel_id=1, source_target_pairs={{0,16},{4,20},{8,24},{12,28},{16,0},{20,4},{24,8},{28,12},{1,17},{... | collective-permute-start | bytes 3145736 | tf_op jit(solution)/shard_map/ppermute | solution.py:1168
  541.1 12.2 %copy-start.7 = (f32[8,512]{1,0:T(8,128)S(1)}, f32[8,512]{1,0:T(8,128)}, u32[]{:S(2)}) copy-start(f32[8,512]{1,0:T(8,128)} %get-tuple-element.180.refs_2_) | copy-start | bytes 49156
  541.1 12.2 %copy-start.17 = (f32[8,512]{1,0:T(8,128)S(1)}, f32[8,512]{1,0:T(8,128)}, u32[]{:S(2)}) copy-start(f32[8,512]{1,0:T(8,128)} %get-tuple-element.170.refs_1_) | copy-start | bytes 49156
  541.1 40.4 %collective-permute-start.26 = (bf16[2,256,768]{2,1,0:T(8,128)(2,1)S(1)}, bf16[2,256,768]{2,1,0:T(8,128)(2,1)S(1)}, u32[]{:S(2)}, u32[]{:S(2)}) collective-permute-start(bf16[2,256,768]{2,1,0:T(8,128)(2,1)S(1)} %copy-done.28), channel_id=1, source_target_pairs={{0,8},{4,12},{8,0},{12,4},{16,24},{20,28},{24,16},{28,20},{1,9},{5... | collective-permute-start | bytes 2359304 | tf_op jit(solution)/shard_map/ppermute | solution.py:1168
  551.3 57.2 %collective-permute-start.28 = (bf16[2,256,768]{2,1,0:T(8,128)(2,1)}, bf16[2,256,768]{2,1,0:T(8,128)(2,1)S(1)}, u32[]{:S(2)}, u32[]{:S(2)}) collective-permute-start(bf16[2,256,768]{2,1,0:T(8,128)(2,1)} %get-tuple-element.191), channel_id=1, source_target_pairs={{0,8},{4,12},{8,0},{12,4},{16,24},{20,28},{24,16},{28,20},{1,9},{5... | collective-permute-start | bytes 2359304 | tf_op jit(solution)/shard_map/ppermute | solution.py:1168
  585.9 28.7 %collective-permute-start.30 = (bf16[1,256,768]{2,1,0:T(8,128)(2,1)}, bf16[1,256,768]{2,1,0:T(8,128)(2,1)S(1)}, u32[]{:S(2)}, u32[]{:S(2)}) collective-permute-start(bf16[1,256,768]{2,1,0:T(8,128)(2,1)} %get-tuple-element.194), channel_id=1, source_target_pairs={{0,16},{4,20},{8,24},{12,28},{16,0},{20,4},{24,8},{28,12},{1,17},{... | collective-permute-start | bytes 1179656 | tf_op jit(solution)/shard_map/ppermute | solution.py:1168
  589.9 23.9 %copy-start.10 = (f32[13,8,128]{2,1,0:T(8,128)S(1)}, f32[13,8,128]{2,1,0:T(8,128)}, u32[]{:S(2)}) copy-start(f32[13,8,128]{2,1,0:T(8,128)} %get-tuple-element.183) | copy-start | bytes 159748
  589.9 23.9 %copy-start.11 = (f32[13,8,128]{2,1,0:T(8,128)S(1)}, f32[13,8,128]{2,1,0:T(8,128)}, u32[]{:S(2)}) copy-start(f32[13,8,128]{2,1,0:T(8,128)} %get-tuple-element.184) | copy-start | bytes 159748
  613.1 18.8 %collective-permute-start.31 = (bf16[1,256,768]{2,1,0:T(8,128)(2,1)}, bf16[1,256,768]{2,1,0:T(8,128)(2,1)S(1)}, u32[]{:S(2)}, u32[]{:S(2)}) collective-permute-start(bf16[1,256,768]{2,1,0:T(8,128)(2,1)} %get-tuple-element.196), channel_id=1, source_target_pairs={{0,16},{4,20},{8,24},{12,28},{16,0},{20,4},{24,8},{28,12},{1,17},{... | collective-permute-start | bytes 1179656 | tf_op jit(solution)/shard_map/ppermute | solution.py:1168
  613.1 7.7 %collective-permute-start.29 = (bf16[1,512,256]{2,1,0:T(8,128)(2,1)}, bf16[1,512,256]{2,1,0:T(8,128)(2,1)S(1)}, u32[]{:S(2)}, u32[]{:S(2)}) collective-permute-start(bf16[1,512,256]{2,1,0:T(8,128)(2,1)} %get-tuple-element.193), channel_id=1, source_target_pairs={{0,4},{4,0},{8,12},{12,8},{16,20},{20,16},{24,28},{28,24},{1,5},{5... | collective-permute-start | bytes 786440 | tf_op jit(solution)/shard_map/ppermute | solution.py:1168
  614.6 17.3 %copy-start.4 = (bf16[1,256,768]{2,1,0:T(8,128)(2,1)}, bf16[1,256,768]{2,1,0:T(8,128)(2,1)S(1)}, u32[]{:S(2)}) copy-start(bf16[1,256,768]{2,1,0:T(8,128)(2,1)S(1)} %collective-permute-done.30.refs_6_) | copy-start | bytes 1179652
  (15 other events, 116.6 us)
Sparse Core Ops, SparseCore 0:
  35.1 49.6 all-gather.1
  237.2 166.5 reduce-scatter.1
